TPU v7x, 32 devices: a whole 2x2x4 slice. The times are simulated.
32 devices in a mesh: gx: 4 (over z), gy: 4 (over x, core), gz: 2 (over y).
Axes of the slice: x: 2, y: 2, z: 4, core: 2. Of those that a mesh axis runs over, the one named last changes fastest.
Arguments:
- loads: bfloat16 [4, 4, 2, 1024, 256], P('gx', 'gy', 'gz'), may hold values from -6 to 6
- start: bfloat16 [4, 4, 2, 1024, 256], P('gx', 'gy', 'gz'), may hold values from -6 to 6
- interface_op: bfloat16 [4, 4, 2, 1024, 1024], P('gx', 'gy', 'gz'), as said below
- block_order: int32 [4, 4, 2, 8], P('gx', 'gy', 'gz'), may hold values from 0 to 7, each once within a row
- interface_weights: float32 [4, 4, 2, 1024], P('gx', 'gy', 'gz'), may hold values from 0.1 to 0.3
- coarse_modes: float32 [4, 4, 2, 32, 1024], P('gx', 'gy', 'gz'), as said below
- region_weights: float32 [4, 4, 2, 32, 16], P('gx', 'gy', 'gz'), as said below
- region_inverse: float32 [4, 256, 256], P('gx', ('gy', 'gz')), as said below
- root_inverse: float32 [64, 64], P('gx'), as said below
Outputs:
- solution: float32 [4, 4, 2, 1024, 256], P('gx', 'gy', 'gz')
Inputs may be any that keep to these rules, and one draw needn't show every extreme that they name: `block_order`: each row lists every number from 0 to 7 once. `interface_op`: each subdomain's matrix has a dominant positive diagonal and full dense off-diagonal part. `region_inverse`: dense, with a dominant positive diagonal. `root_inverse`: dense, with a dominant positive diagonal. `coarse_modes`: dense. `region_weights`: dense.
All inputs are finite; a program needn't handle non-finite values.
Results may differ from a plain program's by a relative error of at most 0.0003.
Values sent between devices are 32-bit elements; how exact they have to be, the bound alone decides.
No kernel may reach another device: no remote copies, remote signals or barrier semaphores. Data moves between devices by JAX's collectives and lax.ppermute only.
A program may use at most 64 MiB of HBM per device.

v0:
```python
import jax
import jax.numpy as jnp
from jax import lax
from jax.sharding import PartitionSpec as P

ITERS = 2


HIGH = lax.Precision.HIGHEST


def with_halo(cells, sides, width):
    for axis, dim in sides:
        count = lax.axis_size(axis)
        ends = count - 1
        head = lax.slice_in_dim(cells, 0, width, axis=dim)
        tail = lax.slice_in_dim(cells, cells.shape[dim] - width, cells.shape[dim], axis=dim)
        cells = jnp.concatenate(
            [
                lax.ppermute(tail, axis, [(i, (i + 1) % count) for i in range(ends)]),
                cells,
                lax.ppermute(head, axis, [((i + 1) % count, i) for i in range(ends)]),
            ],
            axis=dim,
        )
    return cells


def transpose_dot(left, right):
    return lax.dot_general(
        left, right, (((0,), (0,)), ((), ())), precision=HIGH, preferred_element_type=jnp.float32
    )


def per_device(
    loads,
    start,
    interface_op,
    block_order,
    interface_weights,
    coarse_modes,
    region_weights,
    region_inverse,
    root_inverse,
):
    iface = interface_op.shape[-1]
    cases = loads.shape[-1]
    block = iface // 8
    matrix = interface_op.reshape(iface, iface)
    perm = block_order.reshape(8)
    weights = interface_weights.reshape(iface, 1)
    modes = coarse_modes.reshape(coarse_modes.shape[-2], iface)
    mode_count = modes.shape[0]
    root_map = region_weights.reshape(mode_count, region_weights.shape[-1])
    region_rows = region_inverse.reshape(mode_count, region_inverse.shape[-1])
    target = loads.reshape(iface, cases).astype(jnp.float32)
    solution = start.reshape(iface, cases).astype(jnp.float32)
    for step in range(ITERS):
        blocks = solution.astype(jnp.bfloat16).reshape(8, block, cases)
        local_iter = blocks[perm].reshape(iface, cases)
        result = jnp.dot(matrix, local_iter, preferred_element_type=jnp.float32).reshape(
            8, block, cases
        )
        product = jnp.zeros_like(result).at[perm].set(result)
        padded_x = with_halo(product[0:2], (("gx", 0),), 1)
        padded_y = with_halo(product[2:4], (("gy", 0),), 1)
        padded_z = with_halo(product[4:6], (("gz", 0),), 1)
        assembled = jnp.concatenate(
            [
                (product[0] + padded_x[0])[None],
                (product[1] + padded_x[3])[None],
                (product[2] + padded_y[0])[None],
                (product[3] + padded_y[3])[None],
                (product[4] + padded_z[0])[None],
                (product[5] + padded_z[3])[None],
                product[6:],
            ],
            axis=0,
        ).reshape(iface, cases)
        residual = target - assembled
        coarse = jnp.dot(modes, residual, precision=HIGH, preferred_element_type=jnp.float32)
        coeff_piece = lax.all_gather(coarse, ("gy", "gz"), axis=0, tiled=True)
        weight_piece = lax.all_gather(root_map, ("gy", "gz"), axis=0, tiled=True)
        region_part = jnp.dot(
            region_rows, coeff_piece, precision=HIGH, preferred_element_type=jnp.float32
        )
        root_input = transpose_dot(weight_piece, coeff_piece)
        root_part = jnp.dot(
            root_inverse,
            lax.all_gather(root_input, "gx", axis=0, tiled=True),
            precision=HIGH,
            preferred_element_type=jnp.float32,
        )
        amplitude = region_part + jnp.dot(
            root_map, root_part, precision=HIGH, preferred_element_type=jnp.float32
        )
        solution = solution + weights * residual + transpose_dot(modes, amplitude)
    return solution.reshape(1, 1, 1, iface, cases)


def solution(mesh):
    placed = (
        P("gx", "gy", "gz", None, None),
        P("gx", "gy", "gz", None, None),
        P("gx", "gy", "gz", None, None),
        P("gx", "gy", "gz", None),
        P("gx", "gy", "gz", None),
        P("gx", "gy", "gz", None, None),
        P("gx", "gy", "gz", None, None),
        P("gx", ("gy", "gz"), None),
        P("gx", None),
    )
    return jax.shard_map(
        per_device,
        mesh=mesh,
        in_specs=placed,
        out_specs=P("gx", "gy", "gz", None, None),
        check_vma=False,
    )
```

profile of v0, /device:TPU:0, one launch (start us, length us, event | category | flops | bytes accessed | tf_op | source)
XLA Modules:
  0.0 169.9 jit_solution(15214542982226605263)
XLA Ops:
  0.8 2.4 %gather_fusion = bf16[8,128,256]{2,1,0:T(8,128)(2,1)} fusion(bf16[8,128,256]{2,1,0:T(8,128)(2,1)} %bitcast.115, s32[1024]{0:T(1024)S(1)} %pad_clamp_fusion), kind=kCustom, calls=%fused_computation | custom fusion | bytes 1048608 | tf_op jit(solution)/shard_map/gather | solution.py:60
  6.5 2.0 %scatter_fusion = f32[8,128,256]{2,1,0:T(8,128)S(1)} fusion(f32[8,128,256]{2,1,0:T(8,128)S(1)} %broadcast.23.clone, s32[8]{0:T(128)S(1)} %fusion.26, f32[8,128,256]{2,1,0:T(8,128)} %bitcast.112), kind=kCustom, calls=%fused_computation.2 | custom fusion | bytes 3145760 | tf_op jit(solution)/shard_map/scatter | solution.py:64
  8.5 4.9 %collective-permute-start = (f32[1,128,256]{2,1,0:T(8,128)S(1)}, f32[1,128,256]{2,1,0:T(8,128)S(1)}, u32[]{:S(2)}, u32[]{:S(2)}) collective-permute-start(f32[1,128,256]{2,1,0:T(8,128)S(1)} %slice.91), channel_id=1, source_target_pairs={{0,8},{8,16},{16,24},{1,9},{9,17},{17,25},{2,10},{10,18},{18,26},{... | collective-permute-start | bytes 393224 | tf_op jit(solution)/shard_map/ppermute | solution.py:20
  13.4 2.7 %collective-permute-done = f32[1,128,256]{2,1,0:T(8,128)S(1)} collective-permute-done((f32[1,128,256]{2,1,0:T(8,128)S(1)}, f32[1,128,256]{2,1,0:T(8,128)S(1)}, u32[]{:S(2)}, u32[]{:S(2)}) %collective-permute-start) | collective-permute-done | bytes 131104 | tf_op jit(solution)/shard_map/ppermute | solution.py:20
  18.4 2.0 %copy.23 = bf16[1,1,1,1024,256]{3,4,2,1,0:T(8,128)(2,1)} copy(bf16[1,1,1,1024,256]{4,3,2,1,0:T(8,128)(2,1)} %param.10) | data formatting | bytes 1048576 | tf_op args[1]
  20.4 2.1 %copy.24 = bf16[1,1,1,1024,256]{3,4,2,1,0:T(8,128)(2,1)} copy(bf16[1,1,1,1024,256]{4,3,2,1,0:T(8,128)(2,1)} %param.9) | data formatting | bytes 1048576 | tf_op args[0]
  22.5 2.2 %copy.39 = f32[1,1,1,1024,256]{4,3,2,1,0:T(8,128)} copy(bf16[1,1,1,1024,256]{3,4,2,1,0:T(8,128)(2,1)} %copy.24) | data formatting | bytes 1572864 | tf_op jit(solution)/shard_map/convert_element_type | solution.py:56
  25.4 16.0 %all-gather = f32[1,1,1,256,16]{4,2,1,0,3:T(1,128)S(1)} all-gather(f32[1,1,1,32,16]{4,2,1,0,3:T(1,128)} %copy.28), channel_id=2, replica_groups=mesh['gx'=4,'gy'=4,'gz'=2] {'gy','gz'}, dimensions={3}, use_global_device_ids=true | all-gather | bytes 18432 | tf_op jit(solution)/shard_map/all_gather | solution.py:83
  41.4 3.1 %collective-permute-start.2 = (f32[1,128,256]{2,1,0:T(8,128)}, f32[1,128,256]{2,1,0:T(8,128)S(1)}, u32[]{:S(2)}, u32[]{:S(2)}) collective-permute-start(f32[1,128,256]{2,1,0:T(8,128)} %get-tuple-element.14), channel_id=1, source_target_pairs={{0,2},{2,4},{4,6},{1,3},{3,5},{5,7},{8,10},{10,12},{12,14},{9,11},... | collective-permute-start | bytes 393224 | tf_op jit(solution)/shard_map/ppermute | solution.py:20
  45.8 3.0 %collective-permute-start.4 = (f32[1,128,256]{2,1,0:T(8,128)S(1)}, f32[1,128,256]{2,1,0:T(8,128)S(1)}, u32[]{:S(2)}, u32[]{:S(2)}) collective-permute-start(f32[1,128,256]{2,1,0:T(8,128)S(1)} %get-tuple-element.13), channel_id=1, source_target_pairs={{0,1},{2,3},{4,5},{6,7},{8,9},{10,11},{12,13},{14,15},{16,17},{18,... | collective-permute-start | bytes 393224 | tf_op jit(solution)/shard_map/ppermute | solution.py:20
  53.7 3.2 %collective-permute-done.5 = f32[1,128,256]{2,1,0:T(8,128)S(1)} collective-permute-done((f32[1,128,256]{2,1,0:T(8,128)S(1)}, f32[1,128,256]{2,1,0:T(8,128)S(1)}, u32[]{:S(2)}, u32[]{:S(2)}) %collective-permute-start.5) | collective-permute-done | bytes 131104 | tf_op jit(solution)/shard_map/ppermute | solution.py:22
  60.4 15.4 %all_gather.16 = f32[256,256]{1,0:T(8,128)S(1)} all-gather(f32[32,256]{1,0:T(8,128)S(1)} %convolution_bitcast_fusion.3), channel_id=1, replica_groups=mesh['gx'=4,'gy'=4,'gz'=2] {'gy','gz'}, dimensions={0}, use_global_device_ids=true | all-gather | bytes 294912 | tf_op jit(solution)/shard_map/all_gather | solution.py:82
  76.1 15.6 %all_gather.18 = f32[64,256]{1,0:T(8,128)S(1)} all-gather(f32[16,256]{1,0:T(8,128)S(1)} %convolution_bitcast_fusion.5), channel_id=1, replica_groups=mesh['gx'=4,'gy'=4,'gz'=2] {'gx'}, dimensions={0}, use_global_device_ids=true | all-gather | bytes 81920 | tf_op jit(solution)/shard_map/all_gather | solution.py:90
  92.0 2.5 %copy.35 = f32[1024,256]{0,1:T(8,128)} copy(f32[1024,256]{1,0:T(8,128)} %bitcast.107) | data formatting | bytes 2097152 | tf_op jit(solution)/shard_map/reshape | solution.py:79
  95.0 3.5 %fusion.29 = (bf16[1024,256]{0,1:T(8,128)(2,1)}, f32[1024,256]{0,1:T(8,128)}) fusion(f32[256,32]{0,1:T(8,128)S(1)} %convolution_add_fusion.1, f32[1,1,1,32,1024]{4,3,2,1,0:T(8,128)S(1)} %copy-done.6, f32[1024,256]{0,1:T(8,128)} %copy.35, bf16[1,1,1,1024,256]{3,4,2,1,0:T(8,128)(2,1)S(1)} %copy-done.3, f32[1024]{0:T(1024)} %bitcast.119, ...), kind=kOutput, calls=%fused_computation.56 | convolution fusion | flops 102498304 | bytes 3837952 | tf_op jit(solution)/shard_map/dot_general | solution.py:30
  106.5 4.0 %collective-permute-start.6 = (f32[1,128,256]{2,1,0:T(8,128)S(1)}, f32[1,128,256]{2,1,0:T(8,128)S(1)}, u32[]{:S(2)}, u32[]{:S(2)}) collective-permute-start(f32[1,128,256]{2,1,0:T(8,128)S(1)} %slice.98), channel_id=1, source_target_pairs={{0,8},{8,16},{16,24},{1,9},{9,17},{17,25},{2,10},{10,18},{18,26},{... | collective-permute-start | bytes 393224 | tf_op jit(solution)/shard_map/ppermute | solution.py:20
  110.5 2.5 %collective-permute-done.6 = f32[1,128,256]{2,1,0:T(8,128)S(1)} collective-permute-done((f32[1,128,256]{2,1,0:T(8,128)S(1)}, f32[1,128,256]{2,1,0:T(8,128)S(1)}, u32[]{:S(2)}, u32[]{:S(2)}) %collective-permute-start.6) | collective-permute-done | bytes 131104 | tf_op jit(solution)/shard_map/ppermute | solution.py:20
  116.9 3.6 %collective-permute-start.10 = (f32[1,128,256]{2,1,0:T(8,128)S(1)}, f32[1,128,256]{2,1,0:T(8,128)S(1)}, u32[]{:S(2)}, u32[]{:S(2)}) collective-permute-start(f32[1,128,256]{2,1,0:T(8,128)S(1)} %get-tuple-element.7), channel_id=1, source_target_pairs={{0,1},{2,3},{4,5},{6,7},{8,9},{10,11},{12,13},{14,15},{16,17},{18,... | collective-permute-start | bytes 393224 | tf_op jit(solution)/shard_map/ppermute | solution.py:20
  123.6 4.7 %collective-permute-done.11 = f32[1,128,256]{2,1,0:T(8,128)S(1)} collective-permute-done((f32[1,128,256]{2,1,0:T(8,128)S(1)}, f32[1,128,256]{2,1,0:T(8,128)S(1)}, u32[]{:S(2)}, u32[]{:S(2)}) %collective-permute-start.11) | collective-permute-done | bytes 131104 | tf_op jit(solution)/shard_map/ppermute | solution.py:22
  129.3 15.5 %all_gather.19 = f32[256,256]{1,0:T(8,128)S(1)} all-gather(f32[32,256]{1,0:T(8,128)S(1)} %convolution_bitcast_fusion.2), channel_id=1, replica_groups=mesh['gx'=4,'gy'=4,'gz'=2] {'gy','gz'}, dimensions={0}, use_global_device_ids=true | all-gather | bytes 294912 | tf_op jit(solution)/shard_map/all_gather | solution.py:82
  145.5 15.3 %all_gather.20 = f32[64,256]{1,0:T(8,128)S(1)} all-gather(f32[16,256]{1,0:T(8,128)S(1)} %convolution_bitcast_fusion.4), channel_id=1, replica_groups=mesh['gx'=4,'gy'=4,'gz'=2] {'gx'}, dimensions={0}, use_global_device_ids=true | all-gather | bytes 81920 | tf_op jit(solution)/shard_map/all_gather | solution.py:90
  160.9 2.6 %copy.38 = f32[1024,256]{0,1:T(8,128)} copy(f32[1024,256]{1,0:T(8,128)} %bitcast.108) | data formatting | bytes 2097152 | tf_op jit(solution)/shard_map/reshape | solution.py:79
  163.7 3.7 %fusion.11 = f32[1,1,1,1024,256]{3,4,2,1,0:T(8,128)} fusion(f32[256,32]{0,1:T(8,128)S(1)} %convolution_add_fusion, f32[1024,256]{0,1:T(8,128)} %get-tuple-element.18, f32[1024,256]{0,1:T(8,128)} %copy.38, bf16[1,1,1,1024,256]{3,4,2,1,0:T(8,128)(2,1)S(1)} %copy-done.4, f32[1024]{0:T(1024)S(1)} %bitcast.120, f32[1,1,1,32,1024]{4,3,2,1,0:T(8,128)S(1)} %copy-done.6), kind=kOutput, calls=%fused_computation.12 | convolution fusion | flops 101974016 | bytes 3837952 | tf_op jit(solution)/shard_map/dot_general | solution.py:30
  167.4 2.5 %copy.33 = f32[1,1,1,1024,256]{4,3,2,1,0:T(8,128)} copy(f32[1,1,1,1024,256]{3,4,2,1,0:T(8,128)} %fusion.11) | data formatting | bytes 2097152 | tf_op jit(solution)/shard_map/reshape | solution.py:98
  (85 shorter events, 34.3 us)
Async XLA Ops:
  0.0 3.3 %copy-start = (bf16[1,1,1,1024,1024]{4,3,2,1,0:T(8,128)(2,1)S(1)}, bf16[1,1,1,1024,1024]{4,3,2,1,0:T(8,128)(2,1)}, u32[]{:S(2)}) copy-start(bf16[1,1,1,1024,1024]{4,3,2,1,0:T(8,128)(2,1)} %param.11) | copy-start | bytes 6291460
  0.8 5.6 %copy-start.13 = (s32[8]{0:T(128)}, s32[8]{0:T(128)S(1)}, u32[]{:S(2)}) copy-start(s32[8]{0:T(128)S(1)} %fusion.26) | copy-start | bytes 100
  8.5 7.7 %collective-permute-start = (f32[1,128,256]{2,1,0:T(8,128)S(1)}, f32[1,128,256]{2,1,0:T(8,128)S(1)}, u32[]{:S(2)}, u32[]{:S(2)}) collective-permute-start(f32[1,128,256]{2,1,0:T(8,128)S(1)} %slice.91), channel_id=1, source_target_pairs={{0,8},{8,16},{16,24},{1,9},{9,17},{17,25},{2,10},{10,18},{18,26},{... | collective-permute-start | bytes 393224 | tf_op jit(solution)/shard_map/ppermute | solution.py:20
  17.0 7.7 %copy-start.9 = (f32[1,1,1,32,16]{3,4,2,1,0:T(8,128)S(1)}, f32[1,1,1,32,16]{3,4,2,1,0:T(8,128)}, u32[]{:S(2)}) copy-start(f32[1,1,1,32,16]{3,4,2,1,0:T(8,128)} %param.15) | copy-start | bytes 6148
  17.0 33.1 %collective-permute-start.1 = (f32[1,128,256]{2,1,0:T(8,128)}, f32[1,128,256]{2,1,0:T(8,128)}, u32[]{:S(2)}, u32[]{:S(2)}) collective-permute-start(f32[1,128,256]{2,1,0:T(8,128)} %get-tuple-element.16), channel_id=1, source_target_pairs={{8,0},{16,8},{24,16},{9,1},{17,9},{25,17},{10,2},{18,10},{26,18},{... | collective-permute-start | bytes 393224 | tf_op jit(solution)/shard_map/ppermute | solution.py:22
  25.4 32.9 %copy-start.1 = (f32[1,1,1,1024,256]{4,3,2,1,0:T(8,128)S(1)}, f32[1,1,1,1024,256]{4,3,2,1,0:T(8,128)}, u32[]{:S(2)}) copy-start(f32[1,1,1,1024,256]{4,3,2,1,0:T(8,128)} %copy.39) | copy-start | bytes 3145732
  41.4 10.3 %collective-permute-start.2 = (f32[1,128,256]{2,1,0:T(8,128)}, f32[1,128,256]{2,1,0:T(8,128)S(1)}, u32[]{:S(2)}, u32[]{:S(2)}) collective-permute-start(f32[1,128,256]{2,1,0:T(8,128)} %get-tuple-element.14), channel_id=1, source_target_pairs={{0,2},{2,4},{4,6},{1,3},{3,5},{5,7},{8,10},{10,12},{12,14},{9,11},... | collective-permute-start | bytes 393224 | tf_op jit(solution)/shard_map/ppermute | solution.py:20
  44.5 7.9 %collective-permute-start.3 = (f32[1,128,256]{2,1,0:T(8,128)}, f32[1,128,256]{2,1,0:T(8,128)S(1)}, u32[]{:S(2)}, u32[]{:S(2)}) collective-permute-start(f32[1,128,256]{2,1,0:T(8,128)} %get-tuple-element.15), channel_id=1, source_target_pairs={{2,0},{4,2},{6,4},{3,1},{5,3},{7,5},{10,8},{12,10},{14,12},{11,9},... | collective-permute-start | bytes 393224 | tf_op jit(solution)/shard_map/ppermute | solution.py:22
  45.8 7.2 %collective-permute-start.4 = (f32[1,128,256]{2,1,0:T(8,128)S(1)}, f32[1,128,256]{2,1,0:T(8,128)S(1)}, u32[]{:S(2)}, u32[]{:S(2)}) collective-permute-start(f32[1,128,256]{2,1,0:T(8,128)S(1)} %get-tuple-element.13), channel_id=1, source_target_pairs={{0,1},{2,3},{4,5},{6,7},{8,9},{10,11},{12,13},{14,15},{16,17},{18,... | collective-permute-start | bytes 393224 | tf_op jit(solution)/shard_map/ppermute | solution.py:20
  48.8 8.1 %collective-permute-start.5 = (f32[1,128,256]{2,1,0:T(8,128)S(1)}, f32[1,128,256]{2,1,0:T(8,128)S(1)}, u32[]{:S(2)}, u32[]{:S(2)}) collective-permute-start(f32[1,128,256]{2,1,0:T(8,128)S(1)} %get-tuple-element.11), channel_id=1, source_target_pairs={{1,0},{3,2},{5,4},{7,6},{9,8},{11,10},{13,12},{15,14},{17,16},{19,... | collective-permute-start | bytes 393224 | tf_op jit(solution)/shard_map/ppermute | solution.py:22
  53.7 6.0 %copy-start.6 = (f32[1,1,1,32,1024]{4,3,2,1,0:T(8,128)S(1)}, f32[1,1,1,32,1024]{4,3,2,1,0:T(8,128)}, u32[]{:S(2)}) copy-start(f32[1,1,1,32,1024]{4,3,2,1,0:T(8,128)} %param.14) | copy-start | bytes 393220
  58.3 33.5 %copy-start.8 = (f32[1,32,256]{2,1,0:T(8,128)S(1)}, f32[1,32,256]{2,1,0:T(8,128)}, u32[]{:S(2)}) copy-start(f32[1,32,256]{2,1,0:T(8,128)} %param.16) | copy-start | bytes 98308
  59.7 34.9 %copy-start.10 = (f32[16,64]{1,0:T(8,128)S(1)}, f32[16,64]{1,0:T(8,128)}, u32[]{:S(2)}) copy-start(f32[16,64]{1,0:T(8,128)} %param.17) | copy-start | bytes 12292
  59.7 35.2 %copy-start.3 = (bf16[1,1,1,1024,256]{3,4,2,1,0:T(8,128)(2,1)S(1)}, bf16[1,1,1,1024,256]{3,4,2,1,0:T(8,128)(2,1)}, u32[]{:S(2)}) copy-start(bf16[1,1,1,1024,256]{3,4,2,1,0:T(8,128)(2,1)} %copy.24) | copy-start | bytes 1572868
  59.7 35.2 %copy-start.7 = (bf16[1,1,1,1024,256]{3,4,2,1,0:T(8,128)(2,1)S(1)}, bf16[1,1,1,1024,256]{3,4,2,1,0:T(8,128)(2,1)}, u32[]{:S(2)}) copy-start(bf16[1,1,1,1024,256]{3,4,2,1,0:T(8,128)(2,1)} %copy.23) | copy-start | bytes 1572868
  106.5 21.9 %copy-start.2 = (f32[1,1,1,1024,256]{4,3,2,1,0:T(8,128)S(1)}, f32[1,1,1,1024,256]{4,3,2,1,0:T(8,128)}, u32[]{:S(2)}) copy-start(f32[1,1,1,1024,256]{4,3,2,1,0:T(8,128)} %copy.39) | copy-start | bytes 3145732
  106.5 6.5 %collective-permute-start.6 = (f32[1,128,256]{2,1,0:T(8,128)S(1)}, f32[1,128,256]{2,1,0:T(8,128)S(1)}, u32[]{:S(2)}, u32[]{:S(2)}) collective-permute-start(f32[1,128,256]{2,1,0:T(8,128)S(1)} %slice.98), channel_id=1, source_target_pairs={{0,8},{8,16},{16,24},{1,9},{9,17},{17,25},{2,10},{10,18},{18,26},{... | collective-permute-start | bytes 393224 | tf_op jit(solution)/shard_map/ppermute | solution.py:20
  113.0 8.9 %collective-permute-start.7 = (f32[1,128,256]{2,1,0:T(8,128)S(1)}, f32[1,128,256]{2,1,0:T(8,128)S(1)}, u32[]{:S(2)}, u32[]{:S(2)}) collective-permute-start(f32[1,128,256]{2,1,0:T(8,128)S(1)} %get-tuple-element.10), channel_id=1, source_target_pairs={{8,0},{16,8},{24,16},{9,1},{17,9},{25,17},{10,2},{18,10},{26,18},{... | collective-permute-start | bytes 393224 | tf_op jit(solution)/shard_map/ppermute | solution.py:22
  114.3 7.6 %collective-permute-start.8 = (f32[1,128,256]{2,1,0:T(8,128)S(1)}, f32[1,128,256]{2,1,0:T(8,128)S(1)}, u32[]{:S(2)}, u32[]{:S(2)}) collective-permute-start(f32[1,128,256]{2,1,0:T(8,128)S(1)} %get-tuple-element.8), channel_id=1, source_target_pairs={{0,2},{2,4},{4,6},{1,3},{3,5},{5,7},{8,10},{10,12},{12,14},{9,11},... | collective-permute-start | bytes 393224 | tf_op jit(solution)/shard_map/ppermute | solution.py:20
  115.6 6.3 %collective-permute-start.9 = (f32[1,128,256]{2,1,0:T(8,128)S(1)}, f32[1,128,256]{2,1,0:T(8,128)S(1)}, u32[]{:S(2)}, u32[]{:S(2)}) collective-permute-start(f32[1,128,256]{2,1,0:T(8,128)S(1)} %get-tuple-element.9), channel_id=1, source_target_pairs={{2,0},{4,2},{6,4},{3,1},{5,3},{7,5},{10,8},{12,10},{14,12},{11,9},... | collective-permute-start | bytes 393224 | tf_op jit(solution)/shard_map/ppermute | solution.py:22
  116.9 6.6 %collective-permute-start.10 = (f32[1,128,256]{2,1,0:T(8,128)S(1)}, f32[1,128,256]{2,1,0:T(8,128)S(1)}, u32[]{:S(2)}, u32[]{:S(2)}) collective-permute-start(f32[1,128,256]{2,1,0:T(8,128)S(1)} %get-tuple-element.7), channel_id=1, source_target_pairs={{0,1},{2,3},{4,5},{6,7},{8,9},{10,11},{12,13},{14,15},{16,17},{18,... | collective-permute-start | bytes 393224 | tf_op jit(solution)/shard_map/ppermute | solution.py:20
  120.6 7.7 %collective-permute-start.11 = (f32[1,128,256]{2,1,0:T(8,128)S(1)}, f32[1,128,256]{2,1,0:T(8,128)S(1)}, u32[]{:S(2)}, u32[]{:S(2)}) collective-permute-start(f32[1,128,256]{2,1,0:T(8,128)S(1)} %get-tuple-element.5), channel_id=1, source_target_pairs={{1,0},{3,2},{5,4},{7,6},{9,8},{11,10},{13,12},{15,14},{17,16},{19,... | collective-permute-start | bytes 393224 | tf_op jit(solution)/shard_map/ppermute | solution.py:22
  128.5 35.2 %copy-start.4 = (bf16[1,1,1,1024,256]{3,4,2,1,0:T(8,128)(2,1)S(1)}, bf16[1,1,1,1024,256]{3,4,2,1,0:T(8,128)(2,1)}, u32[]{:S(2)}) copy-start(bf16[1,1,1,1024,256]{3,4,2,1,0:T(8,128)(2,1)} %copy.24) | copy-start | bytes 1572868
  128.5 35.2 %copy-start.11 = (f32[1,1,1,1024]{3,2,1,0:T(1,128)S(1)}, f32[1,1,1,1024]{3,2,1,0:T(1,128)}, u32[]{:S(2)}) copy-start(f32[1,1,1,1024]{3,2,1,0:T(1,128)} %param.13) | copy-start | bytes 12292
  (3 other events, 4.9 us)
where the time goes:
time: 171 us; the launch traced here: 170 us
  blocking collectives  77.8 us (45%)
  starting transfers between devices  27.8 us (16%)
  local copies, waits for them, and re-layouts  27.6 us (16%)
  waiting for transfers between devices  14.8 us (9%)
  matrix products  14 us (8%)
  other arithmetic  7.53 us (4%)
    all_gather x2, blocking collectives, per_device(): lax.all_gather(root_input, 'gx', axis=0, tiled=True)  30.9 us
    all_gather x2, blocking collectives, per_device(): coeff_piece = lax.all_gather(coarse, ('gy', 'gz'), axis=0, tiled=True)  30.9 us
    ppermute x6, starting transfers between devices, with_halo(): lax.ppermute(tail, axis, [(i, (i + 1) % count) for i in range(ends)])  20 us
    all_gather x1, blocking collectives, per_device(): weight_piece = lax.all_gather(root_map, ('gy', 'gz'), axis=0, tiled=True)  16 us
    ppermute x6, waiting for transfers between devices, with_halo(): lax.ppermute(head, axis, [((i + 1) % count, i) for i in range(ends)])  7.95 us
    ppermute x6, starting transfers between devices, with_halo(): lax.ppermute(head, axis, [((i + 1) % count, i) for i in range(ends)])  7.87 us
    dot_general x4, matrix products, transpose_dot(): lax.dot_general(left, right, (((0,), (0,)), ((), ())), precision=HIGH, pr...  7.82 us
    ppermute x6, waiting for transfers between devices, with_halo(): lax.ppermute(tail, axis, [(i, (i + 1) % count) for i in range(ends)])  6.81 us
  transfers between devices with their start and end apart: 12, of which 5 were waited for; matrix products, arithmetic and copies ran while one was open for 6% of the time, Pallas kernels for 0%

commit v1 on v0

v1 whole, which is shorter than its diff:
```python
import functools
import itertools

import jax
import jax.numpy as jnp
from jax import lax
from jax.experimental import pallas as pl
from jax.experimental.pallas import tpu as pltpu
from jax.sharding import PartitionSpec as P

ITERS = 2
FACES = 8
AXES = ("gx", "gy", "gz")
F32 = jnp.float32
BF16 = jnp.bfloat16
VMEM = pl.BlockSpec(memory_space=pltpu.VMEM)
SMEM = pl.BlockSpec(memory_space=pltpu.SMEM)
ROWS = (((1,), (0,)), ((), ()))
COLS = (((0,), (0,)), ((), ()))


def neighbour_pairs(count, odd):
    pairs = []
    for low in range(odd, count - 1, 2):
        pairs += [(low, low + 1), (low + 1, low)]
    return pairs


def swap_list(sizes):
    swaps = []
    for dim, count in enumerate(sizes):
        for odd in (0, 1):
            if neighbour_pairs(count, odd):
                swaps.append((dim, odd))
    return swaps


def swap_face(dim, odd):
    high = (lax.axis_index(AXES[dim]) + odd + 1) % 2
    return 2 * dim + high


def partner(index, offset, count):
    if count & (count - 1):
        return (index + offset) % count
    return index ^ offset


def source(index, offset, count):
    if count & (count - 1):
        return lax.rem(index + count - offset, count)
    return index ^ offset


def split(value):
    high = value.astype(BF16)
    return high, (value - high.astype(F32)).astype(BF16)


def dot3(left, right, dims=ROWS):
    left_high, left_low = split(left)
    right_high, right_low = split(right)
    dot = functools.partial(lax.dot_general, dimension_numbers=dims, preferred_element_type=F32)
    return dot(left_high, right_high) + (dot(left_low, right_high) + dot(left_high, right_low))


def call(body, outs, ins, name, scratch=()):
    return pl.pallas_call(
        body,
        out_shape=[jax.ShapeDtypeStruct(shape, dtype) for shape, dtype in outs],
        in_specs=[SMEM if item.dtype == jnp.int32 else VMEM for item in ins],
        out_specs=[VMEM] * len(outs),
        scratch_shapes=list(scratch),
        compiler_params=pltpu.CompilerParams(vmem_limit_bytes=16 * 1024 * 1024),
        name=name,
    )(*ins)


def rows_of(index, height):
    return pl.ds(pl.multiple_of(index * height, height), height)


def multiply(swaps, order, matrix, read, loads, rest, messages, local_iter, product):
    height = matrix.shape[0] // FACES
    for j in range(FACES):
        local_iter[j * height : (j + 1) * height, :] = read(rows_of(order[j], height))
    product[...] = jnp.dot(matrix[...], local_iter[...], preferred_element_type=F32)
    inverse = [rows_of(order[j], height) for j in range(FACES)]
    for j in range(FACES):
        block = slice(j * height, (j + 1) * height)
        rest[inverse[j], :] = loads[inverse[j], :].astype(F32) - product[block, :]
    for (dim, odd), message in zip(swaps, messages):
        face = rows_of(swap_face(dim, odd), height)
        message[...] = loads[face, :].astype(F32) - rest[face, :]


def first_kernel(swaps, order, matrix, start, loads, rest, *more):
    messages, (local_iter, product) = more[: len(swaps)], more[len(swaps) :]

    def read(rows):
        return start[rows, :]

    multiply(swaps, order, matrix, read, loads, rest, messages, local_iter, product)


def residual_kernel(swaps, rest, modes, root_map, *more):
    halos, (residual, coarse, root) = more[: len(swaps)], more[len(swaps) :]
    height = rest.shape[0] // FACES
    residual[...] = rest[...]
    for (dim, odd), halo in zip(swaps, halos):
        face = rows_of(swap_face(dim, odd), height)
        residual[face, :] -= halo[...]
    coarse[...] = dot3(modes[...], residual[...])
    root[...] = dot3(root_map[...], coarse[...], COLS)


def root_kernel(count, coarse, root_inverse, root, *more):
    received, (message, stack) = more[: count - 1], more[count - 1 :]
    modes, height = coarse.shape[0], root.shape[0]
    me = lax.axis_index("gx")
    stack[rows_of(me, height), :] = root[...]
    for offset, piece in enumerate(received, 1):
        stack[rows_of(source(me, offset, count), height), :] = piece[...]
    message[:modes, :] = coarse[...]
    message[modes:, :] = dot3(root_inverse[...], stack[...])


def pair_kernel(modes, first, *more):
    received, out = more[:-1], more[-1]
    height = first.shape[0]
    total = first[modes:, :]
    out[:modes, :] = first[:modes, :]
    for k, piece in enumerate(received, 1):
        out[k * modes : (k + 1) * modes, :] = piece[:modes, :]
        total = total + piece[modes:, :]
    out[(len(received) + 1) * modes :, :] = total


def amplitude_of(members, sizes, region_rows, root_map, own, other, stack):
    modes = root_map.shape[0]
    y, z = lax.axis_index("gy"), lax.axis_index("gz")
    half = sizes[0] // 2
    count = len(members)
    for k, (dy, dz) in enumerate(members):
        at_y = 2 * source(y // 2, dy, half) + y % 2
        at_z = source(z, dz, sizes[1])
        piece = slice(k * modes, (k + 1) * modes)
        stack[rows_of(at_y * sizes[1] + at_z, modes), :] = own[piece, :]
        stack[rows_of((at_y ^ 1) * sizes[1] + at_z, modes), :] = other[piece, :]
    root_part = own[count * modes :, :] + other[count * modes :, :]
    return dot3(region_rows[...], stack[...]) + dot3(root_map[...], root_part)


def update(members, sizes, solution, residual, weights, modes, root_map, region_rows, own, other, stack, write):
    height = residual.shape[0] // FACES
    amplitude = amplitude_of(members, sizes, region_rows, root_map, own, other, stack)
    lanes = residual.shape[1]
    correction = dot3(modes[...], amplitude, COLS)
    for j in range(FACES):
        block = slice(j * height, (j + 1) * height)
        scale = jnp.broadcast_to(weights[:, block], (height, height)).T[:, :1]
        write(
            block,
            solution[block, :].astype(F32) + scale * residual[block, :] + correction[block, :],
        )


def middle_kernel(
    swaps, members, sizes, order, matrix, solution, loads, residual, weights, modes, root_map, region_rows,
    own, other, next_solution, rest, *more
):
    messages, (stack, local_iter, product) = more[: len(swaps)], more[len(swaps) :]

    def write(block, value):
        next_solution[block, :] = value

    update(members, sizes, solution, residual, weights, modes, root_map, region_rows, own, other, stack, write)

    def read(rows):
        return next_solution[rows, :].astype(BF16)

    multiply(swaps, order, matrix, read, loads, rest, messages, local_iter, product)


def last_kernel(
    members, sizes, solution, residual, weights, modes, root_map, region_rows, own, other, next_solution, stack
):
    def write(block, value):
        next_solution[block, :] = value

    update(members, sizes, solution, residual, weights, modes, root_map, region_rows, own, other, stack, write)


def per_device(
    loads,
    start,
    interface_op,
    block_order,
    interface_weights,
    coarse_modes,
    region_weights,
    region_inverse,
    root_inverse,
):
    sizes = tuple(lax.axis_size(axis) for axis in AXES)
    iface = interface_op.shape[-1]
    cases = loads.shape[-1]
    height = iface // FACES
    matrix = interface_op.reshape(iface, iface)
    order = block_order.reshape(FACES)
    weights = interface_weights.reshape(1, iface)
    modes = coarse_modes.reshape(coarse_modes.shape[-2], iface)
    mode_count = modes.shape[0]
    root_map = region_weights.reshape(mode_count, region_weights.shape[-1])
    root_modes = root_map.shape[1]
    region_rows = region_inverse.reshape(mode_count, region_inverse.shape[-1])
    target = loads.reshape(iface, cases)
    solution = start.reshape(iface, cases)

    swaps = swap_list(sizes)
    half = sizes[1] // 2
    members = list(itertools.product(range(half), range(sizes[2])))

    full = ((iface, cases), F32)
    face = ((height, cases), F32)
    work = [pltpu.VMEM((iface, cases), BF16), pltpu.VMEM((iface, cases), F32)]
    stack = [pltpu.VMEM((region_rows.shape[1], cases), F32)]

    for step in range(ITERS):
        if step == 0:
            rest, *messages = call(
                functools.partial(first_kernel, swaps),
                [full] + [face] * len(swaps),
                [order, matrix, solution, target],
                "first_product",
                work,
            )
        else:
            solution, rest, *messages = call(
                functools.partial(middle_kernel, swaps, members, sizes[1:]),
                [full, full] + [face] * len(swaps),
                [order, matrix, solution, target, residual, weights, modes, root_map, region_rows, own, other],
                "update_product",
                stack + work,
            )
        halos = [
            lax.ppermute(message, AXES[dim], neighbour_pairs(sizes[dim], odd))
            for (dim, odd), message in zip(swaps, messages)
        ]
        residual, coarse, root = call(
            functools.partial(residual_kernel, swaps),
            [full, ((mode_count, cases), F32), ((root_modes, cases), F32)],
            [rest, modes, root_map] + halos,
            "residual_coarse",
        )
        received = [
            lax.ppermute(root, "gx", [(i, partner(i, offset, sizes[0])) for i in range(sizes[0])])
            for offset in range(1, sizes[0])
        ]
        (message,) = call(
            functools.partial(root_kernel, sizes[0]),
            [((mode_count + root_modes, cases), F32)],
            [coarse, root_inverse, root] + received,
            "root_part",
            [pltpu.VMEM((root_inverse.shape[1], cases), F32)],
        )
        pieces = []
        for dy, dz in members[1:]:
            moves = [
                (y * sizes[2] + z, (2 * partner(y // 2, dy, half) + y % 2) * sizes[2] + partner(z, dz, sizes[2]))
                for y in range(sizes[1])
                for z in range(sizes[2])
            ]
            pieces.append(lax.ppermute(message, ("gy", "gz"), moves))
        (own,) = call(
            functools.partial(pair_kernel, mode_count),
            [((len(members) * mode_count + root_modes, cases), F32)],
            [message] + pieces,
            "pair_message",
        )
        other = lax.ppermute(own, "gy", neighbour_pairs(sizes[1], 0))
    (solution,) = call(
        functools.partial(last_kernel, members, sizes[1:]),
        [full],
        [solution, residual, weights, modes, root_map, region_rows, own, other],
        "update_last",
        stack,
    )
    return solution.reshape(1, 1, 1, iface, cases)


def solution(mesh):
    placed = (
        P("gx", "gy", "gz", None, None),
        P("gx", "gy", "gz", None, None),
        P("gx", "gy", "gz", None, None),
        P("gx", "gy", "gz", None),
        P("gx", "gy", "gz", None),
        P("gx", "gy", "gz", None, None),
        P("gx", "gy", "gz", None, None),
        P("gx", ("gy", "gz"), None),
        P("gx", None),
    )
    return jax.shard_map(
        per_device,
        mesh=mesh,
        in_specs=placed,
        out_specs=P("gx", "gy", "gz", None, None),
        check_vma=False,
    )
```

time: 171 us -> 70.8 us (0.41)
  blocking collectives: 77.8 us -> 0 us
  local copies, waits for them, and re-layouts: 27.6 us -> 8.02 us
  matrix products: 14 us -> 0 us
  Pallas kernels: 0 us -> 9.75 us
  waiting for transfers between devices: 14.8 us -> 23.2 us
  other arithmetic: 7.53 us -> 0 us
    all_gather x5 -> x0, blocking collectives: 77.8 us -> none  [the longest x2 30.9 us: per_device(): lax.all_gather(root_input, 'gx', axis=0, tiled=True)]
    dot_general x14 -> x0, matrix products: 14 us -> none  [the longest x4 7.82 us: transpose_dot(): lax.dot_general(left, right, (((0,), (0,)), ((), ())), precision=HIGH, pr...]
    reshape x6 -> x0, local copies, waits for them, and re-layouts: 11.5 us -> none  [the longest x2 5.11 us: per_device(): assembled = jnp.concatenate([(product[0] + padded_x[0])[None], (product[1...]
    pallas_call x0 -> x9, Pallas kernels: none -> 9.75 us  [call(): pl.pallas_call(body, out_shape=[jax.ShapeDtypeStruct(shape, dtype) for sh...]
    ppermute x12 -> x24, waiting for transfers between devices: 14.8 us -> 23.2 us  [the longest x10 7.37 us: per_device(): lax.ppermute(message, AXES[dim], neighbour_pairs(sizes[dim], odd))]
    unnamed x10 -> x0, other arithmetic: 4.34 us -> none
    scatter x2 -> x0, local copies, waits for them, and re-layouts: 3.99 us -> none  [per_device(): product = jnp.zeros_like(result).at[perm].set(result)]
    gather x2 -> x0, local copies, waits for them, and re-layouts: 3.92 us -> none  [per_device(): local_iter = blocks[perm].reshape(iface, cases)]
  transfers between devices with their start and end apart: 12 -> 24, of which waited for: 5 -> 14; matrix products, arithmetic and copies ran while one was open for 6% -> 1% of each run, Pallas kernels for 0% -> 0%
where the time goes in v1:
time: 70.8 us; the launch traced here: 70.3 us
  starting transfers between devices  29.2 us (41%)
  waiting for transfers between devices  23.2 us (33%)
  Pallas kernels  9.75 us (14%)
  local copies, waits for them, and re-layouts  8.02 us (11%)
    ppermute x6, starting transfers between devices, per_device(): lax.ppermute(root, 'gx', [(i, partner(i, offset, sizes[0])) for i in rang...  11 us
    pallas_call x9, Pallas kernels, call(): pl.pallas_call(body, out_shape=[jax.ShapeDtypeStruct(shape, dtype) for sh...  9.75 us
    ppermute x6, starting transfers between devices, per_device(): pieces.append(lax.ppermute(message, ('gy', 'gz'), moves))  9.15 us
    ppermute x10, starting transfers between devices, per_device(): lax.ppermute(message, AXES[dim], neighbour_pairs(sizes[dim], odd))  8.89 us
    unnamed x31, local copies, waits for them, and re-layouts  8.02 us
    ppermute x10, waiting for transfers between devices, per_device(): lax.ppermute(message, AXES[dim], neighbour_pairs(sizes[dim], odd))  7.37 us
    ppermute x6, waiting for transfers between devices, per_device(): lax.ppermute(root, 'gx', [(i, partner(i, offset, sizes[0])) for i in rang...  6.97 us
    ppermute x6, waiting for transfers between devices, per_device(): pieces.append(lax.ppermute(message, ('gy', 'gz'), moves))  6.15 us
  transfers between devices with their start and end apart: 24, of which 14 were waited for; matrix products, arithmetic and copies ran while one was open for 1% of the time, Pallas kernels for 0%

profile of v1, /device:TPU:0, one launch (start us, length us, event | category | flops | bytes accessed | tf_op | source)
XLA Modules:
  0.0 70.3 jit_solution(15766429686678674783)
XLA Ops:
  0.0 1.6 %copy-done = bf16[1,1,1,1024,1024]{4,3,2,1,0:T(8,128)(2,1)S(1)} copy-done((bf16[1,1,1,1024,1024]{4,3,2,1,0:T(8,128)(2,1)S(1)}, bf16[1,1,1,1024,1024]{4,3,2,1,0:T(8,128)(2,1)}, u32[]{:S(2)}) %copy-start) | copy-done | bytes 2097176
  4.3 2.1 %first_product.1 = (f32[1024,256]{1,0:T(8,128)S(1)}, f32[128,256]{1,0:T(8,128)}, f32[128,256]{1,0:T(8,128)}, f32[128,256]{1,0:T(8,128)}, f32[128,256]{1,0:T(8,128)}, /*index=5*/f32[128,256]{1,0:T(8,128)}) custom-call(s32[8]{0:T(128)S(1)} %bitcast.27, bf16[1024,1024]{1,0:T(8,128)(2,1)S(1)} %bitcast.9, bf16[1024,256]{1,0:T(8,128)(2,1)S(1)} %bitcast.15, ...), custom_call_target="tpu_custom_call" | custom-call | tf_op jit(solution)/shard_map/first_product/pallas_call | solution.py:68
  7.4 3.0 %collective-permute-start = (f32[128,256]{1,0:T(8,128)}, f32[128,256]{1,0:T(8,128)S(1)}, u32[]{:S(2)}, u32[]{:S(2)}) collective-permute-start(f32[128,256]{1,0:T(8,128)} %get-tuple-element.25), channel_id=1, source_target_pairs={{0,8},{8,0},{16,24},{24,16},{1,9},{9,1},{17,25},{25,17},{2,10},{10... | collective-permute-start | bytes 393224 | tf_op jit(solution)/shard_map/ppermute | solution.py:247
  12.5 1.5 %collective-permute-start.4 = (f32[128,256]{1,0:T(8,128)}, f32[128,256]{1,0:T(8,128)}, u32[]{:S(2)}, u32[]{:S(2)}) collective-permute-start(f32[128,256]{1,0:T(8,128)} %get-tuple-element.29), channel_id=1, source_target_pairs={{0,1},{1,0},{2,3},{3,2},{4,5},{5,4},{6,7},{7,6},{8,9},{9,8},{10,11... | collective-permute-start | bytes 393224 | tf_op jit(solution)/shard_map/ppermute | solution.py:247
  14.8 3.0 %collective-permute-done.4.more_4_ = f32[128,256]{1,0:T(8,128)} collective-permute-done((f32[128,256]{1,0:T(8,128)}, f32[128,256]{1,0:T(8,128)}, u32[]{:S(2)}, u32[]{:S(2)}) %collective-permute-start.4) | collective-permute-done | bytes 131104 | tf_op jit(solution)/shard_map/ppermute | solution.py:247
  19.1 1.8 %residual_coarse.2 = (f32[1024,256]{1,0:T(8,128)S(1)}, f32[32,256]{1,0:T(8,128)S(1)}, f32[16,256]{1,0:T(8,128)S(1)}) custom-call(f32[1024,256]{1,0:T(8,128)S(1)} %copy-done.8, f32[32,1024]{1,0:T(8,128)S(1)} %bitcast.11, f32[32,16]{1,0:T(8,128)S(1)} %bitcast.19, f32[128,256]{1,0:T(8,128)S(1)} %collective-permute-done.more_0_, ...), custom_call_target="tpu_custom_call" | custom-call | tf_op jit(solution)/shard_map/residual_coarse/pallas_call | solution.py:68
  20.9 2.5 %collective-permute-start.7 = (f32[16,256]{1,0:T(8,128)S(1)}, f32[16,256]{1,0:T(8,128)S(1)}, u32[]{:S(2)}, u32[]{:S(2)}) collective-permute-start(f32[16,256]{1,0:T(8,128)S(1)} %get-tuple-element.32.root), channel_id=1, source_target_pairs={{0,24},{8,16},{16,8},{24,0},{1,25},{9,17},{17,9},{25,1},{2,26},{10... | collective-permute-start | bytes 49160 | tf_op jit(solution)/shard_map/ppermute | solution.py:257
  23.4 3.4 %collective-permute-start.6 = (f32[16,256]{1,0:T(8,128)S(1)}, f32[16,256]{1,0:T(8,128)S(1)}, u32[]{:S(2)}, u32[]{:S(2)}) collective-permute-start(f32[16,256]{1,0:T(8,128)S(1)} %get-tuple-element.32.root), channel_id=1, source_target_pairs={{0,16},{8,24},{16,0},{24,8},{1,17},{9,25},{17,1},{25,9},{2,18},{10... | collective-permute-start | bytes 49160 | tf_op jit(solution)/shard_map/ppermute | solution.py:257
  26.7 2.0 %collective-permute-done.6.more_1_ = f32[16,256]{1,0:T(8,128)S(1)} collective-permute-done((f32[16,256]{1,0:T(8,128)S(1)}, f32[16,256]{1,0:T(8,128)S(1)}, u32[]{:S(2)}, u32[]{:S(2)}) %collective-permute-start.6) | collective-permute-done | bytes 16416 | tf_op jit(solution)/shard_map/ppermute | solution.py:257
  28.8 1.7 %collective-permute-done.5.more_0_ = f32[16,256]{1,0:T(8,128)S(1)} collective-permute-done((f32[16,256]{1,0:T(8,128)S(1)}, f32[16,256]{1,0:T(8,128)S(1)}, u32[]{:S(2)}, u32[]{:S(2)}) %collective-permute-start.5) | collective-permute-done | bytes 16416 | tf_op jit(solution)/shard_map/ppermute | solution.py:257
  31.3 3.7 %collective-permute-start.10 = (f32[48,256]{1,0:T(8,128)S(1)}, f32[48,256]{1,0:T(8,128)S(1)}, u32[]{:S(2)}, u32[]{:S(2)}) collective-permute-start(f32[48,256]{1,0:T(8,128)S(1)} %root_part.2.first), channel_id=1, source_target_pairs={{0,5},{1,4},{2,7},{3,6},{4,1},{5,0},{6,3},{7,2},{8,13},{9,12},{10,... | collective-permute-start | bytes 147464 | tf_op jit(solution)/shard_map/ppermute | solution.py:274
  35.6 1.5 %collective-permute-done.10.more_2_ = f32[48,256]{1,0:T(8,128)S(1)} collective-permute-done((f32[48,256]{1,0:T(8,128)S(1)}, f32[48,256]{1,0:T(8,128)S(1)}, u32[]{:S(2)}, u32[]{:S(2)}) %collective-permute-start.10) | collective-permute-done | bytes 49184 | tf_op jit(solution)/shard_map/ppermute | solution.py:274
  37.1 2.0 %collective-permute-done.9.more_1_ = f32[48,256]{1,0:T(8,128)S(1)} collective-permute-done((f32[48,256]{1,0:T(8,128)S(1)}, f32[48,256]{1,0:T(8,128)S(1)}, u32[]{:S(2)}, u32[]{:S(2)}) %collective-permute-start.9) | collective-permute-done | bytes 49184 | tf_op jit(solution)/shard_map/ppermute | solution.py:274
  39.2 1.4 %collective-permute-done.11.other = f32[144,256]{1,0:T(8,128)S(1)} collective-permute-done((f32[144,256]{1,0:T(8,128)S(1)}, f32[144,256]{1,0:T(8,128)S(1)}, u32[]{:S(2)}, u32[]{:S(2)}) %collective-permute-start.11) | collective-permute-done | bytes 147488 | tf_op jit(solution)/shard_map/ppermute | solution.py:281
  40.6 2.9 %update_product.1 = (f32[1024,256]{1,0:T(8,128)S(1)}, f32[1024,256]{1,0:T(8,128)S(1)}, f32[128,256]{1,0:T(8,128)S(1)}, f32[128,256]{1,0:T(8,128)S(1)}, f32[128,2...) custom-call(s32[8]{0:T(128)S(1)} %bitcast.28, bf16[1024,1024]{1,0:T(8,128)(2,1)S(1)} %bitcast.10, ...), custom_call_target="tpu_custom_call" | custom-call | tf_op jit(solution)/shard_map/update_product/pallas_call | solution.py:68
  45.8 3.3 %collective-permute-done.12.more_0_ = f32[128,256]{1,0:T(8,128)S(1)} collective-permute-done((f32[128,256]{1,0:T(8,128)S(1)}, f32[128,256]{1,0:T(8,128)S(1)}, u32[]{:S(2)}, u32[]{:S(2)}) %collective-permute-start.12) | collective-permute-done | bytes 131104 | tf_op jit(solution)/shard_map/ppermute | solution.py:247
  50.9 2.2 %collective-permute-start.19 = (f32[16,256]{1,0:T(8,128)S(1)}, f32[16,256]{1,0:T(8,128)S(1)}, u32[]{:S(2)}, u32[]{:S(2)}) collective-permute-start(f32[16,256]{1,0:T(8,128)S(1)} %get-tuple-element.42.root), channel_id=1, source_target_pairs={{0,24},{8,16},{16,8},{24,0},{1,25},{9,17},{17,9},{25,1},{2,26},{10... | collective-permute-start | bytes 49160 | tf_op jit(solution)/shard_map/ppermute | solution.py:257
  53.1 2.4 %collective-permute-start.18 = (f32[16,256]{1,0:T(8,128)S(1)}, f32[16,256]{1,0:T(8,128)S(1)}, u32[]{:S(2)}, u32[]{:S(2)}) collective-permute-start(f32[16,256]{1,0:T(8,128)S(1)} %get-tuple-element.42.root), channel_id=1, source_target_pairs={{0,16},{8,24},{16,0},{24,8},{1,17},{9,25},{17,1},{25,9},{2,18},{10... | collective-permute-start | bytes 49160 | tf_op jit(solution)/shard_map/ppermute | solution.py:257
  56.5 1.4 %collective-permute-done.18.more_1_ = f32[16,256]{1,0:T(8,128)S(1)} collective-permute-done((f32[16,256]{1,0:T(8,128)S(1)}, f32[16,256]{1,0:T(8,128)S(1)}, u32[]{:S(2)}, u32[]{:S(2)}) %collective-permute-start.18) | collective-permute-done | bytes 16416 | tf_op jit(solution)/shard_map/ppermute | solution.py:257
  57.9 1.4 %collective-permute-done.17.more_0_ = f32[16,256]{1,0:T(8,128)S(1)} collective-permute-done((f32[16,256]{1,0:T(8,128)S(1)}, f32[16,256]{1,0:T(8,128)S(1)}, u32[]{:S(2)}, u32[]{:S(2)}) %collective-permute-start.17) | collective-permute-done | bytes 16416 | tf_op jit(solution)/shard_map/ppermute | solution.py:257
  59.4 3.4 %collective-permute-start.22 = (f32[48,256]{1,0:T(8,128)S(1)}, f32[48,256]{1,0:T(8,128)S(1)}, u32[]{:S(2)}, u32[]{:S(2)}) collective-permute-start(f32[48,256]{1,0:T(8,128)S(1)} %root_part.3.first), channel_id=1, source_target_pairs={{0,5},{1,4},{2,7},{3,6},{4,1},{5,0},{6,3},{7,2},{8,13},{9,12},{10,... | collective-permute-start | bytes 147464 | tf_op jit(solution)/shard_map/ppermute | solution.py:274
  62.9 1.4 %collective-permute-start.20 = (f32[48,256]{1,0:T(8,128)S(1)}, f32[48,256]{1,0:T(8,128)S(1)}, u32[]{:S(2)}, u32[]{:S(2)}) collective-permute-start(f32[48,256]{1,0:T(8,128)S(1)} %root_part.3.first), channel_id=1, source_target_pairs={{0,1},{1,0},{2,3},{3,2},{4,5},{5,4},{6,7},{7,6},{8,9},{9,8},{10,11... | collective-permute-start | bytes 147464 | tf_op jit(solution)/shard_map/ppermute | solution.py:274
  65.3 1.6 %collective-permute-done.21.more_1_ = f32[48,256]{1,0:T(8,128)S(1)} collective-permute-done((f32[48,256]{1,0:T(8,128)S(1)}, f32[48,256]{1,0:T(8,128)S(1)}, u32[]{:S(2)}, u32[]{:S(2)}) %collective-permute-start.21) | collective-permute-done | bytes 49184 | tf_op jit(solution)/shard_map/ppermute | solution.py:274
  68.4 1.9 %update_last.1 = f32[1024,256]{1,0:T(8,128)} custom-call(f32[1024,256]{1,0:T(8,128)S(1)} %get-tuple-element.33.solution, f32[1024,256]{1,0:T(8,128)S(1)} %get-tuple-element.40.residual, f32[1,1024]{1,0:T(1,128)S(1)} %bitcast.26, f32[32,1024]{1,0:T(8,128)S(1)} %bitcast.14, f32[32,16]{1,0:T(8,128)S(1)} %bitcast.22, f32[32,256]{1,0:T(8,128)S(1)} %bitcast.24, ...), custom_call_target="tpu_custom_call" | custom-call | tf_op jit(solution)/shard_map/update_last/pallas_call | solution.py:68
  (64 shorter events, 17.0 us)
Async XLA Ops:
  7.4 7.4 %collective-permute-start = (f32[128,256]{1,0:T(8,128)}, f32[128,256]{1,0:T(8,128)S(1)}, u32[]{:S(2)}, u32[]{:S(2)}) collective-permute-start(f32[128,256]{1,0:T(8,128)} %get-tuple-element.25), channel_id=1, source_target_pairs={{0,8},{8,0},{16,24},{24,16},{1,9},{9,1},{17,25},{25,17},{2,10},{10... | collective-permute-start | bytes 393224 | tf_op jit(solution)/shard_map/ppermute | solution.py:247
  10.5 4.3 %collective-permute-start.1 = (f32[128,256]{1,0:T(8,128)}, f32[128,256]{1,0:T(8,128)S(1)}, u32[]{:S(2)}, u32[]{:S(2)}) collective-permute-start(f32[128,256]{1,0:T(8,128)} %get-tuple-element.26), channel_id=1, source_target_pairs={{8,16},{16,8},{9,17},{17,9},{10,18},{18,10},{11,19},{19,11},{12,20... | collective-permute-start | bytes 393224 | tf_op jit(solution)/shard_map/ppermute | solution.py:247
  11.1 3.7 %collective-permute-start.2 = (f32[128,256]{1,0:T(8,128)}, f32[128,256]{1,0:T(8,128)}, u32[]{:S(2)}, u32[]{:S(2)}) collective-permute-start(f32[128,256]{1,0:T(8,128)} %get-tuple-element.27), channel_id=1, source_target_pairs={{0,2},{2,0},{4,6},{6,4},{1,3},{3,1},{5,7},{7,5},{8,10},{10,8},{12,... | collective-permute-start | bytes 393224 | tf_op jit(solution)/shard_map/ppermute | solution.py:247
  11.2 3.6 %collective-permute-start.3 = (f32[128,256]{1,0:T(8,128)}, f32[128,256]{1,0:T(8,128)}, u32[]{:S(2)}, u32[]{:S(2)}) collective-permute-start(f32[128,256]{1,0:T(8,128)} %get-tuple-element.28), channel_id=1, source_target_pairs={{2,4},{4,2},{3,5},{5,3},{10,12},{12,10},{11,13},{13,11},{18,20},{2... | collective-permute-start | bytes 393224 | tf_op jit(solution)/shard_map/ppermute | solution.py:247
  12.5 5.3 %collective-permute-start.4 = (f32[128,256]{1,0:T(8,128)}, f32[128,256]{1,0:T(8,128)}, u32[]{:S(2)}, u32[]{:S(2)}) collective-permute-start(f32[128,256]{1,0:T(8,128)} %get-tuple-element.29), channel_id=1, source_target_pairs={{0,1},{1,0},{2,3},{3,2},{4,5},{5,4},{6,7},{7,6},{8,9},{9,8},{10,11... | collective-permute-start | bytes 393224 | tf_op jit(solution)/shard_map/ppermute | solution.py:247
  20.9 5.9 %collective-permute-start.7 = (f32[16,256]{1,0:T(8,128)S(1)}, f32[16,256]{1,0:T(8,128)S(1)}, u32[]{:S(2)}, u32[]{:S(2)}) collective-permute-start(f32[16,256]{1,0:T(8,128)S(1)} %get-tuple-element.32.root), channel_id=1, source_target_pairs={{0,24},{8,16},{16,8},{24,0},{1,25},{9,17},{17,9},{25,1},{2,26},{10... | collective-permute-start | bytes 49160 | tf_op jit(solution)/shard_map/ppermute | solution.py:257
  23.4 5.4 %collective-permute-start.6 = (f32[16,256]{1,0:T(8,128)S(1)}, f32[16,256]{1,0:T(8,128)S(1)}, u32[]{:S(2)}, u32[]{:S(2)}) collective-permute-start(f32[16,256]{1,0:T(8,128)S(1)} %get-tuple-element.32.root), channel_id=1, source_target_pairs={{0,16},{8,24},{16,0},{24,8},{1,17},{9,25},{17,1},{25,9},{2,18},{10... | collective-permute-start | bytes 49160 | tf_op jit(solution)/shard_map/ppermute | solution.py:257
  26.7 3.7 %collective-permute-start.5 = (f32[16,256]{1,0:T(8,128)S(1)}, f32[16,256]{1,0:T(8,128)S(1)}, u32[]{:S(2)}, u32[]{:S(2)}) collective-permute-start(f32[16,256]{1,0:T(8,128)S(1)} %get-tuple-element.32.root), channel_id=1, source_target_pairs={{0,8},{8,0},{16,24},{24,16},{1,9},{9,1},{17,25},{25,17},{2,10},{10... | collective-permute-start | bytes 49160 | tf_op jit(solution)/shard_map/ppermute | solution.py:257
  31.3 5.8 %collective-permute-start.10 = (f32[48,256]{1,0:T(8,128)S(1)}, f32[48,256]{1,0:T(8,128)S(1)}, u32[]{:S(2)}, u32[]{:S(2)}) collective-permute-start(f32[48,256]{1,0:T(8,128)S(1)} %root_part.2.first), channel_id=1, source_target_pairs={{0,5},{1,4},{2,7},{3,6},{4,1},{5,0},{6,3},{7,2},{8,13},{9,12},{10,... | collective-permute-start | bytes 147464 | tf_op jit(solution)/shard_map/ppermute | solution.py:274
  35.0 4.1 %collective-permute-start.9 = (f32[48,256]{1,0:T(8,128)S(1)}, f32[48,256]{1,0:T(8,128)S(1)}, u32[]{:S(2)}, u32[]{:S(2)}) collective-permute-start(f32[48,256]{1,0:T(8,128)S(1)} %root_part.2.first), channel_id=1, source_target_pairs={{0,4},{1,5},{2,6},{3,7},{4,0},{5,1},{6,2},{7,3},{8,12},{9,13},{10,... | collective-permute-start | bytes 147464 | tf_op jit(solution)/shard_map/ppermute | solution.py:274
  35.0 4.1 %collective-permute-start.8 = (f32[48,256]{1,0:T(8,128)S(1)}, f32[48,256]{1,0:T(8,128)S(1)}, u32[]{:S(2)}, u32[]{:S(2)}) collective-permute-start(f32[48,256]{1,0:T(8,128)S(1)} %root_part.2.first), channel_id=1, source_target_pairs={{0,1},{1,0},{2,3},{3,2},{4,5},{5,4},{6,7},{7,6},{8,9},{9,8},{10,11... | collective-permute-start | bytes 147464 | tf_op jit(solution)/shard_map/ppermute | solution.py:274
  39.1 1.4 %collective-permute-start.11 = (f32[144,256]{1,0:T(8,128)S(1)}, f32[144,256]{1,0:T(8,128)S(1)}, u32[]{:S(2)}, u32[]{:S(2)}) collective-permute-start(f32[144,256]{1,0:T(8,128)S(1)} %pair_message.2.own), channel_id=1, source_target_pairs={{0,2},{2,0},{4,6},{6,4},{1,3},{3,1},{5,7},{7,5},{8,10},{10,8},{12,... | collective-permute-start | bytes 442376 | tf_op jit(solution)/shard_map/ppermute | solution.py:281
  43.5 5.6 %collective-permute-start.12 = (f32[128,256]{1,0:T(8,128)S(1)}, f32[128,256]{1,0:T(8,128)S(1)}, u32[]{:S(2)}, u32[]{:S(2)}) collective-permute-start(f32[128,256]{1,0:T(8,128)S(1)} %get-tuple-element.35), channel_id=1, source_target_pairs={{0,8},{8,0},{16,24},{24,16},{1,9},{9,1},{17,25},{25,17},{2,10},{10... | collective-permute-start | bytes 393224 | tf_op jit(solution)/shard_map/ppermute | solution.py:247
  43.7 5.4 %collective-permute-start.13 = (f32[128,256]{1,0:T(8,128)S(1)}, f32[128,256]{1,0:T(8,128)S(1)}, u32[]{:S(2)}, u32[]{:S(2)}) collective-permute-start(f32[128,256]{1,0:T(8,128)S(1)} %get-tuple-element.36), channel_id=1, source_target_pairs={{8,16},{16,8},{9,17},{17,9},{10,18},{18,10},{11,19},{19,11},{12,20... | collective-permute-start | bytes 393224 | tf_op jit(solution)/shard_map/ppermute | solution.py:247
  44.4 4.7 %collective-permute-start.14 = (f32[128,256]{1,0:T(8,128)S(1)}, f32[128,256]{1,0:T(8,128)S(1)}, u32[]{:S(2)}, u32[]{:S(2)}) collective-permute-start(f32[128,256]{1,0:T(8,128)S(1)} %get-tuple-element.37), channel_id=1, source_target_pairs={{0,2},{2,0},{4,6},{6,4},{1,3},{3,1},{5,7},{7,5},{8,10},{10,8},{12,... | collective-permute-start | bytes 393224 | tf_op jit(solution)/shard_map/ppermute | solution.py:247
  44.5 4.6 %collective-permute-start.15 = (f32[128,256]{1,0:T(8,128)S(1)}, f32[128,256]{1,0:T(8,128)S(1)}, u32[]{:S(2)}, u32[]{:S(2)}) collective-permute-start(f32[128,256]{1,0:T(8,128)S(1)} %get-tuple-element.38), channel_id=1, source_target_pairs={{2,4},{4,2},{3,5},{5,3},{10,12},{12,10},{11,13},{13,11},{18,20},{2... | collective-permute-start | bytes 393224 | tf_op jit(solution)/shard_map/ppermute | solution.py:247
  45.1 5.0 %collective-permute-start.16 = (f32[128,256]{1,0:T(8,128)S(1)}, f32[128,256]{1,0:T(8,128)S(1)}, u32[]{:S(2)}, u32[]{:S(2)}) collective-permute-start(f32[128,256]{1,0:T(8,128)S(1)} %get-tuple-element.39), channel_id=1, source_target_pairs={{0,1},{1,0},{2,3},{3,2},{4,5},{5,4},{6,7},{7,6},{8,9},{9,8},{10,11... | collective-permute-start | bytes 393224 | tf_op jit(solution)/shard_map/ppermute | solution.py:247
  50.9 5.5 %collective-permute-start.19 = (f32[16,256]{1,0:T(8,128)S(1)}, f32[16,256]{1,0:T(8,128)S(1)}, u32[]{:S(2)}, u32[]{:S(2)}) collective-permute-start(f32[16,256]{1,0:T(8,128)S(1)} %get-tuple-element.42.root), channel_id=1, source_target_pairs={{0,24},{8,16},{16,8},{24,0},{1,25},{9,17},{17,9},{25,1},{2,26},{10... | collective-permute-start | bytes 49160 | tf_op jit(solution)/shard_map/ppermute | solution.py:257
  53.1 4.8 %collective-permute-start.18 = (f32[16,256]{1,0:T(8,128)S(1)}, f32[16,256]{1,0:T(8,128)S(1)}, u32[]{:S(2)}, u32[]{:S(2)}) collective-permute-start(f32[16,256]{1,0:T(8,128)S(1)} %get-tuple-element.42.root), channel_id=1, source_target_pairs={{0,16},{8,24},{16,0},{24,8},{1,17},{9,25},{17,1},{25,9},{2,18},{10... | collective-permute-start | bytes 49160 | tf_op jit(solution)/shard_map/ppermute | solution.py:257
  55.6 3.7 %collective-permute-start.17 = (f32[16,256]{1,0:T(8,128)S(1)}, f32[16,256]{1,0:T(8,128)S(1)}, u32[]{:S(2)}, u32[]{:S(2)}) collective-permute-start(f32[16,256]{1,0:T(8,128)S(1)} %get-tuple-element.42.root), channel_id=1, source_target_pairs={{0,8},{8,0},{16,24},{24,16},{1,9},{9,1},{17,25},{25,17},{2,10},{10... | collective-permute-start | bytes 49160 | tf_op jit(solution)/shard_map/ppermute | solution.py:257
  59.4 5.9 %collective-permute-start.22 = (f32[48,256]{1,0:T(8,128)S(1)}, f32[48,256]{1,0:T(8,128)S(1)}, u32[]{:S(2)}, u32[]{:S(2)}) collective-permute-start(f32[48,256]{1,0:T(8,128)S(1)} %root_part.3.first), channel_id=1, source_target_pairs={{0,5},{1,4},{2,7},{3,6},{4,1},{5,0},{6,3},{7,2},{8,13},{9,12},{10,... | collective-permute-start | bytes 147464 | tf_op jit(solution)/shard_map/ppermute | solution.py:274
  62.9 4.1 %collective-permute-start.21 = (f32[48,256]{1,0:T(8,128)S(1)}, f32[48,256]{1,0:T(8,128)S(1)}, u32[]{:S(2)}, u32[]{:S(2)}) collective-permute-start(f32[48,256]{1,0:T(8,128)S(1)} %root_part.3.first), channel_id=1, source_target_pairs={{0,4},{1,5},{2,6},{3,7},{4,0},{5,1},{6,2},{7,3},{8,12},{9,13},{10,... | collective-permute-start | bytes 147464 | tf_op jit(solution)/shard_map/ppermute | solution.py:274
  62.9 4.1 %collective-permute-start.20 = (f32[48,256]{1,0:T(8,128)S(1)}, f32[48,256]{1,0:T(8,128)S(1)}, u32[]{:S(2)}, u32[]{:S(2)}) collective-permute-start(f32[48,256]{1,0:T(8,128)S(1)} %root_part.3.first), channel_id=1, source_target_pairs={{0,1},{1,0},{2,3},{3,2},{4,5},{5,4},{6,7},{7,6},{8,9},{9,8},{10,11... | collective-permute-start | bytes 147464 | tf_op jit(solution)/shard_map/ppermute | solution.py:274
  67.0 1.4 %collective-permute-start.23 = (f32[144,256]{1,0:T(8,128)S(1)}, f32[144,256]{1,0:T(8,128)S(1)}, u32[]{:S(2)}, u32[]{:S(2)}) collective-permute-start(f32[144,256]{1,0:T(8,128)S(1)} %pair_message.3.own), channel_id=1, source_target_pairs={{0,2},{2,0},{4,6},{6,4},{1,3},{3,1},{5,7},{7,5},{8,10},{10,8},{12,... | collective-permute-start | bytes 442376 | tf_op jit(solution)/shard_map/ppermute | solution.py:281
  (15 other events, 212.7 us)

commit v2 on v1

--- a/solution.py
+++ b/solution.py
@@ -13,8 +13,6 @@
 AXES = ("gx", "gy", "gz")
 F32 = jnp.float32
 BF16 = jnp.bfloat16
-VMEM = pl.BlockSpec(memory_space=pltpu.VMEM)
-SMEM = pl.BlockSpec(memory_space=pltpu.SMEM)
 ROWS = (((1,), (0,)), ((), ()))
 COLS = (((0,), (0,)), ((), ()))
 
@@ -64,53 +62,92 @@
     return dot(left_high, right_high) + (dot(left_low, right_high) + dot(left_high, right_low))
 
 
-def call(body, outs, ins, name, scratch=()):
+def call(body, outs, ins, name, scratch=(), fixed=0):
+    spaces = [pltpu.HBM] * fixed + [pltpu.VMEM] * (len(ins) - fixed)
     return pl.pallas_call(
         body,
-        out_shape=[jax.ShapeDtypeStruct(shape, dtype) for shape, dtype in outs],
-        in_specs=[SMEM if item.dtype == jnp.int32 else VMEM for item in ins],
-        out_specs=[VMEM] * len(outs),
+        out_shape=[item(shape, dtype) for item, shape, dtype in outs],
+        in_specs=[pl.BlockSpec(memory_space=space) for space in spaces],
+        out_specs=[
+            pl.BlockSpec(memory_space=pltpu.HBM if item is jax.ShapeDtypeStruct else pltpu.VMEM)
+            for item, _, _ in outs
+        ],
         scratch_shapes=list(scratch),
-        compiler_params=pltpu.CompilerParams(vmem_limit_bytes=16 * 1024 * 1024),
+        compiler_params=pltpu.CompilerParams(vmem_limit_bytes=8 * 1024 * 1024),
         name=name,
-    )(*ins)
+    )(*[pltpu.with_memory_space_constraint(item, space) for item, space in zip(ins, spaces)])
 
 
 def rows_of(index, height):
     return pl.ds(pl.multiple_of(index * height, height), height)
 
 
-def multiply(swaps, order, matrix, read, loads, rest, messages, local_iter, product):
-    height = matrix.shape[0] // FACES
+def send_rest(swaps, order, loads, product, rest, messages):
+    height = rest.shape[0] // FACES
     for j in range(FACES):
-        local_iter[j * height : (j + 1) * height, :] = read(rows_of(order[j], height))
-    product[...] = jnp.dot(matrix[...], local_iter[...], preferred_element_type=F32)
-    inverse = [rows_of(order[j], height) for j in range(FACES)]
+        face = rows_of(order[0, j], height)
+        rest[face, :] = product[j * height : (j + 1) * height, :]
+    for (dim, odd), message in zip(swaps, messages):
+        message[...] = rest[rows_of(swap_face(dim, odd), height), :]
+    rest[...] = loads[...].astype(F32) - rest[...]
+
+
+def reorder(order, read, local_iter):
+    height = local_iter.shape[0] // FACES
+    for j in range(FACES):
+        local_iter[j * height : (j + 1) * height, :] = read(rows_of(order[0, j], height))
+
+
+def first_kernel(swaps, order_hbm, *refs):
+    hbm, held, refs = refs[:8], refs[8:16], refs[16:]
+    (rest, *messages), scratch = refs[: 1 + len(swaps)], refs[1 + len(swaps) :]
+    matrix, loads, modes_t, modes_s, scale, *small = held
+    order, start, modes, weights, local_iter, product, sems = scratch
+    matrix_hbm, start_hbm, loads_hbm, modes_hbm, weights_hbm, *small_hbm = hbm
+    height = rest.shape[0] // FACES
+    part = matrix.shape[0] // 2
+
+    pairs = [(order_hbm, order), (modes_hbm, modes), (weights_hbm, weights), (start_hbm, start)]
+    pairs += [(matrix_hbm.at[k * part : (k + 1) * part, :], matrix.at[k * part : (k + 1) * part, :]) for k in range(2)]
+    pairs += [(loads_hbm, loads)] + list(zip(small_hbm, small))
+    copies = [pltpu.make_async_copy(*pair, sems.at[k]) for k, pair in enumerate(pairs)]
+    for copy in copies:
+        copy.start()
+    copies[1].wait()
+    high, low = split(modes[...])
+    count = high.shape[0]
+    modes_s[:count, :] = high
+    modes_s[count : 2 * count, :] = low
+    modes_s[2 * count :, :] = high
+    modes_t[...] = jnp.concatenate([high.T, low.T, high.T], axis=1)
+    copies[2].wait()
     for j in range(FACES):
         block = slice(j * height, (j + 1) * height)
-        rest[inverse[j], :] = loads[inverse[j], :].astype(F32) - product[block, :]
-    for (dim, odd), message in zip(swaps, messages):
-        face = rows_of(swap_face(dim, odd), height)
-        message[...] = loads[face, :].astype(F32) - rest[face, :]
-
-
-def first_kernel(swaps, order, matrix, start, loads, rest, *more):
-    messages, (local_iter, product) = more[: len(swaps)], more[len(swaps) :]
-
-    def read(rows):
-        return start[rows, :]
-
-    multiply(swaps, order, matrix, read, loads, rest, messages, local_iter, product)
-
-
-def residual_kernel(swaps, rest, modes, root_map, *more):
+        scale[block, :] = jnp.broadcast_to(weights[:, block], (height, height)).T
+    copies[0].wait()
+    copies[3].wait()
+    reorder(order, lambda rows: start[rows, :], local_iter)
+    for k in range(2):
+        copies[4 + k].wait()
+        rows = slice(k * part, (k + 1) * part)
+        product[rows, :] = jnp.dot(matrix[rows, :], local_iter[...], preferred_element_type=F32)
+    for copy in copies[6:]:
+        copy.wait()
+    send_rest(swaps, order, loads, product, rest, messages)
+
+
+def residual_kernel(swaps, rest, modes_s, root_map, *more):
     halos, (residual, coarse, root) = more[: len(swaps)], more[len(swaps) :]
     height = rest.shape[0] // FACES
+    count = coarse.shape[0]
     residual[...] = rest[...]
     for (dim, odd), halo in zip(swaps, halos):
         face = rows_of(swap_face(dim, odd), height)
         residual[face, :] -= halo[...]
-    coarse[...] = dot3(modes[...], residual[...])
+    high, low = split(residual[...])
+    both = jnp.dot(modes_s[: 2 * count, :], high, preferred_element_type=F32)
+    fine = jnp.dot(modes_s[:count, :], low, preferred_element_type=F32)
+    coarse[...] = both[:count, :] + (both[count:, :] + fine)
     root[...] = dot3(root_map[...], coarse[...], COLS)
 
 
@@ -151,44 +188,48 @@
     return dot3(region_rows[...], stack[...]) + dot3(root_map[...], root_part)
 
 
-def update(members, sizes, solution, residual, weights, modes, root_map, region_rows, own, other, stack, write):
-    height = residual.shape[0] // FACES
-    amplitude = amplitude_of(members, sizes, region_rows, root_map, own, other, stack)
-    lanes = residual.shape[1]
-    correction = dot3(modes[...], amplitude, COLS)
-    for j in range(FACES):
-        block = slice(j * height, (j + 1) * height)
-        scale = jnp.broadcast_to(weights[:, block], (height, height)).T[:, :1]
-        write(
-            block,
-            solution[block, :].astype(F32) + scale * residual[block, :] + correction[block, :],
-        )
+def correction_of(modes_t, amplitude):
+    high, low = split(amplitude)
+    tall = jnp.concatenate([high, high, low], axis=0)
+    return jnp.dot(modes_t[...], tall, preferred_element_type=F32)
+
+
+def scaled(scale, residual, block):
+    lanes = residual.shape[1] // scale.shape[1]
+    return jnp.concatenate([scale[block, :]] * lanes, axis=1) * residual[block, :]
 
 
 def middle_kernel(
-    swaps, members, sizes, order, matrix, solution, loads, residual, weights, modes, root_map, region_rows,
+    swaps, members, sizes, order_hbm, matrix, solution, loads, residual, scale, modes_t, root_map, region_rows,
     own, other, next_solution, rest, *more
 ):
-    messages, (stack, local_iter, product) = more[: len(swaps)], more[len(swaps) :]
-
-    def write(block, value):
-        next_solution[block, :] = value
-
-    update(members, sizes, solution, residual, weights, modes, root_map, region_rows, own, other, stack, write)
-
-    def read(rows):
-        return next_solution[rows, :].astype(BF16)
-
-    multiply(swaps, order, matrix, read, loads, rest, messages, local_iter, product)
+    messages, (stack, local_iter, product, order, sem) = more[: len(swaps)], more[len(swaps) :]
+    copy = pltpu.make_async_copy(order_hbm, order, sem)
+    copy.start()
+    amplitude = amplitude_of(members, sizes, region_rows, root_map, own, other, stack)
+    product[...] = correction_of(modes_t, amplitude)
+    every = slice(0, residual.shape[0])
+    next_solution[...] = solution[...].astype(F32) + scaled(scale, residual, every) + product[...]
+    copy.wait()
+    reorder(order, lambda rows: next_solution[rows, :].astype(BF16), local_iter)
+    product[...] = jnp.dot(matrix[...], local_iter[...], preferred_element_type=F32)
+    send_rest(swaps, order, loads, product, rest, messages)
 
 
 def last_kernel(
-    members, sizes, solution, residual, weights, modes, root_map, region_rows, own, other, next_solution, stack
+    members, sizes, solution, residual, scale, modes_t, root_map, region_rows, own, other, out, stack, result, sems
 ):
-    def write(block, value):
-        next_solution[block, :] = value
-
-    update(members, sizes, solution, residual, weights, modes, root_map, region_rows, own, other, stack, write)
+    amplitude = amplitude_of(members, sizes, region_rows, root_map, own, other, stack)
+    part = result.shape[0] // 4
+    copies = []
+    for k in range(4):
+        block = slice(k * part, (k + 1) * part)
+        base = solution[block, :].astype(F32) + scaled(scale, residual, block)
+        result[block, :] = base + correction_of(modes_t.at[block, :], amplitude)
+        copies.append(pltpu.make_async_copy(result.at[block, :], out.at[block, :], sems.at[k]))
+        copies[-1].start()
+    for copy in copies:
+        copy.wait()
 
 
 def per_device(
@@ -207,7 +248,7 @@
     cases = loads.shape[-1]
     height = iface // FACES
     matrix = interface_op.reshape(iface, iface)
-    order = block_order.reshape(FACES)
+    order = block_order.reshape(1, FACES)
     weights = interface_weights.reshape(1, iface)
     modes = coarse_modes.reshape(coarse_modes.shape[-2], iface)
     mode_count = modes.shape[0]
@@ -221,27 +262,45 @@
     half = sizes[1] // 2
     members = list(itertools.product(range(half), range(sizes[2])))
 
-    full = ((iface, cases), F32)
-    face = ((height, cases), F32)
+    full = (pltpu.VMEM, (iface, cases), F32)
+    face = (pltpu.VMEM, (height, cases), F32)
     work = [pltpu.VMEM((iface, cases), BF16), pltpu.VMEM((iface, cases), F32)]
     stack = [pltpu.VMEM((region_rows.shape[1], cases), F32)]
+    places = [pltpu.SMEM((1, FACES), jnp.int32)]
 
     for step in range(ITERS):
         if step == 0:
-            rest, *messages = call(
+            held = [
+                (pltpu.VMEM, matrix.shape, BF16),
+                (pltpu.VMEM, target.shape, BF16),
+                (pltpu.VMEM, (iface, 3 * mode_count), BF16),
+                (pltpu.VMEM, (3 * mode_count, iface), BF16),
+                (pltpu.VMEM, (iface, height), F32),
+                (pltpu.VMEM, root_map.shape, F32),
+                (pltpu.VMEM, region_rows.shape, F32),
+                (pltpu.VMEM, root_inverse.shape, F32),
+            ]
+            inputs = [order, matrix, solution, target, modes, weights, root_map, region_rows, root_inverse]
+            outs = call(
                 functools.partial(first_kernel, swaps),
-                [full] + [face] * len(swaps),
-                [order, matrix, solution, target],
+                held + [full] + [face] * len(swaps),
+                inputs,
                 "first_product",
-                work,
+                places
+                + [pltpu.VMEM((iface, cases), BF16), pltpu.VMEM(modes.shape, F32), pltpu.VMEM(weights.shape, F32)]
+                + work
+                + [pltpu.SemaphoreType.DMA((10,))],
+                len(inputs),
             )
+            matrix, target, modes_t, modes_s, scale, root_map, region_rows, root_inverse, rest, *messages = outs
         else:
             solution, rest, *messages = call(
                 functools.partial(middle_kernel, swaps, members, sizes[1:]),
                 [full, full] + [face] * len(swaps),
-                [order, matrix, solution, target, residual, weights, modes, root_map, region_rows, own, other],
+                [order, matrix, solution, target, residual, scale, modes_t, root_map, region_rows, own, other],
                 "update_product",
-                stack + work,
+                stack + work + places + [pltpu.SemaphoreType.DMA],
+                1,
             )
         halos = [
             lax.ppermute(message, AXES[dim], neighbour_pairs(sizes[dim], odd))
@@ -249,8 +308,8 @@
         ]
         residual, coarse, root = call(
             functools.partial(residual_kernel, swaps),
-            [full, ((mode_count, cases), F32), ((root_modes, cases), F32)],
-            [rest, modes, root_map] + halos,
+            [full, (pltpu.VMEM, (mode_count, cases), F32), (pltpu.VMEM, (root_modes, cases), F32)],
+            [rest, modes_s, root_map] + halos,
             "residual_coarse",
         )
         received = [
@@ -259,7 +318,7 @@
         ]
         (message,) = call(
             functools.partial(root_kernel, sizes[0]),
-            [((mode_count + root_modes, cases), F32)],
+            [(pltpu.VMEM, (mode_count + root_modes, cases), F32)],
             [coarse, root_inverse, root] + received,
             "root_part",
             [pltpu.VMEM((root_inverse.shape[1], cases), F32)],
@@ -274,17 +333,17 @@
             pieces.append(lax.ppermute(message, ("gy", "gz"), moves))
         (own,) = call(
             functools.partial(pair_kernel, mode_count),
-            [((len(members) * mode_count + root_modes, cases), F32)],
+            [(pltpu.VMEM, (len(members) * mode_count + root_modes, cases), F32)],
             [message] + pieces,
             "pair_message",
         )
         other = lax.ppermute(own, "gy", neighbour_pairs(sizes[1], 0))
     (solution,) = call(
         functools.partial(last_kernel, members, sizes[1:]),
-        [full],
-        [solution, residual, weights, modes, root_map, region_rows, own, other],
+        [(jax.ShapeDtypeStruct, (iface, cases), F32)],
+        [solution, residual, scale, modes_t, root_map, region_rows, own, other],
         "update_last",
-        stack,
+        stack + [pltpu.VMEM((iface, cases), F32), pltpu.SemaphoreType.DMA((4,))],
     )
     return solution.reshape(1, 1, 1, iface, cases)
 

time: 70.8 us -> 62.6 us (0.88)
  local copies, waits for them, and re-layouts: 8.02 us -> 1.38 us
  Pallas kernels: 9.75 us -> 7.99 us
    unnamed x31 -> x3, local copies, waits for them, and re-layouts: 8.02 us -> 1.38 us
    pallas_call x9, Pallas kernels: 9.75 us -> 7.99 us  [call(): pl.pallas_call(body, out_shape=[item(shape, dtype) for item, shape, dtype...]
  transfers between devices with their start and end apart: 24 -> 24, of which waited for: 14 -> 15; matrix products, arithmetic and copies ran while one was open for 1% -> 0% of each run, Pallas kernels for 0% -> 0%
where the time goes in v2:
time: 62.6 us; the launch traced here: 62.4 us
  starting transfers between devices  29.3 us (47%)
  waiting for transfers between devices  23.6 us (38%)
  Pallas kernels  7.99 us (13%)
  local copies, waits for them, and re-layouts  1.38 us (2%)
    ppermute x6, starting transfers between devices, per_device(): lax.ppermute(root, 'gx', [(i, partner(i, offset, sizes[0])) for i in rang...  11 us
    ppermute x6, starting transfers between devices, per_device(): pieces.append(lax.ppermute(message, ('gy', 'gz'), moves))  9.75 us
    ppermute x10, starting transfers between devices, per_device(): lax.ppermute(message, AXES[dim], neighbour_pairs(sizes[dim], odd))  8.38 us
    pallas_call x9, Pallas kernels, call(): pl.pallas_call(body, out_shape=[item(shape, dtype) for item, shape, dtype...  7.99 us
    ppermute x10, waiting for transfers between devices, per_device(): lax.ppermute(message, AXES[dim], neighbour_pairs(sizes[dim], odd))  7.79 us
    ppermute x6, waiting for transfers between devices, per_device(): lax.ppermute(root, 'gx', [(i, partner(i, offset, sizes[0])) for i in rang...  6.96 us
    ppermute x6, waiting for transfers between devices, per_device(): pieces.append(lax.ppermute(message, ('gy', 'gz'), moves))  6.15 us
    ppermute x2, waiting for transfers between devices, per_device(): other = lax.ppermute(own, 'gy', neighbour_pairs(sizes[1], 0))  2.72 us
  transfers between devices with their start and end apart: 24, of which 15 were waited for; matrix products, arithmetic and copies ran while one was open for 0% of the time, Pallas kernels for 0%

profile of v2, /device:TPU:0, one launch (start us, length us, event | category | flops | bytes accessed | tf_op | source)
XLA Modules:
  0.0 62.4 jit_solution(9211921358391074782)
XLA Ops:
  0.0 1.4 %copy.10 = f32[1,1,1,32,16]{4,3,2,1,0:T(8,128)} copy(f32[1,1,1,32,16]{3,4,2,1,0:T(8,128)} %param.15) | data formatting | bytes 4096 | tf_op args[6]
  1.4 3.2 %first_product.1 = (bf16[1024,1024]{1,0:T(8,128)(2,1)S(1)}, bf16[1024,256]{1,0:T(8,128)(2,1)S(1)}, bf16[1024,96]{1,0:T(8,128)(2,1)S(1)}, bf16[96,1024]{1,0:T(8,1...) custom-call(s32[1,8]{1,0:T(1,128)} %bitcast.17, ...), custom_call_target="tpu_custom_call" | custom-call | tf_op jit(solution)/shard_map/first_product/pallas_call | solution.py:67
  4.6 3.1 %collective-permute-start = (f32[128,256]{1,0:T(8,128)S(1)}, f32[128,256]{1,0:T(8,128)S(1)}, u32[]{:S(2)}, u32[]{:S(2)}) collective-permute-start(f32[128,256]{1,0:T(8,128)S(1)} %get-tuple-element.37), channel_id=1, source_target_pairs={{0,8},{8,0},{16,24},{24,16},{1,9},{9,1},{17,25},{25,17},{2,10},{10... | collective-permute-start | bytes 393224 | tf_op jit(solution)/shard_map/ppermute | solution.py:306
  9.1 1.6 %collective-permute-start.4 = (f32[128,256]{1,0:T(8,128)S(1)}, f32[128,256]{1,0:T(8,128)S(1)}, u32[]{:S(2)}, u32[]{:S(2)}) collective-permute-start(f32[128,256]{1,0:T(8,128)S(1)} %get-tuple-element.41), channel_id=1, source_target_pairs={{0,1},{1,0},{2,3},{3,2},{4,5},{5,4},{6,7},{7,6},{8,9},{9,8},{10,11... | collective-permute-start | bytes 393224 | tf_op jit(solution)/shard_map/ppermute | solution.py:306
  11.2 2.9 %collective-permute-done.4.more_4_ = f32[128,256]{1,0:T(8,128)S(1)} collective-permute-done((f32[128,256]{1,0:T(8,128)S(1)}, f32[128,256]{1,0:T(8,128)S(1)}, u32[]{:S(2)}, u32[]{:S(2)}) %collective-permute-start.4) | collective-permute-done | bytes 131104 | tf_op jit(solution)/shard_map/ppermute | solution.py:306
  14.8 2.5 %collective-permute-start.7 = (f32[16,256]{1,0:T(8,128)S(1)}, f32[16,256]{1,0:T(8,128)S(1)}, u32[]{:S(2)}, u32[]{:S(2)}) collective-permute-start(f32[16,256]{1,0:T(8,128)S(1)} %get-tuple-element.48.root), channel_id=1, source_target_pairs={{0,24},{8,16},{16,8},{24,0},{1,25},{9,17},{17,9},{25,1},{2,26},{10... | collective-permute-start | bytes 49160 | tf_op jit(solution)/shard_map/ppermute | solution.py:316
  17.3 3.4 %collective-permute-start.6 = (f32[16,256]{1,0:T(8,128)S(1)}, f32[16,256]{1,0:T(8,128)S(1)}, u32[]{:S(2)}, u32[]{:S(2)}) collective-permute-start(f32[16,256]{1,0:T(8,128)S(1)} %get-tuple-element.48.root), channel_id=1, source_target_pairs={{0,16},{8,24},{16,0},{24,8},{1,17},{9,25},{17,1},{25,9},{2,18},{10... | collective-permute-start | bytes 49160 | tf_op jit(solution)/shard_map/ppermute | solution.py:316
  20.7 1.9 %collective-permute-done.6.more_1_ = f32[16,256]{1,0:T(8,128)S(1)} collective-permute-done((f32[16,256]{1,0:T(8,128)S(1)}, f32[16,256]{1,0:T(8,128)S(1)}, u32[]{:S(2)}, u32[]{:S(2)}) %collective-permute-start.6) | collective-permute-done | bytes 16416 | tf_op jit(solution)/shard_map/ppermute | solution.py:316
  22.6 1.9 %collective-permute-done.5.more_0_ = f32[16,256]{1,0:T(8,128)S(1)} collective-permute-done((f32[16,256]{1,0:T(8,128)S(1)}, f32[16,256]{1,0:T(8,128)S(1)}, u32[]{:S(2)}, u32[]{:S(2)}) %collective-permute-start.5) | collective-permute-done | bytes 16416 | tf_op jit(solution)/shard_map/ppermute | solution.py:316
  24.6 4.3 %collective-permute-start.10 = (f32[48,256]{1,0:T(8,128)S(1)}, f32[48,256]{1,0:T(8,128)S(1)}, u32[]{:S(2)}, u32[]{:S(2)}) collective-permute-start(f32[48,256]{1,0:T(8,128)S(1)} %root_part.2.first), channel_id=1, source_target_pairs={{0,5},{1,4},{2,7},{3,6},{4,1},{5,0},{6,3},{7,2},{8,13},{9,12},{10,... | collective-permute-start | bytes 147464 | tf_op jit(solution)/shard_map/ppermute | solution.py:333
  29.5 1.5 %collective-permute-done.10.more_2_ = f32[48,256]{1,0:T(8,128)S(1)} collective-permute-done((f32[48,256]{1,0:T(8,128)S(1)}, f32[48,256]{1,0:T(8,128)S(1)}, u32[]{:S(2)}, u32[]{:S(2)}) %collective-permute-start.10) | collective-permute-done | bytes 49184 | tf_op jit(solution)/shard_map/ppermute | solution.py:333
  31.0 2.0 %collective-permute-done.9.more_1_ = f32[48,256]{1,0:T(8,128)S(1)} collective-permute-done((f32[48,256]{1,0:T(8,128)S(1)}, f32[48,256]{1,0:T(8,128)S(1)}, u32[]{:S(2)}, u32[]{:S(2)}) %collective-permute-start.9) | collective-permute-done | bytes 49184 | tf_op jit(solution)/shard_map/ppermute | solution.py:333
  33.1 1.4 %collective-permute-done.11.other = f32[144,256]{1,0:T(8,128)S(1)} collective-permute-done((f32[144,256]{1,0:T(8,128)S(1)}, f32[144,256]{1,0:T(8,128)S(1)}, u32[]{:S(2)}, u32[]{:S(2)}) %collective-permute-start.11) | collective-permute-done | bytes 147488 | tf_op jit(solution)/shard_map/ppermute | solution.py:340
  34.4 1.6 %update_product.1 = (f32[1024,256]{1,0:T(8,128)S(1)}, f32[1024,256]{1,0:T(8,128)S(1)}, f32[128,256]{1,0:T(8,128)S(1)}, f32[128,256]{1,0:T(8,128)S(1)}, f32[128,2...) custom-call(s32[1,8]{1,0:T(1,128)} %bitcast.18, bf16[1024,1024]{1,0:T(8,128)(2,1)S(1)} %get-tuple-element.32.matrix, ...), custom_call_target="tpu_custom_call" | custom-call | tf_op jit(solution)/shard_map/update_product/pallas_call | solution.py:67
  38.4 3.3 %collective-permute-done.12.more_0_ = f32[128,256]{1,0:T(8,128)S(1)} collective-permute-done((f32[128,256]{1,0:T(8,128)S(1)}, f32[128,256]{1,0:T(8,128)S(1)}, u32[]{:S(2)}, u32[]{:S(2)}) %collective-permute-start.12) | collective-permute-done | bytes 131104 | tf_op jit(solution)/shard_map/ppermute | solution.py:306
  43.4 2.2 %collective-permute-start.19 = (f32[16,256]{1,0:T(8,128)S(1)}, f32[16,256]{1,0:T(8,128)S(1)}, u32[]{:S(2)}, u32[]{:S(2)}) collective-permute-start(f32[16,256]{1,0:T(8,128)S(1)} %get-tuple-element.58.root), channel_id=1, source_target_pairs={{0,24},{8,16},{16,8},{24,0},{1,25},{9,17},{17,9},{25,1},{2,26},{10... | collective-permute-start | bytes 49160 | tf_op jit(solution)/shard_map/ppermute | solution.py:316
  45.6 2.4 %collective-permute-start.18 = (f32[16,256]{1,0:T(8,128)S(1)}, f32[16,256]{1,0:T(8,128)S(1)}, u32[]{:S(2)}, u32[]{:S(2)}) collective-permute-start(f32[16,256]{1,0:T(8,128)S(1)} %get-tuple-element.58.root), channel_id=1, source_target_pairs={{0,16},{8,24},{16,0},{24,8},{1,17},{9,25},{17,1},{25,9},{2,18},{10... | collective-permute-start | bytes 49160 | tf_op jit(solution)/shard_map/ppermute | solution.py:316
  49.0 1.4 %collective-permute-done.18.more_1_ = f32[16,256]{1,0:T(8,128)S(1)} collective-permute-done((f32[16,256]{1,0:T(8,128)S(1)}, f32[16,256]{1,0:T(8,128)S(1)}, u32[]{:S(2)}, u32[]{:S(2)}) %collective-permute-start.18) | collective-permute-done | bytes 16416 | tf_op jit(solution)/shard_map/ppermute | solution.py:316
  50.4 1.4 %collective-permute-done.17.more_0_ = f32[16,256]{1,0:T(8,128)S(1)} collective-permute-done((f32[16,256]{1,0:T(8,128)S(1)}, f32[16,256]{1,0:T(8,128)S(1)}, u32[]{:S(2)}, u32[]{:S(2)}) %collective-permute-start.17) | collective-permute-done | bytes 16416 | tf_op jit(solution)/shard_map/ppermute | solution.py:316
  51.9 3.4 %collective-permute-start.22 = (f32[48,256]{1,0:T(8,128)S(1)}, f32[48,256]{1,0:T(8,128)S(1)}, u32[]{:S(2)}, u32[]{:S(2)}) collective-permute-start(f32[48,256]{1,0:T(8,128)S(1)} %root_part.3.first), channel_id=1, source_target_pairs={{0,5},{1,4},{2,7},{3,6},{4,1},{5,0},{6,3},{7,2},{8,13},{9,12},{10,... | collective-permute-start | bytes 147464 | tf_op jit(solution)/shard_map/ppermute | solution.py:333
  55.3 1.4 %collective-permute-start.20 = (f32[48,256]{1,0:T(8,128)S(1)}, f32[48,256]{1,0:T(8,128)S(1)}, u32[]{:S(2)}, u32[]{:S(2)}) collective-permute-start(f32[48,256]{1,0:T(8,128)S(1)} %root_part.3.first), channel_id=1, source_target_pairs={{0,1},{1,0},{2,3},{3,2},{4,5},{5,4},{6,7},{7,6},{8,9},{9,8},{10,11... | collective-permute-start | bytes 147464 | tf_op jit(solution)/shard_map/ppermute | solution.py:333
  57.8 1.6 %collective-permute-done.21.more_1_ = f32[48,256]{1,0:T(8,128)S(1)} collective-permute-done((f32[48,256]{1,0:T(8,128)S(1)}, f32[48,256]{1,0:T(8,128)S(1)}, u32[]{:S(2)}, u32[]{:S(2)}) %collective-permute-start.21) | collective-permute-done | bytes 49184 | tf_op jit(solution)/shard_map/ppermute | solution.py:333
  59.5 1.4 %collective-permute-done.23.other = f32[144,256]{1,0:T(8,128)S(1)} collective-permute-done((f32[144,256]{1,0:T(8,128)S(1)}, f32[144,256]{1,0:T(8,128)S(1)}, u32[]{:S(2)}, u32[]{:S(2)}) %collective-permute-start.23) | collective-permute-done | bytes 147488 | tf_op jit(solution)/shard_map/ppermute | solution.py:340
  60.9 1.5 %update_last.1 = f32[1024,256]{1,0:T(8,128)} custom-call(f32[1024,256]{1,0:T(8,128)S(1)} %get-tuple-element.49.solution, f32[1024,256]{1,0:T(8,128)S(1)} %get-tuple-element.56.residual, f32[1024,128]{1,0:T(8,128)S(1)} %get-tuple-element.43.scale, bf16[1024,96]{1,0:T(8,128)(2,1)S(1)} %get-tuple-element.44.modes_t, f32[32,16]{1,0:T(8,128)S(1)} %get-tuple-element.36.root_map, ...), custom_call_target="tpu_custom_call" | custom-call | tf_op jit(solution)/shard_map/update_last/pallas_call | solution.py:67
  (36 shorter events, 9.7 us)
Async XLA Ops:
  4.6 6.6 %collective-permute-start = (f32[128,256]{1,0:T(8,128)S(1)}, f32[128,256]{1,0:T(8,128)S(1)}, u32[]{:S(2)}, u32[]{:S(2)}) collective-permute-start(f32[128,256]{1,0:T(8,128)S(1)} %get-tuple-element.37), channel_id=1, source_target_pairs={{0,8},{8,0},{16,24},{24,16},{1,9},{9,1},{17,25},{25,17},{2,10},{10... | collective-permute-start | bytes 393224 | tf_op jit(solution)/shard_map/ppermute | solution.py:306
  7.7 3.5 %collective-permute-start.1 = (f32[128,256]{1,0:T(8,128)S(1)}, f32[128,256]{1,0:T(8,128)S(1)}, u32[]{:S(2)}, u32[]{:S(2)}) collective-permute-start(f32[128,256]{1,0:T(8,128)S(1)} %get-tuple-element.38), channel_id=1, source_target_pairs={{8,16},{16,8},{9,17},{17,9},{10,18},{18,10},{11,19},{19,11},{12,20... | collective-permute-start | bytes 393224 | tf_op jit(solution)/shard_map/ppermute | solution.py:306
  8.4 2.8 %collective-permute-start.2 = (f32[128,256]{1,0:T(8,128)S(1)}, f32[128,256]{1,0:T(8,128)S(1)}, u32[]{:S(2)}, u32[]{:S(2)}) collective-permute-start(f32[128,256]{1,0:T(8,128)S(1)} %get-tuple-element.39), channel_id=1, source_target_pairs={{0,2},{2,0},{4,6},{6,4},{1,3},{3,1},{5,7},{7,5},{8,10},{10,8},{12,... | collective-permute-start | bytes 393224 | tf_op jit(solution)/shard_map/ppermute | solution.py:306
  8.5 2.8 %collective-permute-start.3 = (f32[128,256]{1,0:T(8,128)S(1)}, f32[128,256]{1,0:T(8,128)S(1)}, u32[]{:S(2)}, u32[]{:S(2)}) collective-permute-start(f32[128,256]{1,0:T(8,128)S(1)} %get-tuple-element.40), channel_id=1, source_target_pairs={{2,4},{4,2},{3,5},{5,3},{10,12},{12,10},{11,13},{13,11},{18,20},{2... | collective-permute-start | bytes 393224 | tf_op jit(solution)/shard_map/ppermute | solution.py:306
  9.1 5.0 %collective-permute-start.4 = (f32[128,256]{1,0:T(8,128)S(1)}, f32[128,256]{1,0:T(8,128)S(1)}, u32[]{:S(2)}, u32[]{:S(2)}) collective-permute-start(f32[128,256]{1,0:T(8,128)S(1)} %get-tuple-element.41), channel_id=1, source_target_pairs={{0,1},{1,0},{2,3},{3,2},{4,5},{5,4},{6,7},{7,6},{8,9},{9,8},{10,11... | collective-permute-start | bytes 393224 | tf_op jit(solution)/shard_map/ppermute | solution.py:306
  14.8 5.9 %collective-permute-start.7 = (f32[16,256]{1,0:T(8,128)S(1)}, f32[16,256]{1,0:T(8,128)S(1)}, u32[]{:S(2)}, u32[]{:S(2)}) collective-permute-start(f32[16,256]{1,0:T(8,128)S(1)} %get-tuple-element.48.root), channel_id=1, source_target_pairs={{0,24},{8,16},{16,8},{24,0},{1,25},{9,17},{17,9},{25,1},{2,26},{10... | collective-permute-start | bytes 49160 | tf_op jit(solution)/shard_map/ppermute | solution.py:316
  17.3 5.3 %collective-permute-start.6 = (f32[16,256]{1,0:T(8,128)S(1)}, f32[16,256]{1,0:T(8,128)S(1)}, u32[]{:S(2)}, u32[]{:S(2)}) collective-permute-start(f32[16,256]{1,0:T(8,128)S(1)} %get-tuple-element.48.root), channel_id=1, source_target_pairs={{0,16},{8,24},{16,0},{24,8},{1,17},{9,25},{17,1},{25,9},{2,18},{10... | collective-permute-start | bytes 49160 | tf_op jit(solution)/shard_map/ppermute | solution.py:316
  20.7 3.7 %collective-permute-start.5 = (f32[16,256]{1,0:T(8,128)S(1)}, f32[16,256]{1,0:T(8,128)S(1)}, u32[]{:S(2)}, u32[]{:S(2)}) collective-permute-start(f32[16,256]{1,0:T(8,128)S(1)} %get-tuple-element.48.root), channel_id=1, source_target_pairs={{0,8},{8,0},{16,24},{24,16},{1,9},{9,1},{17,25},{25,17},{2,10},{10... | collective-permute-start | bytes 49160 | tf_op jit(solution)/shard_map/ppermute | solution.py:316
  24.6 6.4 %collective-permute-start.10 = (f32[48,256]{1,0:T(8,128)S(1)}, f32[48,256]{1,0:T(8,128)S(1)}, u32[]{:S(2)}, u32[]{:S(2)}) collective-permute-start(f32[48,256]{1,0:T(8,128)S(1)} %root_part.2.first), channel_id=1, source_target_pairs={{0,5},{1,4},{2,7},{3,6},{4,1},{5,0},{6,3},{7,2},{8,13},{9,12},{10,... | collective-permute-start | bytes 147464 | tf_op jit(solution)/shard_map/ppermute | solution.py:333
  28.9 4.1 %collective-permute-start.9 = (f32[48,256]{1,0:T(8,128)S(1)}, f32[48,256]{1,0:T(8,128)S(1)}, u32[]{:S(2)}, u32[]{:S(2)}) collective-permute-start(f32[48,256]{1,0:T(8,128)S(1)} %root_part.2.first), channel_id=1, source_target_pairs={{0,4},{1,5},{2,6},{3,7},{4,0},{5,1},{6,2},{7,3},{8,12},{9,13},{10,... | collective-permute-start | bytes 147464 | tf_op jit(solution)/shard_map/ppermute | solution.py:333
  28.9 4.1 %collective-permute-start.8 = (f32[48,256]{1,0:T(8,128)S(1)}, f32[48,256]{1,0:T(8,128)S(1)}, u32[]{:S(2)}, u32[]{:S(2)}) collective-permute-start(f32[48,256]{1,0:T(8,128)S(1)} %root_part.2.first), channel_id=1, source_target_pairs={{0,1},{1,0},{2,3},{3,2},{4,5},{5,4},{6,7},{7,6},{8,9},{9,8},{10,11... | collective-permute-start | bytes 147464 | tf_op jit(solution)/shard_map/ppermute | solution.py:333
  33.0 1.4 %collective-permute-start.11 = (f32[144,256]{1,0:T(8,128)S(1)}, f32[144,256]{1,0:T(8,128)S(1)}, u32[]{:S(2)}, u32[]{:S(2)}) collective-permute-start(f32[144,256]{1,0:T(8,128)S(1)} %pair_message.2.own), channel_id=1, source_target_pairs={{0,2},{2,0},{4,6},{6,4},{1,3},{3,1},{5,7},{7,5},{8,10},{10,8},{12,... | collective-permute-start | bytes 442376 | tf_op jit(solution)/shard_map/ppermute | solution.py:340
  36.1 5.6 %collective-permute-start.12 = (f32[128,256]{1,0:T(8,128)S(1)}, f32[128,256]{1,0:T(8,128)S(1)}, u32[]{:S(2)}, u32[]{:S(2)}) collective-permute-start(f32[128,256]{1,0:T(8,128)S(1)} %get-tuple-element.51), channel_id=1, source_target_pairs={{0,8},{8,0},{16,24},{24,16},{1,9},{9,1},{17,25},{25,17},{2,10},{10... | collective-permute-start | bytes 393224 | tf_op jit(solution)/shard_map/ppermute | solution.py:306
  36.3 5.4 %collective-permute-start.13 = (f32[128,256]{1,0:T(8,128)S(1)}, f32[128,256]{1,0:T(8,128)S(1)}, u32[]{:S(2)}, u32[]{:S(2)}) collective-permute-start(f32[128,256]{1,0:T(8,128)S(1)} %get-tuple-element.52), channel_id=1, source_target_pairs={{8,16},{16,8},{9,17},{17,9},{10,18},{18,10},{11,19},{19,11},{12,20... | collective-permute-start | bytes 393224 | tf_op jit(solution)/shard_map/ppermute | solution.py:306
  37.0 4.7 %collective-permute-start.14 = (f32[128,256]{1,0:T(8,128)S(1)}, f32[128,256]{1,0:T(8,128)S(1)}, u32[]{:S(2)}, u32[]{:S(2)}) collective-permute-start(f32[128,256]{1,0:T(8,128)S(1)} %get-tuple-element.53), channel_id=1, source_target_pairs={{0,2},{2,0},{4,6},{6,4},{1,3},{3,1},{5,7},{7,5},{8,10},{10,8},{12,... | collective-permute-start | bytes 393224 | tf_op jit(solution)/shard_map/ppermute | solution.py:306
  37.1 4.6 %collective-permute-start.15 = (f32[128,256]{1,0:T(8,128)S(1)}, f32[128,256]{1,0:T(8,128)S(1)}, u32[]{:S(2)}, u32[]{:S(2)}) collective-permute-start(f32[128,256]{1,0:T(8,128)S(1)} %get-tuple-element.54), channel_id=1, source_target_pairs={{2,4},{4,2},{3,5},{5,3},{10,12},{12,10},{11,13},{13,11},{18,20},{2... | collective-permute-start | bytes 393224 | tf_op jit(solution)/shard_map/ppermute | solution.py:306
  37.7 5.0 %collective-permute-start.16 = (f32[128,256]{1,0:T(8,128)S(1)}, f32[128,256]{1,0:T(8,128)S(1)}, u32[]{:S(2)}, u32[]{:S(2)}) collective-permute-start(f32[128,256]{1,0:T(8,128)S(1)} %get-tuple-element.55), channel_id=1, source_target_pairs={{0,1},{1,0},{2,3},{3,2},{4,5},{5,4},{6,7},{7,6},{8,9},{9,8},{10,11... | collective-permute-start | bytes 393224 | tf_op jit(solution)/shard_map/ppermute | solution.py:306
  43.4 5.5 %collective-permute-start.19 = (f32[16,256]{1,0:T(8,128)S(1)}, f32[16,256]{1,0:T(8,128)S(1)}, u32[]{:S(2)}, u32[]{:S(2)}) collective-permute-start(f32[16,256]{1,0:T(8,128)S(1)} %get-tuple-element.58.root), channel_id=1, source_target_pairs={{0,24},{8,16},{16,8},{24,0},{1,25},{9,17},{17,9},{25,1},{2,26},{10... | collective-permute-start | bytes 49160 | tf_op jit(solution)/shard_map/ppermute | solution.py:316
  45.6 4.8 %collective-permute-start.18 = (f32[16,256]{1,0:T(8,128)S(1)}, f32[16,256]{1,0:T(8,128)S(1)}, u32[]{:S(2)}, u32[]{:S(2)}) collective-permute-start(f32[16,256]{1,0:T(8,128)S(1)} %get-tuple-element.58.root), channel_id=1, source_target_pairs={{0,16},{8,24},{16,0},{24,8},{1,17},{9,25},{17,1},{25,9},{2,18},{10... | collective-permute-start | bytes 49160 | tf_op jit(solution)/shard_map/ppermute | solution.py:316
  48.0 3.7 %collective-permute-start.17 = (f32[16,256]{1,0:T(8,128)S(1)}, f32[16,256]{1,0:T(8,128)S(1)}, u32[]{:S(2)}, u32[]{:S(2)}) collective-permute-start(f32[16,256]{1,0:T(8,128)S(1)} %get-tuple-element.58.root), channel_id=1, source_target_pairs={{0,8},{8,0},{16,24},{24,16},{1,9},{9,1},{17,25},{25,17},{2,10},{10... | collective-permute-start | bytes 49160 | tf_op jit(solution)/shard_map/ppermute | solution.py:316
  51.9 5.9 %collective-permute-start.22 = (f32[48,256]{1,0:T(8,128)S(1)}, f32[48,256]{1,0:T(8,128)S(1)}, u32[]{:S(2)}, u32[]{:S(2)}) collective-permute-start(f32[48,256]{1,0:T(8,128)S(1)} %root_part.3.first), channel_id=1, source_target_pairs={{0,5},{1,4},{2,7},{3,6},{4,1},{5,0},{6,3},{7,2},{8,13},{9,12},{10,... | collective-permute-start | bytes 147464 | tf_op jit(solution)/shard_map/ppermute | solution.py:333
  55.3 4.1 %collective-permute-start.21 = (f32[48,256]{1,0:T(8,128)S(1)}, f32[48,256]{1,0:T(8,128)S(1)}, u32[]{:S(2)}, u32[]{:S(2)}) collective-permute-start(f32[48,256]{1,0:T(8,128)S(1)} %root_part.3.first), channel_id=1, source_target_pairs={{0,4},{1,5},{2,6},{3,7},{4,0},{5,1},{6,2},{7,3},{8,12},{9,13},{10,... | collective-permute-start | bytes 147464 | tf_op jit(solution)/shard_map/ppermute | solution.py:333
  55.3 4.1 %collective-permute-start.20 = (f32[48,256]{1,0:T(8,128)S(1)}, f32[48,256]{1,0:T(8,128)S(1)}, u32[]{:S(2)}, u32[]{:S(2)}) collective-permute-start(f32[48,256]{1,0:T(8,128)S(1)} %root_part.3.first), channel_id=1, source_target_pairs={{0,1},{1,0},{2,3},{3,2},{4,5},{5,4},{6,7},{7,6},{8,9},{9,8},{10,11... | collective-permute-start | bytes 147464 | tf_op jit(solution)/shard_map/ppermute | solution.py:333
  59.5 1.4 %collective-permute-start.23 = (f32[144,256]{1,0:T(8,128)S(1)}, f32[144,256]{1,0:T(8,128)S(1)}, u32[]{:S(2)}, u32[]{:S(2)}) collective-permute-start(f32[144,256]{1,0:T(8,128)S(1)} %pair_message.3.own), channel_id=1, source_target_pairs={{0,2},{2,0},{4,6},{6,4},{1,3},{3,1},{5,7},{7,5},{8,10},{10,8},{12,... | collective-permute-start | bytes 442376 | tf_op jit(solution)/shard_map/ppermute | solution.py:340
  (1 other events, 33.1 us)

commit v3 on v2

--- a/solution.py
+++ b/solution.py
@@ -17,25 +17,51 @@
 COLS = (((0,), (0,)), ((), ()))
 
 
-def neighbour_pairs(count, odd):
+def neighbour(index, count, odd):
+    other = index + 1 if index % 2 == odd else index - 1
+    return other if 0 <= other < count else None
+
+
+def swap_list(sizes):
+    swaps = [(dim, odd) for odd in (1, 0) for dim in (0, 1, 2) if sizes[dim] > 1 + odd]
+    return sorted(swaps, key=lambda swap: swap == (1, 0))
+
+
+def flat(sizes, place):
+    return (place[0] * sizes[1] + place[1]) * sizes[2] + place[2]
+
+
+def swap_pairs(sizes, dim, odd):
     pairs = []
-    for low in range(odd, count - 1, 2):
-        pairs += [(low, low + 1), (low + 1, low)]
+    for place in itertools.product(*map(range, sizes)):
+        there = list(place)
+        other = neighbour(place[dim], sizes[dim], odd)
+        if other is not None:
+            there[dim] = other
+        elif odd and sizes[dim] % 2 == 0:
+            if dim == 1:
+                there[1] = sizes[1] - 1 - place[1]
+            elif sizes[1] % 2 == 0:
+                there[1] = place[1] ^ 1
+        if tuple(there) != place:
+            pairs.append((flat(sizes, place), flat(sizes, there)))
     return pairs
-
-
-def swap_list(sizes):
-    swaps = []
-    for dim, count in enumerate(sizes):
-        for odd in (0, 1):
-            if neighbour_pairs(count, odd):
-                swaps.append((dim, odd))
-    return swaps
 
 
 def swap_face(dim, odd):
     high = (lax.axis_index(AXES[dim]) + odd + 1) % 2
     return 2 * dim + high
+
+
+def add_halos(swaps, sizes, total, halos):
+    height = total.shape[0] // FACES
+    for (dim, odd), halo in zip(swaps, halos):
+        face = swap_face(dim, odd)
+        other = lax.axis_index(AXES[dim]) + 2 * (face - 2 * dim) - 1
+
+        @pl.when(jnp.logical_and(other >= 0, other < sizes[dim]))
+        def _():
+            total[rows_of(face, height), :] -= halo[...]
 
 
 def partner(index, offset, count):
@@ -99,56 +125,56 @@
 
 
 def first_kernel(swaps, order_hbm, *refs):
-    hbm, held, refs = refs[:8], refs[8:16], refs[16:]
+    hbm, held, refs = refs[:8], refs[8:15], refs[15:]
     (rest, *messages), scratch = refs[: 1 + len(swaps)], refs[1 + len(swaps) :]
-    matrix, loads, modes_t, modes_s, scale, *small = held
-    order, start, modes, weights, local_iter, product, sems = scratch
-    matrix_hbm, start_hbm, loads_hbm, modes_hbm, weights_hbm, *small_hbm = hbm
-    height = rest.shape[0] // FACES
-    part = matrix.shape[0] // 2
-
-    pairs = [(order_hbm, order), (modes_hbm, modes), (weights_hbm, weights), (start_hbm, start)]
-    pairs += [(matrix_hbm.at[k * part : (k + 1) * part, :], matrix.at[k * part : (k + 1) * part, :]) for k in range(2)]
-    pairs += [(loads_hbm, loads)] + list(zip(small_hbm, small))
+    matrix, loads = held[:2]
+    order, start, local_iter, product, sems = scratch
+    matrix_hbm, start_hbm = hbm[:2]
+    parts = 4
+    part = matrix.shape[0] // parts
+
+    pairs = [(order_hbm, order), (start_hbm, start)]
+    for k in range(parts):
+        rows = slice(k * part, (k + 1) * part)
+        pairs.append((matrix_hbm.at[rows, :], matrix.at[rows, :]))
+    pairs += list(zip(hbm[2:], held[1:]))
     copies = [pltpu.make_async_copy(*pair, sems.at[k]) for k, pair in enumerate(pairs)]
     for copy in copies:
         copy.start()
+    copies[0].wait()
     copies[1].wait()
+    reorder(order, lambda rows: start[rows, :], local_iter)
+    for k in range(parts):
+        copies[2 + k].wait()
+        rows = slice(k * part, (k + 1) * part)
+        product[rows, :] = jnp.dot(matrix[rows, :], local_iter[...], preferred_element_type=F32)
+    for copy in copies[2 + parts :]:
+        copy.wait()
+    send_rest(swaps, order, loads, product, rest, messages)
+
+
+def constants_kernel(modes, weights, modes_t, modes_s, scale):
     high, low = split(modes[...])
     count = high.shape[0]
+    height = scale.shape[1]
     modes_s[:count, :] = high
-    modes_s[count : 2 * count, :] = low
-    modes_s[2 * count :, :] = high
+    modes_s[count:, :] = low
     modes_t[...] = jnp.concatenate([high.T, low.T, high.T], axis=1)
-    copies[2].wait()
     for j in range(FACES):
         block = slice(j * height, (j + 1) * height)
         scale[block, :] = jnp.broadcast_to(weights[:, block], (height, height)).T
-    copies[0].wait()
-    copies[3].wait()
-    reorder(order, lambda rows: start[rows, :], local_iter)
-    for k in range(2):
-        copies[4 + k].wait()
-        rows = slice(k * part, (k + 1) * part)
-        product[rows, :] = jnp.dot(matrix[rows, :], local_iter[...], preferred_element_type=F32)
-    for copy in copies[6:]:
-        copy.wait()
-    send_rest(swaps, order, loads, product, rest, messages)
-
-
-def residual_kernel(swaps, rest, modes_s, root_map, *more):
+
+
+def residual_kernel(swaps, sizes, rest, modes_s, root_map, *more):
     halos, (residual, coarse, root) = more[: len(swaps)], more[len(swaps) :]
-    height = rest.shape[0] // FACES
     count = coarse.shape[0]
     residual[...] = rest[...]
-    for (dim, odd), halo in zip(swaps, halos):
-        face = rows_of(swap_face(dim, odd), height)
-        residual[face, :] -= halo[...]
+    add_halos(swaps, sizes, residual, halos)
     high, low = split(residual[...])
-    both = jnp.dot(modes_s[: 2 * count, :], high, preferred_element_type=F32)
+    both = jnp.dot(modes_s[...], high, preferred_element_type=F32)
     fine = jnp.dot(modes_s[:count, :], low, preferred_element_type=F32)
     coarse[...] = both[:count, :] + (both[count:, :] + fine)
-    root[...] = dot3(root_map[...], coarse[...], COLS)
+    root[...] = dot3(root_map[...], coarse[...])
 
 
 def root_kernel(count, coarse, root_inverse, root, *more):
@@ -174,7 +200,7 @@
 
 
 def amplitude_of(members, sizes, region_rows, root_map, own, other, stack):
-    modes = root_map.shape[0]
+    modes = root_map.shape[1]
     y, z = lax.axis_index("gy"), lax.axis_index("gz")
     half = sizes[0] // 2
     count = len(members)
@@ -185,7 +211,7 @@
         stack[rows_of(at_y * sizes[1] + at_z, modes), :] = own[piece, :]
         stack[rows_of((at_y ^ 1) * sizes[1] + at_z, modes), :] = other[piece, :]
     root_part = own[count * modes :, :] + other[count * modes :, :]
-    return dot3(region_rows[...], stack[...]) + dot3(root_map[...], root_part)
+    return dot3(region_rows[...], stack[...]) + dot3(root_map[...], root_part, COLS)
 
 
 def correction_of(modes_t, amplitude):
@@ -252,8 +278,8 @@
     weights = interface_weights.reshape(1, iface)
     modes = coarse_modes.reshape(coarse_modes.shape[-2], iface)
     mode_count = modes.shape[0]
-    root_map = region_weights.reshape(mode_count, region_weights.shape[-1])
-    root_modes = root_map.shape[1]
+    root_map = region_weights.reshape(mode_count, region_weights.shape[-1]).T
+    root_modes = root_map.shape[0]
     region_rows = region_inverse.reshape(mode_count, region_inverse.shape[-1])
     target = loads.reshape(iface, cases)
     solution = start.reshape(iface, cases)
@@ -270,29 +296,27 @@
 
     for step in range(ITERS):
         if step == 0:
-            held = [
-                (pltpu.VMEM, matrix.shape, BF16),
-                (pltpu.VMEM, target.shape, BF16),
-                (pltpu.VMEM, (iface, 3 * mode_count), BF16),
-                (pltpu.VMEM, (3 * mode_count, iface), BF16),
-                (pltpu.VMEM, (iface, height), F32),
-                (pltpu.VMEM, root_map.shape, F32),
-                (pltpu.VMEM, region_rows.shape, F32),
-                (pltpu.VMEM, root_inverse.shape, F32),
-            ]
             inputs = [order, matrix, solution, target, modes, weights, root_map, region_rows, root_inverse]
+            held = [(pltpu.VMEM, item.shape, item.dtype) for item in [matrix] + inputs[3:]]
             outs = call(
                 functools.partial(first_kernel, swaps),
                 held + [full] + [face] * len(swaps),
                 inputs,
                 "first_product",
-                places
-                + [pltpu.VMEM((iface, cases), BF16), pltpu.VMEM(modes.shape, F32), pltpu.VMEM(weights.shape, F32)]
-                + work
-                + [pltpu.SemaphoreType.DMA((10,))],
+                places + [pltpu.VMEM((iface, cases), BF16)] + work + [pltpu.SemaphoreType.DMA((12,))],
                 len(inputs),
             )
-            matrix, target, modes_t, modes_s, scale, root_map, region_rows, root_inverse, rest, *messages = outs
+            matrix, target, modes, weights, root_map, region_rows, root_inverse, rest, *messages = outs
+            modes_t, modes_s, scale = call(
+                constants_kernel,
+                [
+                    (pltpu.VMEM, (iface, 3 * mode_count), BF16),
+                    (pltpu.VMEM, (2 * mode_count, iface), BF16),
+                    (pltpu.VMEM, (iface, height), F32),
+                ],
+                [modes, weights],
+                "constants",
+            )
         else:
             solution, rest, *messages = call(
                 functools.partial(middle_kernel, swaps, members, sizes[1:]),
@@ -303,11 +327,11 @@
                 1,
             )
         halos = [
-            lax.ppermute(message, AXES[dim], neighbour_pairs(sizes[dim], odd))
+            lax.ppermute(message, AXES, swap_pairs(sizes, dim, odd))
             for (dim, odd), message in zip(swaps, messages)
         ]
         residual, coarse, root = call(
-            functools.partial(residual_kernel, swaps),
+            functools.partial(residual_kernel, swaps, sizes),
             [full, (pltpu.VMEM, (mode_count, cases), F32), (pltpu.VMEM, (root_modes, cases), F32)],
             [rest, modes_s, root_map] + halos,
             "residual_coarse",
@@ -337,7 +361,7 @@
             [message] + pieces,
             "pair_message",
         )
-        other = lax.ppermute(own, "gy", neighbour_pairs(sizes[1], 0))
+        other = lax.ppermute(own, AXES, swap_pairs(sizes, 1, 0))
     (solution,) = call(
         functools.partial(last_kernel, members, sizes[1:]),
         [(jax.ShapeDtypeStruct, (iface, cases), F32)],

time: 62.6 us -> 57 us (0.911)
  starting transfers between devices: 29.3 us -> 26.2 us
  waiting for transfers between devices: 23.6 us -> 22.2 us
  local copies, waits for them, and re-layouts: 1.38 us -> 0.01 us
    ppermute x6, starting transfers between devices: 9.75 us -> 6.99 us  [per_device(): pieces.append(lax.ppermute(message, ('gy', 'gz'), moves))]
    ppermute x6, waiting for transfers between devices: 6.96 us -> 4.54 us  [per_device(): lax.ppermute(root, 'gx', [(i, partner(i, offset, sizes[0])) for i in rang...]
    ppermute x6, starting transfers between devices: 11 us -> 8.8 us  [per_device(): lax.ppermute(root, 'gx', [(i, partner(i, offset, sizes[0])) for i in rang...]
    ppermute x12, starting transfers between devices: 8.53 us -> 10.4 us  [the longest x10 10.3 us: per_device(): lax.ppermute(message, AXES, swap_pairs(sizes, dim, odd))]
    unnamed x3 -> x2, local copies, waits for them, and re-layouts: 1.38 us -> 0.01 us
    ppermute x12, waiting for transfers between devices: 10.5 us -> 11.5 us  [the longest x10 8.83 us: per_device(): lax.ppermute(message, AXES, swap_pairs(sizes, dim, odd))]
    pallas_call x9 -> x10, Pallas kernels: 7.99 us -> 8.35 us  [call(): pl.pallas_call(body, out_shape=[item(shape, dtype) for item, shape, dtype...]
  transfers between devices with their start and end apart: 24 -> 24, of which waited for: 15 -> 18; matrix products, arithmetic and copies ran while one was open for 0% -> 0% of each run, Pallas kernels for 0% -> 1%
where the time goes in v3:
time: 57 us; the launch traced here: 56.9 us
  starting transfers between devices  26.2 us (46%)
  waiting for transfers between devices  22.2 us (39%)
  Pallas kernels  8.35 us (15%)
    ppermute x10, starting transfers between devices, per_device(): lax.ppermute(message, AXES, swap_pairs(sizes, dim, odd))  10.3 us
    ppermute x10, waiting for transfers between devices, per_device(): lax.ppermute(message, AXES, swap_pairs(sizes, dim, odd))  8.83 us
    ppermute x6, starting transfers between devices, per_device(): lax.ppermute(root, 'gx', [(i, partner(i, offset, sizes[0])) for i in rang...  8.8 us
    pallas_call x10, Pallas kernels, call(): pl.pallas_call(body, out_shape=[item(shape, dtype) for item, shape, dtype...  8.35 us
    ppermute x6, starting transfers between devices, per_device(): pieces.append(lax.ppermute(message, ('gy', 'gz'), moves))  6.99 us
    ppermute x6, waiting for transfers between devices, per_device(): pieces.append(lax.ppermute(message, ('gy', 'gz'), moves))  6.15 us
    ppermute x6, waiting for transfers between devices, per_device(): lax.ppermute(root, 'gx', [(i, partner(i, offset, sizes[0])) for i in rang...  4.54 us
    ppermute x2, waiting for transfers between devices, per_device(): other = lax.ppermute(own, AXES, swap_pairs(sizes, 1, 0))  2.72 us
  transfers between devices with their start and end apart: 24, of which 18 were waited for; matrix products, arithmetic and copies ran while one was open for 0% of the time, Pallas kernels for 1%

profile of v3, /device:TPU:0, one launch (start us, length us, event | category | flops | bytes accessed | tf_op | source)
XLA Modules:
  0.0 56.9 jit_solution(18371331213253972698)
XLA Ops:
  0.0 3.3 %first_product.1 = (bf16[1024,1024]{1,0:T(8,128)(2,1)S(1)}, bf16[1024,256]{1,0:T(8,128)(2,1)S(1)}, f32[32,1024]{1,0:T(8,128)S(1)}, f32[1,1024]{1,0:T(1,128)S(1)}...) custom-call(s32[1,8]{1,0:T(1,128)} %bitcast.19, ...), custom_call_target="tpu_custom_call" | custom-call | tf_op jit(solution)/shard_map/first_product/pallas_call | solution.py:93
  3.8 2.6 %collective-permute-start.1 = (f32[128,256]{1,0:T(8,128)S(1)}, f32[128,256]{1,0:T(8,128)S(1)}, u32[]{:S(2)}, u32[]{:S(2)}) collective-permute-start(f32[128,256]{1,0:T(8,128)S(1)} %get-tuple-element.42), channel_id=1, source_target_pairs={{0,6},{1,7},{2,4},{3,5},{4,2},{5,3},{6,0},{7,1},{8,14},{9,15},{10,... | collective-permute-start | bytes 393224 | tf_op jit(solution)/shard_map/ppermute | solution.py:330
  6.4 2.2 %collective-permute-start.2 = (f32[128,256]{1,0:T(8,128)S(1)}, f32[128,256]{1,0:T(8,128)S(1)}, u32[]{:S(2)}, u32[]{:S(2)}) collective-permute-start(f32[128,256]{1,0:T(8,128)S(1)} %get-tuple-element.43), channel_id=1, source_target_pairs={{0,8},{1,9},{2,10},{3,11},{4,12},{5,13},{6,14},{7,15},{8,0},{9,1},... | collective-permute-start | bytes 393224 | tf_op jit(solution)/shard_map/ppermute | solution.py:330
  8.6 1.5 %collective-permute-start.3 = (f32[128,256]{1,0:T(8,128)S(1)}, f32[128,256]{1,0:T(8,128)S(1)}, u32[]{:S(2)}, u32[]{:S(2)}) collective-permute-start(f32[128,256]{1,0:T(8,128)S(1)} %get-tuple-element.44), channel_id=1, source_target_pairs={{0,1},{1,0},{2,3},{3,2},{4,5},{5,4},{6,7},{7,6},{8,9},{9,8},{10,11... | collective-permute-start | bytes 393224 | tf_op jit(solution)/shard_map/ppermute | solution.py:330
  11.0 1.6 %collective-permute-done.2.more_2_ = f32[128,256]{1,0:T(8,128)S(1)} collective-permute-done((f32[128,256]{1,0:T(8,128)S(1)}, f32[128,256]{1,0:T(8,128)S(1)}, u32[]{:S(2)}, u32[]{:S(2)}) %collective-permute-start.2) | collective-permute-done | bytes 131104 | tf_op jit(solution)/shard_map/ppermute | solution.py:330
  12.7 2.0 %collective-permute-done.3.more_3_ = f32[128,256]{1,0:T(8,128)S(1)} collective-permute-done((f32[128,256]{1,0:T(8,128)S(1)}, f32[128,256]{1,0:T(8,128)S(1)}, u32[]{:S(2)}, u32[]{:S(2)}) %collective-permute-start.3) | collective-permute-done | bytes 131104 | tf_op jit(solution)/shard_map/ppermute | solution.py:330
  15.3 1.4 %collective-permute-start.7 = (f32[16,256]{1,0:T(8,128)S(1)}, f32[16,256]{1,0:T(8,128)S(1)}, u32[]{:S(2)}, u32[]{:S(2)}) collective-permute-start(f32[16,256]{1,0:T(8,128)S(1)} %get-tuple-element.52.root), channel_id=1, source_target_pairs={{0,24},{8,16},{16,8},{24,0},{1,25},{9,17},{17,9},{25,1},{2,26},{10... | collective-permute-start | bytes 49160 | tf_op jit(solution)/shard_map/ppermute | solution.py:340
  17.0 2.6 %collective-permute-start.5 = (f32[16,256]{1,0:T(8,128)S(1)}, f32[16,256]{1,0:T(8,128)S(1)}, u32[]{:S(2)}, u32[]{:S(2)}) collective-permute-start(f32[16,256]{1,0:T(8,128)S(1)} %get-tuple-element.52.root), channel_id=1, source_target_pairs={{0,8},{8,0},{16,24},{24,16},{1,9},{9,1},{17,25},{25,17},{2,10},{10... | collective-permute-start | bytes 49160 | tf_op jit(solution)/shard_map/ppermute | solution.py:340
  21.6 1.5 %collective-permute-start.10 = (f32[48,256]{1,0:T(8,128)S(1)}, f32[48,256]{1,0:T(8,128)S(1)}, u32[]{:S(2)}, u32[]{:S(2)}) collective-permute-start(f32[48,256]{1,0:T(8,128)S(1)} %root_part.2.first), channel_id=1, source_target_pairs={{0,5},{1,4},{2,7},{3,6},{4,1},{5,0},{6,3},{7,2},{8,13},{9,12},{10,... | collective-permute-start | bytes 147464 | tf_op jit(solution)/shard_map/ppermute | solution.py:357
  23.1 1.5 %collective-permute-start.9 = (f32[48,256]{1,0:T(8,128)S(1)}, f32[48,256]{1,0:T(8,128)S(1)}, u32[]{:S(2)}, u32[]{:S(2)}) collective-permute-start(f32[48,256]{1,0:T(8,128)S(1)} %root_part.2.first), channel_id=1, source_target_pairs={{0,4},{1,5},{2,6},{3,7},{4,0},{5,1},{6,2},{7,3},{8,12},{9,13},{10,... | collective-permute-start | bytes 147464 | tf_op jit(solution)/shard_map/ppermute | solution.py:357
  25.1 1.5 %collective-permute-done.10.more_2_ = f32[48,256]{1,0:T(8,128)S(1)} collective-permute-done((f32[48,256]{1,0:T(8,128)S(1)}, f32[48,256]{1,0:T(8,128)S(1)}, u32[]{:S(2)}, u32[]{:S(2)}) %collective-permute-start.10) | collective-permute-done | bytes 49184 | tf_op jit(solution)/shard_map/ppermute | solution.py:357
  27.2 1.5 %collective-permute-done.8.more_0_ = f32[48,256]{1,0:T(8,128)S(1)} collective-permute-done((f32[48,256]{1,0:T(8,128)S(1)}, f32[48,256]{1,0:T(8,128)S(1)}, u32[]{:S(2)}, u32[]{:S(2)}) %collective-permute-start.8) | collective-permute-done | bytes 49184 | tf_op jit(solution)/shard_map/ppermute | solution.py:357
  28.8 1.4 %collective-permute-done.11.other = f32[144,256]{1,0:T(8,128)S(1)} collective-permute-done((f32[144,256]{1,0:T(8,128)S(1)}, f32[144,256]{1,0:T(8,128)S(1)}, u32[]{:S(2)}, u32[]{:S(2)}) %collective-permute-start.11) | collective-permute-done | bytes 147488 | tf_op jit(solution)/shard_map/ppermute | solution.py:364
  30.2 1.6 %update_product.1 = (f32[1024,256]{1,0:T(8,128)S(1)}, f32[1024,256]{1,0:T(8,128)S(1)}, f32[128,256]{1,0:T(8,128)S(1)}, f32[128,256]{1,0:T(8,128)S(1)}, f32[128,2...) custom-call(s32[1,8]{1,0:T(1,128)} %bitcast.20, bf16[1024,1024]{1,0:T(8,128)(2,1)S(1)} %get-tuple-element.34.matrix, ...), custom_call_target="tpu_custom_call" | custom-call | tf_op jit(solution)/shard_map/update_product/pallas_call | solution.py:93
  32.5 1.8 %collective-permute-start.14 = (f32[128,256]{1,0:T(8,128)S(1)}, f32[128,256]{1,0:T(8,128)S(1)}, u32[]{:S(2)}, u32[]{:S(2)}) collective-permute-start(f32[128,256]{1,0:T(8,128)S(1)} %get-tuple-element.57), channel_id=1, source_target_pairs={{0,8},{1,9},{2,10},{3,11},{4,12},{5,13},{6,14},{7,15},{8,0},{9,1},... | collective-permute-start | bytes 393224 | tf_op jit(solution)/shard_map/ppermute | solution.py:330
  34.9 2.5 %collective-permute-done.13.more_1_ = f32[128,256]{1,0:T(8,128)S(1)} collective-permute-done((f32[128,256]{1,0:T(8,128)S(1)}, f32[128,256]{1,0:T(8,128)S(1)}, u32[]{:S(2)}, u32[]{:S(2)}) %collective-permute-start.13) | collective-permute-done | bytes 131104 | tf_op jit(solution)/shard_map/ppermute | solution.py:330
  38.6 1.5 %collective-permute-done.15.more_3_ = f32[128,256]{1,0:T(8,128)S(1)} collective-permute-done((f32[128,256]{1,0:T(8,128)S(1)}, f32[128,256]{1,0:T(8,128)S(1)}, u32[]{:S(2)}, u32[]{:S(2)}) %collective-permute-start.15) | collective-permute-done | bytes 131104 | tf_op jit(solution)/shard_map/ppermute | solution.py:330
  40.6 2.5 %collective-permute-start.19 = (f32[16,256]{1,0:T(8,128)S(1)}, f32[16,256]{1,0:T(8,128)S(1)}, u32[]{:S(2)}, u32[]{:S(2)}) collective-permute-start(f32[16,256]{1,0:T(8,128)S(1)} %get-tuple-element.62.root), channel_id=1, source_target_pairs={{0,24},{8,16},{16,8},{24,0},{1,25},{9,17},{17,9},{25,1},{2,26},{10... | collective-permute-start | bytes 49160 | tf_op jit(solution)/shard_map/ppermute | solution.py:340
  43.1 1.9 %collective-permute-start.17 = (f32[16,256]{1,0:T(8,128)S(1)}, f32[16,256]{1,0:T(8,128)S(1)}, u32[]{:S(2)}, u32[]{:S(2)}) collective-permute-start(f32[16,256]{1,0:T(8,128)S(1)} %get-tuple-element.62.root), channel_id=1, source_target_pairs={{0,8},{8,0},{16,24},{24,16},{1,9},{9,1},{17,25},{25,17},{2,10},{10... | collective-permute-start | bytes 49160 | tf_op jit(solution)/shard_map/ppermute | solution.py:340
  46.2 1.5 %collective-permute-done.18.more_1_ = f32[16,256]{1,0:T(8,128)S(1)} collective-permute-done((f32[16,256]{1,0:T(8,128)S(1)}, f32[16,256]{1,0:T(8,128)S(1)}, u32[]{:S(2)}, u32[]{:S(2)}) %collective-permute-start.18) | collective-permute-done | bytes 16416 | tf_op jit(solution)/shard_map/ppermute | solution.py:340
  47.9 1.4 %collective-permute-start.22 = (f32[48,256]{1,0:T(8,128)S(1)}, f32[48,256]{1,0:T(8,128)S(1)}, u32[]{:S(2)}, u32[]{:S(2)}) collective-permute-start(f32[48,256]{1,0:T(8,128)S(1)} %root_part.3.first), channel_id=1, source_target_pairs={{0,5},{1,4},{2,7},{3,6},{4,1},{5,0},{6,3},{7,2},{8,13},{9,12},{10,... | collective-permute-start | bytes 147464 | tf_op jit(solution)/shard_map/ppermute | solution.py:357
  49.8 1.5 %collective-permute-start.20 = (f32[48,256]{1,0:T(8,128)S(1)}, f32[48,256]{1,0:T(8,128)S(1)}, u32[]{:S(2)}, u32[]{:S(2)}) collective-permute-start(f32[48,256]{1,0:T(8,128)S(1)} %root_part.3.first), channel_id=1, source_target_pairs={{0,1},{1,0},{2,3},{3,2},{4,5},{5,4},{6,7},{7,6},{8,9},{9,8},{10,11... | collective-permute-start | bytes 147464 | tf_op jit(solution)/shard_map/ppermute | solution.py:357
  51.4 1.5 %collective-permute-done.22.more_2_ = f32[48,256]{1,0:T(8,128)S(1)} collective-permute-done((f32[48,256]{1,0:T(8,128)S(1)}, f32[48,256]{1,0:T(8,128)S(1)}, u32[]{:S(2)}, u32[]{:S(2)}) %collective-permute-start.22) | collective-permute-done | bytes 49184 | tf_op jit(solution)/shard_map/ppermute | solution.py:357
  55.4 1.5 %update_last.1 = f32[1024,256]{1,0:T(8,128)} custom-call(f32[1024,256]{1,0:T(8,128)S(1)} %get-tuple-element.53.solution, f32[1024,256]{1,0:T(8,128)S(1)} %get-tuple-element.60.residual, f32[1024,128]{1,0:T(8,128)S(1)} %get-tuple-element.47.scale, bf16[1024,96]{1,0:T(8,128)(2,1)S(1)} %get-tuple-element.48.modes_t, f32[16,32]{1,0:T(8,128)S(1)} %get-tuple-element.40.root_map, ...), custom_call_target="tpu_custom_call" | custom-call | tf_op jit(solution)/shard_map/update_last/pallas_call | solution.py:93
  (36 shorter events, 13.0 us)
Async XLA Ops:
  3.3 7.7 %collective-permute-start = (f32[128,256]{1,0:T(8,128)S(1)}, f32[128,256]{1,0:T(8,128)S(1)}, u32[]{:S(2)}, u32[]{:S(2)}) collective-permute-start(f32[128,256]{1,0:T(8,128)S(1)} %get-tuple-element.41), channel_id=1, source_target_pairs={{0,2},{1,3},{2,0},{3,1},{4,6},{5,7},{6,4},{7,5},{8,16},{9,17},{10,... | collective-permute-start | bytes 393224 | tf_op jit(solution)/shard_map/ppermute | solution.py:330
  3.8 7.2 %collective-permute-start.1 = (f32[128,256]{1,0:T(8,128)S(1)}, f32[128,256]{1,0:T(8,128)S(1)}, u32[]{:S(2)}, u32[]{:S(2)}) collective-permute-start(f32[128,256]{1,0:T(8,128)S(1)} %get-tuple-element.42), channel_id=1, source_target_pairs={{0,6},{1,7},{2,4},{3,5},{4,2},{5,3},{6,0},{7,1},{8,14},{9,15},{10,... | collective-permute-start | bytes 393224 | tf_op jit(solution)/shard_map/ppermute | solution.py:330
  6.4 6.3 %collective-permute-start.2 = (f32[128,256]{1,0:T(8,128)S(1)}, f32[128,256]{1,0:T(8,128)S(1)}, u32[]{:S(2)}, u32[]{:S(2)}) collective-permute-start(f32[128,256]{1,0:T(8,128)S(1)} %get-tuple-element.43), channel_id=1, source_target_pairs={{0,8},{1,9},{2,10},{3,11},{4,12},{5,13},{6,14},{7,15},{8,0},{9,1},... | collective-permute-start | bytes 393224 | tf_op jit(solution)/shard_map/ppermute | solution.py:330
  8.6 6.1 %collective-permute-start.3 = (f32[128,256]{1,0:T(8,128)S(1)}, f32[128,256]{1,0:T(8,128)S(1)}, u32[]{:S(2)}, u32[]{:S(2)}) collective-permute-start(f32[128,256]{1,0:T(8,128)S(1)} %get-tuple-element.44), channel_id=1, source_target_pairs={{0,1},{1,0},{2,3},{3,2},{4,5},{5,4},{6,7},{7,6},{8,9},{9,8},{10,11... | collective-permute-start | bytes 393224 | tf_op jit(solution)/shard_map/ppermute | solution.py:330
  10.1 4.6 %collective-permute-start.4 = (f32[128,256]{1,0:T(8,128)S(1)}, f32[128,256]{1,0:T(8,128)S(1)}, u32[]{:S(2)}, u32[]{:S(2)}) collective-permute-start(f32[128,256]{1,0:T(8,128)S(1)} %get-tuple-element.45), channel_id=1, source_target_pairs={{0,2},{1,3},{2,0},{3,1},{4,6},{5,7},{6,4},{7,5},{8,10},{9,11},{10,... | collective-permute-start | bytes 393224 | tf_op jit(solution)/shard_map/ppermute | solution.py:330
  15.3 5.5 %collective-permute-start.7 = (f32[16,256]{1,0:T(8,128)S(1)}, f32[16,256]{1,0:T(8,128)S(1)}, u32[]{:S(2)}, u32[]{:S(2)}) collective-permute-start(f32[16,256]{1,0:T(8,128)S(1)} %get-tuple-element.52.root), channel_id=1, source_target_pairs={{0,24},{8,16},{16,8},{24,0},{1,25},{9,17},{17,9},{25,1},{2,26},{10... | collective-permute-start | bytes 49160 | tf_op jit(solution)/shard_map/ppermute | solution.py:340
  16.6 4.7 %collective-permute-start.6 = (f32[16,256]{1,0:T(8,128)S(1)}, f32[16,256]{1,0:T(8,128)S(1)}, u32[]{:S(2)}, u32[]{:S(2)}) collective-permute-start(f32[16,256]{1,0:T(8,128)S(1)} %get-tuple-element.52.root), channel_id=1, source_target_pairs={{0,16},{8,24},{16,0},{24,8},{1,17},{9,25},{17,1},{25,9},{2,18},{10... | collective-permute-start | bytes 49160 | tf_op jit(solution)/shard_map/ppermute | solution.py:340
  17.0 4.4 %collective-permute-start.5 = (f32[16,256]{1,0:T(8,128)S(1)}, f32[16,256]{1,0:T(8,128)S(1)}, u32[]{:S(2)}, u32[]{:S(2)}) collective-permute-start(f32[16,256]{1,0:T(8,128)S(1)} %get-tuple-element.52.root), channel_id=1, source_target_pairs={{0,8},{8,0},{16,24},{24,16},{1,9},{9,1},{17,25},{25,17},{2,10},{10... | collective-permute-start | bytes 49160 | tf_op jit(solution)/shard_map/ppermute | solution.py:340
  21.6 5.0 %collective-permute-start.10 = (f32[48,256]{1,0:T(8,128)S(1)}, f32[48,256]{1,0:T(8,128)S(1)}, u32[]{:S(2)}, u32[]{:S(2)}) collective-permute-start(f32[48,256]{1,0:T(8,128)S(1)} %root_part.2.first), channel_id=1, source_target_pairs={{0,5},{1,4},{2,7},{3,6},{4,1},{5,0},{6,3},{7,2},{8,13},{9,12},{10,... | collective-permute-start | bytes 147464 | tf_op jit(solution)/shard_map/ppermute | solution.py:357
  23.1 4.1 %collective-permute-start.9 = (f32[48,256]{1,0:T(8,128)S(1)}, f32[48,256]{1,0:T(8,128)S(1)}, u32[]{:S(2)}, u32[]{:S(2)}) collective-permute-start(f32[48,256]{1,0:T(8,128)S(1)} %root_part.2.first), channel_id=1, source_target_pairs={{0,4},{1,5},{2,6},{3,7},{4,0},{5,1},{6,2},{7,3},{8,12},{9,13},{10,... | collective-permute-start | bytes 147464 | tf_op jit(solution)/shard_map/ppermute | solution.py:357
  24.6 4.1 %collective-permute-start.8 = (f32[48,256]{1,0:T(8,128)S(1)}, f32[48,256]{1,0:T(8,128)S(1)}, u32[]{:S(2)}, u32[]{:S(2)}) collective-permute-start(f32[48,256]{1,0:T(8,128)S(1)} %root_part.2.first), channel_id=1, source_target_pairs={{0,1},{1,0},{2,3},{3,2},{4,5},{5,4},{6,7},{7,6},{8,9},{9,8},{10,11... | collective-permute-start | bytes 147464 | tf_op jit(solution)/shard_map/ppermute | solution.py:357
  28.7 1.4 %collective-permute-start.11 = (f32[144,256]{1,0:T(8,128)S(1)}, f32[144,256]{1,0:T(8,128)S(1)}, u32[]{:S(2)}, u32[]{:S(2)}) collective-permute-start(f32[144,256]{1,0:T(8,128)S(1)} %pair_message.2.own), channel_id=1, source_target_pairs={{0,2},{1,3},{2,0},{3,1},{4,6},{5,7},{6,4},{7,5},{8,10},{9,11},{10,... | collective-permute-start | bytes 442376 | tf_op jit(solution)/shard_map/ppermute | solution.py:364
  31.8 3.1 %collective-permute-start.12 = (f32[128,256]{1,0:T(8,128)S(1)}, f32[128,256]{1,0:T(8,128)S(1)}, u32[]{:S(2)}, u32[]{:S(2)}) collective-permute-start(f32[128,256]{1,0:T(8,128)S(1)} %get-tuple-element.55), channel_id=1, source_target_pairs={{0,2},{1,3},{2,0},{3,1},{4,6},{5,7},{6,4},{7,5},{8,16},{9,17},{10,... | collective-permute-start | bytes 393224 | tf_op jit(solution)/shard_map/ppermute | solution.py:330
  32.0 5.3 %collective-permute-start.13 = (f32[128,256]{1,0:T(8,128)S(1)}, f32[128,256]{1,0:T(8,128)S(1)}, u32[]{:S(2)}, u32[]{:S(2)}) collective-permute-start(f32[128,256]{1,0:T(8,128)S(1)} %get-tuple-element.56), channel_id=1, source_target_pairs={{0,6},{1,7},{2,4},{3,5},{4,2},{5,3},{6,0},{7,1},{8,14},{9,15},{10,... | collective-permute-start | bytes 393224 | tf_op jit(solution)/shard_map/ppermute | solution.py:330
  32.5 6.1 %collective-permute-start.14 = (f32[128,256]{1,0:T(8,128)S(1)}, f32[128,256]{1,0:T(8,128)S(1)}, u32[]{:S(2)}, u32[]{:S(2)}) collective-permute-start(f32[128,256]{1,0:T(8,128)S(1)} %get-tuple-element.57), channel_id=1, source_target_pairs={{0,8},{1,9},{2,10},{3,11},{4,12},{5,13},{6,14},{7,15},{8,0},{9,1},... | collective-permute-start | bytes 393224 | tf_op jit(solution)/shard_map/ppermute | solution.py:330
  34.3 5.8 %collective-permute-start.15 = (f32[128,256]{1,0:T(8,128)S(1)}, f32[128,256]{1,0:T(8,128)S(1)}, u32[]{:S(2)}, u32[]{:S(2)}) collective-permute-start(f32[128,256]{1,0:T(8,128)S(1)} %get-tuple-element.58), channel_id=1, source_target_pairs={{0,1},{1,0},{2,3},{3,2},{4,5},{5,4},{6,7},{7,6},{8,9},{9,8},{10,11... | collective-permute-start | bytes 393224 | tf_op jit(solution)/shard_map/ppermute | solution.py:330
  34.8 5.2 %collective-permute-start.16 = (f32[128,256]{1,0:T(8,128)S(1)}, f32[128,256]{1,0:T(8,128)S(1)}, u32[]{:S(2)}, u32[]{:S(2)}) collective-permute-start(f32[128,256]{1,0:T(8,128)S(1)} %get-tuple-element.59), channel_id=1, source_target_pairs={{0,2},{1,3},{2,0},{3,1},{4,6},{5,7},{6,4},{7,5},{8,10},{9,11},{10,... | collective-permute-start | bytes 393224 | tf_op jit(solution)/shard_map/ppermute | solution.py:330
  40.6 5.6 %collective-permute-start.19 = (f32[16,256]{1,0:T(8,128)S(1)}, f32[16,256]{1,0:T(8,128)S(1)}, u32[]{:S(2)}, u32[]{:S(2)}) collective-permute-start(f32[16,256]{1,0:T(8,128)S(1)} %get-tuple-element.62.root), channel_id=1, source_target_pairs={{0,24},{8,16},{16,8},{24,0},{1,25},{9,17},{17,9},{25,1},{2,26},{10... | collective-permute-start | bytes 49160 | tf_op jit(solution)/shard_map/ppermute | solution.py:340
  43.1 4.6 %collective-permute-start.18 = (f32[16,256]{1,0:T(8,128)S(1)}, f32[16,256]{1,0:T(8,128)S(1)}, u32[]{:S(2)}, u32[]{:S(2)}) collective-permute-start(f32[16,256]{1,0:T(8,128)S(1)} %get-tuple-element.62.root), channel_id=1, source_target_pairs={{0,16},{8,24},{16,0},{24,8},{1,17},{9,25},{17,1},{25,9},{2,18},{10... | collective-permute-start | bytes 49160 | tf_op jit(solution)/shard_map/ppermute | solution.py:340
  43.1 4.6 %collective-permute-start.17 = (f32[16,256]{1,0:T(8,128)S(1)}, f32[16,256]{1,0:T(8,128)S(1)}, u32[]{:S(2)}, u32[]{:S(2)}) collective-permute-start(f32[16,256]{1,0:T(8,128)S(1)} %get-tuple-element.62.root), channel_id=1, source_target_pairs={{0,8},{8,0},{16,24},{24,16},{1,9},{9,1},{17,25},{25,17},{2,10},{10... | collective-permute-start | bytes 49160 | tf_op jit(solution)/shard_map/ppermute | solution.py:340
  47.9 5.0 %collective-permute-start.22 = (f32[48,256]{1,0:T(8,128)S(1)}, f32[48,256]{1,0:T(8,128)S(1)}, u32[]{:S(2)}, u32[]{:S(2)}) collective-permute-start(f32[48,256]{1,0:T(8,128)S(1)} %root_part.3.first), channel_id=1, source_target_pairs={{0,5},{1,4},{2,7},{3,6},{4,1},{5,0},{6,3},{7,2},{8,13},{9,12},{10,... | collective-permute-start | bytes 147464 | tf_op jit(solution)/shard_map/ppermute | solution.py:357
  49.3 4.1 %collective-permute-start.21 = (f32[48,256]{1,0:T(8,128)S(1)}, f32[48,256]{1,0:T(8,128)S(1)}, u32[]{:S(2)}, u32[]{:S(2)}) collective-permute-start(f32[48,256]{1,0:T(8,128)S(1)} %root_part.3.first), channel_id=1, source_target_pairs={{0,4},{1,5},{2,6},{3,7},{4,0},{5,1},{6,2},{7,3},{8,12},{9,13},{10,... | collective-permute-start | bytes 147464 | tf_op jit(solution)/shard_map/ppermute | solution.py:357
  49.8 4.1 %collective-permute-start.20 = (f32[48,256]{1,0:T(8,128)S(1)}, f32[48,256]{1,0:T(8,128)S(1)}, u32[]{:S(2)}, u32[]{:S(2)}) collective-permute-start(f32[48,256]{1,0:T(8,128)S(1)} %root_part.3.first), channel_id=1, source_target_pairs={{0,1},{1,0},{2,3},{3,2},{4,5},{5,4},{6,7},{7,6},{8,9},{9,8},{10,11... | collective-permute-start | bytes 147464 | tf_op jit(solution)/shard_map/ppermute | solution.py:357
  53.9 1.4 %collective-permute-start.23 = (f32[144,256]{1,0:T(8,128)S(1)}, f32[144,256]{1,0:T(8,128)S(1)}, u32[]{:S(2)}, u32[]{:S(2)}) collective-permute-start(f32[144,256]{1,0:T(8,128)S(1)} %pair_message.3.own), channel_id=1, source_target_pairs={{0,2},{1,3},{2,0},{3,1},{4,6},{5,7},{6,4},{7,5},{8,10},{9,11},{10,... | collective-permute-start | bytes 442376 | tf_op jit(solution)/shard_map/ppermute | solution.py:364
  (1 other events, 30.1 us)

commit v4 on v3

--- a/solution.py
+++ b/solution.py
@@ -53,15 +53,19 @@
     return 2 * dim + high
 
 
+def has_neighbour(dim, face, sizes):
+    other = lax.axis_index(AXES[dim]) + 2 * (face - 2 * dim) - 1
+    return jnp.logical_and(other >= 0, other < sizes[dim])
+
+
 def add_halos(swaps, sizes, total, halos):
     height = total.shape[0] // FACES
     for (dim, odd), halo in zip(swaps, halos):
         face = swap_face(dim, odd)
-        other = lax.axis_index(AXES[dim]) + 2 * (face - 2 * dim) - 1
-
-        @pl.when(jnp.logical_and(other >= 0, other < sizes[dim]))
+
+        @pl.when(has_neighbour(dim, face, sizes))
         def _():
-            total[rows_of(face, height), :] -= halo[...]
+            total[rows_of(face, height), :] -= halo[:height, :]
 
 
 def partner(index, offset, count):
@@ -108,14 +112,13 @@
     return pl.ds(pl.multiple_of(index * height, height), height)
 
 
-def send_rest(swaps, order, loads, product, rest, messages):
+def place_faces(swaps, order, product, rest, messages):
     height = rest.shape[0] // FACES
     for j in range(FACES):
         face = rows_of(order[0, j], height)
         rest[face, :] = product[j * height : (j + 1) * height, :]
     for (dim, odd), message in zip(swaps, messages):
-        message[...] = rest[rows_of(swap_face(dim, odd), height), :]
-    rest[...] = loads[...].astype(F32) - rest[...]
+        message[:height, :] = rest[rows_of(swap_face(dim, odd), height), :]
 
 
 def reorder(order, read, local_iter):
@@ -127,8 +130,8 @@
 def first_kernel(swaps, order_hbm, *refs):
     hbm, held, refs = refs[:8], refs[8:15], refs[15:]
     (rest, *messages), scratch = refs[: 1 + len(swaps)], refs[1 + len(swaps) :]
-    matrix, loads = held[:2]
-    order, start, local_iter, product, sems = scratch
+    matrix, loads, modes, _, root_map = held[:5]
+    order, start, local_iter, product, mapped, sems = scratch
     matrix_hbm, start_hbm = hbm[:2]
     parts = 4
     part = matrix.shape[0] // parts
@@ -150,7 +153,15 @@
         product[rows, :] = jnp.dot(matrix[rows, :], local_iter[...], preferred_element_type=F32)
     for copy in copies[2 + parts :]:
         copy.wait()
-    send_rest(swaps, order, loads, product, rest, messages)
+    place_faces(swaps, order, product, rest, messages)
+    rest[...] = loads[...].astype(F32) - rest[...]
+    mapped[...] = dot3(root_map[...], modes[...])
+    height, lanes = rest.shape[0] // FACES, rest.shape[1]
+    for (dim, odd), message in zip(swaps, messages):
+        link = mapped[:, rows_of(swap_face(dim, odd), height)]
+        extra = message.shape[0] - height
+        for k in range(lanes // height):
+            message[height:, k * height : (k + 1) * height] = link[k * extra : (k + 1) * extra, :]
 
 
 def constants_kernel(modes, weights, modes_t, modes_s, scale):
@@ -165,16 +176,78 @@
         scale[block, :] = jnp.broadcast_to(weights[:, block], (height, height)).T
 
 
-def residual_kernel(swaps, sizes, rest, modes_s, root_map, *more):
-    halos, (residual, coarse, root) = more[: len(swaps)], more[len(swaps) :]
-    count = coarse.shape[0]
-    residual[...] = rest[...]
-    add_halos(swaps, sizes, residual, halos)
+def coarse_of(modes_s, residual, coarse):
+    count = modes_s.shape[0] // 2
     high, low = split(residual[...])
     both = jnp.dot(modes_s[...], high, preferred_element_type=F32)
     fine = jnp.dot(modes_s[:count, :], low, preferred_element_type=F32)
-    coarse[...] = both[:count, :] + (both[count:, :] + fine)
+    coarse[:count, :] = both[:count, :] + (both[count:, :] + fine)
+
+
+def residual_kernel(swaps, sizes, rest, modes_s, root_map, *more):
+    halos, (residual, coarse, root, links) = more[: len(swaps)], more[len(swaps) :]
+    residual[...] = rest[...]
+    add_halos(swaps, sizes, residual, halos)
+    coarse_of(modes_s, residual, coarse)
     root[...] = dot3(root_map[...], coarse[...])
+    height, lanes = rest.shape[0] // FACES, rest.shape[1]
+    count = root.shape[0]
+    for at, ((dim, odd), halo) in enumerate(zip(swaps, halos)):
+        known = has_neighbour(dim, swap_face(dim, odd), sizes)
+        extra = halo.shape[0] - height
+        for k in range(lanes // height):
+            link = halo[height:, k * height : (k + 1) * height]
+            rows = slice(at * count + k * extra, at * count + (k + 1) * extra)
+            links[rows, :] = jnp.where(known, link, 0.0)
+
+
+def links_kernel(swaps, modes, root_map, links, loads, ahead_s, ahead_loads, ahead):
+    count, height = root_map.shape[0], links.shape[1]
+    ahead[...] = jnp.zeros_like(ahead)
+    own = dot3(root_map[...], modes[...])
+    ahead[count : 2 * count, :] = own
+    for at, (dim, odd) in enumerate(swaps):
+        face = swap_face(dim, odd)
+        link = links[at * count : (at + 1) * count, :]
+        if dim == 0:
+            ahead[rows_of(2 * face, count), rows_of(face, height)] = link
+        else:
+            ahead[count : 2 * count, rows_of(face, height)] += link
+    high, low = split(ahead[...])
+    ahead_s[: 3 * count, :] = high
+    ahead_s[3 * count :, :] = low
+    high, low = split(own)
+    ahead_loads[...] = jnp.zeros_like(ahead_loads)
+    dot = functools.partial(jnp.dot, preferred_element_type=F32)
+    ahead_loads[count : 2 * count, :] = dot(high, loads[...]) + dot(low, loads[...])
+
+
+def merged_kernel(
+    swaps, sizes, ride, rest, modes_s, root_inverse, ahead, *more
+):
+    halos, more = more[: len(swaps)], more[len(swaps) :]
+    received, (residual, message, stack) = more[:-3], more[-3:]
+    residual[...] = rest[...]
+    add_halos(swaps, sizes, residual, halos)
+    coarse_of(modes_s, residual, message)
+    modes, height = modes_s.shape[0] // 2, rest.shape[0] // FACES
+    count = message.shape[0] - modes
+    me = lax.axis_index("gx")
+    stack[...] = jnp.zeros_like(stack)
+    pieces = [(me, ahead)]
+    for (dim, odd), halo in zip(swaps, halos):
+        if ride and (dim, odd) == (0, 0):
+            pieces.append((me ^ 1, halo.at[height:, :]))
+    for offset, piece in received_offsets(ride, sizes[0], received):
+        pieces.append((source(me, offset, sizes[0]), piece))
+    for index, piece in pieces:
+        rows = pl.ds(pl.multiple_of(index * count, count), 3 * count)
+        stack[rows, :] += piece[...]
+    message[modes:, :] = dot3(root_inverse[...], stack[count:-count, :])
+
+
+def received_offsets(ride, count, pieces):
+    return list(zip(range(count - 1, ride, -1), pieces))
 
 
 def root_kernel(count, coarse, root_inverse, root, *more):
@@ -227,7 +300,7 @@
 
 def middle_kernel(
     swaps, members, sizes, order_hbm, matrix, solution, loads, residual, scale, modes_t, root_map, region_rows,
-    own, other, next_solution, rest, *more
+    own, other, ahead_s, ahead_loads, next_solution, rest, ahead, *more
 ):
     messages, (stack, local_iter, product, order, sem) = more[: len(swaps)], more[len(swaps) :]
     copy = pltpu.make_async_copy(order_hbm, order, sem)
@@ -239,7 +312,17 @@
     copy.wait()
     reorder(order, lambda rows: next_solution[rows, :].astype(BF16), local_iter)
     product[...] = jnp.dot(matrix[...], local_iter[...], preferred_element_type=F32)
-    send_rest(swaps, order, loads, product, rest, messages)
+    place_faces(swaps, order, product, rest, messages)
+    count = ahead.shape[0]
+    high, low = split(rest[...])
+    both = jnp.dot(ahead_s[...], high, preferred_element_type=F32)
+    fine = jnp.dot(ahead_s[:count, :], low, preferred_element_type=F32)
+    ahead[...] = ahead_loads[...] - (both[:count, :] + (both[count:, :] + fine))
+    height = rest.shape[0] // FACES
+    for message in messages:
+        if message.shape[0] > height:
+            message[height:, :] = ahead[...]
+    rest[...] = loads[...].astype(F32) - rest[...]
 
 
 def last_kernel(
@@ -288,22 +371,41 @@
     half = sizes[1] // 2
     members = list(itertools.product(range(half), range(sizes[2])))
 
+    ride = int(sizes[0] & (sizes[0] - 1) == 0)
     full = (pltpu.VMEM, (iface, cases), F32)
-    face = (pltpu.VMEM, (height, cases), F32)
     work = [pltpu.VMEM((iface, cases), BF16), pltpu.VMEM((iface, cases), F32)]
     stack = [pltpu.VMEM((region_rows.shape[1], cases), F32)]
     places = [pltpu.SMEM((1, FACES), jnp.int32)]
 
+    def held(rows):
+        return (pltpu.VMEM, (rows, cases), F32)
+
+    def along(value, offset):
+        pairs = []
+        for place in itertools.product(*map(range, sizes)):
+            there = (partner(place[0], offset, sizes[0]),) + place[1:]
+            pairs.append((flat(sizes, place), flat(sizes, there)))
+        return lax.ppermute(value, AXES, pairs)
+
+    def exchange(messages):
+        return [
+            lax.ppermute(message, AXES, swap_pairs(sizes, dim, odd))
+            for (dim, odd), message in zip(swaps, messages)
+        ]
+
     for step in range(ITERS):
         if step == 0:
             inputs = [order, matrix, solution, target, modes, weights, root_map, region_rows, root_inverse]
-            held = [(pltpu.VMEM, item.shape, item.dtype) for item in [matrix] + inputs[3:]]
+            kept = [(pltpu.VMEM, item.shape, item.dtype) for item in [matrix] + inputs[3:]]
             outs = call(
                 functools.partial(first_kernel, swaps),
-                held + [full] + [face] * len(swaps),
+                kept + [full] + [held(height + root_modes * height // cases)] * len(swaps),
                 inputs,
                 "first_product",
-                places + [pltpu.VMEM((iface, cases), BF16)] + work + [pltpu.SemaphoreType.DMA((12,))],
+                places
+                + [pltpu.VMEM((iface, cases), BF16)]
+                + work
+                + [pltpu.VMEM((root_modes, iface), F32), pltpu.SemaphoreType.DMA((12,))],
                 len(inputs),
             )
             matrix, target, modes, weights, root_map, region_rows, root_inverse, rest, *messages = outs
@@ -317,36 +419,48 @@
                 [modes, weights],
                 "constants",
             )
+            halos = exchange(messages)
+            residual, coarse, root, links = call(
+                functools.partial(residual_kernel, swaps, sizes),
+                [full, held(mode_count), held(root_modes), (pltpu.VMEM, (len(swaps) * root_modes, height), F32)],
+                [rest, modes_s, root_map] + halos,
+                "residual_coarse",
+            )
+            received = [along(root, offset) for offset in range(1, sizes[0])]
+            (message,) = call(
+                functools.partial(root_kernel, sizes[0]),
+                [held(mode_count + root_modes)],
+                [coarse, root_inverse, root] + received,
+                "root_part",
+                [pltpu.VMEM((root_inverse.shape[1], cases), F32)],
+            )
+            ahead_s, ahead_loads = call(
+                functools.partial(links_kernel, swaps),
+                [(pltpu.VMEM, (6 * root_modes, iface), BF16), held(3 * root_modes)],
+                [modes, root_map, links, target],
+                "links",
+                [pltpu.VMEM((3 * root_modes, iface), F32)],
+            )
         else:
-            solution, rest, *messages = call(
+            extra = [3 * root_modes if ride and swap == (0, 0) else 0 for swap in swaps]
+            solution, rest, ahead, *messages = call(
                 functools.partial(middle_kernel, swaps, members, sizes[1:]),
-                [full, full] + [face] * len(swaps),
-                [order, matrix, solution, target, residual, scale, modes_t, root_map, region_rows, own, other],
+                [full, full, held(3 * root_modes)] + [held(height + more) for more in extra],
+                [order, matrix, solution, target, residual, scale, modes_t, root_map, region_rows, own, other]
+                + [ahead_s, ahead_loads],
                 "update_product",
                 stack + work + places + [pltpu.SemaphoreType.DMA],
                 1,
             )
-        halos = [
-            lax.ppermute(message, AXES, swap_pairs(sizes, dim, odd))
-            for (dim, odd), message in zip(swaps, messages)
-        ]
-        residual, coarse, root = call(
-            functools.partial(residual_kernel, swaps, sizes),
-            [full, (pltpu.VMEM, (mode_count, cases), F32), (pltpu.VMEM, (root_modes, cases), F32)],
-            [rest, modes_s, root_map] + halos,
-            "residual_coarse",
-        )
-        received = [
-            lax.ppermute(root, "gx", [(i, partner(i, offset, sizes[0])) for i in range(sizes[0])])
-            for offset in range(1, sizes[0])
-        ]
-        (message,) = call(
-            functools.partial(root_kernel, sizes[0]),
-            [(pltpu.VMEM, (mode_count + root_modes, cases), F32)],
-            [coarse, root_inverse, root] + received,
-            "root_part",
-            [pltpu.VMEM((root_inverse.shape[1], cases), F32)],
-        )
+            received = [along(ahead, offset) for offset in range(sizes[0] - 1, ride, -1)]
+            halos = exchange(messages)
+            residual, message = call(
+                functools.partial(merged_kernel, swaps, sizes, ride),
+                [full, held(mode_count + root_modes)],
+                [rest, modes_s, root_inverse, ahead] + halos + received,
+                "residual_root",
+                [pltpu.VMEM((root_inverse.shape[1] + 2 * root_modes, cases), F32)],
+            )
         pieces = []
         for dy, dz in members[1:]:
             moves = [
@@ -357,7 +471,7 @@
             pieces.append(lax.ppermute(message, ("gy", "gz"), moves))
         (own,) = call(
             functools.partial(pair_kernel, mode_count),
-            [(pltpu.VMEM, (len(members) * mode_count + root_modes, cases), F32)],
+            [held(len(members) * mode_count + root_modes)],
             [message] + pieces,
             "pair_message",
         )

time: 57 us -> 53.6 us (0.940)
  waiting for transfers between devices: 22.2 us -> 19.9 us
  starting transfers between devices: 26.2 us -> 24.3 us
  Pallas kernels: 8.35 us -> 9.16 us
    ppermute x16 -> x15, waiting for transfers between devices: 13.4 us -> 11.4 us  [the longest x10 6.79 us: exchange(): lax.ppermute(message, AXES, swap_pairs(sizes, dim, odd))]
    ppermute x16 -> x15, starting transfers between devices: 19.1 us -> 17.2 us  [the longest x5 8.75 us: along(): return lax.ppermute(value, AXES, pairs)]
    pallas_call x10, Pallas kernels: 8.35 us -> 9.16 us  [call(): pl.pallas_call(body, out_shape=[item(shape, dtype) for item, shape, dtype...]
  transfers between devices with their start and end apart: 24 -> 23, of which waited for: 18 -> 17; matrix products, arithmetic and copies ran while one was open for 0% -> 0% of each run, Pallas kernels for 1% -> 2%
where the time goes in v4:
time: 53.6 us; the launch traced here: 53.5 us
  starting transfers between devices  24.3 us (45%)
  waiting for transfers between devices  19.9 us (37%)
  Pallas kernels  9.16 us (17%)
    pallas_call x10, Pallas kernels, call(): pl.pallas_call(body, out_shape=[item(shape, dtype) for item, shape, dtype...  9.16 us
    ppermute x5, starting transfers between devices, along(): return lax.ppermute(value, AXES, pairs)  8.75 us
    ppermute x10, starting transfers between devices, exchange(): lax.ppermute(message, AXES, swap_pairs(sizes, dim, odd))  8.4 us
    ppermute x6, starting transfers between devices, per_device(): pieces.append(lax.ppermute(message, ('gy', 'gz'), moves))  7.05 us
    ppermute x10, waiting for transfers between devices, exchange(): lax.ppermute(message, AXES, swap_pairs(sizes, dim, odd))  6.79 us
    ppermute x6, waiting for transfers between devices, per_device(): pieces.append(lax.ppermute(message, ('gy', 'gz'), moves))  6.15 us
    ppermute x5, waiting for transfers between devices, along(): return lax.ppermute(value, AXES, pairs)  4.59 us
    ppermute x2, waiting for transfers between devices, per_device(): other = lax.ppermute(own, AXES, swap_pairs(sizes, 1, 0))  2.32 us
  transfers between devices with their start and end apart: 23, of which 17 were waited for; matrix products, arithmetic and copies ran while one was open for 0% of the time, Pallas kernels for 2%

profile of v4, /device:TPU:0, one launch (start us, length us, event | category | flops | bytes accessed | tf_op | source)
XLA Modules:
  0.0 53.5 jit_solution(5334375737649307773)
XLA Ops:
  0.0 3.4 %first_product.1 = (bf16[1024,1024]{1,0:T(8,128)(2,1)S(1)}, bf16[1024,256]{1,0:T(8,128)(2,1)S(1)}, f32[32,1024]{1,0:T(8,128)S(1)}, f32[1,1024]{1,0:T(1,128)S(1)}...) custom-call(s32[1,8]{1,0:T(1,128)} %bitcast.19, ...), custom_call_target="tpu_custom_call" | custom-call | tf_op jit(solution)/shard_map/first_product/pallas_call | solution.py:97
  3.9 2.6 %collective-permute-start.1 = (f32[136,256]{1,0:T(8,128)S(1)}, f32[136,256]{1,0:T(8,128)S(1)}, u32[]{:S(2)}, u32[]{:S(2)}) collective-permute-start(f32[136,256]{1,0:T(8,128)S(1)} %get-tuple-element.45), channel_id=1, source_target_pairs={{0,6},{1,7},{2,4},{3,5},{4,2},{5,3},{6,0},{7,1},{8,14},{9,15},{10,... | collective-permute-start | bytes 417800 | tf_op jit(solution)/shard_map/ppermute | solution.py:392
  6.5 2.2 %collective-permute-start.2 = (f32[136,256]{1,0:T(8,128)S(1)}, f32[136,256]{1,0:T(8,128)S(1)}, u32[]{:S(2)}, u32[]{:S(2)}) collective-permute-start(f32[136,256]{1,0:T(8,128)S(1)} %get-tuple-element.46), channel_id=1, source_target_pairs={{0,8},{1,9},{2,10},{3,11},{4,12},{5,13},{6,14},{7,15},{8,0},{9,1},... | collective-permute-start | bytes 417800 | tf_op jit(solution)/shard_map/ppermute | solution.py:392
  8.7 1.5 %collective-permute-start.3 = (f32[136,256]{1,0:T(8,128)S(1)}, f32[136,256]{1,0:T(8,128)S(1)}, u32[]{:S(2)}, u32[]{:S(2)}) collective-permute-start(f32[136,256]{1,0:T(8,128)S(1)} %get-tuple-element.47), channel_id=1, source_target_pairs={{0,1},{1,0},{2,3},{3,2},{4,5},{5,4},{6,7},{7,6},{8,9},{9,8},{10,11... | collective-permute-start | bytes 417800 | tf_op jit(solution)/shard_map/ppermute | solution.py:392
  11.2 1.8 %collective-permute-done.2.more_2_ = f32[136,256]{1,0:T(8,128)S(1)} collective-permute-done((f32[136,256]{1,0:T(8,128)S(1)}, f32[136,256]{1,0:T(8,128)S(1)}, u32[]{:S(2)}, u32[]{:S(2)}) %collective-permute-start.2) | collective-permute-done | bytes 139296 | tf_op jit(solution)/shard_map/ppermute | solution.py:392
  13.0 2.0 %collective-permute-done.3.more_3_ = f32[136,256]{1,0:T(8,128)S(1)} collective-permute-done((f32[136,256]{1,0:T(8,128)S(1)}, f32[136,256]{1,0:T(8,128)S(1)}, u32[]{:S(2)}, u32[]{:S(2)}) %collective-permute-start.3) | collective-permute-done | bytes 139296 | tf_op jit(solution)/shard_map/ppermute | solution.py:392
  15.5 1.4 %collective-permute-start.7 = (f32[16,256]{1,0:T(8,128)S(1)}, f32[16,256]{1,0:T(8,128)S(1)}, u32[]{:S(2)}, u32[]{:S(2)}) collective-permute-start(f32[16,256]{1,0:T(8,128)S(1)} %get-tuple-element.55.root), channel_id=1, source_target_pairs={{0,24},{1,25},{2,26},{3,27},{4,28},{5,29},{6,30},{7,31},{8,16},{9,... | collective-permute-start | bytes 49160 | tf_op jit(solution)/shard_map/ppermute | solution.py:388
  17.3 2.6 %collective-permute-start.5 = (f32[16,256]{1,0:T(8,128)S(1)}, f32[16,256]{1,0:T(8,128)S(1)}, u32[]{:S(2)}, u32[]{:S(2)}) collective-permute-start(f32[16,256]{1,0:T(8,128)S(1)} %get-tuple-element.55.root), channel_id=1, source_target_pairs={{0,8},{1,9},{2,10},{3,11},{4,12},{5,13},{6,14},{7,15},{8,0},{9,1},... | collective-permute-start | bytes 49160 | tf_op jit(solution)/shard_map/ppermute | solution.py:388
  19.9 1.1 %collective-permute-done.7.more_2_ = f32[16,256]{1,0:T(8,128)S(1)} collective-permute-done((f32[16,256]{1,0:T(8,128)S(1)}, f32[16,256]{1,0:T(8,128)S(1)}, u32[]{:S(2)}, u32[]{:S(2)}) %collective-permute-start.7) | collective-permute-done | bytes 16416 | tf_op jit(solution)/shard_map/ppermute | solution.py:388
  21.9 1.5 %collective-permute-start.10 = (f32[48,256]{1,0:T(8,128)S(1)}, f32[48,256]{1,0:T(8,128)S(1)}, u32[]{:S(2)}, u32[]{:S(2)}) collective-permute-start(f32[48,256]{1,0:T(8,128)S(1)} %root_part.1.first), channel_id=1, source_target_pairs={{0,5},{1,4},{2,7},{3,6},{4,1},{5,0},{6,3},{7,2},{8,13},{9,12},{10,... | collective-permute-start | bytes 147464 | tf_op jit(solution)/shard_map/ppermute | solution.py:471
  23.4 1.5 %collective-permute-start.9 = (f32[48,256]{1,0:T(8,128)S(1)}, f32[48,256]{1,0:T(8,128)S(1)}, u32[]{:S(2)}, u32[]{:S(2)}) collective-permute-start(f32[48,256]{1,0:T(8,128)S(1)} %root_part.1.first), channel_id=1, source_target_pairs={{0,4},{1,5},{2,6},{3,7},{4,0},{5,1},{6,2},{7,3},{8,12},{9,13},{10,... | collective-permute-start | bytes 147464 | tf_op jit(solution)/shard_map/ppermute | solution.py:471
  25.4 1.5 %collective-permute-done.10.more_2_ = f32[48,256]{1,0:T(8,128)S(1)} collective-permute-done((f32[48,256]{1,0:T(8,128)S(1)}, f32[48,256]{1,0:T(8,128)S(1)}, u32[]{:S(2)}, u32[]{:S(2)}) %collective-permute-start.10) | collective-permute-done | bytes 49184 | tf_op jit(solution)/shard_map/ppermute | solution.py:471
  27.5 1.5 %collective-permute-done.8.more_0_ = f32[48,256]{1,0:T(8,128)S(1)} collective-permute-done((f32[48,256]{1,0:T(8,128)S(1)}, f32[48,256]{1,0:T(8,128)S(1)}, u32[]{:S(2)}, u32[]{:S(2)}) %collective-permute-start.8) | collective-permute-done | bytes 49184 | tf_op jit(solution)/shard_map/ppermute | solution.py:471
  30.4 2.2 %update_product.1 = (f32[1024,256]{1,0:T(8,128)S(1)}, f32[1024,256]{1,0:T(8,128)S(1)}, f32[48,256]{1,0:T(8,128)S(1)}, f32[128,256]{1,0:T(8,128)S(1)}, f32[128,25...) custom-call(s32[1,8]{1,0:T(1,128)} %bitcast.20, ...), custom_call_target="tpu_custom_call" | custom-call | tf_op jit(solution)/shard_map/update_product/pallas_call | solution.py:97
  32.6 1.9 %collective-permute-start.18 = (f32[48,256]{1,0:T(8,128)S(1)}, f32[48,256]{1,0:T(8,128)S(1)}, u32[]{:S(2)}, u32[]{:S(2)}) collective-permute-start(f32[48,256]{1,0:T(8,128)S(1)} %get-tuple-element.61.ahead), channel_id=1, source_target_pairs={{0,16},{1,17},{2,18},{3,19},{4,20},{5,21},{6,22},{7,23},{8,24},{9,... | collective-permute-start | bytes 147464 | tf_op jit(solution)/shard_map/ppermute | solution.py:388
  34.5 2.5 %collective-permute-start.17 = (f32[48,256]{1,0:T(8,128)S(1)}, f32[48,256]{1,0:T(8,128)S(1)}, u32[]{:S(2)}, u32[]{:S(2)}) collective-permute-start(f32[48,256]{1,0:T(8,128)S(1)} %get-tuple-element.61.ahead), channel_id=1, source_target_pairs={{0,24},{1,25},{2,26},{3,27},{4,28},{5,29},{6,30},{7,31},{8,16},{9,... | collective-permute-start | bytes 147464 | tf_op jit(solution)/shard_map/ppermute | solution.py:388
  39.0 1.9 %collective-permute-done.17.more_5_ = f32[48,256]{1,0:T(8,128)S(1)} collective-permute-done((f32[48,256]{1,0:T(8,128)S(1)}, f32[48,256]{1,0:T(8,128)S(1)}, u32[]{:S(2)}, u32[]{:S(2)}) %collective-permute-start.17) | collective-permute-done | bytes 49184 | tf_op jit(solution)/shard_map/ppermute | solution.py:388
  40.9 1.2 %collective-permute-done.13.more_1_ = f32[128,256]{1,0:T(8,128)S(1)} collective-permute-done((f32[128,256]{1,0:T(8,128)S(1)}, f32[128,256]{1,0:T(8,128)S(1)}, u32[]{:S(2)}, u32[]{:S(2)}) %collective-permute-start.13) | collective-permute-done | bytes 131104 | tf_op jit(solution)/shard_map/ppermute | solution.py:392
  42.1 1.3 %collective-permute-done.15.more_3_ = f32[128,256]{1,0:T(8,128)S(1)} collective-permute-done((f32[128,256]{1,0:T(8,128)S(1)}, f32[128,256]{1,0:T(8,128)S(1)}, u32[]{:S(2)}, u32[]{:S(2)}) %collective-permute-start.15) | collective-permute-done | bytes 131104 | tf_op jit(solution)/shard_map/ppermute | solution.py:392
  45.0 1.4 %collective-permute-start.20 = (f32[48,256]{1,0:T(8,128)S(1)}, f32[48,256]{1,0:T(8,128)S(1)}, u32[]{:S(2)}, u32[]{:S(2)}) collective-permute-start(f32[48,256]{1,0:T(8,128)S(1)} %get-tuple-element.68.first), channel_id=1, source_target_pairs={{0,4},{1,5},{2,6},{3,7},{4,0},{5,1},{6,2},{7,3},{8,12},{9,13},{10,... | collective-permute-start | bytes 147464 | tf_op jit(solution)/shard_map/ppermute | solution.py:471
  46.4 1.5 %collective-permute-start.19 = (f32[48,256]{1,0:T(8,128)S(1)}, f32[48,256]{1,0:T(8,128)S(1)}, u32[]{:S(2)}, u32[]{:S(2)}) collective-permute-start(f32[48,256]{1,0:T(8,128)S(1)} %get-tuple-element.68.first), channel_id=1, source_target_pairs={{0,1},{1,0},{2,3},{3,2},{4,5},{5,4},{6,7},{7,6},{8,9},{9,8},{10,11... | collective-permute-start | bytes 147464 | tf_op jit(solution)/shard_map/ppermute | solution.py:471
  47.9 1.5 %collective-permute-done.21.more_2_ = f32[48,256]{1,0:T(8,128)S(1)} collective-permute-done((f32[48,256]{1,0:T(8,128)S(1)}, f32[48,256]{1,0:T(8,128)S(1)}, u32[]{:S(2)}, u32[]{:S(2)}) %collective-permute-start.21) | collective-permute-done | bytes 49184 | tf_op jit(solution)/shard_map/ppermute | solution.py:471
  50.6 1.4 %collective-permute-done.22.other = f32[144,256]{1,0:T(8,128)S(1)} collective-permute-done((f32[144,256]{1,0:T(8,128)S(1)}, f32[144,256]{1,0:T(8,128)S(1)}, u32[]{:S(2)}, u32[]{:S(2)}) %collective-permute-start.22) | collective-permute-done | bytes 147488 | tf_op jit(solution)/shard_map/ppermute | solution.py:478
  52.0 1.5 %update_last.1 = f32[1024,256]{1,0:T(8,128)} custom-call(f32[1024,256]{1,0:T(8,128)S(1)} %get-tuple-element.59.solution, f32[1024,256]{1,0:T(8,128)S(1)} %get-tuple-element.67.residual, f32[1024,128]{1,0:T(8,128)S(1)} %get-tuple-element.50.scale, bf16[1024,96]{1,0:T(8,128)(2,1)S(1)} %get-tuple-element.51.modes_t, f32[16,32]{1,0:T(8,128)S(1)} %get-tuple-element.43.root_map, ...), custom_call_target="tpu_custom_call" | custom-call | tf_op jit(solution)/shard_map/update_last/pallas_call | solution.py:97
  (34 shorter events, 10.5 us)
Async XLA Ops:
  3.4 27.0 %copy-start = (bf16[1,1,1,1024,256]{4,3,2,1,0:T(8,128)(2,1)S(1)}, bf16[1,1,1,1024,256]{4,3,2,1,0:T(8,128)(2,1)}, u32[]{:S(2)}) copy-start(bf16[1,1,1,1024,256]{4,3,2,1,0:T(8,128)(2,1)} %param.10) | copy-start | bytes 1572868
  3.4 7.7 %collective-permute-start = (f32[136,256]{1,0:T(8,128)S(1)}, f32[136,256]{1,0:T(8,128)S(1)}, u32[]{:S(2)}, u32[]{:S(2)}) collective-permute-start(f32[136,256]{1,0:T(8,128)S(1)} %get-tuple-element.44), channel_id=1, source_target_pairs={{0,2},{1,3},{2,0},{3,1},{4,6},{5,7},{6,4},{7,5},{8,16},{9,17},{10,... | collective-permute-start | bytes 417800 | tf_op jit(solution)/shard_map/ppermute | solution.py:392
  3.9 7.2 %collective-permute-start.1 = (f32[136,256]{1,0:T(8,128)S(1)}, f32[136,256]{1,0:T(8,128)S(1)}, u32[]{:S(2)}, u32[]{:S(2)}) collective-permute-start(f32[136,256]{1,0:T(8,128)S(1)} %get-tuple-element.45), channel_id=1, source_target_pairs={{0,6},{1,7},{2,4},{3,5},{4,2},{5,3},{6,0},{7,1},{8,14},{9,15},{10,... | collective-permute-start | bytes 417800 | tf_op jit(solution)/shard_map/ppermute | solution.py:392
  6.5 6.4 %collective-permute-start.2 = (f32[136,256]{1,0:T(8,128)S(1)}, f32[136,256]{1,0:T(8,128)S(1)}, u32[]{:S(2)}, u32[]{:S(2)}) collective-permute-start(f32[136,256]{1,0:T(8,128)S(1)} %get-tuple-element.46), channel_id=1, source_target_pairs={{0,8},{1,9},{2,10},{3,11},{4,12},{5,13},{6,14},{7,15},{8,0},{9,1},... | collective-permute-start | bytes 417800 | tf_op jit(solution)/shard_map/ppermute | solution.py:392
  8.7 6.3 %collective-permute-start.3 = (f32[136,256]{1,0:T(8,128)S(1)}, f32[136,256]{1,0:T(8,128)S(1)}, u32[]{:S(2)}, u32[]{:S(2)}) collective-permute-start(f32[136,256]{1,0:T(8,128)S(1)} %get-tuple-element.47), channel_id=1, source_target_pairs={{0,1},{1,0},{2,3},{3,2},{4,5},{5,4},{6,7},{7,6},{8,9},{9,8},{10,11... | collective-permute-start | bytes 417800 | tf_op jit(solution)/shard_map/ppermute | solution.py:392
  10.2 4.7 %collective-permute-start.4 = (f32[136,256]{1,0:T(8,128)S(1)}, f32[136,256]{1,0:T(8,128)S(1)}, u32[]{:S(2)}, u32[]{:S(2)}) collective-permute-start(f32[136,256]{1,0:T(8,128)S(1)} %get-tuple-element.48), channel_id=1, source_target_pairs={{0,2},{1,3},{2,0},{3,1},{4,6},{5,7},{6,4},{7,5},{8,10},{9,11},{10,... | collective-permute-start | bytes 417800 | tf_op jit(solution)/shard_map/ppermute | solution.py:392
  15.5 5.5 %collective-permute-start.7 = (f32[16,256]{1,0:T(8,128)S(1)}, f32[16,256]{1,0:T(8,128)S(1)}, u32[]{:S(2)}, u32[]{:S(2)}) collective-permute-start(f32[16,256]{1,0:T(8,128)S(1)} %get-tuple-element.55.root), channel_id=1, source_target_pairs={{0,24},{1,25},{2,26},{3,27},{4,28},{5,29},{6,30},{7,31},{8,16},{9,... | collective-permute-start | bytes 49160 | tf_op jit(solution)/shard_map/ppermute | solution.py:388
  16.9 4.7 %collective-permute-start.6 = (f32[16,256]{1,0:T(8,128)S(1)}, f32[16,256]{1,0:T(8,128)S(1)}, u32[]{:S(2)}, u32[]{:S(2)}) collective-permute-start(f32[16,256]{1,0:T(8,128)S(1)} %get-tuple-element.55.root), channel_id=1, source_target_pairs={{0,16},{1,17},{2,18},{3,19},{4,20},{5,21},{6,22},{7,23},{8,24},{9,... | collective-permute-start | bytes 49160 | tf_op jit(solution)/shard_map/ppermute | solution.py:388
  17.3 4.4 %collective-permute-start.5 = (f32[16,256]{1,0:T(8,128)S(1)}, f32[16,256]{1,0:T(8,128)S(1)}, u32[]{:S(2)}, u32[]{:S(2)}) collective-permute-start(f32[16,256]{1,0:T(8,128)S(1)} %get-tuple-element.55.root), channel_id=1, source_target_pairs={{0,8},{1,9},{2,10},{3,11},{4,12},{5,13},{6,14},{7,15},{8,0},{9,1},... | collective-permute-start | bytes 49160 | tf_op jit(solution)/shard_map/ppermute | solution.py:388
  21.9 5.0 %collective-permute-start.10 = (f32[48,256]{1,0:T(8,128)S(1)}, f32[48,256]{1,0:T(8,128)S(1)}, u32[]{:S(2)}, u32[]{:S(2)}) collective-permute-start(f32[48,256]{1,0:T(8,128)S(1)} %root_part.1.first), channel_id=1, source_target_pairs={{0,5},{1,4},{2,7},{3,6},{4,1},{5,0},{6,3},{7,2},{8,13},{9,12},{10,... | collective-permute-start | bytes 147464 | tf_op jit(solution)/shard_map/ppermute | solution.py:471
  23.4 4.1 %collective-permute-start.9 = (f32[48,256]{1,0:T(8,128)S(1)}, f32[48,256]{1,0:T(8,128)S(1)}, u32[]{:S(2)}, u32[]{:S(2)}) collective-permute-start(f32[48,256]{1,0:T(8,128)S(1)} %root_part.1.first), channel_id=1, source_target_pairs={{0,4},{1,5},{2,6},{3,7},{4,0},{5,1},{6,2},{7,3},{8,12},{9,13},{10,... | collective-permute-start | bytes 147464 | tf_op jit(solution)/shard_map/ppermute | solution.py:471
  24.9 4.1 %collective-permute-start.8 = (f32[48,256]{1,0:T(8,128)S(1)}, f32[48,256]{1,0:T(8,128)S(1)}, u32[]{:S(2)}, u32[]{:S(2)}) collective-permute-start(f32[48,256]{1,0:T(8,128)S(1)} %root_part.1.first), channel_id=1, source_target_pairs={{0,1},{1,0},{2,3},{3,2},{4,5},{5,4},{6,7},{7,6},{8,9},{9,8},{10,11... | collective-permute-start | bytes 147464 | tf_op jit(solution)/shard_map/ppermute | solution.py:471
  29.0 1.4 %collective-permute-start.11 = (f32[144,256]{1,0:T(8,128)S(1)}, f32[144,256]{1,0:T(8,128)S(1)}, u32[]{:S(2)}, u32[]{:S(2)}) collective-permute-start(f32[144,256]{1,0:T(8,128)S(1)} %pair_message.2.own), channel_id=1, source_target_pairs={{0,2},{1,3},{2,0},{3,1},{4,6},{5,7},{6,4},{7,5},{8,10},{9,11},{10,... | collective-permute-start | bytes 442376 | tf_op jit(solution)/shard_map/ppermute | solution.py:478
  32.6 5.8 %collective-permute-start.18 = (f32[48,256]{1,0:T(8,128)S(1)}, f32[48,256]{1,0:T(8,128)S(1)}, u32[]{:S(2)}, u32[]{:S(2)}) collective-permute-start(f32[48,256]{1,0:T(8,128)S(1)} %get-tuple-element.61.ahead), channel_id=1, source_target_pairs={{0,16},{1,17},{2,18},{3,19},{4,20},{5,21},{6,22},{7,23},{8,24},{9,... | collective-permute-start | bytes 147464 | tf_op jit(solution)/shard_map/ppermute | solution.py:388
  34.5 6.4 %collective-permute-start.17 = (f32[48,256]{1,0:T(8,128)S(1)}, f32[48,256]{1,0:T(8,128)S(1)}, u32[]{:S(2)}, u32[]{:S(2)}) collective-permute-start(f32[48,256]{1,0:T(8,128)S(1)} %get-tuple-element.61.ahead), channel_id=1, source_target_pairs={{0,24},{1,25},{2,26},{3,27},{4,28},{5,29},{6,30},{7,31},{8,16},{9,... | collective-permute-start | bytes 147464 | tf_op jit(solution)/shard_map/ppermute | solution.py:388
  37.0 6.9 %collective-permute-start.14 = (f32[176,256]{1,0:T(8,128)S(1)}, f32[176,256]{1,0:T(8,128)S(1)}, u32[]{:S(2)}, u32[]{:S(2)}) collective-permute-start(f32[176,256]{1,0:T(8,128)S(1)} %get-tuple-element.64), channel_id=1, source_target_pairs={{0,8},{1,9},{2,10},{3,11},{4,12},{5,13},{6,14},{7,15},{8,0},{9,1},... | collective-permute-start | bytes 540680 | tf_op jit(solution)/shard_map/ppermute | solution.py:392
  37.0 4.0 %collective-permute-start.12 = (f32[128,256]{1,0:T(8,128)S(1)}, f32[128,256]{1,0:T(8,128)S(1)}, u32[]{:S(2)}, u32[]{:S(2)}) collective-permute-start(f32[128,256]{1,0:T(8,128)S(1)} %get-tuple-element.62), channel_id=1, source_target_pairs={{0,2},{1,3},{2,0},{3,1},{4,6},{5,7},{6,4},{7,5},{8,16},{9,17},{10,... | collective-permute-start | bytes 393224 | tf_op jit(solution)/shard_map/ppermute | solution.py:392
  37.0 5.2 %collective-permute-start.13 = (f32[128,256]{1,0:T(8,128)S(1)}, f32[128,256]{1,0:T(8,128)S(1)}, u32[]{:S(2)}, u32[]{:S(2)}) collective-permute-start(f32[128,256]{1,0:T(8,128)S(1)} %get-tuple-element.63), channel_id=1, source_target_pairs={{0,6},{1,7},{2,4},{3,5},{4,2},{5,3},{6,0},{7,1},{8,14},{9,15},{10,... | collective-permute-start | bytes 393224 | tf_op jit(solution)/shard_map/ppermute | solution.py:392
  38.5 5.0 %collective-permute-start.15 = (f32[128,256]{1,0:T(8,128)S(1)}, f32[128,256]{1,0:T(8,128)S(1)}, u32[]{:S(2)}, u32[]{:S(2)}) collective-permute-start(f32[128,256]{1,0:T(8,128)S(1)} %get-tuple-element.65), channel_id=1, source_target_pairs={{0,1},{1,0},{2,3},{3,2},{4,5},{5,4},{6,7},{7,6},{8,9},{9,8},{10,11... | collective-permute-start | bytes 393224 | tf_op jit(solution)/shard_map/ppermute | solution.py:392
  40.9 2.5 %collective-permute-start.16 = (f32[128,256]{1,0:T(8,128)S(1)}, f32[128,256]{1,0:T(8,128)S(1)}, u32[]{:S(2)}, u32[]{:S(2)}) collective-permute-start(f32[128,256]{1,0:T(8,128)S(1)} %get-tuple-element.66), channel_id=1, source_target_pairs={{0,2},{1,3},{2,0},{3,1},{4,6},{5,7},{6,4},{7,5},{8,10},{9,11},{10,... | collective-permute-start | bytes 393224 | tf_op jit(solution)/shard_map/ppermute | solution.py:392
  44.4 5.1 %collective-permute-start.21 = (f32[48,256]{1,0:T(8,128)S(1)}, f32[48,256]{1,0:T(8,128)S(1)}, u32[]{:S(2)}, u32[]{:S(2)}) collective-permute-start(f32[48,256]{1,0:T(8,128)S(1)} %get-tuple-element.68.first), channel_id=1, source_target_pairs={{0,5},{1,4},{2,7},{3,6},{4,1},{5,0},{6,3},{7,2},{8,13},{9,12},{10,... | collective-permute-start | bytes 147464 | tf_op jit(solution)/shard_map/ppermute | solution.py:471
  45.0 4.4 %collective-permute-start.20 = (f32[48,256]{1,0:T(8,128)S(1)}, f32[48,256]{1,0:T(8,128)S(1)}, u32[]{:S(2)}, u32[]{:S(2)}) collective-permute-start(f32[48,256]{1,0:T(8,128)S(1)} %get-tuple-element.68.first), channel_id=1, source_target_pairs={{0,4},{1,5},{2,6},{3,7},{4,0},{5,1},{6,2},{7,3},{8,12},{9,13},{10,... | collective-permute-start | bytes 147464 | tf_op jit(solution)/shard_map/ppermute | solution.py:471
  46.4 4.1 %collective-permute-start.19 = (f32[48,256]{1,0:T(8,128)S(1)}, f32[48,256]{1,0:T(8,128)S(1)}, u32[]{:S(2)}, u32[]{:S(2)}) collective-permute-start(f32[48,256]{1,0:T(8,128)S(1)} %get-tuple-element.68.first), channel_id=1, source_target_pairs={{0,1},{1,0},{2,3},{3,2},{4,5},{5,4},{6,7},{7,6},{8,9},{9,8},{10,11... | collective-permute-start | bytes 147464 | tf_op jit(solution)/shard_map/ppermute | solution.py:471
  50.5 1.4 %collective-permute-start.22 = (f32[144,256]{1,0:T(8,128)S(1)}, f32[144,256]{1,0:T(8,128)S(1)}, u32[]{:S(2)}, u32[]{:S(2)}) collective-permute-start(f32[144,256]{1,0:T(8,128)S(1)} %pair_message.3.own), channel_id=1, source_target_pairs={{0,2},{1,3},{2,0},{3,1},{4,6},{5,7},{6,4},{7,5},{8,10},{9,11},{10,... | collective-permute-start | bytes 442376 | tf_op jit(solution)/shard_map/ppermute | solution.py:478

commit v5 on v4

v5 whole, which is shorter than its diff:
```python
import functools
import itertools

import jax
import jax.numpy as jnp
from jax import lax
from jax.experimental import pallas as pl
from jax.experimental.pallas import tpu as pltpu
from jax.sharding import PartitionSpec as P

ITERS = 2
FACES = 8
AXES = ("gx", "gy", "gz")
F32 = jnp.float32
BF16 = jnp.bfloat16
ROWS = (((1,), (0,)), ((), ()))
COLS = (((0,), (0,)), ((), ()))


def neighbour(index, count, odd):
    other = index + 1 if index % 2 == odd else index - 1
    return other if 0 <= other < count else None


def swap_list(sizes):
    swaps = [(dim, odd) for odd in (1, 0) for dim in (0, 1, 2) if sizes[dim] > 1 + odd]
    return sorted(swaps, key=lambda swap: swap == (1, 0))


def flat(sizes, place):
    return (place[0] * sizes[1] + place[1]) * sizes[2] + place[2]


def swap_pairs(sizes, dim, odd):
    pairs = []
    for place in itertools.product(*map(range, sizes)):
        there = list(place)
        other = neighbour(place[dim], sizes[dim], odd)
        if other is not None:
            there[dim] = other
        elif odd and sizes[dim] % 2 == 0:
            if dim == 1:
                there[1] = sizes[1] - 1 - place[1]
            elif sizes[1] % 2 == 0:
                there[1] = place[1] ^ 1
        if tuple(there) != place:
            pairs.append((flat(sizes, place), flat(sizes, there)))
    return pairs


def swap_face(dim, odd):
    high = (lax.axis_index(AXES[dim]) + odd + 1) % 2
    return 2 * dim + high


def has_neighbour(dim, face, sizes):
    other = lax.axis_index(AXES[dim]) + 2 * (face - 2 * dim) - 1
    return jnp.logical_and(other >= 0, other < sizes[dim])


def partner(index, offset, count):
    if count & (count - 1):
        return (index + offset) % count
    return index ^ offset


def source(index, offset, count):
    if count & (count - 1):
        return lax.rem(index + count - offset, count)
    return index ^ offset


def split(value):
    high = value.astype(BF16)
    return high, (value - high.astype(F32)).astype(BF16)


def dot3(left, right, dims=ROWS):
    left_high, left_low = split(left)
    right_high, right_low = split(right)
    dot = functools.partial(lax.dot_general, dimension_numbers=dims, preferred_element_type=F32)
    return dot(left_high, right_high) + (dot(left_low, right_high) + dot(left_high, right_low))


def call(body, outs, ins, name, scratch=(), fixed=0):
    spaces = [pltpu.HBM] * fixed + [pltpu.VMEM] * (len(ins) - fixed)
    return pl.pallas_call(
        body,
        out_shape=[item(shape, dtype) for item, shape, dtype in outs],
        in_specs=[pl.BlockSpec(memory_space=space) for space in spaces],
        out_specs=[
            pl.BlockSpec(memory_space=pltpu.HBM if item is jax.ShapeDtypeStruct else pltpu.VMEM)
            for item, _, _ in outs
        ],
        scratch_shapes=list(scratch),
        compiler_params=pltpu.CompilerParams(vmem_limit_bytes=8 * 1024 * 1024),
        name=name,
    )(*[pltpu.with_memory_space_constraint(item, space) for item, space in zip(ins, spaces)])


def rows_of(index, height):
    return pl.ds(pl.multiple_of(index * height, height), height)


def send_faces(swaps, placed, messages):
    height = placed.shape[0] // FACES
    for (dim, odd), message in zip(swaps, messages):
        message[:height, :] = placed[rows_of(swap_face(dim, odd), height), :]


def first_kernel(swaps, order_hbm, start_hbm, matrix_hbm, modes_hbm, root_hbm, matrix, modes, root_map, placed, *more):
    messages, (order, start, local_iter, mapped, sems) = more[: len(swaps)], more[len(swaps) :]
    pairs = [(order_hbm, order), (start_hbm, start), (matrix_hbm, matrix), (modes_hbm, modes), (root_hbm, root_map)]
    copies = [pltpu.make_async_copy(*pair, sems.at[k]) for k, pair in enumerate(pairs)]
    for copy in copies:
        copy.start()
    height, lanes = placed.shape[0] // FACES, placed.shape[1]
    copies[0].wait()
    copies[1].wait()
    for j in range(FACES):
        local_iter[j * height : (j + 1) * height, :] = start[rows_of(order[0, j], height), :]
    copies[3].wait()
    copies[4].wait()
    mapped[...] = dot3(root_map[...], modes[...])
    for (dim, odd), message in zip(swaps, messages):
        link = mapped[:, rows_of(swap_face(dim, odd), height)]
        extra = message.shape[0] - height
        for k in range(lanes // height):
            message[height:, k * height : (k + 1) * height] = link[k * extra : (k + 1) * extra, :]
    copies[2].wait()
    product = jnp.dot(matrix[...], local_iter[...], preferred_element_type=F32)
    for j in range(FACES):
        placed[rows_of(order[0, j], height), :] = product[j * height : (j + 1) * height, :]
    send_faces(swaps, placed, messages)


def constants_kernel(
    swaps, sizes, order_hbm, matrix, modes, weights, loads, placed,
    modes_t, scale, modes_f, matrix_f, modes_a, modes_b, ready, wide, order, sem
):
    copy = pltpu.make_async_copy(order_hbm, order, sem)
    copy.start()
    count, height = modes.shape[0], scale.shape[1]
    high, low = split(modes[...])
    modes_t[...] = jnp.concatenate([high.T, low.T, high.T], axis=1)
    for j in range(FACES):
        block = slice(j * height, (j + 1) * height)
        scale[block, :] = jnp.broadcast_to(weights[:, block], (height, height)).T
    for at, (dim, odd) in enumerate(swaps):
        face = swap_face(dim, odd)
        columns = modes[:, rows_of(face, height)]
        columns = jnp.where(has_neighbour(dim, face, sizes), columns, 0.0)
        block = slice(at * height, (at + 1) * height)
        modes_f[:count, block], modes_f[count:, block] = split(columns)
    dot = functools.partial(jnp.dot, preferred_element_type=F32)
    modes_b[...] = dot(high, loads[...]) + dot(low, loads[...])
    ready[...] = modes_b[...] - dot3(modes[...], placed[...])
    copy.wait()
    for j in range(FACES):
        block = slice(j * height, (j + 1) * height)
        wide[:, rows_of(order[0, j], height)] = matrix[:, block]
    for j in range(FACES):
        block = slice(j * height, (j + 1) * height)
        matrix_f[rows_of(order[0, j], height), :] = wide[block, :]
    modes_a[:count, :], modes_a[count:, :] = split(dot(high, matrix_f[...]) + dot(low, matrix_f[...]))


def coarse_of(swaps, sizes, ready, modes_f, halos, stack):
    height, count = stack.shape[0] // len(swaps), ready.shape[0]
    for at, ((dim, odd), halo) in enumerate(zip(swaps, halos)):
        known = has_neighbour(dim, swap_face(dim, odd), sizes)
        stack[at * height : (at + 1) * height, :] = jnp.where(known, halo[:height, :], 0.0)
    high, low = split(stack[...])
    both = jnp.dot(modes_f[...], high, preferred_element_type=F32)
    fine = jnp.dot(modes_f[:count, :], low, preferred_element_type=F32)
    return ready[...] - (both[:count, :] + (both[count:, :] + fine))


def coarse_kernel(swaps, sizes, ready, modes_f, root_map, *more):
    halos, (coarse, root, stack) = more[: len(swaps)], more[len(swaps) :]
    coarse[...] = coarse_of(swaps, sizes, ready, modes_f, halos, stack)
    root[...] = dot3(root_map[...], coarse[...])


def base_kernel(swaps, sizes, solution, loads, placed, scale, *more):
    halos, base = more[: len(swaps)], more[-1]
    height, lanes = scale.shape[1], placed.shape[1]

    def wide(rows):
        return jnp.concatenate([scale[rows, :]] * (lanes // height), axis=1)

    for j in range(FACES):
        rows = slice(j * height, (j + 1) * height)
        rest = loads[rows, :].astype(F32) - placed[rows, :]
        base[rows, :] = solution[rows, :].astype(F32) + wide(rows) * rest
    for (dim, odd), halo in zip(swaps, halos):
        face = swap_face(dim, odd)
        rows = rows_of(face, height)

        @pl.when(has_neighbour(dim, face, sizes))
        def _():
            base[rows, :] -= wide(rows) * halo[:height, :]


def links_kernel(swaps, sizes, modes, root_map, loads, matrix_f, modes_a, *more):
    halos, (tail, ahead_loads, ahead) = more[: len(swaps)], more[len(swaps) :]
    count, height = root_map.shape[0], loads.shape[0] // FACES
    lanes = loads.shape[1]
    ahead[...] = jnp.zeros_like(ahead)
    own = dot3(root_map[...], modes[...])
    ahead[count : 2 * count, :] = own
    for (dim, odd), halo in zip(swaps, halos):
        face = swap_face(dim, odd)
        known = has_neighbour(dim, face, sizes)
        extra = halo.shape[0] - height
        pieces = [halo[height:, k * height : (k + 1) * height] for k in range(lanes // height)]
        link = jnp.where(known, jnp.concatenate(pieces, axis=0), 0.0)
        if dim == 0:
            ahead[rows_of(2 * face, count), rows_of(face, height)] = link
        else:
            ahead[count : 2 * count, rows_of(face, height)] += link
    dot = functools.partial(jnp.dot, preferred_element_type=F32)
    high, low = split(ahead[...])
    both = dot(jnp.concatenate([high, low], axis=0), matrix_f[...])
    done = modes_a.shape[0]
    tail[:done, :] = modes_a[...]
    high, low = split(both[: 3 * count, :] + both[3 * count :, :])
    tail[done : done + 3 * count, :] = high
    tail[done + 3 * count :, :] = low
    high, low = split(own)
    ahead_loads[...] = jnp.zeros_like(ahead_loads)
    ahead_loads[count : 2 * count, :] = dot(high, loads[...]) + dot(low, loads[...])


def merged_kernel(swaps, sizes, ride, ready, modes_f, root_inverse, ahead, *more):
    halos, more = more[: len(swaps)], more[len(swaps) :]
    received, (message, faces, stack) = more[:-3], more[-3:]
    modes, height = ready.shape[0], faces.shape[0] // len(swaps)
    count = message.shape[0] - modes
    message[:modes, :] = coarse_of(swaps, sizes, ready, modes_f, halos, faces)
    me = lax.axis_index("gx")
    stack[...] = jnp.zeros_like(stack)
    pieces = [(me, ahead)]
    for (dim, odd), halo in zip(swaps, halos):
        if ride and (dim, odd) == (0, 0):
            pieces.append((me ^ 1, halo.at[height:, :]))
    for offset, piece in zip(range(1 + ride, sizes[0]), received):
        pieces.append((source(me, offset, sizes[0]), piece))
    for index, piece in pieces:
        rows = pl.ds(pl.multiple_of(index * count, count), 3 * count)
        stack[rows, :] += piece[...]
    message[modes:, :] = dot3(root_inverse[...], stack[count:-count, :])


def root_kernel(count, coarse, root_inverse, root, *more):
    received, (message, stack) = more[: count - 1], more[count - 1 :]
    modes, height = coarse.shape[0], root.shape[0]
    me = lax.axis_index("gx")
    stack[rows_of(me, height), :] = root[...]
    for offset, piece in enumerate(received, 1):
        stack[rows_of(source(me, offset, count), height), :] = piece[...]
    message[:modes, :] = coarse[...]
    message[modes:, :] = dot3(root_inverse[...], stack[...])


def pair_kernel(modes, first, *more):
    received, out = more[:-1], more[-1]
    height = first.shape[0]
    total = first[modes:, :]
    out[:modes, :] = first[:modes, :]
    for k, piece in enumerate(received, 1):
        out[k * modes : (k + 1) * modes, :] = piece[:modes, :]
        total = total + piece[modes:, :]
    out[(len(received) + 1) * modes :, :] = total


def amplitude_of(members, sizes, region_rows, root_map, own, other, stack):
    modes = root_map.shape[1]
    y, z = lax.axis_index("gy"), lax.axis_index("gz")
    half = sizes[0] // 2
    count = len(members)
    for k, (dy, dz) in enumerate(members):
        at_y = 2 * source(y // 2, dy, half) + y % 2
        at_z = source(z, dz, sizes[1])
        piece = slice(k * modes, (k + 1) * modes)
        stack[rows_of(at_y * sizes[1] + at_z, modes), :] = own[piece, :]
        stack[rows_of((at_y ^ 1) * sizes[1] + at_z, modes), :] = other[piece, :]
    root_part = own[count * modes :, :] + other[count * modes :, :]
    return dot3(region_rows[...], stack[...]) + dot3(root_map[...], root_part, COLS)


def correction_factor(amplitude):
    high, low = split(amplitude)
    return jnp.concatenate([high, high, low], axis=0)


def middle_kernel(
    swaps, members, sizes, base, modes_t, root_map, region_rows, own, other, matrix_f, tail, modes_b, ahead_loads,
    next_solution, placed, ready, ahead, *more
):
    messages, (stack,) = more[: len(swaps)], more[len(swaps) :]
    height = placed.shape[0] // FACES
    amplitude = amplitude_of(members, sizes, region_rows, root_map, own, other, stack)
    tall = correction_factor(amplitude)
    next_solution[...] = base[...] + jnp.dot(modes_t[...], tall, preferred_element_type=F32)
    local_iter = next_solution[...].astype(BF16)
    placed[...] = jnp.dot(matrix_f[...], local_iter, preferred_element_type=F32)
    more = jnp.dot(tail[...], local_iter, preferred_element_type=F32)
    modes, count = ready.shape[0], ahead.shape[0]
    ready[...] = modes_b[...] - (more[:modes, :] + more[modes : 2 * modes, :])
    more = more[2 * modes :, :]
    ahead[...] = ahead_loads[...] - (more[:count, :] + more[count:, :])
    send_faces(swaps, placed, messages)
    for message in messages:
        if message.shape[0] > height:
            message[height:, :] = ahead[...]


def last_kernel(members, sizes, base, modes_t, root_map, region_rows, own, other, out, stack, result, sems):
    amplitude = amplitude_of(members, sizes, region_rows, root_map, own, other, stack)
    tall = correction_factor(amplitude)
    parts = sems.shape[0]
    part = result.shape[0] // parts
    copies = []
    for k in range(parts):
        rows = slice(k * part, (k + 1) * part)
        result[rows, :] = base[rows, :] + jnp.dot(modes_t[rows, :], tall, preferred_element_type=F32)
        copies.append(pltpu.make_async_copy(result.at[rows, :], out.at[rows, :], sems.at[k]))
        copies[-1].start()
    for copy in copies:
        copy.wait()


def per_device(
    loads,
    start,
    interface_op,
    block_order,
    interface_weights,
    coarse_modes,
    region_weights,
    region_inverse,
    root_inverse,
):
    sizes = tuple(lax.axis_size(axis) for axis in AXES)
    iface = interface_op.shape[-1]
    cases = loads.shape[-1]
    height = iface // FACES
    matrix = interface_op.reshape(iface, iface)
    order = block_order.reshape(1, FACES)
    weights = interface_weights.reshape(1, iface)
    modes = coarse_modes.reshape(coarse_modes.shape[-2], iface)
    mode_count = modes.shape[0]
    root_map = region_weights.reshape(mode_count, region_weights.shape[-1]).T
    root_modes = root_map.shape[0]
    region_rows = region_inverse.reshape(mode_count, region_inverse.shape[-1])
    target = loads.reshape(iface, cases)
    solution = start.reshape(iface, cases)

    swaps = swap_list(sizes)
    half = sizes[1] // 2
    members = list(itertools.product(range(half), range(sizes[2])))

    ride = int(sizes[0] & (sizes[0] - 1) == 0)
    full = (pltpu.VMEM, (iface, cases), F32)
    places = [pltpu.SMEM((1, FACES), jnp.int32)]
    stack = [pltpu.VMEM((region_rows.shape[1], cases), F32)]
    faces = [pltpu.VMEM((len(swaps) * height, cases), F32)]

    def wide(rows, dtype=BF16):
        return (pltpu.VMEM, (rows, iface), dtype)

    def held(rows):
        return (pltpu.VMEM, (rows, cases), F32)

    def along(value, offset):
        pairs = []
        for place in itertools.product(*map(range, sizes)):
            there = (partner(place[0], offset, sizes[0]),) + place[1:]
            pairs.append((flat(sizes, place), flat(sizes, there)))
        return lax.ppermute(value, AXES, pairs)

    def exchange(messages):
        return [
            lax.ppermute(message, AXES, swap_pairs(sizes, dim, odd))
            for (dim, odd), message in zip(swaps, messages)
        ]

    def base_of(solution, placed, halos):
        return call(
            functools.partial(base_kernel, swaps, sizes),
            [full],
            [solution, target, placed, scale] + halos,
            "base",
        )[0]

    for step in range(ITERS):
        if step == 0:
            inputs = [order, solution, matrix, modes, root_map]
            matrix, modes, root_map, placed, *messages = call(
                functools.partial(first_kernel, swaps),
                [(pltpu.VMEM, item.shape, item.dtype) for item in inputs[2:]]
                + [full]
                + [held(height + root_modes * height // cases)] * len(swaps),
                inputs,
                "first_product",
                places
                + [pltpu.VMEM((iface, cases), BF16)] * 2
                + [pltpu.VMEM((root_modes, iface), F32), pltpu.SemaphoreType.DMA((5,))],
                len(inputs),
            )
            modes_t, scale, modes_f, matrix_f, modes_a, modes_b, ready = call(
                functools.partial(constants_kernel, swaps, sizes),
                [
                    (pltpu.VMEM, (iface, 3 * mode_count), BF16),
                    (pltpu.VMEM, (iface, height), F32),
                    (pltpu.VMEM, (2 * mode_count, len(swaps) * height), BF16),
                    wide(iface),
                    wide(2 * mode_count),
                    held(mode_count),
                    held(mode_count),
                ],
                [order, matrix, modes, weights, target, placed],
                "constants",
                [pltpu.VMEM((iface, iface), BF16)] + places + [pltpu.SemaphoreType.DMA],
                1,
            )
            halos = exchange(messages)
            coarse, root = call(
                functools.partial(coarse_kernel, swaps, sizes),
                [held(mode_count), held(root_modes)],
                [ready, modes_f, root_map] + halos,
                "coarse",
                faces,
            )
            received = [along(root, offset) for offset in range(1, sizes[0])]
            base = base_of(solution, placed, halos)
            tail, ahead_loads = call(
                functools.partial(links_kernel, swaps, sizes),
                [wide(2 * mode_count + 6 * root_modes), held(3 * root_modes)],
                [modes, root_map, target, matrix_f, modes_a] + halos,
                "links",
                [pltpu.VMEM((3 * root_modes, iface), F32)],
            )
            (message,) = call(
                functools.partial(root_kernel, sizes[0]),
                [held(mode_count + root_modes)],
                [coarse, root_inverse, root] + received,
                "root_part",
                [pltpu.VMEM((root_inverse.shape[1], cases), F32)],
            )
        else:
            extra = [3 * root_modes if ride and swap == (0, 0) else 0 for swap in swaps]
            solution, placed, ready, ahead, *messages = call(
                functools.partial(middle_kernel, swaps, members, sizes[1:]),
                [full, full, held(mode_count), held(3 * root_modes)] + [held(height + more) for more in extra],
                [base, modes_t, root_map, region_rows, own, other, matrix_f, tail, modes_b, ahead_loads],
                "update_product",
                stack,
            )
            received = [along(ahead, offset) for offset in range(1 + ride, sizes[0])]
            halos = exchange(messages)
            (message,) = call(
                functools.partial(merged_kernel, swaps, sizes, ride),
                [held(mode_count + root_modes)],
                [ready, modes_f, root_inverse, ahead] + halos + received,
                "coarse_root",
                faces + [pltpu.VMEM((root_inverse.shape[1] + 2 * root_modes, cases), F32)],
            )
            base = base_of(solution, placed, halos)
        pieces = []
        for dy, dz in members[1:]:
            moves = [
                (y * sizes[2] + z, (2 * partner(y // 2, dy, half) + y % 2) * sizes[2] + partner(z, dz, sizes[2]))
                for y in range(sizes[1])
                for z in range(sizes[2])
            ]
            pieces.append(lax.ppermute(message, ("gy", "gz"), moves))
        (own,) = call(
            functools.partial(pair_kernel, mode_count),
            [held(len(members) * mode_count + root_modes)],
            [message] + pieces,
            "pair_message",
        )
        other = lax.ppermute(own, AXES, swap_pairs(sizes, 1, 0))
    (solution,) = call(
        functools.partial(last_kernel, members, sizes[1:]),
        [(jax.ShapeDtypeStruct, (iface, cases), F32)],
        [base, modes_t, root_map, region_rows, own, other],
        "update_last",
        stack + [pltpu.VMEM((iface, cases), F32), pltpu.SemaphoreType.DMA((FACES,))],
    )
    return solution.reshape(1, 1, 1, iface, cases)


def solution(mesh):
    placed = (
        P("gx", "gy", "gz", None, None),
        P("gx", "gy", "gz", None, None),
        P("gx", "gy", "gz", None, None),
        P("gx", "gy", "gz", None),
        P("gx", "gy", "gz", None),
        P("gx", "gy", "gz", None, None),
        P("gx", "gy", "gz", None, None),
        P("gx", ("gy", "gz"), None),
        P("gx", None),
    )
    return jax.shard_map(
        per_device,
        mesh=mesh,
        in_specs=placed,
        out_specs=P("gx", "gy", "gz", None, None),
        check_vma=False,
    )
```

time: 53.6 us -> 52 us (0.970)
  waiting for transfers between devices: 19.9 us -> 16.7 us
  Pallas kernels: 9.16 us -> 10.6 us
    ppermute x10, waiting for transfers between devices: 6.79 us -> 4.09 us  [exchange(): lax.ppermute(message, AXES, swap_pairs(sizes, dim, odd))]
    pallas_call x10 -> x12, Pallas kernels: 9.16 us -> 10.6 us  [call(): pl.pallas_call(body, out_shape=[item(shape, dtype) for item, shape, dtype...]
    ppermute x2, waiting for transfers between devices: 2.32 us -> 1.37 us  [per_device(): other = lax.ppermute(own, AXES, swap_pairs(sizes, 1, 0))]
    ppermute x10, starting transfers between devices: 8.4 us -> 9.36 us  [exchange(): lax.ppermute(message, AXES, swap_pairs(sizes, dim, odd))]
    ppermute x5, starting transfers between devices: 8.75 us -> 7.86 us  [along(): return lax.ppermute(value, AXES, pairs)]
    ppermute x5, waiting for transfers between devices: 4.59 us -> 5.14 us  [along(): return lax.ppermute(value, AXES, pairs)]
  transfers between devices with their start and end apart: 23 -> 23, of which waited for: 17 -> 15; matrix products, arithmetic and copies ran while one was open for 0% -> 0% of each run, Pallas kernels for 2% -> 8%
where the time goes in v5:
time: 52 us; the launch traced here: 51.9 us
  starting transfers between devices  24.4 us (47%)
  waiting for transfers between devices  16.7 us (32%)
  Pallas kernels  10.6 us (20%)
    pallas_call x12, Pallas kernels, call(): pl.pallas_call(body, out_shape=[item(shape, dtype) for item, shape, dtype...  10.6 us
    ppermute x10, starting transfers between devices, exchange(): lax.ppermute(message, AXES, swap_pairs(sizes, dim, odd))  9.36 us
    ppermute x5, starting transfers between devices, along(): return lax.ppermute(value, AXES, pairs)  7.86 us
    ppermute x6, starting transfers between devices, per_device(): pieces.append(lax.ppermute(message, ('gy', 'gz'), moves))  7.05 us
    ppermute x6, waiting for transfers between devices, per_device(): pieces.append(lax.ppermute(message, ('gy', 'gz'), moves))  6.15 us
    ppermute x5, waiting for transfers between devices, along(): return lax.ppermute(value, AXES, pairs)  5.14 us
    ppermute x10, waiting for transfers between devices, exchange(): lax.ppermute(message, AXES, swap_pairs(sizes, dim, odd))  4.09 us
    ppermute x2, waiting for transfers between devices, per_device(): other = lax.ppermute(own, AXES, swap_pairs(sizes, 1, 0))  1.37 us
  transfers between devices with their start and end apart: 23, of which 15 were waited for; matrix products, arithmetic and copies ran while one was open for 0% of the time, Pallas kernels for 8%

profile of v5, /device:TPU:0, one launch (start us, length us, event | category | flops | bytes accessed | tf_op | source)
XLA Modules:
  0.0 51.9 jit_solution(10725425098881467585)
XLA Ops:
  0.0 2.7 %first_product.1 = (bf16[1024,1024]{1,0:T(8,128)(2,1)S(1)}, f32[32,1024]{1,0:T(8,128)S(1)}, f32[16,32]{1,0:T(8,128)S(1)}, f32[1024,256]{1,0:T(8,128)S(1)}, f32[1...) custom-call(s32[1,8]{1,0:T(1,128)} %bitcast.23, ...), custom_call_target="tpu_custom_call" | custom-call | tf_op jit(solution)/shard_map/first_product/pallas_call | solution.py:87
  3.2 2.6 %collective-permute-start.1 = (f32[136,256]{1,0:T(8,128)S(1)}, f32[136,256]{1,0:T(8,128)S(1)}, u32[]{:S(2)}, u32[]{:S(2)}) collective-permute-start(f32[136,256]{1,0:T(8,128)S(1)} %get-tuple-element.39), channel_id=1, source_target_pairs={{0,6},{1,7},{2,4},{3,5},{4,2},{5,3},{6,0},{7,1},{8,14},{9,15},{10,... | collective-permute-start | bytes 417800 | tf_op jit(solution)/shard_map/ppermute | solution.py:385
  5.9 2.2 %collective-permute-start.2 = (f32[136,256]{1,0:T(8,128)S(1)}, f32[136,256]{1,0:T(8,128)S(1)}, u32[]{:S(2)}, u32[]{:S(2)}) collective-permute-start(f32[136,256]{1,0:T(8,128)S(1)} %get-tuple-element.40), channel_id=1, source_target_pairs={{0,8},{1,9},{2,10},{3,11},{4,12},{5,13},{6,14},{7,15},{8,0},{9,1},... | collective-permute-start | bytes 417800 | tf_op jit(solution)/shard_map/ppermute | solution.py:385
  8.0 1.5 %collective-permute-start.3 = (f32[136,256]{1,0:T(8,128)S(1)}, f32[136,256]{1,0:T(8,128)S(1)}, u32[]{:S(2)}, u32[]{:S(2)}) collective-permute-start(f32[136,256]{1,0:T(8,128)S(1)} %get-tuple-element.41), channel_id=1, source_target_pairs={{0,1},{1,0},{2,3},{3,2},{4,5},{5,4},{6,7},{7,6},{8,9},{9,8},{10,11... | collective-permute-start | bytes 417800 | tf_op jit(solution)/shard_map/ppermute | solution.py:385
  10.0 2.8 %constants.1 = (bf16[1024,96]{1,0:T(8,128)(2,1)S(1)}, f32[1024,128]{1,0:T(8,128)S(1)}, bf16[64,640]{1,0:T(8,128)(2,1)S(1)}, bf16[1024,1024]{1,0:T(8,128)(2,1)S(1...) custom-call(s32[1,8]{1,0:T(1,128)} %bitcast.24, ...), custom_call_target="tpu_custom_call" | custom-call | tf_op jit(solution)/shard_map/constants/pallas_call | solution.py:87
  12.8 1.5 %collective-permute-done.3.more_3_ = f32[136,256]{1,0:T(8,128)S(1)} collective-permute-done((f32[136,256]{1,0:T(8,128)S(1)}, f32[136,256]{1,0:T(8,128)S(1)}, u32[]{:S(2)}, u32[]{:S(2)}) %collective-permute-start.3) | collective-permute-done | bytes 139296 | tf_op jit(solution)/shard_map/ppermute | solution.py:385
  14.7 1.4 %collective-permute-start.7 = (f32[16,256]{1,0:T(8,128)S(1)}, f32[16,256]{1,0:T(8,128)S(1)}, u32[]{:S(2)}, u32[]{:S(2)}) collective-permute-start(f32[16,256]{1,0:T(8,128)S(1)} %get-tuple-element.48.root), channel_id=1, source_target_pairs={{0,24},{1,25},{2,26},{3,27},{4,28},{5,29},{6,30},{7,31},{8,16},{9,... | collective-permute-start | bytes 49160 | tf_op jit(solution)/shard_map/ppermute | solution.py:381
  16.4 2.6 %collective-permute-start.5 = (f32[16,256]{1,0:T(8,128)S(1)}, f32[16,256]{1,0:T(8,128)S(1)}, u32[]{:S(2)}, u32[]{:S(2)}) collective-permute-start(f32[16,256]{1,0:T(8,128)S(1)} %get-tuple-element.48.root), channel_id=1, source_target_pairs={{0,8},{1,9},{2,10},{3,11},{4,12},{5,13},{6,14},{7,15},{8,0},{9,1},... | collective-permute-start | bytes 49160 | tf_op jit(solution)/shard_map/ppermute | solution.py:381
  19.1 1.1 %collective-permute-done.7.more_2_ = f32[16,256]{1,0:T(8,128)S(1)} collective-permute-done((f32[16,256]{1,0:T(8,128)S(1)}, f32[16,256]{1,0:T(8,128)S(1)}, u32[]{:S(2)}, u32[]{:S(2)}) %collective-permute-start.7) | collective-permute-done | bytes 16416 | tf_op jit(solution)/shard_map/ppermute | solution.py:381
  21.0 1.5 %collective-permute-start.10 = (f32[48,256]{1,0:T(8,128)S(1)}, f32[48,256]{1,0:T(8,128)S(1)}, u32[]{:S(2)}, u32[]{:S(2)}) collective-permute-start(f32[48,256]{1,0:T(8,128)S(1)} %root_part.1.first), channel_id=1, source_target_pairs={{0,5},{1,4},{2,7},{3,6},{4,1},{5,0},{6,3},{7,2},{8,13},{9,12},{10,... | collective-permute-start | bytes 147464 | tf_op jit(solution)/shard_map/ppermute | solution.py:478
  22.5 1.5 %collective-permute-start.9 = (f32[48,256]{1,0:T(8,128)S(1)}, f32[48,256]{1,0:T(8,128)S(1)}, u32[]{:S(2)}, u32[]{:S(2)}) collective-permute-start(f32[48,256]{1,0:T(8,128)S(1)} %root_part.1.first), channel_id=1, source_target_pairs={{0,4},{1,5},{2,6},{3,7},{4,0},{5,1},{6,2},{7,3},{8,12},{9,13},{10,... | collective-permute-start | bytes 147464 | tf_op jit(solution)/shard_map/ppermute | solution.py:478
  24.5 1.5 %collective-permute-done.10.more_2_ = f32[48,256]{1,0:T(8,128)S(1)} collective-permute-done((f32[48,256]{1,0:T(8,128)S(1)}, f32[48,256]{1,0:T(8,128)S(1)}, u32[]{:S(2)}, u32[]{:S(2)}) %collective-permute-start.10) | collective-permute-done | bytes 49184 | tf_op jit(solution)/shard_map/ppermute | solution.py:478
  26.6 1.5 %collective-permute-done.8.more_0_ = f32[48,256]{1,0:T(8,128)S(1)} collective-permute-done((f32[48,256]{1,0:T(8,128)S(1)}, f32[48,256]{1,0:T(8,128)S(1)}, u32[]{:S(2)}, u32[]{:S(2)}) %collective-permute-start.8) | collective-permute-done | bytes 49184 | tf_op jit(solution)/shard_map/ppermute | solution.py:478
  29.6 1.4 %update_product.1 = (f32[1024,256]{1,0:T(8,128)S(1)}, f32[1024,256]{1,0:T(8,128)S(1)}, f32[32,256]{1,0:T(8,128)S(1)}, f32[48,256]{1,0:T(8,128)S(1)}, f32[128,256...) custom-call(f32[1024,256]{1,0:T(8,128)S(1)} %base.2, ...), custom_call_target="tpu_custom_call" | custom-call | tf_op jit(solution)/shard_map/update_product/pallas_call | solution.py:87
  31.0 2.3 %collective-permute-start.18 = (f32[48,256]{1,0:T(8,128)S(1)}, f32[48,256]{1,0:T(8,128)S(1)}, u32[]{:S(2)}, u32[]{:S(2)}) collective-permute-start(f32[48,256]{1,0:T(8,128)S(1)} %get-tuple-element.62.ahead), channel_id=1, source_target_pairs={{0,24},{1,25},{2,26},{3,27},{4,28},{5,29},{6,30},{7,31},{8,16},{9,... | collective-permute-start | bytes 147464 | tf_op jit(solution)/shard_map/ppermute | solution.py:381
  33.3 1.1 %collective-permute-start.17 = (f32[48,256]{1,0:T(8,128)S(1)}, f32[48,256]{1,0:T(8,128)S(1)}, u32[]{:S(2)}, u32[]{:S(2)}) collective-permute-start(f32[48,256]{1,0:T(8,128)S(1)} %get-tuple-element.62.ahead), channel_id=1, source_target_pairs={{0,16},{1,17},{2,18},{3,19},{4,20},{5,21},{6,22},{7,23},{8,24},{9,... | collective-permute-start | bytes 147464 | tf_op jit(solution)/shard_map/ppermute | solution.py:381
  36.1 1.4 %collective-permute-done.18.more_6_ = f32[48,256]{1,0:T(8,128)S(1)} collective-permute-done((f32[48,256]{1,0:T(8,128)S(1)}, f32[48,256]{1,0:T(8,128)S(1)}, u32[]{:S(2)}, u32[]{:S(2)}) %collective-permute-start.18) | collective-permute-done | bytes 49184 | tf_op jit(solution)/shard_map/ppermute | solution.py:381
  38.0 1.9 %collective-permute-done.17.more_5_ = f32[48,256]{1,0:T(8,128)S(1)} collective-permute-done((f32[48,256]{1,0:T(8,128)S(1)}, f32[48,256]{1,0:T(8,128)S(1)}, u32[]{:S(2)}, u32[]{:S(2)}) %collective-permute-start.17) | collective-permute-done | bytes 49184 | tf_op jit(solution)/shard_map/ppermute | solution.py:381
  40.6 1.9 %collective-permute-done.15.more_3_ = f32[128,256]{1,0:T(8,128)S(1)} collective-permute-done((f32[128,256]{1,0:T(8,128)S(1)}, f32[128,256]{1,0:T(8,128)S(1)}, u32[]{:S(2)}, u32[]{:S(2)}) %collective-permute-start.15) | collective-permute-done | bytes 131104 | tf_op jit(solution)/shard_map/ppermute | solution.py:385
  43.3 1.5 %collective-permute-start.20 = (f32[48,256]{1,0:T(8,128)S(1)}, f32[48,256]{1,0:T(8,128)S(1)}, u32[]{:S(2)}, u32[]{:S(2)}) collective-permute-start(f32[48,256]{1,0:T(8,128)S(1)} %coarse_root.1.first), channel_id=1, source_target_pairs={{0,4},{1,5},{2,6},{3,7},{4,0},{5,1},{6,2},{7,3},{8,12},{9,13},{10,... | collective-permute-start | bytes 147464 | tf_op jit(solution)/shard_map/ppermute | solution.py:478
  44.8 1.5 %collective-permute-start.19 = (f32[48,256]{1,0:T(8,128)S(1)}, f32[48,256]{1,0:T(8,128)S(1)}, u32[]{:S(2)}, u32[]{:S(2)}) collective-permute-start(f32[48,256]{1,0:T(8,128)S(1)} %coarse_root.1.first), channel_id=1, source_target_pairs={{0,1},{1,0},{2,3},{3,2},{4,5},{5,4},{6,7},{7,6},{8,9},{9,8},{10,11... | collective-permute-start | bytes 147464 | tf_op jit(solution)/shard_map/ppermute | solution.py:478
  46.3 1.5 %collective-permute-done.21.more_2_ = f32[48,256]{1,0:T(8,128)S(1)} collective-permute-done((f32[48,256]{1,0:T(8,128)S(1)}, f32[48,256]{1,0:T(8,128)S(1)}, u32[]{:S(2)}, u32[]{:S(2)}) %collective-permute-start.21) | collective-permute-done | bytes 49184 | tf_op jit(solution)/shard_map/ppermute | solution.py:478
  47.8 1.1 %collective-permute-done.19.more_0_ = f32[48,256]{1,0:T(8,128)S(1)} collective-permute-done((f32[48,256]{1,0:T(8,128)S(1)}, f32[48,256]{1,0:T(8,128)S(1)}, u32[]{:S(2)}, u32[]{:S(2)}) %collective-permute-start.19) | collective-permute-done | bytes 49184 | tf_op jit(solution)/shard_map/ppermute | solution.py:478
  50.4 1.5 %update_last.1 = f32[1024,256]{1,0:T(8,128)} custom-call(f32[1024,256]{1,0:T(8,128)S(1)} %base.3, bf16[1024,96]{1,0:T(8,128)(2,1)S(1)} %get-tuple-element.43.modes_t, f32[16,32]{1,0:T(8,128)S(1)} %get-tuple-element.44.root_map, f32[32,256]{1,0:T(8,128)S(1)} %bitcast.18, f32[144,256]{1,0:T(8,128)S(1)} %pair_message.3.own, ...), custom_call_target="tpu_custom_call" | custom-call | tf_op jit(solution)/shard_map/update_last/pallas_call | solution.py:87
  (44 shorter events, 10.1 us)
Async XLA Ops:
  2.7 10.0 %collective-permute-start = (f32[136,256]{1,0:T(8,128)S(1)}, f32[136,256]{1,0:T(8,128)S(1)}, u32[]{:S(2)}, u32[]{:S(2)}) collective-permute-start(f32[136,256]{1,0:T(8,128)S(1)} %get-tuple-element.38), channel_id=1, source_target_pairs={{0,2},{1,3},{2,0},{3,1},{4,6},{5,7},{6,4},{7,5},{8,16},{9,17},{10,... | collective-permute-start | bytes 417800 | tf_op jit(solution)/shard_map/ppermute | solution.py:385
  3.2 9.5 %collective-permute-start.1 = (f32[136,256]{1,0:T(8,128)S(1)}, f32[136,256]{1,0:T(8,128)S(1)}, u32[]{:S(2)}, u32[]{:S(2)}) collective-permute-start(f32[136,256]{1,0:T(8,128)S(1)} %get-tuple-element.39), channel_id=1, source_target_pairs={{0,6},{1,7},{2,4},{3,5},{4,2},{5,3},{6,0},{7,1},{8,14},{9,15},{10,... | collective-permute-start | bytes 417800 | tf_op jit(solution)/shard_map/ppermute | solution.py:385
  5.9 6.9 %collective-permute-start.2 = (f32[136,256]{1,0:T(8,128)S(1)}, f32[136,256]{1,0:T(8,128)S(1)}, u32[]{:S(2)}, u32[]{:S(2)}) collective-permute-start(f32[136,256]{1,0:T(8,128)S(1)} %get-tuple-element.40), channel_id=1, source_target_pairs={{0,8},{1,9},{2,10},{3,11},{4,12},{5,13},{6,14},{7,15},{8,0},{9,1},... | collective-permute-start | bytes 417800 | tf_op jit(solution)/shard_map/ppermute | solution.py:385
  8.0 6.3 %collective-permute-start.3 = (f32[136,256]{1,0:T(8,128)S(1)}, f32[136,256]{1,0:T(8,128)S(1)}, u32[]{:S(2)}, u32[]{:S(2)}) collective-permute-start(f32[136,256]{1,0:T(8,128)S(1)} %get-tuple-element.41), channel_id=1, source_target_pairs={{0,1},{1,0},{2,3},{3,2},{4,5},{5,4},{6,7},{7,6},{8,9},{9,8},{10,11... | collective-permute-start | bytes 417800 | tf_op jit(solution)/shard_map/ppermute | solution.py:385
  9.6 4.7 %collective-permute-start.4 = (f32[136,256]{1,0:T(8,128)S(1)}, f32[136,256]{1,0:T(8,128)S(1)}, u32[]{:S(2)}, u32[]{:S(2)}) collective-permute-start(f32[136,256]{1,0:T(8,128)S(1)} %get-tuple-element.42), channel_id=1, source_target_pairs={{0,2},{1,3},{2,0},{3,1},{4,6},{5,7},{6,4},{7,5},{8,10},{9,11},{10,... | collective-permute-start | bytes 417800 | tf_op jit(solution)/shard_map/ppermute | solution.py:385
  10.0 18.3 %copy-start.1 = (bf16[1,1,1,1024,256]{4,3,2,1,0:T(8,128)(2,1)S(1)}, bf16[1,1,1,1024,256]{4,3,2,1,0:T(8,128)(2,1)}, u32[]{:S(2)}) copy-start(bf16[1,1,1,1024,256]{4,3,2,1,0:T(8,128)(2,1)} %param.10) | copy-start | bytes 1572868
  14.7 5.5 %collective-permute-start.7 = (f32[16,256]{1,0:T(8,128)S(1)}, f32[16,256]{1,0:T(8,128)S(1)}, u32[]{:S(2)}, u32[]{:S(2)}) collective-permute-start(f32[16,256]{1,0:T(8,128)S(1)} %get-tuple-element.48.root), channel_id=1, source_target_pairs={{0,24},{1,25},{2,26},{3,27},{4,28},{5,29},{6,30},{7,31},{8,16},{9,... | collective-permute-start | bytes 49160 | tf_op jit(solution)/shard_map/ppermute | solution.py:381
  16.0 4.7 %collective-permute-start.6 = (f32[16,256]{1,0:T(8,128)S(1)}, f32[16,256]{1,0:T(8,128)S(1)}, u32[]{:S(2)}, u32[]{:S(2)}) collective-permute-start(f32[16,256]{1,0:T(8,128)S(1)} %get-tuple-element.48.root), channel_id=1, source_target_pairs={{0,16},{1,17},{2,18},{3,19},{4,20},{5,21},{6,22},{7,23},{8,24},{9,... | collective-permute-start | bytes 49160 | tf_op jit(solution)/shard_map/ppermute | solution.py:381
  16.4 4.5 %collective-permute-start.5 = (f32[16,256]{1,0:T(8,128)S(1)}, f32[16,256]{1,0:T(8,128)S(1)}, u32[]{:S(2)}, u32[]{:S(2)}) collective-permute-start(f32[16,256]{1,0:T(8,128)S(1)} %get-tuple-element.48.root), channel_id=1, source_target_pairs={{0,8},{1,9},{2,10},{3,11},{4,12},{5,13},{6,14},{7,15},{8,0},{9,1},... | collective-permute-start | bytes 49160 | tf_op jit(solution)/shard_map/ppermute | solution.py:381
  21.0 5.0 %collective-permute-start.10 = (f32[48,256]{1,0:T(8,128)S(1)}, f32[48,256]{1,0:T(8,128)S(1)}, u32[]{:S(2)}, u32[]{:S(2)}) collective-permute-start(f32[48,256]{1,0:T(8,128)S(1)} %root_part.1.first), channel_id=1, source_target_pairs={{0,5},{1,4},{2,7},{3,6},{4,1},{5,0},{6,3},{7,2},{8,13},{9,12},{10,... | collective-permute-start | bytes 147464 | tf_op jit(solution)/shard_map/ppermute | solution.py:478
  22.5 4.1 %collective-permute-start.9 = (f32[48,256]{1,0:T(8,128)S(1)}, f32[48,256]{1,0:T(8,128)S(1)}, u32[]{:S(2)}, u32[]{:S(2)}) collective-permute-start(f32[48,256]{1,0:T(8,128)S(1)} %root_part.1.first), channel_id=1, source_target_pairs={{0,4},{1,5},{2,6},{3,7},{4,0},{5,1},{6,2},{7,3},{8,12},{9,13},{10,... | collective-permute-start | bytes 147464 | tf_op jit(solution)/shard_map/ppermute | solution.py:478
  24.0 4.1 %collective-permute-start.8 = (f32[48,256]{1,0:T(8,128)S(1)}, f32[48,256]{1,0:T(8,128)S(1)}, u32[]{:S(2)}, u32[]{:S(2)}) collective-permute-start(f32[48,256]{1,0:T(8,128)S(1)} %root_part.1.first), channel_id=1, source_target_pairs={{0,1},{1,0},{2,3},{3,2},{4,5},{5,4},{6,7},{7,6},{8,9},{9,8},{10,11... | collective-permute-start | bytes 147464 | tf_op jit(solution)/shard_map/ppermute | solution.py:478
  28.1 1.4 %collective-permute-start.11 = (f32[144,256]{1,0:T(8,128)S(1)}, f32[144,256]{1,0:T(8,128)S(1)}, u32[]{:S(2)}, u32[]{:S(2)}) collective-permute-start(f32[144,256]{1,0:T(8,128)S(1)} %pair_message.2.own), channel_id=1, source_target_pairs={{0,2},{1,3},{2,0},{3,1},{4,6},{5,7},{6,4},{7,5},{8,10},{9,11},{10,... | collective-permute-start | bytes 442376 | tf_op jit(solution)/shard_map/ppermute | solution.py:485
  31.0 6.5 %collective-permute-start.18 = (f32[48,256]{1,0:T(8,128)S(1)}, f32[48,256]{1,0:T(8,128)S(1)}, u32[]{:S(2)}, u32[]{:S(2)}) collective-permute-start(f32[48,256]{1,0:T(8,128)S(1)} %get-tuple-element.62.ahead), channel_id=1, source_target_pairs={{0,24},{1,25},{2,26},{3,27},{4,28},{5,29},{6,30},{7,31},{8,16},{9,... | collective-permute-start | bytes 147464 | tf_op jit(solution)/shard_map/ppermute | solution.py:381
  33.3 6.6 %collective-permute-start.17 = (f32[48,256]{1,0:T(8,128)S(1)}, f32[48,256]{1,0:T(8,128)S(1)}, u32[]{:S(2)}, u32[]{:S(2)}) collective-permute-start(f32[48,256]{1,0:T(8,128)S(1)} %get-tuple-element.62.ahead), channel_id=1, source_target_pairs={{0,16},{1,17},{2,18},{3,19},{4,20},{5,21},{6,22},{7,23},{8,24},{9,... | collective-permute-start | bytes 147464 | tf_op jit(solution)/shard_map/ppermute | solution.py:381
  34.5 8.0 %collective-permute-start.14 = (f32[176,256]{1,0:T(8,128)S(1)}, f32[176,256]{1,0:T(8,128)S(1)}, u32[]{:S(2)}, u32[]{:S(2)}) collective-permute-start(f32[176,256]{1,0:T(8,128)S(1)} %get-tuple-element.58), channel_id=1, source_target_pairs={{0,8},{1,9},{2,10},{3,11},{4,12},{5,13},{6,14},{7,15},{8,0},{9,1},... | collective-permute-start | bytes 540680 | tf_op jit(solution)/shard_map/ppermute | solution.py:385
  35.5 4.5 %collective-permute-start.12 = (f32[128,256]{1,0:T(8,128)S(1)}, f32[128,256]{1,0:T(8,128)S(1)}, u32[]{:S(2)}, u32[]{:S(2)}) collective-permute-start(f32[128,256]{1,0:T(8,128)S(1)} %get-tuple-element.56), channel_id=1, source_target_pairs={{0,2},{1,3},{2,0},{3,1},{4,6},{5,7},{6,4},{7,5},{8,16},{9,17},{10,... | collective-permute-start | bytes 393224 | tf_op jit(solution)/shard_map/ppermute | solution.py:385
  35.5 5.2 %collective-permute-start.13 = (f32[128,256]{1,0:T(8,128)S(1)}, f32[128,256]{1,0:T(8,128)S(1)}, u32[]{:S(2)}, u32[]{:S(2)}) collective-permute-start(f32[128,256]{1,0:T(8,128)S(1)} %get-tuple-element.57), channel_id=1, source_target_pairs={{0,6},{1,7},{2,4},{3,5},{4,2},{5,3},{6,0},{7,1},{8,14},{9,15},{10,... | collective-permute-start | bytes 393224 | tf_op jit(solution)/shard_map/ppermute | solution.py:385
  37.5 5.0 %collective-permute-start.15 = (f32[128,256]{1,0:T(8,128)S(1)}, f32[128,256]{1,0:T(8,128)S(1)}, u32[]{:S(2)}, u32[]{:S(2)}) collective-permute-start(f32[128,256]{1,0:T(8,128)S(1)} %get-tuple-element.59), channel_id=1, source_target_pairs={{0,1},{1,0},{2,3},{3,2},{4,5},{5,4},{6,7},{7,6},{8,9},{9,8},{10,11... | collective-permute-start | bytes 393224 | tf_op jit(solution)/shard_map/ppermute | solution.py:385
  39.9 2.6 %collective-permute-start.16 = (f32[128,256]{1,0:T(8,128)S(1)}, f32[128,256]{1,0:T(8,128)S(1)}, u32[]{:S(2)}, u32[]{:S(2)}) collective-permute-start(f32[128,256]{1,0:T(8,128)S(1)} %get-tuple-element.60), channel_id=1, source_target_pairs={{0,2},{1,3},{2,0},{3,1},{4,6},{5,7},{6,4},{7,5},{8,10},{9,11},{10,... | collective-permute-start | bytes 393224 | tf_op jit(solution)/shard_map/ppermute | solution.py:385
  42.8 5.1 %collective-permute-start.21 = (f32[48,256]{1,0:T(8,128)S(1)}, f32[48,256]{1,0:T(8,128)S(1)}, u32[]{:S(2)}, u32[]{:S(2)}) collective-permute-start(f32[48,256]{1,0:T(8,128)S(1)} %coarse_root.1.first), channel_id=1, source_target_pairs={{0,5},{1,4},{2,7},{3,6},{4,1},{5,0},{6,3},{7,2},{8,13},{9,12},{10,... | collective-permute-start | bytes 147464 | tf_op jit(solution)/shard_map/ppermute | solution.py:478
  43.3 4.5 %collective-permute-start.20 = (f32[48,256]{1,0:T(8,128)S(1)}, f32[48,256]{1,0:T(8,128)S(1)}, u32[]{:S(2)}, u32[]{:S(2)}) collective-permute-start(f32[48,256]{1,0:T(8,128)S(1)} %coarse_root.1.first), channel_id=1, source_target_pairs={{0,4},{1,5},{2,6},{3,7},{4,0},{5,1},{6,2},{7,3},{8,12},{9,13},{10,... | collective-permute-start | bytes 147464 | tf_op jit(solution)/shard_map/ppermute | solution.py:478
  44.8 4.1 %collective-permute-start.19 = (f32[48,256]{1,0:T(8,128)S(1)}, f32[48,256]{1,0:T(8,128)S(1)}, u32[]{:S(2)}, u32[]{:S(2)}) collective-permute-start(f32[48,256]{1,0:T(8,128)S(1)} %coarse_root.1.first), channel_id=1, source_target_pairs={{0,1},{1,0},{2,3},{3,2},{4,5},{5,4},{6,7},{7,6},{8,9},{9,8},{10,11... | collective-permute-start | bytes 147464 | tf_op jit(solution)/shard_map/ppermute | solution.py:478
  48.9 1.4 %collective-permute-start.22 = (f32[144,256]{1,0:T(8,128)S(1)}, f32[144,256]{1,0:T(8,128)S(1)}, u32[]{:S(2)}, u32[]{:S(2)}) collective-permute-start(f32[144,256]{1,0:T(8,128)S(1)} %pair_message.3.own), channel_id=1, source_target_pairs={{0,2},{1,3},{2,0},{3,1},{4,6},{5,7},{6,4},{7,5},{8,10},{9,11},{10,... | collective-permute-start | bytes 442376 | tf_op jit(solution)/shard_map/ppermute | solution.py:485
  (4 other events, 31.9 us)

commit v6 on v5

--- a/solution.py
+++ b/solution.py
@@ -135,7 +135,7 @@
 
 
 def constants_kernel(
-    swaps, sizes, order_hbm, matrix, modes, weights, loads, placed,
+    swaps, sizes, order_hbm, matrix, modes, root_map, weights, loads, placed,
     modes_t, scale, modes_f, matrix_f, modes_a, modes_b, ready, wide, order, sem
 ):
     copy = pltpu.make_async_copy(order_hbm, order, sem)
@@ -151,10 +151,14 @@
         columns = modes[:, rows_of(face, height)]
         columns = jnp.where(has_neighbour(dim, face, sizes), columns, 0.0)
         block = slice(at * height, (at + 1) * height)
-        modes_f[:count, block], modes_f[count:, block] = split(columns)
+        modes_f[:count, block], modes_f[count : 2 * count, block] = split(columns)
+        rows = root_map.shape[0]
+        parts = split(dot3(root_map[...], columns))
+        modes_f[2 * count : 2 * count + rows, block], modes_f[2 * count + rows :, block] = parts
     dot = functools.partial(jnp.dot, preferred_element_type=F32)
     modes_b[...] = dot(high, loads[...]) + dot(low, loads[...])
-    ready[...] = modes_b[...] - dot3(modes[...], placed[...])
+    ready[:count, :] = modes_b[...] - dot3(modes[...], placed[...])
+    ready[count:, :] = dot3(root_map[...], ready[:count, :])
     copy.wait()
     for j in range(FACES):
         block = slice(j * height, (j + 1) * height)
@@ -165,21 +169,23 @@
     modes_a[:count, :], modes_a[count:, :] = split(dot(high, matrix_f[...]) + dot(low, matrix_f[...]))
 
 
-def coarse_of(swaps, sizes, ready, modes_f, halos, stack):
-    height, count = stack.shape[0] // len(swaps), ready.shape[0]
+def stack_halos(swaps, sizes, halos, stack):
+    height = stack.shape[0] // len(swaps)
     for at, ((dim, odd), halo) in enumerate(zip(swaps, halos)):
         known = has_neighbour(dim, swap_face(dim, odd), sizes)
         stack[at * height : (at + 1) * height, :] = jnp.where(known, halo[:height, :], 0.0)
-    high, low = split(stack[...])
+    return split(stack[...])
+
+
+def coarse_kernel(swaps, sizes, ready, modes_f, *more):
+    halos, (coarse, root, stack) = more[: len(swaps)], more[len(swaps) :]
+    modes, count = coarse.shape[0], root.shape[0]
+    high, low = stack_halos(swaps, sizes, halos, stack)
     both = jnp.dot(modes_f[...], high, preferred_element_type=F32)
-    fine = jnp.dot(modes_f[:count, :], low, preferred_element_type=F32)
-    return ready[...] - (both[:count, :] + (both[count:, :] + fine))
-
-
-def coarse_kernel(swaps, sizes, ready, modes_f, root_map, *more):
-    halos, (coarse, root, stack) = more[: len(swaps)], more[len(swaps) :]
-    coarse[...] = coarse_of(swaps, sizes, ready, modes_f, halos, stack)
-    root[...] = dot3(root_map[...], coarse[...])
+    fine = jnp.dot(modes_f[: 2 * modes + count, :], low, preferred_element_type=F32)
+    coarse[...] = ready[:modes, :] - (both[:modes, :] + (both[modes : 2 * modes, :] + fine[:modes, :]))
+    at = 2 * modes
+    root[...] = ready[modes:, :] - (both[at : at + count, :] + (both[at + count :, :] + fine[at:, :]))
 
 
 def base_kernel(swaps, sizes, solution, loads, placed, scale, *more):
@@ -237,7 +243,10 @@
     received, (message, faces, stack) = more[:-3], more[-3:]
     modes, height = ready.shape[0], faces.shape[0] // len(swaps)
     count = message.shape[0] - modes
-    message[:modes, :] = coarse_of(swaps, sizes, ready, modes_f, halos, faces)
+    high, low = stack_halos(swaps, sizes, halos, faces)
+    both = jnp.dot(modes_f[: 2 * modes, :], high, preferred_element_type=F32)
+    fine = jnp.dot(modes_f[:modes, :], low, preferred_element_type=F32)
+    message[:modes, :] = ready[...] - (both[:modes, :] + (both[modes:, :] + fine))
     me = lax.axis_index("gx")
     stack[...] = jnp.zeros_like(stack)
     pieces = [(me, ahead)]
@@ -263,30 +272,51 @@
     message[modes:, :] = dot3(root_inverse[...], stack[...])
 
 
-def pair_kernel(modes, first, *more):
-    received, out = more[:-1], more[-1]
-    height = first.shape[0]
-    total = first[modes:, :]
-    out[:modes, :] = first[:modes, :]
-    for k, piece in enumerate(received, 1):
-        out[k * modes : (k + 1) * modes, :] = piece[:modes, :]
-        total = total + piece[modes:, :]
-    out[(len(received) + 1) * modes :, :] = total
-
-
-def amplitude_of(members, sizes, region_rows, root_map, own, other, stack):
-    modes = root_map.shape[1]
+def pack_kernel(region_rows, root_map, packed):
+    modes, width = region_rows.shape[0], root_map.shape[1]
+    packed[...] = jnp.zeros_like(packed)
+    packed[:modes, :] = region_rows[...]
+    packed[modes:, :width] = root_map[...]
+
+
+def parts_kernel(members, sizes, packed, sibling, factors):
+    modes, order = factors.shape[0] // 4, packed.shape[1]
+    count = packed.shape[0] - modes
     y, z = lax.axis_index("gy"), lax.axis_index("gz")
     half = sizes[0] // 2
-    count = len(members)
+    depth = len(members) * modes
+    row = lax.broadcasted_iota(jnp.int32, (order, depth), 0)
+    column = lax.broadcasted_iota(jnp.int32, (order, depth), 1)
+    wanted = jnp.full((order, depth), -1, jnp.int32)
     for k, (dy, dz) in enumerate(members):
         at_y = 2 * source(y // 2, dy, half) + y % 2
-        at_z = source(z, dz, sizes[1])
-        piece = slice(k * modes, (k + 1) * modes)
-        stack[rows_of(at_y * sizes[1] + at_z, modes), :] = own[piece, :]
-        stack[rows_of((at_y ^ 1) * sizes[1] + at_z, modes), :] = other[piece, :]
-    root_part = own[count * modes :, :] + other[count * modes :, :]
-    return dot3(region_rows[...], stack[...]) + dot3(root_map[...], root_part, COLS)
+        first = (at_y * sizes[1] + source(z, dz, sizes[1])) * modes
+        inside = jnp.logical_and(column >= k * modes, column < (k + 1) * modes)
+        wanted = jnp.where(inside, first + column - k * modes, wanted)
+    chosen = jnp.where(row == wanted, 1.0, 0.0).astype(BF16)
+    for at, whole in enumerate((packed, sibling)):
+        for level, piece in enumerate(split(whole[:modes, :])):
+            rows = slice((2 * level + at) * modes, (2 * level + at + 1) * modes)
+            factors[rows, :depth] = jnp.dot(piece, chosen, preferred_element_type=F32).astype(BF16)
+        for level, piece in enumerate(split(whole[modes:, :modes].T)):
+            rows = slice((2 * level + at) * modes, (2 * level + at + 1) * modes)
+            factors[rows, depth:] = piece
+
+
+def pair_kernel(modes, factors, first, *more):
+    received, (own, out, tall) = more[:-3], more[-3:]
+    total = first[modes:, :]
+    tall[:modes, :] = first[:modes, :]
+    for k, piece in enumerate(received, 1):
+        tall[k * modes : (k + 1) * modes, :] = piece[:modes, :]
+        total = total + piece[modes:, :]
+    tall[(len(received) + 1) * modes :, :] = total
+    high, low = split(tall[...])
+    both = jnp.dot(factors[...], high, preferred_element_type=F32)
+    fine = jnp.dot(factors[: 2 * modes, :], low, preferred_element_type=F32)
+    total = both[: 2 * modes, :] + (both[2 * modes :, :] + fine)
+    own[...] = total[:modes, :]
+    out[...] = total[modes:, :]
 
 
 def correction_factor(amplitude):
@@ -295,13 +325,11 @@
 
 
 def middle_kernel(
-    swaps, members, sizes, base, modes_t, root_map, region_rows, own, other, matrix_f, tail, modes_b, ahead_loads,
-    next_solution, placed, ready, ahead, *more
+    swaps, base, modes_t, own, other, matrix_f, tail, modes_b, ahead_loads,
+    next_solution, placed, ready, ahead, *messages
 ):
-    messages, (stack,) = more[: len(swaps)], more[len(swaps) :]
     height = placed.shape[0] // FACES
-    amplitude = amplitude_of(members, sizes, region_rows, root_map, own, other, stack)
-    tall = correction_factor(amplitude)
+    tall = correction_factor(own[...] + other[...])
     next_solution[...] = base[...] + jnp.dot(modes_t[...], tall, preferred_element_type=F32)
     local_iter = next_solution[...].astype(BF16)
     placed[...] = jnp.dot(matrix_f[...], local_iter, preferred_element_type=F32)
@@ -316,9 +344,8 @@
             message[height:, :] = ahead[...]
 
 
-def last_kernel(members, sizes, base, modes_t, root_map, region_rows, own, other, out, stack, result, sems):
-    amplitude = amplitude_of(members, sizes, region_rows, root_map, own, other, stack)
-    tall = correction_factor(amplitude)
+def last_kernel(base, modes_t, own, other, out, result, sems):
+    tall = correction_factor(own[...] + other[...])
     parts = sems.shape[0]
     part = result.shape[0] // parts
     copies = []
@@ -364,7 +391,6 @@
     ride = int(sizes[0] & (sizes[0] - 1) == 0)
     full = (pltpu.VMEM, (iface, cases), F32)
     places = [pltpu.SMEM((1, FACES), jnp.int32)]
-    stack = [pltpu.VMEM((region_rows.shape[1], cases), F32)]
     faces = [pltpu.VMEM((len(swaps) * height, cases), F32)]
 
     def wide(rows, dtype=BF16):
@@ -414,13 +440,13 @@
                 [
                     (pltpu.VMEM, (iface, 3 * mode_count), BF16),
                     (pltpu.VMEM, (iface, height), F32),
-                    (pltpu.VMEM, (2 * mode_count, len(swaps) * height), BF16),
+                    (pltpu.VMEM, (2 * mode_count + 2 * root_modes, len(swaps) * height), BF16),
                     wide(iface),
                     wide(2 * mode_count),
                     held(mode_count),
-                    held(mode_count),
+                    held(mode_count + root_modes),
                 ],
-                [order, matrix, modes, weights, target, placed],
+                [order, matrix, modes, root_map, weights, target, placed],
                 "constants",
                 [pltpu.VMEM((iface, iface), BF16)] + places + [pltpu.SemaphoreType.DMA],
                 1,
@@ -429,11 +455,24 @@
             coarse, root = call(
                 functools.partial(coarse_kernel, swaps, sizes),
                 [held(mode_count), held(root_modes)],
-                [ready, modes_f, root_map] + halos,
+                [ready, modes_f] + halos,
                 "coarse",
                 faces,
             )
             received = [along(root, offset) for offset in range(1, sizes[0])]
+            packed = call(
+                pack_kernel,
+                [(pltpu.VMEM, (mode_count + root_modes, region_rows.shape[1]), F32)],
+                [region_rows, root_map],
+                "pack",
+            )[0]
+            sibling = lax.ppermute(packed, AXES, swap_pairs(sizes, 1, 0))
+            (factors,) = call(
+                functools.partial(parts_kernel, members, sizes[1:]),
+                [(pltpu.VMEM, (4 * mode_count, len(members) * mode_count + root_modes), BF16)],
+                [packed, sibling],
+                "parts",
+            )
             base = base_of(solution, placed, halos)
             tail, ahead_loads = call(
                 functools.partial(links_kernel, swaps, sizes),
@@ -452,11 +491,10 @@
         else:
             extra = [3 * root_modes if ride and swap == (0, 0) else 0 for swap in swaps]
             solution, placed, ready, ahead, *messages = call(
-                functools.partial(middle_kernel, swaps, members, sizes[1:]),
+                functools.partial(middle_kernel, swaps),
                 [full, full, held(mode_count), held(3 * root_modes)] + [held(height + more) for more in extra],
-                [base, modes_t, root_map, region_rows, own, other, matrix_f, tail, modes_b, ahead_loads],
+                [base, modes_t, own, other, matrix_f, tail, modes_b, ahead_loads],
                 "update_product",
-                stack,
             )
             received = [along(ahead, offset) for offset in range(1 + ride, sizes[0])]
             halos = exchange(messages)
@@ -476,19 +514,20 @@
                 for z in range(sizes[2])
             ]
             pieces.append(lax.ppermute(message, ("gy", "gz"), moves))
-        (own,) = call(
+        own, given = call(
             functools.partial(pair_kernel, mode_count),
-            [held(len(members) * mode_count + root_modes)],
-            [message] + pieces,
-            "pair_message",
+            [held(mode_count), held(mode_count)],
+            [factors, message] + pieces,
+            "amplitude_parts",
+            [pltpu.VMEM((len(members) * mode_count + root_modes, cases), F32)],
         )
-        other = lax.ppermute(own, AXES, swap_pairs(sizes, 1, 0))
+        other = lax.ppermute(given, AXES, swap_pairs(sizes, 1, 0))
     (solution,) = call(
-        functools.partial(last_kernel, members, sizes[1:]),
+        last_kernel,
         [(jax.ShapeDtypeStruct, (iface, cases), F32)],
-        [base, modes_t, root_map, region_rows, own, other],
+        [base, modes_t, own, other],
         "update_last",
-        stack + [pltpu.VMEM((iface, cases), F32), pltpu.SemaphoreType.DMA((FACES,))],
+        [pltpu.VMEM((iface, cases), F32), pltpu.SemaphoreType.DMA((4,))],
     )
     return solution.reshape(1, 1, 1, iface, cases)
 

time: 52 us -> 51.5 us (level)
    ppermute x2 -> x3, waiting for transfers between devices: 1.37 us -> 1.05 us  [the longest x2 1.05 us: per_device(): other = lax.ppermute(given, AXES, swap_pairs(sizes, 1, 0))]
    pallas_call x12 -> x14, Pallas kernels: 10.6 us -> 10.3 us  [call(): pl.pallas_call(body, out_shape=[item(shape, dtype) for item, shape, dtype...]
  transfers between devices with their start and end apart: 23 -> 24, of which waited for: 15 -> 15; matrix products, arithmetic and copies ran while one was open for 0% -> 0% of each run, Pallas kernels for 8% -> 8%
where the time goes in v6:
time: 51.5 us; the launch traced here: 51.3 us
  starting transfers between devices  24.5 us (48%)
  waiting for transfers between devices  16.4 us (32%)
  Pallas kernels  10.3 us (20%)
    pallas_call x14, Pallas kernels, call(): pl.pallas_call(body, out_shape=[item(shape, dtype) for item, shape, dtype...  10.3 us
    ppermute x10, starting transfers between devices, exchange(): lax.ppermute(message, AXES, swap_pairs(sizes, dim, odd))  9.35 us
    ppermute x5, starting transfers between devices, along(): return lax.ppermute(value, AXES, pairs)  7.93 us
    ppermute x6, starting transfers between devices, per_device(): pieces.append(lax.ppermute(message, ('gy', 'gz'), moves))  7.05 us
    ppermute x6, waiting for transfers between devices, per_device(): pieces.append(lax.ppermute(message, ('gy', 'gz'), moves))  5.97 us
    ppermute x5, waiting for transfers between devices, along(): return lax.ppermute(value, AXES, pairs)  5.21 us
    ppermute x10, waiting for transfers between devices, exchange(): lax.ppermute(message, AXES, swap_pairs(sizes, dim, odd))  4.13 us
    ppermute x2, waiting for transfers between devices, per_device(): other = lax.ppermute(given, AXES, swap_pairs(sizes, 1, 0))  1.05 us
  transfers between devices with their start and end apart: 24, of which 15 were waited for; matrix products, arithmetic and copies ran while one was open for 0% of the time, Pallas kernels for 8%

profile of v6, /device:TPU:0, one launch (start us, length us, event | category | flops | bytes accessed | tf_op | source)
XLA Modules:
  0.0 51.3 jit_solution(2282743514726228911)
XLA Ops:
  0.0 2.7 %first_product.1 = (bf16[1024,1024]{1,0:T(8,128)(2,1)S(1)}, f32[32,1024]{1,0:T(8,128)S(1)}, f32[16,32]{1,0:T(8,128)S(1)}, f32[1024,256]{1,0:T(8,128)S(1)}, f32[1...) custom-call(s32[1,8]{1,0:T(1,128)} %bitcast.22, ...), custom_call_target="tpu_custom_call" | custom-call | tf_op jit(solution)/shard_map/first_product/pallas_call | solution.py:87
  3.2 2.6 %collective-permute-start.1 = (f32[136,256]{1,0:T(8,128)S(1)}, f32[136,256]{1,0:T(8,128)S(1)}, u32[]{:S(2)}, u32[]{:S(2)}) collective-permute-start(f32[136,256]{1,0:T(8,128)S(1)} %get-tuple-element.44), channel_id=1, source_target_pairs={{0,6},{1,7},{2,4},{3,5},{4,2},{5,3},{6,0},{7,1},{8,14},{9,15},{10,... | collective-permute-start | bytes 417800 | tf_op jit(solution)/shard_map/ppermute | solution.py:411
  5.9 2.2 %collective-permute-start.2 = (f32[136,256]{1,0:T(8,128)S(1)}, f32[136,256]{1,0:T(8,128)S(1)}, u32[]{:S(2)}, u32[]{:S(2)}) collective-permute-start(f32[136,256]{1,0:T(8,128)S(1)} %get-tuple-element.45), channel_id=1, source_target_pairs={{0,8},{1,9},{2,10},{3,11},{4,12},{5,13},{6,14},{7,15},{8,0},{9,1},... | collective-permute-start | bytes 417800 | tf_op jit(solution)/shard_map/ppermute | solution.py:411
  8.0 1.5 %collective-permute-start.3 = (f32[136,256]{1,0:T(8,128)S(1)}, f32[136,256]{1,0:T(8,128)S(1)}, u32[]{:S(2)}, u32[]{:S(2)}) collective-permute-start(f32[136,256]{1,0:T(8,128)S(1)} %get-tuple-element.46), channel_id=1, source_target_pairs={{0,1},{1,0},{2,3},{3,2},{4,5},{5,4},{6,7},{7,6},{8,9},{9,8},{10,11... | collective-permute-start | bytes 417800 | tf_op jit(solution)/shard_map/ppermute | solution.py:411
  10.0 2.6 %constants.1 = (bf16[1024,96]{1,0:T(8,128)(2,1)S(1)}, f32[1024,128]{1,0:T(8,128)S(1)}, bf16[96,640]{1,0:T(8,128)(2,1)S(1)}, bf16[1024,1024]{1,0:T(8,128)(2,1)S(1...) custom-call(s32[1,8]{1,0:T(1,128)} %bitcast.23, ...), custom_call_target="tpu_custom_call" | custom-call | tf_op jit(solution)/shard_map/constants/pallas_call | solution.py:87
  12.6 1.7 %collective-permute-done.3.more_3_ = f32[136,256]{1,0:T(8,128)S(1)} collective-permute-done((f32[136,256]{1,0:T(8,128)S(1)}, f32[136,256]{1,0:T(8,128)S(1)}, u32[]{:S(2)}, u32[]{:S(2)}) %collective-permute-start.3) | collective-permute-done | bytes 139296 | tf_op jit(solution)/shard_map/ppermute | solution.py:411
  14.6 1.4 %collective-permute-start.8 = (f32[16,256]{1,0:T(8,128)S(1)}, f32[16,256]{1,0:T(8,128)S(1)}, u32[]{:S(2)}, u32[]{:S(2)}) collective-permute-start(f32[16,256]{1,0:T(8,128)S(1)} %get-tuple-element.52.root), channel_id=1, source_target_pairs={{0,24},{1,25},{2,26},{3,27},{4,28},{5,29},{6,30},{7,31},{8,16},{9,... | collective-permute-start | bytes 49160 | tf_op jit(solution)/shard_map/ppermute | solution.py:407
  16.4 2.6 %collective-permute-start.6 = (f32[16,256]{1,0:T(8,128)S(1)}, f32[16,256]{1,0:T(8,128)S(1)}, u32[]{:S(2)}, u32[]{:S(2)}) collective-permute-start(f32[16,256]{1,0:T(8,128)S(1)} %get-tuple-element.52.root), channel_id=1, source_target_pairs={{0,8},{1,9},{2,10},{3,11},{4,12},{5,13},{6,14},{7,15},{8,0},{9,1},... | collective-permute-start | bytes 49160 | tf_op jit(solution)/shard_map/ppermute | solution.py:407
  19.1 1.1 %collective-permute-done.8.more_2_ = f32[16,256]{1,0:T(8,128)S(1)} collective-permute-done((f32[16,256]{1,0:T(8,128)S(1)}, f32[16,256]{1,0:T(8,128)S(1)}, u32[]{:S(2)}, u32[]{:S(2)}) %collective-permute-start.8) | collective-permute-done | bytes 16416 | tf_op jit(solution)/shard_map/ppermute | solution.py:407
  21.0 1.5 %collective-permute-start.11 = (f32[48,256]{1,0:T(8,128)S(1)}, f32[48,256]{1,0:T(8,128)S(1)}, u32[]{:S(2)}, u32[]{:S(2)}) collective-permute-start(f32[48,256]{1,0:T(8,128)S(1)} %root_part.1.first), channel_id=1, source_target_pairs={{0,5},{1,4},{2,7},{3,6},{4,1},{5,0},{6,3},{7,2},{8,13},{9,12},{10,... | collective-permute-start | bytes 147464 | tf_op jit(solution)/shard_map/ppermute | solution.py:516
  22.5 1.5 %collective-permute-start.10 = (f32[48,256]{1,0:T(8,128)S(1)}, f32[48,256]{1,0:T(8,128)S(1)}, u32[]{:S(2)}, u32[]{:S(2)}) collective-permute-start(f32[48,256]{1,0:T(8,128)S(1)} %root_part.1.first), channel_id=1, source_target_pairs={{0,4},{1,5},{2,6},{3,7},{4,0},{5,1},{6,2},{7,3},{8,12},{9,13},{10,... | collective-permute-start | bytes 147464 | tf_op jit(solution)/shard_map/ppermute | solution.py:516
  24.7 1.3 %collective-permute-done.11.more_2_ = f32[48,256]{1,0:T(8,128)S(1)} collective-permute-done((f32[48,256]{1,0:T(8,128)S(1)}, f32[48,256]{1,0:T(8,128)S(1)}, u32[]{:S(2)}, u32[]{:S(2)}) %collective-permute-start.11) | collective-permute-done | bytes 49184 | tf_op jit(solution)/shard_map/ppermute | solution.py:516
  26.6 1.5 %collective-permute-done.9.more_0_ = f32[48,256]{1,0:T(8,128)S(1)} collective-permute-done((f32[48,256]{1,0:T(8,128)S(1)}, f32[48,256]{1,0:T(8,128)S(1)}, u32[]{:S(2)}, u32[]{:S(2)}) %collective-permute-start.9) | collective-permute-done | bytes 49184 | tf_op jit(solution)/shard_map/ppermute | solution.py:516
  29.5 1.2 %update_product.1 = (f32[1024,256]{1,0:T(8,128)S(1)}, f32[1024,256]{1,0:T(8,128)S(1)}, f32[32,256]{1,0:T(8,128)S(1)}, f32[48,256]{1,0:T(8,128)S(1)}, f32[128,256...) custom-call(f32[1024,256]{1,0:T(8,128)S(1)} %base.2, ...), custom_call_target="tpu_custom_call" | custom-call | tf_op jit(solution)/shard_map/update_product/pallas_call | solution.py:87
  30.7 2.4 %collective-permute-start.19 = (f32[48,256]{1,0:T(8,128)S(1)}, f32[48,256]{1,0:T(8,128)S(1)}, u32[]{:S(2)}, u32[]{:S(2)}) collective-permute-start(f32[48,256]{1,0:T(8,128)S(1)} %get-tuple-element.68.ahead), channel_id=1, source_target_pairs={{0,24},{1,25},{2,26},{3,27},{4,28},{5,29},{6,30},{7,31},{8,16},{9,... | collective-permute-start | bytes 147464 | tf_op jit(solution)/shard_map/ppermute | solution.py:407
  33.1 1.1 %collective-permute-start.18 = (f32[48,256]{1,0:T(8,128)S(1)}, f32[48,256]{1,0:T(8,128)S(1)}, u32[]{:S(2)}, u32[]{:S(2)}) collective-permute-start(f32[48,256]{1,0:T(8,128)S(1)} %get-tuple-element.68.ahead), channel_id=1, source_target_pairs={{0,16},{1,17},{2,18},{3,19},{4,20},{5,21},{6,22},{7,23},{8,24},{9,... | collective-permute-start | bytes 147464 | tf_op jit(solution)/shard_map/ppermute | solution.py:407
  35.8 1.4 %collective-permute-done.19.more_6_ = f32[48,256]{1,0:T(8,128)S(1)} collective-permute-done((f32[48,256]{1,0:T(8,128)S(1)}, f32[48,256]{1,0:T(8,128)S(1)}, u32[]{:S(2)}, u32[]{:S(2)}) %collective-permute-start.19) | collective-permute-done | bytes 49184 | tf_op jit(solution)/shard_map/ppermute | solution.py:407
  37.8 2.0 %collective-permute-done.18.more_5_ = f32[48,256]{1,0:T(8,128)S(1)} collective-permute-done((f32[48,256]{1,0:T(8,128)S(1)}, f32[48,256]{1,0:T(8,128)S(1)}, u32[]{:S(2)}, u32[]{:S(2)}) %collective-permute-start.18) | collective-permute-done | bytes 49184 | tf_op jit(solution)/shard_map/ppermute | solution.py:407
  40.4 1.9 %collective-permute-done.16.more_3_ = f32[128,256]{1,0:T(8,128)S(1)} collective-permute-done((f32[128,256]{1,0:T(8,128)S(1)}, f32[128,256]{1,0:T(8,128)S(1)}, u32[]{:S(2)}, u32[]{:S(2)}) %collective-permute-start.16) | collective-permute-done | bytes 131104 | tf_op jit(solution)/shard_map/ppermute | solution.py:411
  43.1 1.5 %collective-permute-start.21 = (f32[48,256]{1,0:T(8,128)S(1)}, f32[48,256]{1,0:T(8,128)S(1)}, u32[]{:S(2)}, u32[]{:S(2)}) collective-permute-start(f32[48,256]{1,0:T(8,128)S(1)} %coarse_root.1.first), channel_id=1, source_target_pairs={{0,4},{1,5},{2,6},{3,7},{4,0},{5,1},{6,2},{7,3},{8,12},{9,13},{10,... | collective-permute-start | bytes 147464 | tf_op jit(solution)/shard_map/ppermute | solution.py:516
  44.6 1.5 %collective-permute-start.20 = (f32[48,256]{1,0:T(8,128)S(1)}, f32[48,256]{1,0:T(8,128)S(1)}, u32[]{:S(2)}, u32[]{:S(2)}) collective-permute-start(f32[48,256]{1,0:T(8,128)S(1)} %coarse_root.1.first), channel_id=1, source_target_pairs={{0,1},{1,0},{2,3},{3,2},{4,5},{5,4},{6,7},{7,6},{8,9},{9,8},{10,11... | collective-permute-start | bytes 147464 | tf_op jit(solution)/shard_map/ppermute | solution.py:516
  46.1 1.5 %collective-permute-done.22.more_2_ = f32[48,256]{1,0:T(8,128)S(1)} collective-permute-done((f32[48,256]{1,0:T(8,128)S(1)}, f32[48,256]{1,0:T(8,128)S(1)}, u32[]{:S(2)}, u32[]{:S(2)}) %collective-permute-start.22) | collective-permute-done | bytes 49184 | tf_op jit(solution)/shard_map/ppermute | solution.py:516
  47.6 1.1 %collective-permute-done.20.more_0_ = f32[48,256]{1,0:T(8,128)S(1)} collective-permute-done((f32[48,256]{1,0:T(8,128)S(1)}, f32[48,256]{1,0:T(8,128)S(1)}, u32[]{:S(2)}, u32[]{:S(2)}) %collective-permute-start.20) | collective-permute-done | bytes 49184 | tf_op jit(solution)/shard_map/ppermute | solution.py:516
  50.1 1.2 %update_last.1 = f32[1024,256]{1,0:T(8,128)} custom-call(f32[1024,256]{1,0:T(8,128)S(1)} %base.3, bf16[1024,96]{1,0:T(8,128)(2,1)S(1)} %get-tuple-element.48.modes_t, f32[32,256]{1,0:T(8,128)S(1)} %get-tuple-element.69.own, f32[32,256]{1,0:T(8,128)S(1)} %collective-permute-done.23.other), custom_call_target="tpu_custom_call" | custom-call | tf_op jit(solution)/shard_map/update_last/pallas_call | solution.py:87
  (48 shorter events, 10.1 us)
Async XLA Ops:
  2.7 9.8 %collective-permute-start = (f32[136,256]{1,0:T(8,128)S(1)}, f32[136,256]{1,0:T(8,128)S(1)}, u32[]{:S(2)}, u32[]{:S(2)}) collective-permute-start(f32[136,256]{1,0:T(8,128)S(1)} %get-tuple-element.43), channel_id=1, source_target_pairs={{0,2},{1,3},{2,0},{3,1},{4,6},{5,7},{6,4},{7,5},{8,16},{9,17},{10,... | collective-permute-start | bytes 417800 | tf_op jit(solution)/shard_map/ppermute | solution.py:411
  3.2 9.3 %collective-permute-start.1 = (f32[136,256]{1,0:T(8,128)S(1)}, f32[136,256]{1,0:T(8,128)S(1)}, u32[]{:S(2)}, u32[]{:S(2)}) collective-permute-start(f32[136,256]{1,0:T(8,128)S(1)} %get-tuple-element.44), channel_id=1, source_target_pairs={{0,6},{1,7},{2,4},{3,5},{4,2},{5,3},{6,0},{7,1},{8,14},{9,15},{10,... | collective-permute-start | bytes 417800 | tf_op jit(solution)/shard_map/ppermute | solution.py:411
  5.9 6.7 %collective-permute-start.2 = (f32[136,256]{1,0:T(8,128)S(1)}, f32[136,256]{1,0:T(8,128)S(1)}, u32[]{:S(2)}, u32[]{:S(2)}) collective-permute-start(f32[136,256]{1,0:T(8,128)S(1)} %get-tuple-element.45), channel_id=1, source_target_pairs={{0,8},{1,9},{2,10},{3,11},{4,12},{5,13},{6,14},{7,15},{8,0},{9,1},... | collective-permute-start | bytes 417800 | tf_op jit(solution)/shard_map/ppermute | solution.py:411
  8.0 6.3 %collective-permute-start.3 = (f32[136,256]{1,0:T(8,128)S(1)}, f32[136,256]{1,0:T(8,128)S(1)}, u32[]{:S(2)}, u32[]{:S(2)}) collective-permute-start(f32[136,256]{1,0:T(8,128)S(1)} %get-tuple-element.46), channel_id=1, source_target_pairs={{0,1},{1,0},{2,3},{3,2},{4,5},{5,4},{6,7},{7,6},{8,9},{9,8},{10,11... | collective-permute-start | bytes 417800 | tf_op jit(solution)/shard_map/ppermute | solution.py:411
  9.6 4.7 %collective-permute-start.4 = (f32[136,256]{1,0:T(8,128)S(1)}, f32[136,256]{1,0:T(8,128)S(1)}, u32[]{:S(2)}, u32[]{:S(2)}) collective-permute-start(f32[136,256]{1,0:T(8,128)S(1)} %get-tuple-element.47), channel_id=1, source_target_pairs={{0,2},{1,3},{2,0},{3,1},{4,6},{5,7},{6,4},{7,5},{8,10},{9,11},{10,... | collective-permute-start | bytes 417800 | tf_op jit(solution)/shard_map/ppermute | solution.py:411
  14.6 5.6 %collective-permute-start.8 = (f32[16,256]{1,0:T(8,128)S(1)}, f32[16,256]{1,0:T(8,128)S(1)}, u32[]{:S(2)}, u32[]{:S(2)}) collective-permute-start(f32[16,256]{1,0:T(8,128)S(1)} %get-tuple-element.52.root), channel_id=1, source_target_pairs={{0,24},{1,25},{2,26},{3,27},{4,28},{5,29},{6,30},{7,31},{8,16},{9,... | collective-permute-start | bytes 49160 | tf_op jit(solution)/shard_map/ppermute | solution.py:407
  16.0 4.7 %collective-permute-start.7 = (f32[16,256]{1,0:T(8,128)S(1)}, f32[16,256]{1,0:T(8,128)S(1)}, u32[]{:S(2)}, u32[]{:S(2)}) collective-permute-start(f32[16,256]{1,0:T(8,128)S(1)} %get-tuple-element.52.root), channel_id=1, source_target_pairs={{0,16},{1,17},{2,18},{3,19},{4,20},{5,21},{6,22},{7,23},{8,24},{9,... | collective-permute-start | bytes 49160 | tf_op jit(solution)/shard_map/ppermute | solution.py:407
  16.4 4.5 %collective-permute-start.6 = (f32[16,256]{1,0:T(8,128)S(1)}, f32[16,256]{1,0:T(8,128)S(1)}, u32[]{:S(2)}, u32[]{:S(2)}) collective-permute-start(f32[16,256]{1,0:T(8,128)S(1)} %get-tuple-element.52.root), channel_id=1, source_target_pairs={{0,8},{1,9},{2,10},{3,11},{4,12},{5,13},{6,14},{7,15},{8,0},{9,1},... | collective-permute-start | bytes 49160 | tf_op jit(solution)/shard_map/ppermute | solution.py:407
  19.1 5.4 %collective-permute-start.5 = (f32[48,256]{1,0:T(8,128)S(1)}, f32[48,256]{1,0:T(8,128)S(1)}, u32[]{:S(2)}, u32[]{:S(2)}) collective-permute-start(f32[48,256]{1,0:T(8,128)S(1)} %pack.1.packed), channel_id=1, source_target_pairs={{0,2},{1,3},{2,0},{3,1},{4,6},{5,7},{6,4},{7,5},{8,10},{9,11},{10,... | collective-permute-start | bytes 147464 | tf_op jit(solution)/shard_map/ppermute | solution.py:469
  21.0 5.0 %collective-permute-start.11 = (f32[48,256]{1,0:T(8,128)S(1)}, f32[48,256]{1,0:T(8,128)S(1)}, u32[]{:S(2)}, u32[]{:S(2)}) collective-permute-start(f32[48,256]{1,0:T(8,128)S(1)} %root_part.1.first), channel_id=1, source_target_pairs={{0,5},{1,4},{2,7},{3,6},{4,1},{5,0},{6,3},{7,2},{8,13},{9,12},{10,... | collective-permute-start | bytes 147464 | tf_op jit(solution)/shard_map/ppermute | solution.py:516
  22.5 4.1 %collective-permute-start.10 = (f32[48,256]{1,0:T(8,128)S(1)}, f32[48,256]{1,0:T(8,128)S(1)}, u32[]{:S(2)}, u32[]{:S(2)}) collective-permute-start(f32[48,256]{1,0:T(8,128)S(1)} %root_part.1.first), channel_id=1, source_target_pairs={{0,4},{1,5},{2,6},{3,7},{4,0},{5,1},{6,2},{7,3},{8,12},{9,13},{10,... | collective-permute-start | bytes 147464 | tf_op jit(solution)/shard_map/ppermute | solution.py:516
  24.0 4.1 %collective-permute-start.9 = (f32[48,256]{1,0:T(8,128)S(1)}, f32[48,256]{1,0:T(8,128)S(1)}, u32[]{:S(2)}, u32[]{:S(2)}) collective-permute-start(f32[48,256]{1,0:T(8,128)S(1)} %root_part.1.first), channel_id=1, source_target_pairs={{0,1},{1,0},{2,3},{3,2},{4,5},{5,4},{6,7},{7,6},{8,9},{9,8},{10,11... | collective-permute-start | bytes 147464 | tf_op jit(solution)/shard_map/ppermute | solution.py:516
  28.3 1.3 %collective-permute-start.12 = (f32[32,256]{1,0:T(8,128)S(1)}, f32[32,256]{1,0:T(8,128)S(1)}, u32[]{:S(2)}, u32[]{:S(2)}) collective-permute-start(f32[32,256]{1,0:T(8,128)S(1)} %get-tuple-element.54), channel_id=1, source_target_pairs={{0,2},{1,3},{2,0},{3,1},{4,6},{5,7},{6,4},{7,5},{8,10},{9,11},{10,... | collective-permute-start | bytes 98312 | tf_op jit(solution)/shard_map/ppermute | solution.py:524
  30.7 6.5 %collective-permute-start.19 = (f32[48,256]{1,0:T(8,128)S(1)}, f32[48,256]{1,0:T(8,128)S(1)}, u32[]{:S(2)}, u32[]{:S(2)}) collective-permute-start(f32[48,256]{1,0:T(8,128)S(1)} %get-tuple-element.68.ahead), channel_id=1, source_target_pairs={{0,24},{1,25},{2,26},{3,27},{4,28},{5,29},{6,30},{7,31},{8,16},{9,... | collective-permute-start | bytes 147464 | tf_op jit(solution)/shard_map/ppermute | solution.py:407
  33.1 6.7 %collective-permute-start.18 = (f32[48,256]{1,0:T(8,128)S(1)}, f32[48,256]{1,0:T(8,128)S(1)}, u32[]{:S(2)}, u32[]{:S(2)}) collective-permute-start(f32[48,256]{1,0:T(8,128)S(1)} %get-tuple-element.68.ahead), channel_id=1, source_target_pairs={{0,16},{1,17},{2,18},{3,19},{4,20},{5,21},{6,22},{7,23},{8,24},{9,... | collective-permute-start | bytes 147464 | tf_op jit(solution)/shard_map/ppermute | solution.py:407
  34.2 8.0 %collective-permute-start.15 = (f32[176,256]{1,0:T(8,128)S(1)}, f32[176,256]{1,0:T(8,128)S(1)}, u32[]{:S(2)}, u32[]{:S(2)}) collective-permute-start(f32[176,256]{1,0:T(8,128)S(1)} %get-tuple-element.64), channel_id=1, source_target_pairs={{0,8},{1,9},{2,10},{3,11},{4,12},{5,13},{6,14},{7,15},{8,0},{9,1},... | collective-permute-start | bytes 540680 | tf_op jit(solution)/shard_map/ppermute | solution.py:411
  35.2 4.6 %collective-permute-start.13 = (f32[128,256]{1,0:T(8,128)S(1)}, f32[128,256]{1,0:T(8,128)S(1)}, u32[]{:S(2)}, u32[]{:S(2)}) collective-permute-start(f32[128,256]{1,0:T(8,128)S(1)} %get-tuple-element.62), channel_id=1, source_target_pairs={{0,2},{1,3},{2,0},{3,1},{4,6},{5,7},{6,4},{7,5},{8,16},{9,17},{10,... | collective-permute-start | bytes 393224 | tf_op jit(solution)/shard_map/ppermute | solution.py:411
  35.2 5.2 %collective-permute-start.14 = (f32[128,256]{1,0:T(8,128)S(1)}, f32[128,256]{1,0:T(8,128)S(1)}, u32[]{:S(2)}, u32[]{:S(2)}) collective-permute-start(f32[128,256]{1,0:T(8,128)S(1)} %get-tuple-element.63), channel_id=1, source_target_pairs={{0,6},{1,7},{2,4},{3,5},{4,2},{5,3},{6,0},{7,1},{8,14},{9,15},{10,... | collective-permute-start | bytes 393224 | tf_op jit(solution)/shard_map/ppermute | solution.py:411
  37.3 5.0 %collective-permute-start.16 = (f32[128,256]{1,0:T(8,128)S(1)}, f32[128,256]{1,0:T(8,128)S(1)}, u32[]{:S(2)}, u32[]{:S(2)}) collective-permute-start(f32[128,256]{1,0:T(8,128)S(1)} %get-tuple-element.65), channel_id=1, source_target_pairs={{0,1},{1,0},{2,3},{3,2},{4,5},{5,4},{6,7},{7,6},{8,9},{9,8},{10,11... | collective-permute-start | bytes 393224 | tf_op jit(solution)/shard_map/ppermute | solution.py:411
  39.8 2.4 %collective-permute-start.17 = (f32[128,256]{1,0:T(8,128)S(1)}, f32[128,256]{1,0:T(8,128)S(1)}, u32[]{:S(2)}, u32[]{:S(2)}) collective-permute-start(f32[128,256]{1,0:T(8,128)S(1)} %get-tuple-element.66), channel_id=1, source_target_pairs={{0,2},{1,3},{2,0},{3,1},{4,6},{5,7},{6,4},{7,5},{8,10},{9,11},{10,... | collective-permute-start | bytes 393224 | tf_op jit(solution)/shard_map/ppermute | solution.py:411
  42.5 5.1 %collective-permute-start.22 = (f32[48,256]{1,0:T(8,128)S(1)}, f32[48,256]{1,0:T(8,128)S(1)}, u32[]{:S(2)}, u32[]{:S(2)}) collective-permute-start(f32[48,256]{1,0:T(8,128)S(1)} %coarse_root.1.first), channel_id=1, source_target_pairs={{0,5},{1,4},{2,7},{3,6},{4,1},{5,0},{6,3},{7,2},{8,13},{9,12},{10,... | collective-permute-start | bytes 147464 | tf_op jit(solution)/shard_map/ppermute | solution.py:516
  43.1 4.5 %collective-permute-start.21 = (f32[48,256]{1,0:T(8,128)S(1)}, f32[48,256]{1,0:T(8,128)S(1)}, u32[]{:S(2)}, u32[]{:S(2)}) collective-permute-start(f32[48,256]{1,0:T(8,128)S(1)} %coarse_root.1.first), channel_id=1, source_target_pairs={{0,4},{1,5},{2,6},{3,7},{4,0},{5,1},{6,2},{7,3},{8,12},{9,13},{10,... | collective-permute-start | bytes 147464 | tf_op jit(solution)/shard_map/ppermute | solution.py:516
  44.6 4.1 %collective-permute-start.20 = (f32[48,256]{1,0:T(8,128)S(1)}, f32[48,256]{1,0:T(8,128)S(1)}, u32[]{:S(2)}, u32[]{:S(2)}) collective-permute-start(f32[48,256]{1,0:T(8,128)S(1)} %coarse_root.1.first), channel_id=1, source_target_pairs={{0,1},{1,0},{2,3},{3,2},{4,5},{5,4},{6,7},{7,6},{8,9},{9,8},{10,11... | collective-permute-start | bytes 147464 | tf_op jit(solution)/shard_map/ppermute | solution.py:516
  48.8 1.3 %collective-permute-start.23 = (f32[32,256]{1,0:T(8,128)S(1)}, f32[32,256]{1,0:T(8,128)S(1)}, u32[]{:S(2)}, u32[]{:S(2)}) collective-permute-start(f32[32,256]{1,0:T(8,128)S(1)} %get-tuple-element.70), channel_id=1, source_target_pairs={{0,2},{1,3},{2,0},{3,1},{4,6},{5,7},{6,4},{7,5},{8,10},{9,11},{10,... | collective-permute-start | bytes 98312 | tf_op jit(solution)/shard_map/ppermute | solution.py:524
  (5 other events, 58.3 us)

commit v7 on v6

--- a/solution.py
+++ b/solution.py
@@ -23,7 +23,7 @@
 
 
 def swap_list(sizes):
-    swaps = [(dim, odd) for odd in (1, 0) for dim in (0, 1, 2) if sizes[dim] > 1 + odd]
+    swaps = [(dim, odd) for odd in (1, 0) for dim in (1, 0, 2) if sizes[dim] > 1 + odd]
     return sorted(swaps, key=lambda swap: swap == (1, 0))
 
 
@@ -70,6 +70,20 @@
     return index ^ offset
 
 
+def nearest(count):
+    return int(count & (count - 1) == 0)
+
+
+def far_offsets(count, near):
+    offsets = list(range(near, count))
+    paired = list(zip(offsets[0::2], offsets[1::2]))
+    return paired, offsets[2 * len(paired) :]
+
+
+def core_offset(pair):
+    return jnp.where(lax.axis_index("gy") % 2 == 0, pair[0], pair[1])
+
+
 def split(value):
     high = value.astype(BF16)
     return high, (value - high.astype(F32)).astype(BF16)
@@ -108,9 +122,11 @@
         message[:height, :] = placed[rows_of(swap_face(dim, odd), height), :]
 
 
-def first_kernel(swaps, order_hbm, start_hbm, matrix_hbm, modes_hbm, root_hbm, matrix, modes, root_map, placed, *more):
+def first_kernel(swaps, order_hbm, start_hbm, *refs):
+    hbm, held, (placed, *more) = refs[:4], refs[4:8], refs[8:]
+    matrix, modes, root_map, region_rows = held
     messages, (order, start, local_iter, mapped, sems) = more[: len(swaps)], more[len(swaps) :]
-    pairs = [(order_hbm, order), (start_hbm, start), (matrix_hbm, matrix), (modes_hbm, modes), (root_hbm, root_map)]
+    pairs = [(order_hbm, order), (start_hbm, start)] + list(zip(hbm, held))
     copies = [pltpu.make_async_copy(*pair, sems.at[k]) for k, pair in enumerate(pairs)]
     for copy in copies:
         copy.start()
@@ -124,9 +140,18 @@
     mapped[...] = dot3(root_map[...], modes[...])
     for (dim, odd), message in zip(swaps, messages):
         link = mapped[:, rows_of(swap_face(dim, odd), height)]
-        extra = message.shape[0] - height
+        extra = link.shape[0] * height // lanes
+        end = height + extra
         for k in range(lanes // height):
-            message[height:, k * height : (k + 1) * height] = link[k * extra : (k + 1) * extra, :]
+            message[height:end, k * height : (k + 1) * height] = link[k * extra : (k + 1) * extra, :]
+        if (dim, odd) == (1, 0):
+            copies[5].wait()
+            rows = region_rows.shape[0]
+            message[end:, :] = jnp.zeros_like(message[end:, :])
+            message[end : end + root_map.shape[0], :rows] = root_map[...]
+            end += root_map.shape[0]
+            for k in range(region_rows.shape[1] // lanes):
+                message[end + k * rows : end + (k + 1) * rows, :] = region_rows[:, k * lanes : (k + 1) * lanes]
     copies[2].wait()
     product = jnp.dot(matrix[...], local_iter[...], preferred_element_type=F32)
     for j in range(FACES):
@@ -218,8 +243,8 @@
     for (dim, odd), halo in zip(swaps, halos):
         face = swap_face(dim, odd)
         known = has_neighbour(dim, face, sizes)
-        extra = halo.shape[0] - height
-        pieces = [halo[height:, k * height : (k + 1) * height] for k in range(lanes // height)]
+        end = height + count * height // lanes
+        pieces = [halo[height:end, k * height : (k + 1) * height] for k in range(lanes // height)]
         link = jnp.where(known, jnp.concatenate(pieces, axis=0), 0.0)
         if dim == 0:
             ahead[rows_of(2 * face, count), rows_of(face, height)] = link
@@ -253,7 +278,8 @@
     for (dim, odd), halo in zip(swaps, halos):
         if ride and (dim, odd) == (0, 0):
             pieces.append((me ^ 1, halo.at[height:, :]))
-    for offset, piece in zip(range(1 + ride, sizes[0]), received):
+    paired, single = far_offsets(sizes[0], 1 + ride)
+    for offset, piece in zip([core_offset(pair) for pair in paired] + single, received):
         pieces.append((source(me, offset, sizes[0]), piece))
     for index, piece in pieces:
         rows = pl.ds(pl.multiple_of(index * count, count), 3 * count)
@@ -261,27 +287,31 @@
     message[modes:, :] = dot3(root_inverse[...], stack[count:-count, :])
 
 
+def sum_kernel(own, other, total):
+    total[...] = own[...] + other[other.shape[0] - own.shape[0] :, :]
+
+
 def root_kernel(count, coarse, root_inverse, root, *more):
-    received, (message, stack) = more[: count - 1], more[count - 1 :]
+    received, (message, stack) = more[:-2], more[-2:]
     modes, height = coarse.shape[0], root.shape[0]
     me = lax.axis_index("gx")
+    paired, single = far_offsets(count, 1 + nearest(count))
+    offsets = [core_offset(pair) for pair in paired] + list(range(1, 1 + nearest(count))) + single
+    stack[...] = jnp.zeros_like(stack)
     stack[rows_of(me, height), :] = root[...]
-    for offset, piece in enumerate(received, 1):
+    for offset, piece in zip(offsets, received):
         stack[rows_of(source(me, offset, count), height), :] = piece[...]
     message[:modes, :] = coarse[...]
     message[modes:, :] = dot3(root_inverse[...], stack[...])
 
 
-def pack_kernel(region_rows, root_map, packed):
-    modes, width = region_rows.shape[0], root_map.shape[1]
-    packed[...] = jnp.zeros_like(packed)
-    packed[:modes, :] = region_rows[...]
-    packed[modes:, :width] = root_map[...]
-
-
-def parts_kernel(members, sizes, packed, sibling, factors):
-    modes, order = factors.shape[0] // 4, packed.shape[1]
-    count = packed.shape[0] - modes
+def parts_kernel(members, sizes, region_rows, root_map, halo, factors):
+    modes, order = region_rows.shape
+    count, lanes = root_map.shape[0], halo.shape[1]
+    blocks = order // lanes
+    at = halo.shape[0] - blocks * modes
+    other_rows = jnp.concatenate([halo[at + k * modes : at + (k + 1) * modes, :] for k in range(blocks)], axis=1)
+    other_map = halo[at - count : at, :modes]
     y, z = lax.axis_index("gy"), lax.axis_index("gz")
     half = sizes[0] // 2
     depth = len(members) * modes
@@ -294,11 +324,11 @@
         inside = jnp.logical_and(column >= k * modes, column < (k + 1) * modes)
         wanted = jnp.where(inside, first + column - k * modes, wanted)
     chosen = jnp.where(row == wanted, 1.0, 0.0).astype(BF16)
-    for at, whole in enumerate((packed, sibling)):
-        for level, piece in enumerate(split(whole[:modes, :])):
+    for at, (whole, maps) in enumerate(((region_rows[...], root_map[...]), (other_rows, other_map))):
+        for level, piece in enumerate(split(whole)):
             rows = slice((2 * level + at) * modes, (2 * level + at + 1) * modes)
             factors[rows, :depth] = jnp.dot(piece, chosen, preferred_element_type=F32).astype(BF16)
-        for level, piece in enumerate(split(whole[modes:, :modes].T)):
+        for level, piece in enumerate(split(maps.T)):
             rows = slice((2 * level + at) * modes, (2 * level + at + 1) * modes)
             factors[rows, depth:] = piece
 
@@ -388,7 +418,9 @@
     half = sizes[1] // 2
     members = list(itertools.product(range(half), range(sizes[2])))
 
-    ride = int(sizes[0] & (sizes[0] - 1) == 0)
+    ride = nearest(sizes[0])
+    paired, single = far_offsets(sizes[0], 1 + ride)
+    core = swaps.index((1, 0))
     full = (pltpu.VMEM, (iface, cases), F32)
     places = [pltpu.SMEM((1, FACES), jnp.int32)]
     faces = [pltpu.VMEM((len(swaps) * height, cases), F32)]
@@ -402,15 +434,20 @@
     def along(value, offset):
         pairs = []
         for place in itertools.product(*map(range, sizes)):
-            there = (partner(place[0], offset, sizes[0]),) + place[1:]
+            step = offset if isinstance(offset, int) else offset[place[1] % 2]
+            there = (partner(place[0], step, sizes[0]),) + place[1:]
             pairs.append((flat(sizes, place), flat(sizes, there)))
         return lax.ppermute(value, AXES, pairs)
 
-    def exchange(messages):
-        return [
-            lax.ppermute(message, AXES, swap_pairs(sizes, dim, odd))
-            for (dim, odd), message in zip(swaps, messages)
-        ]
+    def exchange(messages, order):
+        moved = {}
+        for dim, odd in order:
+            message = messages[swaps.index((dim, odd))]
+            moved[dim, odd] = lax.ppermute(message, AXES, swap_pairs(sizes, dim, odd))
+        return [moved[swap] for swap in swaps]
+
+    def core_sum(own, other):
+        return call(sum_kernel, [held(own.shape[0])], [own, other], "core_sum")[0]
 
     def base_of(solution, placed, halos):
         return call(
@@ -422,17 +459,19 @@
 
     for step in range(ITERS):
         if step == 0:
-            inputs = [order, solution, matrix, modes, root_map]
-            matrix, modes, root_map, placed, *messages = call(
+            inputs = [order, solution, matrix, modes, root_map, region_rows]
+            rows = [height + root_modes * height // cases] * len(swaps)
+            rows[core] += root_modes + mode_count * (region_rows.shape[1] // cases)
+            matrix, modes, root_map, region_rows, placed, *messages = call(
                 functools.partial(first_kernel, swaps),
                 [(pltpu.VMEM, item.shape, item.dtype) for item in inputs[2:]]
                 + [full]
-                + [held(height + root_modes * height // cases)] * len(swaps),
+                + [held(count) for count in rows],
                 inputs,
                 "first_product",
                 places
                 + [pltpu.VMEM((iface, cases), BF16)] * 2
-                + [pltpu.VMEM((root_modes, iface), F32), pltpu.SemaphoreType.DMA((5,))],
+                + [pltpu.VMEM((root_modes, iface), F32), pltpu.SemaphoreType.DMA((6,))],
                 len(inputs),
             )
             modes_t, scale, modes_f, matrix_f, modes_a, modes_b, ready = call(
@@ -451,7 +490,7 @@
                 [pltpu.VMEM((iface, iface), BF16)] + places + [pltpu.SemaphoreType.DMA],
                 1,
             )
-            halos = exchange(messages)
+            halos = exchange(messages, swaps)
             coarse, root = call(
                 functools.partial(coarse_kernel, swaps, sizes),
                 [held(mode_count), held(root_modes)],
@@ -459,18 +498,13 @@
                 "coarse",
                 faces,
             )
-            received = [along(root, offset) for offset in range(1, sizes[0])]
-            packed = call(
-                pack_kernel,
-                [(pltpu.VMEM, (mode_count + root_modes, region_rows.shape[1]), F32)],
-                [region_rows, root_map],
-                "pack",
-            )[0]
-            sibling = lax.ppermute(packed, AXES, swap_pairs(sizes, 1, 0))
+            both = core_sum(root, lax.ppermute(root, AXES, swap_pairs(sizes, 1, 0)))
+            received = [along(root, offset) for offset in list(range(1, 1 + ride)) + single]
+            received = [along(both, pair) for pair in paired] + received
             (factors,) = call(
                 functools.partial(parts_kernel, members, sizes[1:]),
                 [(pltpu.VMEM, (4 * mode_count, len(members) * mode_count + root_modes), BF16)],
-                [packed, sibling],
+                [region_rows, root_map, halos[core]],
                 "parts",
             )
             base = base_of(solution, placed, halos)
@@ -489,15 +523,16 @@
                 [pltpu.VMEM((root_inverse.shape[1], cases), F32)],
             )
         else:
-            extra = [3 * root_modes if ride and swap == (0, 0) else 0 for swap in swaps]
+            extra = [3 * root_modes * int(swap == (1, 0) or (ride and swap == (0, 0))) for swap in swaps]
             solution, placed, ready, ahead, *messages = call(
                 functools.partial(middle_kernel, swaps),
                 [full, full, held(mode_count), held(3 * root_modes)] + [held(height + more) for more in extra],
                 [base, modes_t, own, other, matrix_f, tail, modes_b, ahead_loads],
                 "update_product",
             )
-            received = [along(ahead, offset) for offset in range(1 + ride, sizes[0])]
-            halos = exchange(messages)
+            halos = exchange(messages, sorted(swaps, key=lambda swap: (swap != (1, 0), swap[0] == 1, swap)))
+            both = core_sum(ahead, halos[core])
+            received = [along(both, pair) for pair in paired] + [along(ahead, offset) for offset in single]
             (message,) = call(
                 functools.partial(merged_kernel, swaps, sizes, ride),
                 [held(mode_count + root_modes)],

time: 51.5 us -> 49.5 us (0.961)
  starting transfers between devices: 24.5 us -> 21.7 us
  waiting for transfers between devices: 16.4 us -> 17.1 us
    ppermute x5 -> x3, starting transfers between devices: 7.93 us -> 4.02 us  [along(): return lax.ppermute(value, AXES, pairs)]
    ppermute x11, starting transfers between devices: 9.41 us -> 10.4 us  [the longest x10 10.4 us: exchange(): moved[dim, odd] = lax.ppermute(message, AXES, swap_pairs(sizes, dim, odd))]
    ppermute x5 -> x3, waiting for transfers between devices: 5.21 us -> 5.48 us  [along(): return lax.ppermute(value, AXES, pairs)]
    pallas_call x14 -> x15, Pallas kernels: 10.3 us -> 10.4 us  [call(): pl.pallas_call(body, out_shape=[item(shape, dtype) for item, shape, dtype...]
  transfers between devices with their start and end apart: 24 -> 22, of which waited for: 15 -> 15; matrix products, arithmetic and copies ran while one was open for 0% -> 0% of each run, Pallas kernels for 8% -> 9%
where the time goes in v7:
time: 49.5 us; the launch traced here: 49.3 us
  starting transfers between devices  21.7 us (44%)
  waiting for transfers between devices  17.1 us (35%)
  Pallas kernels  10.4 us (21%)
    pallas_call x15, Pallas kernels, call(): pl.pallas_call(body, out_shape=[item(shape, dtype) for item, shape, dtype...  10.4 us
    ppermute x10, starting transfers between devices, exchange(): moved[dim, odd] = lax.ppermute(message, AXES, swap_pairs(sizes, dim, odd))  10.4 us
    ppermute x6, starting transfers between devices, per_device(): pieces.append(lax.ppermute(message, ('gy', 'gz'), moves))  7.05 us
    ppermute x6, waiting for transfers between devices, per_device(): pieces.append(lax.ppermute(message, ('gy', 'gz'), moves))  5.99 us
    ppermute x3, waiting for transfers between devices, along(): return lax.ppermute(value, AXES, pairs)  5.48 us
    ppermute x3, starting transfers between devices, along(): return lax.ppermute(value, AXES, pairs)  4.02 us
    ppermute x10, waiting for transfers between devices, exchange(): moved[dim, odd] = lax.ppermute(message, AXES, swap_pairs(sizes, dim, odd))  3.69 us
    ppermute x2, waiting for transfers between devices, per_device(): other = lax.ppermute(given, AXES, swap_pairs(sizes, 1, 0))  1.08 us
  transfers between devices with their start and end apart: 22, of which 15 were waited for; matrix products, arithmetic and copies ran while one was open for 0% of the time, Pallas kernels for 9%

profile of v7, /device:TPU:0, one launch (start us, length us, event | category | flops | bytes accessed | tf_op | source)
XLA Modules:
  0.0 49.3 jit_solution(3724060856696616707)
XLA Ops:
  0.0 2.7 %first_product.1 = (bf16[1024,1024]{1,0:T(8,128)(2,1)S(1)}, f32[32,1024]{1,0:T(8,128)S(1)}, f32[16,32]{1,0:T(8,128)S(1)}, f32[32,256]{1,0:T(8,128)S(1)}, f32[102...) custom-call(s32[1,8]{1,0:T(1,128)} %bitcast.22, ...), custom_call_target="tpu_custom_call" | custom-call | tf_op jit(solution)/shard_map/first_product/pallas_call | solution.py:101
  3.3 2.6 %collective-permute-start = (f32[136,256]{1,0:T(8,128)S(1)}, f32[136,256]{1,0:T(8,128)S(1)}, u32[]{:S(2)}, u32[]{:S(2)}) collective-permute-start(f32[136,256]{1,0:T(8,128)S(1)} %get-tuple-element.44), channel_id=1, source_target_pairs={{0,6},{1,7},{2,4},{3,5},{4,2},{5,3},{6,0},{7,1},{8,14},{9,15},{10,... | collective-permute-start | bytes 417800 | tf_op jit(solution)/shard_map/ppermute | solution.py:446
  5.9 3.1 %collective-permute-start.2 = (f32[136,256]{1,0:T(8,128)S(1)}, f32[136,256]{1,0:T(8,128)S(1)}, u32[]{:S(2)}, u32[]{:S(2)}) collective-permute-start(f32[136,256]{1,0:T(8,128)S(1)} %get-tuple-element.46), channel_id=1, source_target_pairs={{0,8},{1,9},{2,10},{3,11},{4,12},{5,13},{6,14},{7,15},{8,0},{9,1},... | collective-permute-start | bytes 417800 | tf_op jit(solution)/shard_map/ppermute | solution.py:446
  9.0 1.5 %collective-permute-start.3 = (f32[136,256]{1,0:T(8,128)S(1)}, f32[136,256]{1,0:T(8,128)S(1)}, u32[]{:S(2)}, u32[]{:S(2)}) collective-permute-start(f32[136,256]{1,0:T(8,128)S(1)} %get-tuple-element.47), channel_id=1, source_target_pairs={{0,1},{1,0},{2,3},{3,2},{4,5},{5,4},{6,7},{7,6},{8,9},{9,8},{10,11... | collective-permute-start | bytes 417800 | tf_op jit(solution)/shard_map/ppermute | solution.py:446
  10.6 2.8 %constants.1 = (bf16[1024,96]{1,0:T(8,128)(2,1)S(1)}, f32[1024,128]{1,0:T(8,128)S(1)}, bf16[96,640]{1,0:T(8,128)(2,1)S(1)}, bf16[1024,1024]{1,0:T(8,128)(2,1)S(1...) custom-call(s32[1,8]{1,0:T(1,128)} %bitcast.23, ...), custom_call_target="tpu_custom_call" | custom-call | tf_op jit(solution)/shard_map/constants/pallas_call | solution.py:101
  13.4 0.7 %collective-permute-done.3.more_3_ = f32[136,256]{1,0:T(8,128)S(1)} collective-permute-done((f32[136,256]{1,0:T(8,128)S(1)}, f32[136,256]{1,0:T(8,128)S(1)}, u32[]{:S(2)}, u32[]{:S(2)}) %collective-permute-start.3) | collective-permute-done | bytes 139296 | tf_op jit(solution)/shard_map/ppermute | solution.py:446
  14.8 0.8 %collective-permute-done.5.other = f32[16,256]{1,0:T(8,128)S(1)} collective-permute-done((f32[16,256]{1,0:T(8,128)S(1)}, f32[16,256]{1,0:T(8,128)S(1)}, u32[]{:S(2)}, u32[]{:S(2)}) %collective-permute-start.5) | collective-permute-done | bytes 16416 | tf_op jit(solution)/shard_map/ppermute | solution.py:501
  15.7 1.7 %collective-permute-start.6 = (f32[16,256]{1,0:T(8,128)S(1)}, f32[16,256]{1,0:T(8,128)S(1)}, u32[]{:S(2)}, u32[]{:S(2)}) collective-permute-start(f32[16,256]{1,0:T(8,128)S(1)} %core_sum.2), channel_id=1, source_target_pairs={{0,16},{1,17},{2,26},{3,27},{4,20},{5,21},{6,30},{7,31},{8,24},{9,... | collective-permute-start | bytes 49160 | tf_op jit(solution)/shard_map/ppermute | solution.py:440
  17.4 0.9 %collective-permute-done.7.more_1_ = f32[16,256]{1,0:T(8,128)S(1)} collective-permute-done((f32[16,256]{1,0:T(8,128)S(1)}, f32[16,256]{1,0:T(8,128)S(1)}, u32[]{:S(2)}, u32[]{:S(2)}) %collective-permute-start.7) | collective-permute-done | bytes 16416 | tf_op jit(solution)/shard_map/ppermute | solution.py:440
  18.3 2.0 %collective-permute-done.6.more_0_ = f32[16,256]{1,0:T(8,128)S(1)} collective-permute-done((f32[16,256]{1,0:T(8,128)S(1)}, f32[16,256]{1,0:T(8,128)S(1)}, u32[]{:S(2)}, u32[]{:S(2)}) %collective-permute-start.6) | collective-permute-done | bytes 16416 | tf_op jit(solution)/shard_map/ppermute | solution.py:440
  20.5 1.5 %collective-permute-start.10 = (f32[48,256]{1,0:T(8,128)S(1)}, f32[48,256]{1,0:T(8,128)S(1)}, u32[]{:S(2)}, u32[]{:S(2)}) collective-permute-start(f32[48,256]{1,0:T(8,128)S(1)} %root_part.1.first), channel_id=1, source_target_pairs={{0,5},{1,4},{2,7},{3,6},{4,1},{5,0},{6,3},{7,2},{8,13},{9,12},{10,... | collective-permute-start | bytes 147464 | tf_op jit(solution)/shard_map/ppermute | solution.py:551
  22.0 1.5 %collective-permute-start.9 = (f32[48,256]{1,0:T(8,128)S(1)}, f32[48,256]{1,0:T(8,128)S(1)}, u32[]{:S(2)}, u32[]{:S(2)}) collective-permute-start(f32[48,256]{1,0:T(8,128)S(1)} %root_part.1.first), channel_id=1, source_target_pairs={{0,4},{1,5},{2,6},{3,7},{4,0},{5,1},{6,2},{7,3},{8,12},{9,13},{10,... | collective-permute-start | bytes 147464 | tf_op jit(solution)/shard_map/ppermute | solution.py:551
  24.1 1.4 %collective-permute-done.10.more_2_ = f32[48,256]{1,0:T(8,128)S(1)} collective-permute-done((f32[48,256]{1,0:T(8,128)S(1)}, f32[48,256]{1,0:T(8,128)S(1)}, u32[]{:S(2)}, u32[]{:S(2)}) %collective-permute-start.10) | collective-permute-done | bytes 49184 | tf_op jit(solution)/shard_map/ppermute | solution.py:551
  26.1 1.4 %collective-permute-done.8.more_0_ = f32[48,256]{1,0:T(8,128)S(1)} collective-permute-done((f32[48,256]{1,0:T(8,128)S(1)}, f32[48,256]{1,0:T(8,128)S(1)}, u32[]{:S(2)}, u32[]{:S(2)}) %collective-permute-start.8) | collective-permute-done | bytes 49184 | tf_op jit(solution)/shard_map/ppermute | solution.py:551
  29.0 1.2 %update_product.1 = (f32[1024,256]{1,0:T(8,128)S(1)}, f32[1024,256]{1,0:T(8,128)S(1)}, f32[32,256]{1,0:T(8,128)S(1)}, f32[48,256]{1,0:T(8,128)S(1)}, f32[128,256...) custom-call(f32[1024,256]{1,0:T(8,128)S(1)} %base.2, ...), custom_call_target="tpu_custom_call" | custom-call | tf_op jit(solution)/shard_map/update_product/pallas_call | solution.py:101
  30.6 1.0 %collective-permute-start.14 = (f32[176,256]{1,0:T(8,128)S(1)}, f32[176,256]{1,0:T(8,128)S(1)}, u32[]{:S(2)}, u32[]{:S(2)}) collective-permute-start(f32[176,256]{1,0:T(8,128)S(1)} %get-tuple-element.66), channel_id=1, source_target_pairs={{0,8},{1,9},{2,10},{3,11},{4,12},{5,13},{6,14},{7,15},{8,0},{9,1},... | collective-permute-start | bytes 540680 | tf_op jit(solution)/shard_map/ppermute | solution.py:446
  32.8 1.9 %collective-permute-start.17 = (f32[48,256]{1,0:T(8,128)S(1)}, f32[48,256]{1,0:T(8,128)S(1)}, u32[]{:S(2)}, u32[]{:S(2)}) collective-permute-start(f32[48,256]{1,0:T(8,128)S(1)} %core_sum.3), channel_id=1, source_target_pairs={{0,16},{1,17},{2,26},{3,27},{4,20},{5,21},{6,30},{7,31},{8,24},{9,... | collective-permute-start | bytes 147464 | tf_op jit(solution)/shard_map/ppermute | solution.py:440
  34.7 2.7 %collective-permute-done.12.more_0_ = f32[128,256]{1,0:T(8,128)S(1)} collective-permute-done((f32[128,256]{1,0:T(8,128)S(1)}, f32[128,256]{1,0:T(8,128)S(1)}, u32[]{:S(2)}, u32[]{:S(2)}) %collective-permute-start.12) | collective-permute-done | bytes 131104 | tf_op jit(solution)/shard_map/ppermute | solution.py:446
  37.7 2.6 %collective-permute-done.17.more_5_ = f32[48,256]{1,0:T(8,128)S(1)} collective-permute-done((f32[48,256]{1,0:T(8,128)S(1)}, f32[48,256]{1,0:T(8,128)S(1)}, u32[]{:S(2)}, u32[]{:S(2)}) %collective-permute-start.17) | collective-permute-done | bytes 49184 | tf_op jit(solution)/shard_map/ppermute | solution.py:440
  40.5 1.5 %collective-permute-start.20 = (f32[48,256]{1,0:T(8,128)S(1)}, f32[48,256]{1,0:T(8,128)S(1)}, u32[]{:S(2)}, u32[]{:S(2)}) collective-permute-start(f32[48,256]{1,0:T(8,128)S(1)} %coarse_root.1.first), channel_id=1, source_target_pairs={{0,5},{1,4},{2,7},{3,6},{4,1},{5,0},{6,3},{7,2},{8,13},{9,12},{10,... | collective-permute-start | bytes 147464 | tf_op jit(solution)/shard_map/ppermute | solution.py:551
  42.6 1.5 %collective-permute-start.18 = (f32[48,256]{1,0:T(8,128)S(1)}, f32[48,256]{1,0:T(8,128)S(1)}, u32[]{:S(2)}, u32[]{:S(2)}) collective-permute-start(f32[48,256]{1,0:T(8,128)S(1)} %coarse_root.1.first), channel_id=1, source_target_pairs={{0,1},{1,0},{2,3},{3,2},{4,5},{5,4},{6,7},{7,6},{8,9},{9,8},{10,11... | collective-permute-start | bytes 147464 | tf_op jit(solution)/shard_map/ppermute | solution.py:551
  44.1 1.5 %collective-permute-done.20.more_2_ = f32[48,256]{1,0:T(8,128)S(1)} collective-permute-done((f32[48,256]{1,0:T(8,128)S(1)}, f32[48,256]{1,0:T(8,128)S(1)}, u32[]{:S(2)}, u32[]{:S(2)}) %collective-permute-start.20) | collective-permute-done | bytes 49184 | tf_op jit(solution)/shard_map/ppermute | solution.py:551
  47.2 0.9 %collective-permute-done.21.other = f32[32,256]{1,0:T(8,128)S(1)} collective-permute-done((f32[32,256]{1,0:T(8,128)S(1)}, f32[32,256]{1,0:T(8,128)S(1)}, u32[]{:S(2)}, u32[]{:S(2)}) %collective-permute-start.21) | collective-permute-done | bytes 32800 | tf_op jit(solution)/shard_map/ppermute | solution.py:559
  48.1 1.2 %update_last.1 = f32[1024,256]{1,0:T(8,128)} custom-call(f32[1024,256]{1,0:T(8,128)S(1)} %base.3, bf16[1024,96]{1,0:T(8,128)(2,1)S(1)} %get-tuple-element.49.modes_t, f32[32,256]{1,0:T(8,128)S(1)} %get-tuple-element.71.own, f32[32,256]{1,0:T(8,128)S(1)} %collective-permute-done.21.other), custom_call_target="tpu_custom_call" | custom-call | tf_op jit(solution)/shard_map/update_last/pallas_call | solution.py:101
  (43 shorter events, 8.4 us)
Async XLA Ops:
  0.0 10.6 %copy-start = (bf16[1,1,1,1024,256]{4,3,2,1,0:T(8,128)(2,1)S(1)}, bf16[1,1,1,1024,256]{4,3,2,1,0:T(8,128)(2,1)}, u32[]{:S(2)}) copy-start(bf16[1,1,1,1024,256]{4,3,2,1,0:T(8,128)(2,1)} %param.9) | copy-start | bytes 1572868
  2.7 11.4 %collective-permute-start.4 = (f32[184,256]{1,0:T(8,128)S(1)}, f32[184,256]{1,0:T(8,128)S(1)}, u32[]{:S(2)}, u32[]{:S(2)}) collective-permute-start(f32[184,256]{1,0:T(8,128)S(1)} %get-tuple-element.48), channel_id=1, source_target_pairs={{0,2},{1,3},{2,0},{3,1},{4,6},{5,7},{6,4},{7,5},{8,10},{9,11},{10,... | collective-permute-start | bytes 565256 | tf_op jit(solution)/shard_map/ppermute | solution.py:446
  3.3 10.1 %collective-permute-start = (f32[136,256]{1,0:T(8,128)S(1)}, f32[136,256]{1,0:T(8,128)S(1)}, u32[]{:S(2)}, u32[]{:S(2)}) collective-permute-start(f32[136,256]{1,0:T(8,128)S(1)} %get-tuple-element.44), channel_id=1, source_target_pairs={{0,6},{1,7},{2,4},{3,5},{4,2},{5,3},{6,0},{7,1},{8,14},{9,15},{10,... | collective-permute-start | bytes 417800 | tf_op jit(solution)/shard_map/ppermute | solution.py:446
  5.9 7.5 %collective-permute-start.1 = (f32[136,256]{1,0:T(8,128)S(1)}, f32[136,256]{1,0:T(8,128)S(1)}, u32[]{:S(2)}, u32[]{:S(2)}) collective-permute-start(f32[136,256]{1,0:T(8,128)S(1)} %get-tuple-element.45), channel_id=1, source_target_pairs={{0,2},{1,3},{2,0},{3,1},{4,6},{5,7},{6,4},{7,5},{8,16},{9,17},{10,... | collective-permute-start | bytes 417800 | tf_op jit(solution)/shard_map/ppermute | solution.py:446
  5.9 7.4 %collective-permute-start.2 = (f32[136,256]{1,0:T(8,128)S(1)}, f32[136,256]{1,0:T(8,128)S(1)}, u32[]{:S(2)}, u32[]{:S(2)}) collective-permute-start(f32[136,256]{1,0:T(8,128)S(1)} %get-tuple-element.46), channel_id=1, source_target_pairs={{0,8},{1,9},{2,10},{3,11},{4,12},{5,13},{6,14},{7,15},{8,0},{9,1},... | collective-permute-start | bytes 417800 | tf_op jit(solution)/shard_map/ppermute | solution.py:446
  9.0 5.1 %collective-permute-start.3 = (f32[136,256]{1,0:T(8,128)S(1)}, f32[136,256]{1,0:T(8,128)S(1)}, u32[]{:S(2)}, u32[]{:S(2)}) collective-permute-start(f32[136,256]{1,0:T(8,128)S(1)} %get-tuple-element.47), channel_id=1, source_target_pairs={{0,1},{1,0},{2,3},{3,2},{4,5},{5,4},{6,7},{7,6},{8,9},{9,8},{10,11... | collective-permute-start | bytes 417800 | tf_op jit(solution)/shard_map/ppermute | solution.py:446
  10.6 17.2 %copy-start.1 = (bf16[1,1,1,1024,256]{4,3,2,1,0:T(8,128)(2,1)S(1)}, bf16[1,1,1,1024,256]{4,3,2,1,0:T(8,128)(2,1)}, u32[]{:S(2)}) copy-start(bf16[1,1,1,1024,256]{4,3,2,1,0:T(8,128)(2,1)} %param.10) | copy-start | bytes 1572868
  14.4 1.2 %collective-permute-start.5 = (f32[16,256]{1,0:T(8,128)S(1)}, f32[16,256]{1,0:T(8,128)S(1)}, u32[]{:S(2)}, u32[]{:S(2)}) collective-permute-start(f32[16,256]{1,0:T(8,128)S(1)} %get-tuple-element.54.own.root), channel_id=1, source_target_pairs={{0,2},{1,3},{2,0},{3,1},{4,6},{5,7},{6,4},{7,5},{8,10},{9,11},{10,... | collective-permute-start | bytes 49160 | tf_op jit(solution)/shard_map/ppermute | solution.py:501
  14.5 3.8 %collective-permute-start.7 = (f32[16,256]{1,0:T(8,128)S(1)}, f32[16,256]{1,0:T(8,128)S(1)}, u32[]{:S(2)}, u32[]{:S(2)}) collective-permute-start(f32[16,256]{1,0:T(8,128)S(1)} %get-tuple-element.54.own.root), channel_id=1, source_target_pairs={{0,8},{1,9},{2,10},{3,11},{4,12},{5,13},{6,14},{7,15},{8,0},{9,1},... | collective-permute-start | bytes 49160 | tf_op jit(solution)/shard_map/ppermute | solution.py:440
  15.7 4.6 %collective-permute-start.6 = (f32[16,256]{1,0:T(8,128)S(1)}, f32[16,256]{1,0:T(8,128)S(1)}, u32[]{:S(2)}, u32[]{:S(2)}) collective-permute-start(f32[16,256]{1,0:T(8,128)S(1)} %core_sum.2), channel_id=1, source_target_pairs={{0,16},{1,17},{2,26},{3,27},{4,20},{5,21},{6,30},{7,31},{8,24},{9,... | collective-permute-start | bytes 49160 | tf_op jit(solution)/shard_map/ppermute | solution.py:440
  20.5 5.1 %collective-permute-start.10 = (f32[48,256]{1,0:T(8,128)S(1)}, f32[48,256]{1,0:T(8,128)S(1)}, u32[]{:S(2)}, u32[]{:S(2)}) collective-permute-start(f32[48,256]{1,0:T(8,128)S(1)} %root_part.1.first), channel_id=1, source_target_pairs={{0,5},{1,4},{2,7},{3,6},{4,1},{5,0},{6,3},{7,2},{8,13},{9,12},{10,... | collective-permute-start | bytes 147464 | tf_op jit(solution)/shard_map/ppermute | solution.py:551
  22.0 4.2 %collective-permute-start.9 = (f32[48,256]{1,0:T(8,128)S(1)}, f32[48,256]{1,0:T(8,128)S(1)}, u32[]{:S(2)}, u32[]{:S(2)}) collective-permute-start(f32[48,256]{1,0:T(8,128)S(1)} %root_part.1.first), channel_id=1, source_target_pairs={{0,4},{1,5},{2,6},{3,7},{4,0},{5,1},{6,2},{7,3},{8,12},{9,13},{10,... | collective-permute-start | bytes 147464 | tf_op jit(solution)/shard_map/ppermute | solution.py:551
  23.4 4.1 %collective-permute-start.8 = (f32[48,256]{1,0:T(8,128)S(1)}, f32[48,256]{1,0:T(8,128)S(1)}, u32[]{:S(2)}, u32[]{:S(2)}) collective-permute-start(f32[48,256]{1,0:T(8,128)S(1)} %root_part.1.first), channel_id=1, source_target_pairs={{0,1},{1,0},{2,3},{3,2},{4,5},{5,4},{6,7},{7,6},{8,9},{9,8},{10,11... | collective-permute-start | bytes 147464 | tf_op jit(solution)/shard_map/ppermute | solution.py:551
  27.7 1.3 %collective-permute-start.11 = (f32[32,256]{1,0:T(8,128)S(1)}, f32[32,256]{1,0:T(8,128)S(1)}, u32[]{:S(2)}, u32[]{:S(2)}) collective-permute-start(f32[32,256]{1,0:T(8,128)S(1)} %get-tuple-element.56), channel_id=1, source_target_pairs={{0,2},{1,3},{2,0},{3,1},{4,6},{5,7},{6,4},{7,5},{8,10},{9,11},{10,... | collective-permute-start | bytes 98312 | tf_op jit(solution)/shard_map/ppermute | solution.py:559
  30.2 2.6 %collective-permute-start.16 = (f32[176,256]{1,0:T(8,128)S(1)}, f32[176,256]{1,0:T(8,128)S(1)}, u32[]{:S(2)}, u32[]{:S(2)}) collective-permute-start(f32[176,256]{1,0:T(8,128)S(1)} %get-tuple-element.68), channel_id=1, source_target_pairs={{0,2},{1,3},{2,0},{3,1},{4,6},{5,7},{6,4},{7,5},{8,10},{9,11},{10,... | collective-permute-start | bytes 540680 | tf_op jit(solution)/shard_map/ppermute | solution.py:446
  30.6 7.0 %collective-permute-start.14 = (f32[176,256]{1,0:T(8,128)S(1)}, f32[176,256]{1,0:T(8,128)S(1)}, u32[]{:S(2)}, u32[]{:S(2)}) collective-permute-start(f32[176,256]{1,0:T(8,128)S(1)} %get-tuple-element.66), channel_id=1, source_target_pairs={{0,8},{1,9},{2,10},{3,11},{4,12},{5,13},{6,14},{7,15},{8,0},{9,1},... | collective-permute-start | bytes 540680 | tf_op jit(solution)/shard_map/ppermute | solution.py:446
  31.6 5.8 %collective-permute-start.12 = (f32[128,256]{1,0:T(8,128)S(1)}, f32[128,256]{1,0:T(8,128)S(1)}, u32[]{:S(2)}, u32[]{:S(2)}) collective-permute-start(f32[128,256]{1,0:T(8,128)S(1)} %get-tuple-element.64), channel_id=1, source_target_pairs={{0,6},{1,7},{2,4},{3,5},{4,2},{5,3},{6,0},{7,1},{8,14},{9,15},{10,... | collective-permute-start | bytes 393224 | tf_op jit(solution)/shard_map/ppermute | solution.py:446
  31.6 5.8 %collective-permute-start.13 = (f32[128,256]{1,0:T(8,128)S(1)}, f32[128,256]{1,0:T(8,128)S(1)}, u32[]{:S(2)}, u32[]{:S(2)}) collective-permute-start(f32[128,256]{1,0:T(8,128)S(1)} %get-tuple-element.65), channel_id=1, source_target_pairs={{0,2},{1,3},{2,0},{3,1},{4,6},{5,7},{6,4},{7,5},{8,16},{9,17},{10,... | collective-permute-start | bytes 393224 | tf_op jit(solution)/shard_map/ppermute | solution.py:446
  32.3 5.4 %collective-permute-start.15 = (f32[128,256]{1,0:T(8,128)S(1)}, f32[128,256]{1,0:T(8,128)S(1)}, u32[]{:S(2)}, u32[]{:S(2)}) collective-permute-start(f32[128,256]{1,0:T(8,128)S(1)} %get-tuple-element.67), channel_id=1, source_target_pairs={{0,1},{1,0},{2,3},{3,2},{4,5},{5,4},{6,7},{7,6},{8,9},{9,8},{10,11... | collective-permute-start | bytes 393224 | tf_op jit(solution)/shard_map/ppermute | solution.py:446
  32.8 7.5 %collective-permute-start.17 = (f32[48,256]{1,0:T(8,128)S(1)}, f32[48,256]{1,0:T(8,128)S(1)}, u32[]{:S(2)}, u32[]{:S(2)}) collective-permute-start(f32[48,256]{1,0:T(8,128)S(1)} %core_sum.3), channel_id=1, source_target_pairs={{0,16},{1,17},{2,26},{3,27},{4,20},{5,21},{6,30},{7,31},{8,24},{9,... | collective-permute-start | bytes 147464 | tf_op jit(solution)/shard_map/ppermute | solution.py:440
  40.5 5.1 %collective-permute-start.20 = (f32[48,256]{1,0:T(8,128)S(1)}, f32[48,256]{1,0:T(8,128)S(1)}, u32[]{:S(2)}, u32[]{:S(2)}) collective-permute-start(f32[48,256]{1,0:T(8,128)S(1)} %coarse_root.1.first), channel_id=1, source_target_pairs={{0,5},{1,4},{2,7},{3,6},{4,1},{5,0},{6,3},{7,2},{8,13},{9,12},{10,... | collective-permute-start | bytes 147464 | tf_op jit(solution)/shard_map/ppermute | solution.py:551
  42.0 4.1 %collective-permute-start.19 = (f32[48,256]{1,0:T(8,128)S(1)}, f32[48,256]{1,0:T(8,128)S(1)}, u32[]{:S(2)}, u32[]{:S(2)}) collective-permute-start(f32[48,256]{1,0:T(8,128)S(1)} %coarse_root.1.first), channel_id=1, source_target_pairs={{0,4},{1,5},{2,6},{3,7},{4,0},{5,1},{6,2},{7,3},{8,12},{9,13},{10,... | collective-permute-start | bytes 147464 | tf_op jit(solution)/shard_map/ppermute | solution.py:551
  42.6 4.1 %collective-permute-start.18 = (f32[48,256]{1,0:T(8,128)S(1)}, f32[48,256]{1,0:T(8,128)S(1)}, u32[]{:S(2)}, u32[]{:S(2)}) collective-permute-start(f32[48,256]{1,0:T(8,128)S(1)} %coarse_root.1.first), channel_id=1, source_target_pairs={{0,1},{1,0},{2,3},{3,2},{4,5},{5,4},{6,7},{7,6},{8,9},{9,8},{10,11... | collective-permute-start | bytes 147464 | tf_op jit(solution)/shard_map/ppermute | solution.py:551
  46.8 1.3 %collective-permute-start.21 = (f32[32,256]{1,0:T(8,128)S(1)}, f32[32,256]{1,0:T(8,128)S(1)}, u32[]{:S(2)}, u32[]{:S(2)}) collective-permute-start(f32[32,256]{1,0:T(8,128)S(1)} %get-tuple-element.72), channel_id=1, source_target_pairs={{0,2},{1,3},{2,0},{3,1},{4,6},{5,7},{6,4},{7,5},{8,10},{9,11},{10,... | collective-permute-start | bytes 98312 | tf_op jit(solution)/shard_map/ppermute | solution.py:559
  (2 other events, 20.3 us)

commit v8 on v7

--- a/solution.py
+++ b/solution.py
@@ -11,6 +11,8 @@
 ITERS = 2
 FACES = 8
 AXES = ("gx", "gy", "gz")
+FIRST_ORDER = ((1, 1), (2, 1), (2, 0), (0, 0), (0, 1), (1, 0))
+LATER_ORDER = ((1, 0), (0, 0), (0, 1), (2, 1), (2, 0), (1, 1))
 F32 = jnp.float32
 BF16 = jnp.bfloat16
 ROWS = (((1,), (0,)), ((), ()))
@@ -22,9 +24,8 @@
     return other if 0 <= other < count else None
 
 
-def swap_list(sizes):
-    swaps = [(dim, odd) for odd in (1, 0) for dim in (1, 0, 2) if sizes[dim] > 1 + odd]
-    return sorted(swaps, key=lambda swap: swap == (1, 0))
+def swap_list(sizes, wanted):
+    return [swap for swap in wanted if sizes[swap[0]] > 1 + swap[1]]
 
 
 def flat(sizes, place):
@@ -123,8 +124,8 @@
 
 
 def first_kernel(swaps, order_hbm, start_hbm, *refs):
-    hbm, held, (placed, *more) = refs[:4], refs[4:8], refs[8:]
-    matrix, modes, root_map, region_rows = held
+    hbm, held, (placed, *more) = refs[:3], refs[3:6], refs[6:]
+    matrix, modes, root_map = held
     messages, (order, start, local_iter, mapped, sems) = more[: len(swaps)], more[len(swaps) :]
     pairs = [(order_hbm, order), (start_hbm, start)] + list(zip(hbm, held))
     copies = [pltpu.make_async_copy(*pair, sems.at[k]) for k, pair in enumerate(pairs)]
@@ -144,14 +145,6 @@
         end = height + extra
         for k in range(lanes // height):
             message[height:end, k * height : (k + 1) * height] = link[k * extra : (k + 1) * extra, :]
-        if (dim, odd) == (1, 0):
-            copies[5].wait()
-            rows = region_rows.shape[0]
-            message[end:, :] = jnp.zeros_like(message[end:, :])
-            message[end : end + root_map.shape[0], :rows] = root_map[...]
-            end += root_map.shape[0]
-            for k in range(region_rows.shape[1] // lanes):
-                message[end + k * rows : end + (k + 1) * rows, :] = region_rows[:, k * lanes : (k + 1) * lanes]
     copies[2].wait()
     product = jnp.dot(matrix[...], local_iter[...], preferred_element_type=F32)
     for j in range(FACES):
@@ -194,23 +187,31 @@
     modes_a[:count, :], modes_a[count:, :] = split(dot(high, matrix_f[...]) + dot(low, matrix_f[...]))
 
 
-def stack_halos(swaps, sizes, halos, stack):
+def stack_halos(layout, swaps, sizes, halos, stack):
     height = stack.shape[0] // len(swaps)
-    for at, ((dim, odd), halo) in enumerate(zip(swaps, halos)):
+    for (dim, odd), halo in zip(swaps, halos):
+        at = layout.index((dim, odd))
         known = has_neighbour(dim, swap_face(dim, odd), sizes)
         stack[at * height : (at + 1) * height, :] = jnp.where(known, halo[:height, :], 0.0)
     return split(stack[...])
 
 
-def coarse_kernel(swaps, sizes, ready, modes_f, *more):
-    halos, (coarse, root, stack) = more[: len(swaps)], more[len(swaps) :]
+def coarse_kernel(swaps, sizes, ready, modes_f, region_rows, root_map, *more):
+    halos, (coarse, root, note, stack) = more[: len(swaps)], more[len(swaps) :]
     modes, count = coarse.shape[0], root.shape[0]
-    high, low = stack_halos(swaps, sizes, halos, stack)
+    high, low = stack_halos(swaps, swaps, sizes, halos, stack)
     both = jnp.dot(modes_f[...], high, preferred_element_type=F32)
     fine = jnp.dot(modes_f[: 2 * modes + count, :], low, preferred_element_type=F32)
     coarse[...] = ready[:modes, :] - (both[:modes, :] + (both[modes : 2 * modes, :] + fine[:modes, :]))
     at = 2 * modes
     root[...] = ready[modes:, :] - (both[at : at + count, :] + (both[at + count :, :] + fine[at:, :]))
+    lanes = root.shape[1]
+    note[:count, :] = jnp.zeros_like(root)
+    note[:count, :modes] = root_map[...]
+    for k in range(region_rows.shape[1] // lanes):
+        rows = slice(count + k * modes, count + (k + 1) * modes)
+        note[rows, :] = region_rows[:, k * lanes : (k + 1) * lanes]
+    note[-count:, :] = root[...]
 
 
 def base_kernel(swaps, sizes, solution, loads, placed, scale, *more):
@@ -263,12 +264,12 @@
     ahead_loads[count : 2 * count, :] = dot(high, loads[...]) + dot(low, loads[...])
 
 
-def merged_kernel(swaps, sizes, ride, ready, modes_f, root_inverse, ahead, *more):
+def merged_kernel(layout, swaps, sizes, ride, ready, modes_f, root_inverse, ahead, *more):
     halos, more = more[: len(swaps)], more[len(swaps) :]
     received, (message, faces, stack) = more[:-3], more[-3:]
     modes, height = ready.shape[0], faces.shape[0] // len(swaps)
     count = message.shape[0] - modes
-    high, low = stack_halos(swaps, sizes, halos, faces)
+    high, low = stack_halos(layout, swaps, sizes, halos, faces)
     both = jnp.dot(modes_f[: 2 * modes, :], high, preferred_element_type=F32)
     fine = jnp.dot(modes_f[:modes, :], low, preferred_element_type=F32)
     message[:modes, :] = ready[...] - (both[:modes, :] + (both[modes:, :] + fine))
@@ -305,13 +306,12 @@
     message[modes:, :] = dot3(root_inverse[...], stack[...])
 
 
-def parts_kernel(members, sizes, region_rows, root_map, halo, factors):
+def parts_kernel(members, sizes, region_rows, root_map, note, factors):
     modes, order = region_rows.shape
-    count, lanes = root_map.shape[0], halo.shape[1]
-    blocks = order // lanes
-    at = halo.shape[0] - blocks * modes
-    other_rows = jnp.concatenate([halo[at + k * modes : at + (k + 1) * modes, :] for k in range(blocks)], axis=1)
-    other_map = halo[at - count : at, :modes]
+    count, lanes = root_map.shape[0], note.shape[1]
+    other_map = note[:count, :modes]
+    blocks = [slice(count + k * modes, count + (k + 1) * modes) for k in range(order // lanes)]
+    other_rows = jnp.concatenate([note[rows, :] for rows in blocks], axis=1)
     y, z = lax.axis_index("gy"), lax.axis_index("gz")
     half = sizes[0] // 2
     depth = len(members) * modes
@@ -414,13 +414,14 @@
     target = loads.reshape(iface, cases)
     solution = start.reshape(iface, cases)
 
-    swaps = swap_list(sizes)
+    swaps = swap_list(sizes, FIRST_ORDER)
+    later = swap_list(sizes, LATER_ORDER)
     half = sizes[1] // 2
     members = list(itertools.product(range(half), range(sizes[2])))
 
     ride = nearest(sizes[0])
     paired, single = far_offsets(sizes[0], 1 + ride)
-    core = swaps.index((1, 0))
+    core = later.index((1, 0))
     full = (pltpu.VMEM, (iface, cases), F32)
     places = [pltpu.SMEM((1, FACES), jnp.int32)]
     faces = [pltpu.VMEM((len(swaps) * height, cases), F32)]
@@ -440,18 +441,16 @@
         return lax.ppermute(value, AXES, pairs)
 
     def exchange(messages, order):
-        moved = {}
-        for dim, odd in order:
-            message = messages[swaps.index((dim, odd))]
-            moved[dim, odd] = lax.ppermute(message, AXES, swap_pairs(sizes, dim, odd))
-        return [moved[swap] for swap in swaps]
+        return [
+            lax.ppermute(message, AXES, swap_pairs(sizes, dim, odd)) for (dim, odd), message in zip(order, messages)
+        ]
 
     def core_sum(own, other):
         return call(sum_kernel, [held(own.shape[0])], [own, other], "core_sum")[0]
 
-    def base_of(solution, placed, halos):
+    def base_of(order, solution, placed, halos):
         return call(
-            functools.partial(base_kernel, swaps, sizes),
+            functools.partial(base_kernel, order, sizes),
             [full],
             [solution, target, placed, scale] + halos,
             "base",
@@ -459,19 +458,17 @@
 
     for step in range(ITERS):
         if step == 0:
-            inputs = [order, solution, matrix, modes, root_map, region_rows]
-            rows = [height + root_modes * height // cases] * len(swaps)
-            rows[core] += root_modes + mode_count * (region_rows.shape[1] // cases)
-            matrix, modes, root_map, region_rows, placed, *messages = call(
+            inputs = [order, solution, matrix, modes, root_map]
+            matrix, modes, root_map, placed, *messages = call(
                 functools.partial(first_kernel, swaps),
                 [(pltpu.VMEM, item.shape, item.dtype) for item in inputs[2:]]
                 + [full]
-                + [held(count) for count in rows],
+                + [held(height + root_modes * height // cases)] * len(swaps),
                 inputs,
                 "first_product",
                 places
                 + [pltpu.VMEM((iface, cases), BF16)] * 2
-                + [pltpu.VMEM((root_modes, iface), F32), pltpu.SemaphoreType.DMA((6,))],
+                + [pltpu.VMEM((root_modes, iface), F32), pltpu.SemaphoreType.DMA((5,))],
                 len(inputs),
             )
             modes_t, scale, modes_f, matrix_f, modes_a, modes_b, ready = call(
@@ -491,23 +488,25 @@
                 1,
             )
             halos = exchange(messages, swaps)
-            coarse, root = call(
+            blocks = region_rows.shape[1] // cases
+            coarse, root, note = call(
                 functools.partial(coarse_kernel, swaps, sizes),
-                [held(mode_count), held(root_modes)],
-                [ready, modes_f] + halos,
+                [held(mode_count), held(root_modes), held(2 * root_modes + mode_count * blocks)],
+                [ready, modes_f, region_rows, root_map] + halos,
                 "coarse",
                 faces,
             )
-            both = core_sum(root, lax.ppermute(root, AXES, swap_pairs(sizes, 1, 0)))
+            note = lax.ppermute(note, AXES, swap_pairs(sizes, 1, 0))
+            both = core_sum(root, note)
             received = [along(root, offset) for offset in list(range(1, 1 + ride)) + single]
             received = [along(both, pair) for pair in paired] + received
             (factors,) = call(
                 functools.partial(parts_kernel, members, sizes[1:]),
                 [(pltpu.VMEM, (4 * mode_count, len(members) * mode_count + root_modes), BF16)],
-                [region_rows, root_map, halos[core]],
+                [region_rows, root_map, note],
                 "parts",
             )
-            base = base_of(solution, placed, halos)
+            base = base_of(swaps, solution, placed, halos)
             tail, ahead_loads = call(
                 functools.partial(links_kernel, swaps, sizes),
                 [wide(2 * mode_count + 6 * root_modes), held(3 * root_modes)],
@@ -523,24 +522,24 @@
                 [pltpu.VMEM((root_inverse.shape[1], cases), F32)],
             )
         else:
-            extra = [3 * root_modes * int(swap == (1, 0) or (ride and swap == (0, 0))) for swap in swaps]
+            extra = [3 * root_modes * int(swap == (1, 0) or (ride and swap == (0, 0))) for swap in later]
             solution, placed, ready, ahead, *messages = call(
-                functools.partial(middle_kernel, swaps),
+                functools.partial(middle_kernel, later),
                 [full, full, held(mode_count), held(3 * root_modes)] + [held(height + more) for more in extra],
                 [base, modes_t, own, other, matrix_f, tail, modes_b, ahead_loads],
                 "update_product",
             )
-            halos = exchange(messages, sorted(swaps, key=lambda swap: (swap != (1, 0), swap[0] == 1, swap)))
+            halos = exchange(messages, later)
             both = core_sum(ahead, halos[core])
             received = [along(both, pair) for pair in paired] + [along(ahead, offset) for offset in single]
             (message,) = call(
-                functools.partial(merged_kernel, swaps, sizes, ride),
+                functools.partial(merged_kernel, swaps, later, sizes, ride),
                 [held(mode_count + root_modes)],
                 [ready, modes_f, root_inverse, ahead] + halos + received,
                 "coarse_root",
                 faces + [pltpu.VMEM((root_inverse.shape[1] + 2 * root_modes, cases), F32)],
             )
-            base = base_of(solution, placed, halos)
+            base = base_of(later, solution, placed, halos)
         pieces = []
         for dy, dz in members[1:]:
             moves = [

time: 49.5 us -> 48 us (0.970)
  waiting for transfers between devices: 17.1 us -> 13.5 us
  starting transfers between devices: 21.7 us -> 24 us
    ppermute x3, starting transfers between devices: 4.02 us -> 7.17 us  [along(): return lax.ppermute(value, AXES, pairs)]
    ppermute x3, waiting for transfers between devices: 5.48 us -> 2.95 us  [along(): return lax.ppermute(value, AXES, pairs)]
    ppermute x11, starting transfers between devices: 10.4 us -> 9.55 us  [the longest x10 9.48 us: exchange(): lax.ppermute(message, AXES, swap_pairs(sizes, dim, odd))]
    ppermute x6, waiting for transfers between devices: 5.99 us -> 5.1 us  [per_device(): pieces.append(lax.ppermute(message, ('gy', 'gz'), moves))]
  transfers between devices with their start and end apart: 22 -> 22, of which waited for: 15 -> 12; matrix products, arithmetic and copies ran while one was open for 0% -> 0% of each run, Pallas kernels for 9% -> 8%
where the time goes in v8:
time: 48 us; the launch traced here: 47.9 us
  starting transfers between devices  24 us (50%)
  waiting for transfers between devices  13.5 us (28%)
  Pallas kernels  10.2 us (21%)
    pallas_call x15, Pallas kernels, call(): pl.pallas_call(body, out_shape=[item(shape, dtype) for item, shape, dtype...  10.2 us
    ppermute x10, starting transfers between devices, exchange(): lax.ppermute(message, AXES, swap_pairs(sizes, dim, odd))  9.48 us
    ppermute x3, starting transfers between devices, along(): return lax.ppermute(value, AXES, pairs)  7.17 us
    ppermute x6, starting transfers between devices, per_device(): pieces.append(lax.ppermute(message, ('gy', 'gz'), moves))  7.15 us
    ppermute x6, waiting for transfers between devices, per_device(): pieces.append(lax.ppermute(message, ('gy', 'gz'), moves))  5.1 us
    ppermute x10, waiting for transfers between devices, exchange(): lax.ppermute(message, AXES, swap_pairs(sizes, dim, odd))  4.34 us
    ppermute x3, waiting for transfers between devices, along(): return lax.ppermute(value, AXES, pairs)  2.95 us
    ppermute x2, waiting for transfers between devices, per_device(): other = lax.ppermute(given, AXES, swap_pairs(sizes, 1, 0))  1.07 us
  transfers between devices with their start and end apart: 22, of which 12 were waited for; matrix products, arithmetic and copies ran while one was open for 0% of the time, Pallas kernels for 8%

profile of v8, /device:TPU:0, one launch (start us, length us, event | category | flops | bytes accessed | tf_op | source)
XLA Modules:
  0.0 47.9 jit_solution(4472084249891215456)
XLA Ops:
  0.0 2.7 %first_product.1 = (bf16[1024,1024]{1,0:T(8,128)(2,1)S(1)}, f32[32,1024]{1,0:T(8,128)S(1)}, f32[16,32]{1,0:T(8,128)S(1)}, f32[1024,256]{1,0:T(8,128)S(1)}, f32[1...) custom-call(s32[1,8]{1,0:T(1,128)} %bitcast.23, ...), custom_call_target="tpu_custom_call" | custom-call | tf_op jit(solution)/shard_map/first_product/pallas_call | solution.py:102
  2.7 2.4 %collective-permute-start = (f32[136,256]{1,0:T(8,128)S(1)}, f32[136,256]{1,0:T(8,128)S(1)}, u32[]{:S(2)}, u32[]{:S(2)}) collective-permute-start(f32[136,256]{1,0:T(8,128)S(1)} %get-tuple-element.44), channel_id=1, source_target_pairs={{0,6},{1,7},{2,4},{3,5},{4,2},{5,3},{6,0},{7,1},{8,14},{9,15},{10,... | collective-permute-start | bytes 417800 | tf_op jit(solution)/shard_map/ppermute | solution.py:445
  5.2 1.5 %collective-permute-start.1 = (f32[136,256]{1,0:T(8,128)S(1)}, f32[136,256]{1,0:T(8,128)S(1)}, u32[]{:S(2)}, u32[]{:S(2)}) collective-permute-start(f32[136,256]{1,0:T(8,128)S(1)} %get-tuple-element.45), channel_id=1, source_target_pairs={{0,1},{1,0},{2,3},{3,2},{4,5},{5,4},{6,7},{7,6},{8,9},{9,8},{10,11... | collective-permute-start | bytes 417800 | tf_op jit(solution)/shard_map/ppermute | solution.py:445
  6.7 1.6 %collective-permute-start.2 = (f32[136,256]{1,0:T(8,128)S(1)}, f32[136,256]{1,0:T(8,128)S(1)}, u32[]{:S(2)}, u32[]{:S(2)}) collective-permute-start(f32[136,256]{1,0:T(8,128)S(1)} %get-tuple-element.46), channel_id=1, source_target_pairs={{0,8},{1,9},{2,10},{3,11},{4,12},{5,13},{6,14},{7,15},{8,0},{9,1},... | collective-permute-start | bytes 417800 | tf_op jit(solution)/shard_map/ppermute | solution.py:445
  8.8 2.6 %constants.1 = (bf16[1024,96]{1,0:T(8,128)(2,1)S(1)}, f32[1024,128]{1,0:T(8,128)S(1)}, bf16[96,640]{1,0:T(8,128)(2,1)S(1)}, bf16[1024,1024]{1,0:T(8,128)(2,1)S(1...) custom-call(s32[1,8]{1,0:T(1,128)} %bitcast.24, ...), custom_call_target="tpu_custom_call" | custom-call | tf_op jit(solution)/shard_map/constants/pallas_call | solution.py:102
  11.4 1.3 %collective-permute-done.2.more_2_ = f32[136,256]{1,0:T(8,128)S(1)} collective-permute-done((f32[136,256]{1,0:T(8,128)S(1)}, f32[136,256]{1,0:T(8,128)S(1)}, u32[]{:S(2)}, u32[]{:S(2)}) %collective-permute-start.2) | collective-permute-done | bytes 139296 | tf_op jit(solution)/shard_map/ppermute | solution.py:445
  13.1 2.7 %collective-permute-start.7 = (f32[16,256]{1,0:T(8,128)S(1)}, f32[16,256]{1,0:T(8,128)S(1)}, u32[]{:S(2)}, u32[]{:S(2)}) collective-permute-start(f32[16,256]{1,0:T(8,128)S(1)} %get-tuple-element.54.own.root), channel_id=1, source_target_pairs={{0,8},{1,9},{2,10},{3,11},{4,12},{5,13},{6,14},{7,15},{8,0},{9,1},... | collective-permute-start | bytes 49160 | tf_op jit(solution)/shard_map/ppermute | solution.py:441
  15.8 2.4 %collective-permute-start.6 = (f32[16,256]{1,0:T(8,128)S(1)}, f32[16,256]{1,0:T(8,128)S(1)}, u32[]{:S(2)}, u32[]{:S(2)}) collective-permute-start(f32[16,256]{1,0:T(8,128)S(1)} %core_sum.2), channel_id=1, source_target_pairs={{0,16},{1,17},{2,26},{3,27},{4,20},{5,21},{6,30},{7,31},{8,24},{9,... | collective-permute-start | bytes 49160 | tf_op jit(solution)/shard_map/ppermute | solution.py:441
  18.2 2.4 %collective-permute-done.6.more_0_ = f32[16,256]{1,0:T(8,128)S(1)} collective-permute-done((f32[16,256]{1,0:T(8,128)S(1)}, f32[16,256]{1,0:T(8,128)S(1)}, u32[]{:S(2)}, u32[]{:S(2)}) %collective-permute-start.6) | collective-permute-done | bytes 16416 | tf_op jit(solution)/shard_map/ppermute | solution.py:441
  21.2 1.5 %collective-permute-start.9 = (f32[48,256]{1,0:T(8,128)S(1)}, f32[48,256]{1,0:T(8,128)S(1)}, u32[]{:S(2)}, u32[]{:S(2)}) collective-permute-start(f32[48,256]{1,0:T(8,128)S(1)} %root_part.1.first), channel_id=1, source_target_pairs={{0,4},{1,5},{2,6},{3,7},{4,0},{5,1},{6,2},{7,3},{8,12},{9,13},{10,... | collective-permute-start | bytes 147464 | tf_op jit(solution)/shard_map/ppermute | solution.py:550
  22.7 1.5 %collective-permute-start.8 = (f32[48,256]{1,0:T(8,128)S(1)}, f32[48,256]{1,0:T(8,128)S(1)}, u32[]{:S(2)}, u32[]{:S(2)}) collective-permute-start(f32[48,256]{1,0:T(8,128)S(1)} %root_part.1.first), channel_id=1, source_target_pairs={{0,1},{1,0},{2,3},{3,2},{4,5},{5,4},{6,7},{7,6},{8,9},{9,8},{10,11... | collective-permute-start | bytes 147464 | tf_op jit(solution)/shard_map/ppermute | solution.py:550
  24.4 1.4 %collective-permute-done.10.more_2_ = f32[48,256]{1,0:T(8,128)S(1)} collective-permute-done((f32[48,256]{1,0:T(8,128)S(1)}, f32[48,256]{1,0:T(8,128)S(1)}, u32[]{:S(2)}, u32[]{:S(2)}) %collective-permute-start.10) | collective-permute-done | bytes 49184 | tf_op jit(solution)/shard_map/ppermute | solution.py:550
  25.8 1.0 %collective-permute-done.8.more_0_ = f32[48,256]{1,0:T(8,128)S(1)} collective-permute-done((f32[48,256]{1,0:T(8,128)S(1)}, f32[48,256]{1,0:T(8,128)S(1)}, u32[]{:S(2)}, u32[]{:S(2)}) %collective-permute-start.8) | collective-permute-done | bytes 49184 | tf_op jit(solution)/shard_map/ppermute | solution.py:550
  28.2 1.2 %update_product.1 = (f32[1024,256]{1,0:T(8,128)S(1)}, f32[1024,256]{1,0:T(8,128)S(1)}, f32[32,256]{1,0:T(8,128)S(1)}, f32[48,256]{1,0:T(8,128)S(1)}, f32[176,256...) custom-call(f32[1024,256]{1,0:T(8,128)S(1)} %base.2, ...), custom_call_target="tpu_custom_call" | custom-call | tf_op jit(solution)/shard_map/update_product/pallas_call | solution.py:102
  29.9 1.1 %collective-permute-start.13 = (f32[176,256]{1,0:T(8,128)S(1)}, f32[176,256]{1,0:T(8,128)S(1)}, u32[]{:S(2)}, u32[]{:S(2)}) collective-permute-start(f32[176,256]{1,0:T(8,128)S(1)} %get-tuple-element.65), channel_id=1, source_target_pairs={{0,8},{1,9},{2,10},{3,11},{4,12},{5,13},{6,14},{7,15},{8,0},{9,1},... | collective-permute-start | bytes 540680 | tf_op jit(solution)/shard_map/ppermute | solution.py:445
  31.0 1.5 %collective-permute-start.15 = (f32[128,256]{1,0:T(8,128)S(1)}, f32[128,256]{1,0:T(8,128)S(1)}, u32[]{:S(2)}, u32[]{:S(2)}) collective-permute-start(f32[128,256]{1,0:T(8,128)S(1)} %get-tuple-element.67), channel_id=1, source_target_pairs={{0,1},{1,0},{2,3},{3,2},{4,5},{5,4},{6,7},{7,6},{8,9},{9,8},{10,11... | collective-permute-start | bytes 393224 | tf_op jit(solution)/shard_map/ppermute | solution.py:445
  32.9 2.1 %collective-permute-start.17 = (f32[48,256]{1,0:T(8,128)S(1)}, f32[48,256]{1,0:T(8,128)S(1)}, u32[]{:S(2)}, u32[]{:S(2)}) collective-permute-start(f32[48,256]{1,0:T(8,128)S(1)} %core_sum.3), channel_id=1, source_target_pairs={{0,16},{1,17},{2,26},{3,27},{4,20},{5,21},{6,30},{7,31},{8,24},{9,... | collective-permute-start | bytes 147464 | tf_op jit(solution)/shard_map/ppermute | solution.py:441
  35.0 1.9 %collective-permute-done.15.more_3_ = f32[128,256]{1,0:T(8,128)S(1)} collective-permute-done((f32[128,256]{1,0:T(8,128)S(1)}, f32[128,256]{1,0:T(8,128)S(1)}, u32[]{:S(2)}, u32[]{:S(2)}) %collective-permute-start.15) | collective-permute-done | bytes 131104 | tf_op jit(solution)/shard_map/ppermute | solution.py:445
  36.9 1.1 %collective-permute-done.16.more_4_ = f32[128,256]{1,0:T(8,128)S(1)} collective-permute-done((f32[128,256]{1,0:T(8,128)S(1)}, f32[128,256]{1,0:T(8,128)S(1)}, u32[]{:S(2)}, u32[]{:S(2)}) %collective-permute-start.16) | collective-permute-done | bytes 131104 | tf_op jit(solution)/shard_map/ppermute | solution.py:445
  38.9 1.5 %collective-permute-start.20 = (f32[48,256]{1,0:T(8,128)S(1)}, f32[48,256]{1,0:T(8,128)S(1)}, u32[]{:S(2)}, u32[]{:S(2)}) collective-permute-start(f32[48,256]{1,0:T(8,128)S(1)} %coarse_root.1.first), channel_id=1, source_target_pairs={{0,5},{1,4},{2,7},{3,6},{4,1},{5,0},{6,3},{7,2},{8,13},{9,12},{10,... | collective-permute-start | bytes 147464 | tf_op jit(solution)/shard_map/ppermute | solution.py:550
  41.1 1.4 %collective-permute-start.18 = (f32[48,256]{1,0:T(8,128)S(1)}, f32[48,256]{1,0:T(8,128)S(1)}, u32[]{:S(2)}, u32[]{:S(2)}) collective-permute-start(f32[48,256]{1,0:T(8,128)S(1)} %coarse_root.1.first), channel_id=1, source_target_pairs={{0,1},{1,0},{2,3},{3,2},{4,5},{5,4},{6,7},{7,6},{8,9},{9,8},{10,11... | collective-permute-start | bytes 147464 | tf_op jit(solution)/shard_map/ppermute | solution.py:550
  42.5 1.8 %collective-permute-done.20.more_2_ = f32[48,256]{1,0:T(8,128)S(1)} collective-permute-done((f32[48,256]{1,0:T(8,128)S(1)}, f32[48,256]{1,0:T(8,128)S(1)}, u32[]{:S(2)}, u32[]{:S(2)}) %collective-permute-start.20) | collective-permute-done | bytes 49184 | tf_op jit(solution)/shard_map/ppermute | solution.py:550
  45.7 0.9 %collective-permute-done.21.other = f32[32,256]{1,0:T(8,128)S(1)} collective-permute-done((f32[32,256]{1,0:T(8,128)S(1)}, f32[32,256]{1,0:T(8,128)S(1)}, u32[]{:S(2)}, u32[]{:S(2)}) %collective-permute-start.21) | collective-permute-done | bytes 32800 | tf_op jit(solution)/shard_map/ppermute | solution.py:558
  46.7 1.2 %update_last.1 = f32[1024,256]{1,0:T(8,128)} custom-call(f32[1024,256]{1,0:T(8,128)S(1)} %base.3, bf16[1024,96]{1,0:T(8,128)(2,1)S(1)} %get-tuple-element.49.modes_t, f32[32,256]{1,0:T(8,128)S(1)} %get-tuple-element.71.own, f32[32,256]{1,0:T(8,128)S(1)} %collective-permute-done.21.other), custom_call_target="tpu_custom_call" | custom-call | tf_op jit(solution)/shard_map/update_last/pallas_call | solution.py:102
  (45 shorter events, 7.0 us)
Async XLA Ops:
  2.7 8.7 %collective-permute-start = (f32[136,256]{1,0:T(8,128)S(1)}, f32[136,256]{1,0:T(8,128)S(1)}, u32[]{:S(2)}, u32[]{:S(2)}) collective-permute-start(f32[136,256]{1,0:T(8,128)S(1)} %get-tuple-element.44), channel_id=1, source_target_pairs={{0,6},{1,7},{2,4},{3,5},{4,2},{5,3},{6,0},{7,1},{8,14},{9,15},{10,... | collective-permute-start | bytes 417800 | tf_op jit(solution)/shard_map/ppermute | solution.py:445
  5.2 6.3 %collective-permute-start.1 = (f32[136,256]{1,0:T(8,128)S(1)}, f32[136,256]{1,0:T(8,128)S(1)}, u32[]{:S(2)}, u32[]{:S(2)}) collective-permute-start(f32[136,256]{1,0:T(8,128)S(1)} %get-tuple-element.45), channel_id=1, source_target_pairs={{0,1},{1,0},{2,3},{3,2},{4,5},{5,4},{6,7},{7,6},{8,9},{9,8},{10,11... | collective-permute-start | bytes 417800 | tf_op jit(solution)/shard_map/ppermute | solution.py:445
  6.7 6.0 %collective-permute-start.2 = (f32[136,256]{1,0:T(8,128)S(1)}, f32[136,256]{1,0:T(8,128)S(1)}, u32[]{:S(2)}, u32[]{:S(2)}) collective-permute-start(f32[136,256]{1,0:T(8,128)S(1)} %get-tuple-element.46), channel_id=1, source_target_pairs={{0,8},{1,9},{2,10},{3,11},{4,12},{5,13},{6,14},{7,15},{8,0},{9,1},... | collective-permute-start | bytes 417800 | tf_op jit(solution)/shard_map/ppermute | solution.py:445
  8.3 4.4 %collective-permute-start.3 = (f32[136,256]{1,0:T(8,128)S(1)}, f32[136,256]{1,0:T(8,128)S(1)}, u32[]{:S(2)}, u32[]{:S(2)}) collective-permute-start(f32[136,256]{1,0:T(8,128)S(1)} %get-tuple-element.47), channel_id=1, source_target_pairs={{0,2},{1,3},{2,0},{3,1},{4,6},{5,7},{6,4},{7,5},{8,16},{9,17},{10,... | collective-permute-start | bytes 417800 | tf_op jit(solution)/shard_map/ppermute | solution.py:445
  8.4 4.3 %collective-permute-start.4 = (f32[136,256]{1,0:T(8,128)S(1)}, f32[136,256]{1,0:T(8,128)S(1)}, u32[]{:S(2)}, u32[]{:S(2)}) collective-permute-start(f32[136,256]{1,0:T(8,128)S(1)} %get-tuple-element.48), channel_id=1, source_target_pairs={{0,2},{1,3},{2,0},{3,1},{4,6},{5,7},{6,4},{7,5},{8,10},{9,11},{10,... | collective-permute-start | bytes 417800 | tf_op jit(solution)/shard_map/ppermute | solution.py:445
  8.8 11.7 %copy-start.3 = (f32[16,64]{1,0:T(8,128)S(1)}, f32[16,64]{1,0:T(8,128)}, u32[]{:S(2)}) copy-start(f32[16,64]{1,0:T(8,128)} %root_inverse.3) | copy-start | bytes 12292
  8.8 18.2 %copy-start.1 = (bf16[1,1,1,1024,256]{4,3,2,1,0:T(8,128)(2,1)S(1)}, bf16[1,1,1,1024,256]{4,3,2,1,0:T(8,128)(2,1)}, u32[]{:S(2)}) copy-start(bf16[1,1,1,1024,256]{4,3,2,1,0:T(8,128)(2,1)} %param.10) | copy-start | bytes 1572868
  13.0 2.8 %collective-permute-start.5 = (f32[64,256]{1,0:T(8,128)S(1)}, f32[64,256]{1,0:T(8,128)S(1)}, u32[]{:S(2)}, u32[]{:S(2)}) collective-permute-start(f32[64,256]{1,0:T(8,128)S(1)} %get-tuple-element.52), channel_id=1, source_target_pairs={{0,2},{1,3},{2,0},{3,1},{4,6},{5,7},{6,4},{7,5},{8,10},{9,11},{10,... | collective-permute-start | bytes 196616 | tf_op jit(solution)/shard_map/ppermute | solution.py:499
  13.1 5.1 %collective-permute-start.7 = (f32[16,256]{1,0:T(8,128)S(1)}, f32[16,256]{1,0:T(8,128)S(1)}, u32[]{:S(2)}, u32[]{:S(2)}) collective-permute-start(f32[16,256]{1,0:T(8,128)S(1)} %get-tuple-element.54.own.root), channel_id=1, source_target_pairs={{0,8},{1,9},{2,10},{3,11},{4,12},{5,13},{6,14},{7,15},{8,0},{9,1},... | collective-permute-start | bytes 49160 | tf_op jit(solution)/shard_map/ppermute | solution.py:441
  15.8 4.7 %collective-permute-start.6 = (f32[16,256]{1,0:T(8,128)S(1)}, f32[16,256]{1,0:T(8,128)S(1)}, u32[]{:S(2)}, u32[]{:S(2)}) collective-permute-start(f32[16,256]{1,0:T(8,128)S(1)} %core_sum.2), channel_id=1, source_target_pairs={{0,16},{1,17},{2,26},{3,27},{4,20},{5,21},{6,30},{7,31},{8,24},{9,... | collective-permute-start | bytes 49160 | tf_op jit(solution)/shard_map/ppermute | solution.py:441
  20.7 5.1 %collective-permute-start.10 = (f32[48,256]{1,0:T(8,128)S(1)}, f32[48,256]{1,0:T(8,128)S(1)}, u32[]{:S(2)}, u32[]{:S(2)}) collective-permute-start(f32[48,256]{1,0:T(8,128)S(1)} %root_part.1.first), channel_id=1, source_target_pairs={{0,5},{1,4},{2,7},{3,6},{4,1},{5,0},{6,3},{7,2},{8,13},{9,12},{10,... | collective-permute-start | bytes 147464 | tf_op jit(solution)/shard_map/ppermute | solution.py:550
  21.2 4.6 %collective-permute-start.9 = (f32[48,256]{1,0:T(8,128)S(1)}, f32[48,256]{1,0:T(8,128)S(1)}, u32[]{:S(2)}, u32[]{:S(2)}) collective-permute-start(f32[48,256]{1,0:T(8,128)S(1)} %root_part.1.first), channel_id=1, source_target_pairs={{0,4},{1,5},{2,6},{3,7},{4,0},{5,1},{6,2},{7,3},{8,12},{9,13},{10,... | collective-permute-start | bytes 147464 | tf_op jit(solution)/shard_map/ppermute | solution.py:550
  22.7 4.1 %collective-permute-start.8 = (f32[48,256]{1,0:T(8,128)S(1)}, f32[48,256]{1,0:T(8,128)S(1)}, u32[]{:S(2)}, u32[]{:S(2)}) collective-permute-start(f32[48,256]{1,0:T(8,128)S(1)} %root_part.1.first), channel_id=1, source_target_pairs={{0,1},{1,0},{2,3},{3,2},{4,5},{5,4},{6,7},{7,6},{8,9},{9,8},{10,11... | collective-permute-start | bytes 147464 | tf_op jit(solution)/shard_map/ppermute | solution.py:550
  26.9 1.3 %collective-permute-start.11 = (f32[32,256]{1,0:T(8,128)S(1)}, f32[32,256]{1,0:T(8,128)S(1)}, u32[]{:S(2)}, u32[]{:S(2)}) collective-permute-start(f32[32,256]{1,0:T(8,128)S(1)} %get-tuple-element.56), channel_id=1, source_target_pairs={{0,2},{1,3},{2,0},{3,1},{4,6},{5,7},{6,4},{7,5},{8,10},{9,11},{10,... | collective-permute-start | bytes 98312 | tf_op jit(solution)/shard_map/ppermute | solution.py:558
  29.4 3.4 %collective-permute-start.12 = (f32[176,256]{1,0:T(8,128)S(1)}, f32[176,256]{1,0:T(8,128)S(1)}, u32[]{:S(2)}, u32[]{:S(2)}) collective-permute-start(f32[176,256]{1,0:T(8,128)S(1)} %get-tuple-element.64), channel_id=1, source_target_pairs={{0,2},{1,3},{2,0},{3,1},{4,6},{5,7},{6,4},{7,5},{8,10},{9,11},{10,... | collective-permute-start | bytes 540680 | tf_op jit(solution)/shard_map/ppermute | solution.py:445
  29.9 8.1 %collective-permute-start.13 = (f32[176,256]{1,0:T(8,128)S(1)}, f32[176,256]{1,0:T(8,128)S(1)}, u32[]{:S(2)}, u32[]{:S(2)}) collective-permute-start(f32[176,256]{1,0:T(8,128)S(1)} %get-tuple-element.65), channel_id=1, source_target_pairs={{0,8},{1,9},{2,10},{3,11},{4,12},{5,13},{6,14},{7,15},{8,0},{9,1},... | collective-permute-start | bytes 540680 | tf_op jit(solution)/shard_map/ppermute | solution.py:445
  31.0 4.0 %collective-permute-start.14 = (f32[128,256]{1,0:T(8,128)S(1)}, f32[128,256]{1,0:T(8,128)S(1)}, u32[]{:S(2)}, u32[]{:S(2)}) collective-permute-start(f32[128,256]{1,0:T(8,128)S(1)} %get-tuple-element.66), channel_id=1, source_target_pairs={{0,2},{1,3},{2,0},{3,1},{4,6},{5,7},{6,4},{7,5},{8,16},{9,17},{10,... | collective-permute-start | bytes 393224 | tf_op jit(solution)/shard_map/ppermute | solution.py:445
  31.0 5.9 %collective-permute-start.15 = (f32[128,256]{1,0:T(8,128)S(1)}, f32[128,256]{1,0:T(8,128)S(1)}, u32[]{:S(2)}, u32[]{:S(2)}) collective-permute-start(f32[128,256]{1,0:T(8,128)S(1)} %get-tuple-element.67), channel_id=1, source_target_pairs={{0,1},{1,0},{2,3},{3,2},{4,5},{5,4},{6,7},{7,6},{8,9},{9,8},{10,11... | collective-permute-start | bytes 393224 | tf_op jit(solution)/shard_map/ppermute | solution.py:445
  32.5 5.5 %collective-permute-start.16 = (f32[128,256]{1,0:T(8,128)S(1)}, f32[128,256]{1,0:T(8,128)S(1)}, u32[]{:S(2)}, u32[]{:S(2)}) collective-permute-start(f32[128,256]{1,0:T(8,128)S(1)} %get-tuple-element.68), channel_id=1, source_target_pairs={{0,6},{1,7},{2,4},{3,5},{4,2},{5,3},{6,0},{7,1},{8,14},{9,15},{10,... | collective-permute-start | bytes 393224 | tf_op jit(solution)/shard_map/ppermute | solution.py:445
  32.9 5.7 %collective-permute-start.17 = (f32[48,256]{1,0:T(8,128)S(1)}, f32[48,256]{1,0:T(8,128)S(1)}, u32[]{:S(2)}, u32[]{:S(2)}) collective-permute-start(f32[48,256]{1,0:T(8,128)S(1)} %core_sum.3), channel_id=1, source_target_pairs={{0,16},{1,17},{2,26},{3,27},{4,20},{5,21},{6,30},{7,31},{8,24},{9,... | collective-permute-start | bytes 147464 | tf_op jit(solution)/shard_map/ppermute | solution.py:441
  38.9 5.4 %collective-permute-start.20 = (f32[48,256]{1,0:T(8,128)S(1)}, f32[48,256]{1,0:T(8,128)S(1)}, u32[]{:S(2)}, u32[]{:S(2)}) collective-permute-start(f32[48,256]{1,0:T(8,128)S(1)} %coarse_root.1.first), channel_id=1, source_target_pairs={{0,5},{1,4},{2,7},{3,6},{4,1},{5,0},{6,3},{7,2},{8,13},{9,12},{10,... | collective-permute-start | bytes 147464 | tf_op jit(solution)/shard_map/ppermute | solution.py:550
  40.4 4.1 %collective-permute-start.19 = (f32[48,256]{1,0:T(8,128)S(1)}, f32[48,256]{1,0:T(8,128)S(1)}, u32[]{:S(2)}, u32[]{:S(2)}) collective-permute-start(f32[48,256]{1,0:T(8,128)S(1)} %coarse_root.1.first), channel_id=1, source_target_pairs={{0,4},{1,5},{2,6},{3,7},{4,0},{5,1},{6,2},{7,3},{8,12},{9,13},{10,... | collective-permute-start | bytes 147464 | tf_op jit(solution)/shard_map/ppermute | solution.py:550
  41.1 4.1 %collective-permute-start.18 = (f32[48,256]{1,0:T(8,128)S(1)}, f32[48,256]{1,0:T(8,128)S(1)}, u32[]{:S(2)}, u32[]{:S(2)}) collective-permute-start(f32[48,256]{1,0:T(8,128)S(1)} %coarse_root.1.first), channel_id=1, source_target_pairs={{0,1},{1,0},{2,3},{3,2},{4,5},{5,4},{6,7},{7,6},{8,9},{9,8},{10,11... | collective-permute-start | bytes 147464 | tf_op jit(solution)/shard_map/ppermute | solution.py:550
  45.4 1.3 %collective-permute-start.21 = (f32[32,256]{1,0:T(8,128)S(1)}, f32[32,256]{1,0:T(8,128)S(1)}, u32[]{:S(2)}, u32[]{:S(2)}) collective-permute-start(f32[32,256]{1,0:T(8,128)S(1)} %get-tuple-element.72), channel_id=1, source_target_pairs={{0,2},{1,3},{2,0},{3,1},{4,6},{5,7},{6,4},{7,5},{8,10},{9,11},{10,... | collective-permute-start | bytes 98312 | tf_op jit(solution)/shard_map/ppermute | solution.py:558
  (3 other events, 27.6 us)

commit v9 on v8

--- a/solution.py
+++ b/solution.py
@@ -83,6 +83,10 @@
 
 def core_offset(pair):
     return jnp.where(lax.axis_index("gy") % 2 == 0, pair[0], pair[1])
+
+
+def crossing(dy, dz):
+    return int(dy != 0 or dz != 0)
 
 
 def split(value):
@@ -319,7 +323,7 @@
     column = lax.broadcasted_iota(jnp.int32, (order, depth), 1)
     wanted = jnp.full((order, depth), -1, jnp.int32)
     for k, (dy, dz) in enumerate(members):
-        at_y = 2 * source(y // 2, dy, half) + y % 2
+        at_y = 2 * source(y // 2, dy, half) + (y + crossing(dy, dz)) % 2
         first = (at_y * sizes[1] + source(z, dz, sizes[1])) * modes
         inside = jnp.logical_and(column >= k * modes, column < (k + 1) * modes)
         wanted = jnp.where(inside, first + column - k * modes, wanted)
@@ -436,7 +440,7 @@
         pairs = []
         for place in itertools.product(*map(range, sizes)):
             step = offset if isinstance(offset, int) else offset[place[1] % 2]
-            there = (partner(place[0], step, sizes[0]),) + place[1:]
+            there = (partner(place[0], step, sizes[0]), place[1], place[2])
             pairs.append((flat(sizes, place), flat(sizes, there)))
         return lax.ppermute(value, AXES, pairs)
 
@@ -542,12 +546,12 @@
             base = base_of(later, solution, placed, halos)
         pieces = []
         for dy, dz in members[1:]:
-            moves = [
-                (y * sizes[2] + z, (2 * partner(y // 2, dy, half) + y % 2) * sizes[2] + partner(z, dz, sizes[2]))
-                for y in range(sizes[1])
-                for z in range(sizes[2])
-            ]
-            pieces.append(lax.ppermute(message, ("gy", "gz"), moves))
+            moves = []
+            for place in itertools.product(*map(range, sizes)):
+                x, y, z = place
+                at_y = 2 * partner(y // 2, dy, half) + (y + crossing(dy, dz)) % 2
+                moves.append((flat(sizes, place), flat(sizes, (x, at_y, partner(z, dz, sizes[2])))))
+            pieces.append(lax.ppermute(message, AXES, moves))
         own, given = call(
             functools.partial(pair_kernel, mode_count),
             [held(mode_count), held(mode_count)],

time: 48 us -> 47.2 us (0.983)
  starting transfers between devices: 24 us -> 22.4 us
  waiting for transfers between devices: 13.5 us -> 14.3 us
    ppermute x6, starting transfers between devices: 7.15 us -> 5.71 us  [per_device(): pieces.append(lax.ppermute(message, AXES, moves))]
    ppermute x6, waiting for transfers between devices: 5.1 us -> 5.98 us  [per_device(): pieces.append(lax.ppermute(message, AXES, moves))]
  transfers between devices with their start and end apart: 22 -> 22, of which waited for: 12 -> 11; matrix products, arithmetic and copies ran while one was open for 0% -> 0% of each run, Pallas kernels for 8% -> 9%
where the time goes in v9:
time: 47.2 us; the launch traced here: 47.1 us
  starting transfers between devices  22.4 us (47%)
  waiting for transfers between devices  14.3 us (30%)
  Pallas kernels  10.2 us (22%)
    pallas_call x15, Pallas kernels, call(): pl.pallas_call(body, out_shape=[item(shape, dtype) for item, shape, dtype...  10.2 us
    ppermute x10, starting transfers between devices, exchange(): lax.ppermute(message, AXES, swap_pairs(sizes, dim, odd))  9.21 us
    ppermute x3, starting transfers between devices, along(): return lax.ppermute(value, AXES, pairs)  7.04 us
    ppermute x6, waiting for transfers between devices, per_device(): pieces.append(lax.ppermute(message, AXES, moves))  5.98 us
    ppermute x6, starting transfers between devices, per_device(): pieces.append(lax.ppermute(message, AXES, moves))  5.71 us
    ppermute x10, waiting for transfers between devices, exchange(): lax.ppermute(message, AXES, swap_pairs(sizes, dim, odd))  3.98 us
    ppermute x3, waiting for transfers between devices, along(): return lax.ppermute(value, AXES, pairs)  3.43 us
  transfers between devices with their start and end apart: 22, of which 11 were waited for; matrix products, arithmetic and copies ran while one was open for 0% of the time, Pallas kernels for 9%

profile of v9, /device:TPU:0, one launch (start us, length us, event | category | flops | bytes accessed | tf_op | source)
XLA Modules:
  0.0 47.1 jit_solution(2041963286319062733)
XLA Ops:
  0.0 2.7 %first_product.1 = (bf16[1024,1024]{1,0:T(8,128)(2,1)S(1)}, f32[32,1024]{1,0:T(8,128)S(1)}, f32[16,32]{1,0:T(8,128)S(1)}, f32[1024,256]{1,0:T(8,128)S(1)}, f32[1...) custom-call(s32[1,8]{1,0:T(1,128)} %bitcast.23, ...), custom_call_target="tpu_custom_call" | custom-call | tf_op jit(solution)/shard_map/first_product/pallas_call | solution.py:106
  2.7 2.4 %collective-permute-start = (f32[136,256]{1,0:T(8,128)S(1)}, f32[136,256]{1,0:T(8,128)S(1)}, u32[]{:S(2)}, u32[]{:S(2)}) collective-permute-start(f32[136,256]{1,0:T(8,128)S(1)} %get-tuple-element.44), channel_id=1, source_target_pairs={{0,6},{1,7},{2,4},{3,5},{4,2},{5,3},{6,0},{7,1},{8,14},{9,15},{10,... | collective-permute-start | bytes 417800 | tf_op jit(solution)/shard_map/ppermute | solution.py:449
  5.2 1.5 %collective-permute-start.1 = (f32[136,256]{1,0:T(8,128)S(1)}, f32[136,256]{1,0:T(8,128)S(1)}, u32[]{:S(2)}, u32[]{:S(2)}) collective-permute-start(f32[136,256]{1,0:T(8,128)S(1)} %get-tuple-element.45), channel_id=1, source_target_pairs={{0,1},{1,0},{2,3},{3,2},{4,5},{5,4},{6,7},{7,6},{8,9},{9,8},{10,11... | collective-permute-start | bytes 417800 | tf_op jit(solution)/shard_map/ppermute | solution.py:449
  6.7 1.6 %collective-permute-start.2 = (f32[136,256]{1,0:T(8,128)S(1)}, f32[136,256]{1,0:T(8,128)S(1)}, u32[]{:S(2)}, u32[]{:S(2)}) collective-permute-start(f32[136,256]{1,0:T(8,128)S(1)} %get-tuple-element.46), channel_id=1, source_target_pairs={{0,8},{1,9},{2,10},{3,11},{4,12},{5,13},{6,14},{7,15},{8,0},{9,1},... | collective-permute-start | bytes 417800 | tf_op jit(solution)/shard_map/ppermute | solution.py:449
  8.8 2.6 %constants.1 = (bf16[1024,96]{1,0:T(8,128)(2,1)S(1)}, f32[1024,128]{1,0:T(8,128)S(1)}, bf16[96,640]{1,0:T(8,128)(2,1)S(1)}, bf16[1024,1024]{1,0:T(8,128)(2,1)S(1...) custom-call(s32[1,8]{1,0:T(1,128)} %bitcast.24, ...), custom_call_target="tpu_custom_call" | custom-call | tf_op jit(solution)/shard_map/constants/pallas_call | solution.py:106
  11.4 1.3 %collective-permute-done.2.more_2_ = f32[136,256]{1,0:T(8,128)S(1)} collective-permute-done((f32[136,256]{1,0:T(8,128)S(1)}, f32[136,256]{1,0:T(8,128)S(1)}, u32[]{:S(2)}, u32[]{:S(2)}) %collective-permute-start.2) | collective-permute-done | bytes 139296 | tf_op jit(solution)/shard_map/ppermute | solution.py:449
  13.1 2.7 %collective-permute-start.7 = (f32[16,256]{1,0:T(8,128)S(1)}, f32[16,256]{1,0:T(8,128)S(1)}, u32[]{:S(2)}, u32[]{:S(2)}) collective-permute-start(f32[16,256]{1,0:T(8,128)S(1)} %get-tuple-element.54.own.root), channel_id=1, source_target_pairs={{0,8},{1,9},{2,10},{3,11},{4,12},{5,13},{6,14},{7,15},{8,0},{9,1},... | collective-permute-start | bytes 49160 | tf_op jit(solution)/shard_map/ppermute | solution.py:445
  15.8 2.4 %collective-permute-start.6 = (f32[16,256]{1,0:T(8,128)S(1)}, f32[16,256]{1,0:T(8,128)S(1)}, u32[]{:S(2)}, u32[]{:S(2)}) collective-permute-start(f32[16,256]{1,0:T(8,128)S(1)} %core_sum.2), channel_id=1, source_target_pairs={{0,16},{1,17},{2,26},{3,27},{4,20},{5,21},{6,30},{7,31},{8,24},{9,... | collective-permute-start | bytes 49160 | tf_op jit(solution)/shard_map/ppermute | solution.py:445
  18.2 2.4 %collective-permute-done.6.more_0_ = f32[16,256]{1,0:T(8,128)S(1)} collective-permute-done((f32[16,256]{1,0:T(8,128)S(1)}, f32[16,256]{1,0:T(8,128)S(1)}, u32[]{:S(2)}, u32[]{:S(2)}) %collective-permute-start.6) | collective-permute-done | bytes 16416 | tf_op jit(solution)/shard_map/ppermute | solution.py:445
  20.8 1.6 %collective-permute-start.9 = (f32[48,256]{1,0:T(8,128)S(1)}, f32[48,256]{1,0:T(8,128)S(1)}, u32[]{:S(2)}, u32[]{:S(2)}) collective-permute-start(f32[48,256]{1,0:T(8,128)S(1)} %root_part.1.first), channel_id=1, source_target_pairs={{0,6},{1,7},{2,4},{3,5},{4,2},{5,3},{6,0},{7,1},{8,14},{9,15},{10,... | collective-permute-start | bytes 147464 | tf_op jit(solution)/shard_map/ppermute | solution.py:554
  22.4 1.1 %collective-permute-start.8 = (f32[48,256]{1,0:T(8,128)S(1)}, f32[48,256]{1,0:T(8,128)S(1)}, u32[]{:S(2)}, u32[]{:S(2)}) collective-permute-start(f32[48,256]{1,0:T(8,128)S(1)} %root_part.1.first), channel_id=1, source_target_pairs={{0,3},{1,2},{2,1},{3,0},{4,7},{5,6},{6,5},{7,4},{8,11},{9,10},{10,... | collective-permute-start | bytes 147464 | tf_op jit(solution)/shard_map/ppermute | solution.py:554
  23.7 1.8 %collective-permute-done.10.more_2_ = f32[48,256]{1,0:T(8,128)S(1)} collective-permute-done((f32[48,256]{1,0:T(8,128)S(1)}, f32[48,256]{1,0:T(8,128)S(1)}, u32[]{:S(2)}, u32[]{:S(2)}) %collective-permute-start.10) | collective-permute-done | bytes 49184 | tf_op jit(solution)/shard_map/ppermute | solution.py:554
  25.6 1.1 %collective-permute-done.8.more_0_ = f32[48,256]{1,0:T(8,128)S(1)} collective-permute-done((f32[48,256]{1,0:T(8,128)S(1)}, f32[48,256]{1,0:T(8,128)S(1)}, u32[]{:S(2)}, u32[]{:S(2)}) %collective-permute-start.8) | collective-permute-done | bytes 49184 | tf_op jit(solution)/shard_map/ppermute | solution.py:554
  28.1 1.2 %update_product.1 = (f32[1024,256]{1,0:T(8,128)S(1)}, f32[1024,256]{1,0:T(8,128)S(1)}, f32[32,256]{1,0:T(8,128)S(1)}, f32[48,256]{1,0:T(8,128)S(1)}, f32[176,256...) custom-call(f32[1024,256]{1,0:T(8,128)S(1)} %base.2, ...), custom_call_target="tpu_custom_call" | custom-call | tf_op jit(solution)/shard_map/update_product/pallas_call | solution.py:106
  30.6 1.1 %collective-permute-start.15 = (f32[128,256]{1,0:T(8,128)S(1)}, f32[128,256]{1,0:T(8,128)S(1)}, u32[]{:S(2)}, u32[]{:S(2)}) collective-permute-start(f32[128,256]{1,0:T(8,128)S(1)} %get-tuple-element.67), channel_id=1, source_target_pairs={{0,1},{1,0},{2,3},{3,2},{4,5},{5,4},{6,7},{7,6},{8,9},{9,8},{10,11... | collective-permute-start | bytes 393224 | tf_op jit(solution)/shard_map/ppermute | solution.py:449
  31.6 0.8 %collective-permute-start.16 = (f32[128,256]{1,0:T(8,128)S(1)}, f32[128,256]{1,0:T(8,128)S(1)}, u32[]{:S(2)}, u32[]{:S(2)}) collective-permute-start(f32[128,256]{1,0:T(8,128)S(1)} %get-tuple-element.68), channel_id=1, source_target_pairs={{0,6},{1,7},{2,4},{3,5},{4,2},{5,3},{6,0},{7,1},{8,14},{9,15},{10,... | collective-permute-start | bytes 393224 | tf_op jit(solution)/shard_map/ppermute | solution.py:449
  32.5 2.0 %collective-permute-start.17 = (f32[48,256]{1,0:T(8,128)S(1)}, f32[48,256]{1,0:T(8,128)S(1)}, u32[]{:S(2)}, u32[]{:S(2)}) collective-permute-start(f32[48,256]{1,0:T(8,128)S(1)} %core_sum.3), channel_id=1, source_target_pairs={{0,16},{1,17},{2,26},{3,27},{4,20},{5,21},{6,30},{7,31},{8,24},{9,... | collective-permute-start | bytes 147464 | tf_op jit(solution)/shard_map/ppermute | solution.py:445
  34.5 2.0 %collective-permute-done.15.more_3_ = f32[128,256]{1,0:T(8,128)S(1)} collective-permute-done((f32[128,256]{1,0:T(8,128)S(1)}, f32[128,256]{1,0:T(8,128)S(1)}, u32[]{:S(2)}, u32[]{:S(2)}) %collective-permute-start.15) | collective-permute-done | bytes 131104 | tf_op jit(solution)/shard_map/ppermute | solution.py:449
  37.1 1.1 %collective-permute-done.17.more_5_ = f32[48,256]{1,0:T(8,128)S(1)} collective-permute-done((f32[48,256]{1,0:T(8,128)S(1)}, f32[48,256]{1,0:T(8,128)S(1)}, u32[]{:S(2)}, u32[]{:S(2)}) %collective-permute-start.17) | collective-permute-done | bytes 49184 | tf_op jit(solution)/shard_map/ppermute | solution.py:445
  38.5 1.1 %collective-permute-start.20 = (f32[48,256]{1,0:T(8,128)S(1)}, f32[48,256]{1,0:T(8,128)S(1)}, u32[]{:S(2)}, u32[]{:S(2)}) collective-permute-start(f32[48,256]{1,0:T(8,128)S(1)} %coarse_root.1.first), channel_id=1, source_target_pairs={{0,7},{1,6},{2,5},{3,4},{4,3},{5,2},{6,1},{7,0},{8,15},{9,14},{10,... | collective-permute-start | bytes 147464 | tf_op jit(solution)/shard_map/ppermute | solution.py:554
  39.8 1.6 %collective-permute-start.18 = (f32[48,256]{1,0:T(8,128)S(1)}, f32[48,256]{1,0:T(8,128)S(1)}, u32[]{:S(2)}, u32[]{:S(2)}) collective-permute-start(f32[48,256]{1,0:T(8,128)S(1)} %coarse_root.1.first), channel_id=1, source_target_pairs={{0,3},{1,2},{2,1},{3,0},{4,7},{5,6},{6,5},{7,4},{8,11},{9,10},{10,... | collective-permute-start | bytes 147464 | tf_op jit(solution)/shard_map/ppermute | solution.py:554
  41.4 1.9 %collective-permute-done.20.more_2_ = f32[48,256]{1,0:T(8,128)S(1)} collective-permute-done((f32[48,256]{1,0:T(8,128)S(1)}, f32[48,256]{1,0:T(8,128)S(1)}, u32[]{:S(2)}, u32[]{:S(2)}) %collective-permute-start.20) | collective-permute-done | bytes 49184 | tf_op jit(solution)/shard_map/ppermute | solution.py:554
  43.3 1.1 %collective-permute-done.18.more_0_ = f32[48,256]{1,0:T(8,128)S(1)} collective-permute-done((f32[48,256]{1,0:T(8,128)S(1)}, f32[48,256]{1,0:T(8,128)S(1)}, u32[]{:S(2)}, u32[]{:S(2)}) %collective-permute-start.18) | collective-permute-done | bytes 49184 | tf_op jit(solution)/shard_map/ppermute | solution.py:554
  45.8 1.2 %update_last.1 = f32[1024,256]{1,0:T(8,128)} custom-call(f32[1024,256]{1,0:T(8,128)S(1)} %base.3, bf16[1024,96]{1,0:T(8,128)(2,1)S(1)} %get-tuple-element.49.modes_t, f32[32,256]{1,0:T(8,128)S(1)} %get-tuple-element.71.own, f32[32,256]{1,0:T(8,128)S(1)} %collective-permute-done.21.other), custom_call_target="tpu_custom_call" | custom-call | tf_op jit(solution)/shard_map/update_last/pallas_call | solution.py:106
  (45 shorter events, 6.7 us)
Async XLA Ops:
  2.7 8.7 %collective-permute-start = (f32[136,256]{1,0:T(8,128)S(1)}, f32[136,256]{1,0:T(8,128)S(1)}, u32[]{:S(2)}, u32[]{:S(2)}) collective-permute-start(f32[136,256]{1,0:T(8,128)S(1)} %get-tuple-element.44), channel_id=1, source_target_pairs={{0,6},{1,7},{2,4},{3,5},{4,2},{5,3},{6,0},{7,1},{8,14},{9,15},{10,... | collective-permute-start | bytes 417800 | tf_op jit(solution)/shard_map/ppermute | solution.py:449
  5.2 6.3 %collective-permute-start.1 = (f32[136,256]{1,0:T(8,128)S(1)}, f32[136,256]{1,0:T(8,128)S(1)}, u32[]{:S(2)}, u32[]{:S(2)}) collective-permute-start(f32[136,256]{1,0:T(8,128)S(1)} %get-tuple-element.45), channel_id=1, source_target_pairs={{0,1},{1,0},{2,3},{3,2},{4,5},{5,4},{6,7},{7,6},{8,9},{9,8},{10,11... | collective-permute-start | bytes 417800 | tf_op jit(solution)/shard_map/ppermute | solution.py:449
  6.7 6.0 %collective-permute-start.2 = (f32[136,256]{1,0:T(8,128)S(1)}, f32[136,256]{1,0:T(8,128)S(1)}, u32[]{:S(2)}, u32[]{:S(2)}) collective-permute-start(f32[136,256]{1,0:T(8,128)S(1)} %get-tuple-element.46), channel_id=1, source_target_pairs={{0,8},{1,9},{2,10},{3,11},{4,12},{5,13},{6,14},{7,15},{8,0},{9,1},... | collective-permute-start | bytes 417800 | tf_op jit(solution)/shard_map/ppermute | solution.py:449
  8.3 4.4 %collective-permute-start.3 = (f32[136,256]{1,0:T(8,128)S(1)}, f32[136,256]{1,0:T(8,128)S(1)}, u32[]{:S(2)}, u32[]{:S(2)}) collective-permute-start(f32[136,256]{1,0:T(8,128)S(1)} %get-tuple-element.47), channel_id=1, source_target_pairs={{0,2},{1,3},{2,0},{3,1},{4,6},{5,7},{6,4},{7,5},{8,16},{9,17},{10,... | collective-permute-start | bytes 417800 | tf_op jit(solution)/shard_map/ppermute | solution.py:449
  8.4 4.3 %collective-permute-start.4 = (f32[136,256]{1,0:T(8,128)S(1)}, f32[136,256]{1,0:T(8,128)S(1)}, u32[]{:S(2)}, u32[]{:S(2)}) collective-permute-start(f32[136,256]{1,0:T(8,128)S(1)} %get-tuple-element.48), channel_id=1, source_target_pairs={{0,2},{1,3},{2,0},{3,1},{4,6},{5,7},{6,4},{7,5},{8,10},{9,11},{10,... | collective-permute-start | bytes 417800 | tf_op jit(solution)/shard_map/ppermute | solution.py:449
  8.8 11.7 %copy-start.3 = (f32[16,64]{1,0:T(8,128)S(1)}, f32[16,64]{1,0:T(8,128)}, u32[]{:S(2)}) copy-start(f32[16,64]{1,0:T(8,128)} %root_inverse.3) | copy-start | bytes 12292
  8.8 18.2 %copy-start.1 = (bf16[1,1,1,1024,256]{4,3,2,1,0:T(8,128)(2,1)S(1)}, bf16[1,1,1,1024,256]{4,3,2,1,0:T(8,128)(2,1)}, u32[]{:S(2)}) copy-start(bf16[1,1,1,1024,256]{4,3,2,1,0:T(8,128)(2,1)} %param.10) | copy-start | bytes 1572868
  13.0 2.8 %collective-permute-start.5 = (f32[64,256]{1,0:T(8,128)S(1)}, f32[64,256]{1,0:T(8,128)S(1)}, u32[]{:S(2)}, u32[]{:S(2)}) collective-permute-start(f32[64,256]{1,0:T(8,128)S(1)} %get-tuple-element.52), channel_id=1, source_target_pairs={{0,2},{1,3},{2,0},{3,1},{4,6},{5,7},{6,4},{7,5},{8,10},{9,11},{10,... | collective-permute-start | bytes 196616 | tf_op jit(solution)/shard_map/ppermute | solution.py:503
  13.1 5.1 %collective-permute-start.7 = (f32[16,256]{1,0:T(8,128)S(1)}, f32[16,256]{1,0:T(8,128)S(1)}, u32[]{:S(2)}, u32[]{:S(2)}) collective-permute-start(f32[16,256]{1,0:T(8,128)S(1)} %get-tuple-element.54.own.root), channel_id=1, source_target_pairs={{0,8},{1,9},{2,10},{3,11},{4,12},{5,13},{6,14},{7,15},{8,0},{9,1},... | collective-permute-start | bytes 49160 | tf_op jit(solution)/shard_map/ppermute | solution.py:445
  15.8 4.7 %collective-permute-start.6 = (f32[16,256]{1,0:T(8,128)S(1)}, f32[16,256]{1,0:T(8,128)S(1)}, u32[]{:S(2)}, u32[]{:S(2)}) collective-permute-start(f32[16,256]{1,0:T(8,128)S(1)} %core_sum.2), channel_id=1, source_target_pairs={{0,16},{1,17},{2,26},{3,27},{4,20},{5,21},{6,30},{7,31},{8,24},{9,... | collective-permute-start | bytes 49160 | tf_op jit(solution)/shard_map/ppermute | solution.py:445
  20.7 4.8 %collective-permute-start.10 = (f32[48,256]{1,0:T(8,128)S(1)}, f32[48,256]{1,0:T(8,128)S(1)}, u32[]{:S(2)}, u32[]{:S(2)}) collective-permute-start(f32[48,256]{1,0:T(8,128)S(1)} %root_part.1.first), channel_id=1, source_target_pairs={{0,7},{1,6},{2,5},{3,4},{4,3},{5,2},{6,1},{7,0},{8,15},{9,14},{10,... | collective-permute-start | bytes 147464 | tf_op jit(solution)/shard_map/ppermute | solution.py:554
  20.8 4.8 %collective-permute-start.9 = (f32[48,256]{1,0:T(8,128)S(1)}, f32[48,256]{1,0:T(8,128)S(1)}, u32[]{:S(2)}, u32[]{:S(2)}) collective-permute-start(f32[48,256]{1,0:T(8,128)S(1)} %root_part.1.first), channel_id=1, source_target_pairs={{0,6},{1,7},{2,4},{3,5},{4,2},{5,3},{6,0},{7,1},{8,14},{9,15},{10,... | collective-permute-start | bytes 147464 | tf_op jit(solution)/shard_map/ppermute | solution.py:554
  22.4 4.3 %collective-permute-start.8 = (f32[48,256]{1,0:T(8,128)S(1)}, f32[48,256]{1,0:T(8,128)S(1)}, u32[]{:S(2)}, u32[]{:S(2)}) collective-permute-start(f32[48,256]{1,0:T(8,128)S(1)} %root_part.1.first), channel_id=1, source_target_pairs={{0,3},{1,2},{2,1},{3,0},{4,7},{5,6},{6,5},{7,4},{8,11},{9,10},{10,... | collective-permute-start | bytes 147464 | tf_op jit(solution)/shard_map/ppermute | solution.py:554
  26.8 1.3 %collective-permute-start.11 = (f32[32,256]{1,0:T(8,128)S(1)}, f32[32,256]{1,0:T(8,128)S(1)}, u32[]{:S(2)}, u32[]{:S(2)}) collective-permute-start(f32[32,256]{1,0:T(8,128)S(1)} %get-tuple-element.56), channel_id=1, source_target_pairs={{0,2},{1,3},{2,0},{3,1},{4,6},{5,7},{6,4},{7,5},{8,10},{9,11},{10,... | collective-permute-start | bytes 98312 | tf_op jit(solution)/shard_map/ppermute | solution.py:562
  29.3 3.2 %collective-permute-start.12 = (f32[176,256]{1,0:T(8,128)S(1)}, f32[176,256]{1,0:T(8,128)S(1)}, u32[]{:S(2)}, u32[]{:S(2)}) collective-permute-start(f32[176,256]{1,0:T(8,128)S(1)} %get-tuple-element.64), channel_id=1, source_target_pairs={{0,2},{1,3},{2,0},{3,1},{4,6},{5,7},{6,4},{7,5},{8,10},{9,11},{10,... | collective-permute-start | bytes 540680 | tf_op jit(solution)/shard_map/ppermute | solution.py:449
  29.8 7.4 %collective-permute-start.13 = (f32[176,256]{1,0:T(8,128)S(1)}, f32[176,256]{1,0:T(8,128)S(1)}, u32[]{:S(2)}, u32[]{:S(2)}) collective-permute-start(f32[176,256]{1,0:T(8,128)S(1)} %get-tuple-element.65), channel_id=1, source_target_pairs={{0,8},{1,9},{2,10},{3,11},{4,12},{5,13},{6,14},{7,15},{8,0},{9,1},... | collective-permute-start | bytes 540680 | tf_op jit(solution)/shard_map/ppermute | solution.py:449
  30.6 3.9 %collective-permute-start.14 = (f32[128,256]{1,0:T(8,128)S(1)}, f32[128,256]{1,0:T(8,128)S(1)}, u32[]{:S(2)}, u32[]{:S(2)}) collective-permute-start(f32[128,256]{1,0:T(8,128)S(1)} %get-tuple-element.66), channel_id=1, source_target_pairs={{0,2},{1,3},{2,0},{3,1},{4,6},{5,7},{6,4},{7,5},{8,16},{9,17},{10,... | collective-permute-start | bytes 393224 | tf_op jit(solution)/shard_map/ppermute | solution.py:449
  30.6 5.9 %collective-permute-start.15 = (f32[128,256]{1,0:T(8,128)S(1)}, f32[128,256]{1,0:T(8,128)S(1)}, u32[]{:S(2)}, u32[]{:S(2)}) collective-permute-start(f32[128,256]{1,0:T(8,128)S(1)} %get-tuple-element.67), channel_id=1, source_target_pairs={{0,1},{1,0},{2,3},{3,2},{4,5},{5,4},{6,7},{7,6},{8,9},{9,8},{10,11... | collective-permute-start | bytes 393224 | tf_op jit(solution)/shard_map/ppermute | solution.py:449
  31.6 5.5 %collective-permute-start.16 = (f32[128,256]{1,0:T(8,128)S(1)}, f32[128,256]{1,0:T(8,128)S(1)}, u32[]{:S(2)}, u32[]{:S(2)}) collective-permute-start(f32[128,256]{1,0:T(8,128)S(1)} %get-tuple-element.68), channel_id=1, source_target_pairs={{0,6},{1,7},{2,4},{3,5},{4,2},{5,3},{6,0},{7,1},{8,14},{9,15},{10,... | collective-permute-start | bytes 393224 | tf_op jit(solution)/shard_map/ppermute | solution.py:449
  32.5 5.7 %collective-permute-start.17 = (f32[48,256]{1,0:T(8,128)S(1)}, f32[48,256]{1,0:T(8,128)S(1)}, u32[]{:S(2)}, u32[]{:S(2)}) collective-permute-start(f32[48,256]{1,0:T(8,128)S(1)} %core_sum.3), channel_id=1, source_target_pairs={{0,16},{1,17},{2,26},{3,27},{4,20},{5,21},{6,30},{7,31},{8,24},{9,... | collective-permute-start | bytes 147464 | tf_op jit(solution)/shard_map/ppermute | solution.py:445
  38.5 4.8 %collective-permute-start.20 = (f32[48,256]{1,0:T(8,128)S(1)}, f32[48,256]{1,0:T(8,128)S(1)}, u32[]{:S(2)}, u32[]{:S(2)}) collective-permute-start(f32[48,256]{1,0:T(8,128)S(1)} %coarse_root.1.first), channel_id=1, source_target_pairs={{0,7},{1,6},{2,5},{3,4},{4,3},{5,2},{6,1},{7,0},{8,15},{9,14},{10,... | collective-permute-start | bytes 147464 | tf_op jit(solution)/shard_map/ppermute | solution.py:554
  39.6 3.8 %collective-permute-start.19 = (f32[48,256]{1,0:T(8,128)S(1)}, f32[48,256]{1,0:T(8,128)S(1)}, u32[]{:S(2)}, u32[]{:S(2)}) collective-permute-start(f32[48,256]{1,0:T(8,128)S(1)} %coarse_root.1.first), channel_id=1, source_target_pairs={{0,6},{1,7},{2,4},{3,5},{4,2},{5,3},{6,0},{7,1},{8,14},{9,15},{10,... | collective-permute-start | bytes 147464 | tf_op jit(solution)/shard_map/ppermute | solution.py:554
  39.8 4.6 %collective-permute-start.18 = (f32[48,256]{1,0:T(8,128)S(1)}, f32[48,256]{1,0:T(8,128)S(1)}, u32[]{:S(2)}, u32[]{:S(2)}) collective-permute-start(f32[48,256]{1,0:T(8,128)S(1)} %coarse_root.1.first), channel_id=1, source_target_pairs={{0,3},{1,2},{2,1},{3,0},{4,7},{5,6},{6,5},{7,4},{8,11},{9,10},{10,... | collective-permute-start | bytes 147464 | tf_op jit(solution)/shard_map/ppermute | solution.py:554
  44.6 1.3 %collective-permute-start.21 = (f32[32,256]{1,0:T(8,128)S(1)}, f32[32,256]{1,0:T(8,128)S(1)}, u32[]{:S(2)}, u32[]{:S(2)}) collective-permute-start(f32[32,256]{1,0:T(8,128)S(1)} %get-tuple-element.72), channel_id=1, source_target_pairs={{0,2},{1,3},{2,0},{3,1},{4,6},{5,7},{6,4},{7,5},{8,10},{9,11},{10,... | collective-permute-start | bytes 98312 | tf_op jit(solution)/shard_map/ppermute | solution.py:562
  (3 other events, 27.6 us)

commit v10 on v9

--- a/solution.py
+++ b/solution.py
@@ -11,7 +11,7 @@
 ITERS = 2
 FACES = 8
 AXES = ("gx", "gy", "gz")
-FIRST_ORDER = ((1, 1), (2, 1), (2, 0), (0, 0), (0, 1), (1, 0))
+FIRST_ORDER = ((0, 0), (2, 1), (2, 0), (1, 1), (0, 1), (1, 0))
 LATER_ORDER = ((1, 0), (0, 0), (0, 1), (2, 1), (2, 0), (1, 1))
 F32 = jnp.float32
 BF16 = jnp.bfloat16

time: 47.2 us -> 46.7 us (0.989)
  waiting for transfers between devices: 14.3 us -> 13.2 us
    ppermute x3, starting transfers between devices: 7.04 us -> 6.42 us  [along(): return lax.ppermute(value, AXES, pairs)]
    ppermute x10, starting transfers between devices: 9.21 us -> 9.76 us  [exchange(): lax.ppermute(message, AXES, swap_pairs(sizes, dim, odd))]
    ppermute x3, waiting for transfers between devices: 3.43 us -> 2.9 us  [along(): return lax.ppermute(value, AXES, pairs)]
  transfers between devices with their start and end apart: 22 -> 22, of which waited for: 11 -> 12; matrix products, arithmetic and copies ran while one was open for 0% -> 0% of each run, Pallas kernels for 9% -> 9%
where the time goes in v10:
time: 46.7 us; the launch traced here: 46.6 us
  starting transfers between devices  22.7 us (49%)
  waiting for transfers between devices  13.2 us (28%)
  Pallas kernels  10.5 us (22%)
    pallas_call x15, Pallas kernels, call(): pl.pallas_call(body, out_shape=[item(shape, dtype) for item, shape, dtype...  10.5 us
    ppermute x10, starting transfers between devices, exchange(): lax.ppermute(message, AXES, swap_pairs(sizes, dim, odd))  9.76 us
    ppermute x3, starting transfers between devices, along(): return lax.ppermute(value, AXES, pairs)  6.42 us
    ppermute x6, starting transfers between devices, per_device(): pieces.append(lax.ppermute(message, AXES, moves))  5.76 us
    ppermute x6, waiting for transfers between devices, per_device(): pieces.append(lax.ppermute(message, AXES, moves))  5.69 us
    ppermute x10, waiting for transfers between devices, exchange(): lax.ppermute(message, AXES, swap_pairs(sizes, dim, odd))  3.94 us
    ppermute x3, waiting for transfers between devices, along(): return lax.ppermute(value, AXES, pairs)  2.9 us
  transfers between devices with their start and end apart: 22, of which 12 were waited for; matrix products, arithmetic and copies ran while one was open for 0% of the time, Pallas kernels for 9%

profile of v10, /device:TPU:0, one launch (start us, length us, event | category | flops | bytes accessed | tf_op | source)
XLA Modules:
  0.0 46.6 jit_solution(12124033725386461028)
XLA Ops:
  0.0 2.7 %first_product.1 = (bf16[1024,1024]{1,0:T(8,128)(2,1)S(1)}, f32[32,1024]{1,0:T(8,128)S(1)}, f32[16,32]{1,0:T(8,128)S(1)}, f32[1024,256]{1,0:T(8,128)S(1)}, f32[1...) custom-call(s32[1,8]{1,0:T(1,128)} %bitcast.23, ...), custom_call_target="tpu_custom_call" | custom-call | tf_op jit(solution)/shard_map/first_product/pallas_call | solution.py:106
  2.7 3.1 %collective-permute-start = (f32[136,256]{1,0:T(8,128)S(1)}, f32[136,256]{1,0:T(8,128)S(1)}, u32[]{:S(2)}, u32[]{:S(2)}) collective-permute-start(f32[136,256]{1,0:T(8,128)S(1)} %get-tuple-element.44), channel_id=1, source_target_pairs={{0,8},{1,9},{2,10},{3,11},{4,12},{5,13},{6,14},{7,15},{8,0},{9,1},... | collective-permute-start | bytes 417800 | tf_op jit(solution)/shard_map/ppermute | solution.py:449
  5.8 1.5 %collective-permute-start.1 = (f32[136,256]{1,0:T(8,128)S(1)}, f32[136,256]{1,0:T(8,128)S(1)}, u32[]{:S(2)}, u32[]{:S(2)}) collective-permute-start(f32[136,256]{1,0:T(8,128)S(1)} %get-tuple-element.45), channel_id=1, source_target_pairs={{0,1},{1,0},{2,3},{3,2},{4,5},{5,4},{6,7},{7,6},{8,9},{9,8},{10,11... | collective-permute-start | bytes 417800 | tf_op jit(solution)/shard_map/ppermute | solution.py:449
  7.7 1.2 %collective-permute-start.3 = (f32[136,256]{1,0:T(8,128)S(1)}, f32[136,256]{1,0:T(8,128)S(1)}, u32[]{:S(2)}, u32[]{:S(2)}) collective-permute-start(f32[136,256]{1,0:T(8,128)S(1)} %get-tuple-element.47), channel_id=1, source_target_pairs={{0,2},{1,3},{2,0},{3,1},{4,6},{5,7},{6,4},{7,5},{8,16},{9,17},{10,... | collective-permute-start | bytes 417800 | tf_op jit(solution)/shard_map/ppermute | solution.py:449
  9.0 2.9 %constants.1 = (bf16[1024,96]{1,0:T(8,128)(2,1)S(1)}, f32[1024,128]{1,0:T(8,128)S(1)}, bf16[96,640]{1,0:T(8,128)(2,1)S(1)}, bf16[1024,1024]{1,0:T(8,128)(2,1)S(1...) custom-call(s32[1,8]{1,0:T(1,128)} %bitcast.24, ...), custom_call_target="tpu_custom_call" | custom-call | tf_op jit(solution)/shard_map/constants/pallas_call | solution.py:106
  11.9 1.4 %collective-permute-done.2.more_2_ = f32[136,256]{1,0:T(8,128)S(1)} collective-permute-done((f32[136,256]{1,0:T(8,128)S(1)}, f32[136,256]{1,0:T(8,128)S(1)}, u32[]{:S(2)}, u32[]{:S(2)}) %collective-permute-start.2) | collective-permute-done | bytes 139296 | tf_op jit(solution)/shard_map/ppermute | solution.py:449
  13.8 1.8 %collective-permute-start.7 = (f32[16,256]{1,0:T(8,128)S(1)}, f32[16,256]{1,0:T(8,128)S(1)}, u32[]{:S(2)}, u32[]{:S(2)}) collective-permute-start(f32[16,256]{1,0:T(8,128)S(1)} %get-tuple-element.54.own.root), channel_id=1, source_target_pairs={{0,8},{1,9},{2,10},{3,11},{4,12},{5,13},{6,14},{7,15},{8,0},{9,1},... | collective-permute-start | bytes 49160 | tf_op jit(solution)/shard_map/ppermute | solution.py:445
  15.6 2.6 %collective-permute-start.6 = (f32[16,256]{1,0:T(8,128)S(1)}, f32[16,256]{1,0:T(8,128)S(1)}, u32[]{:S(2)}, u32[]{:S(2)}) collective-permute-start(f32[16,256]{1,0:T(8,128)S(1)} %core_sum.2), channel_id=1, source_target_pairs={{0,16},{1,17},{2,26},{3,27},{4,20},{5,21},{6,30},{7,31},{8,24},{9,... | collective-permute-start | bytes 49160 | tf_op jit(solution)/shard_map/ppermute | solution.py:445
  18.2 2.1 %collective-permute-done.6.more_0_ = f32[16,256]{1,0:T(8,128)S(1)} collective-permute-done((f32[16,256]{1,0:T(8,128)S(1)}, f32[16,256]{1,0:T(8,128)S(1)}, u32[]{:S(2)}, u32[]{:S(2)}) %collective-permute-start.6) | collective-permute-done | bytes 16416 | tf_op jit(solution)/shard_map/ppermute | solution.py:445
  20.5 0.8 %collective-permute-start.10 = (f32[48,256]{1,0:T(8,128)S(1)}, f32[48,256]{1,0:T(8,128)S(1)}, u32[]{:S(2)}, u32[]{:S(2)}) collective-permute-start(f32[48,256]{1,0:T(8,128)S(1)} %root_part.1.first), channel_id=1, source_target_pairs={{0,7},{1,6},{2,5},{3,4},{4,3},{5,2},{6,1},{7,0},{8,15},{9,14},{10,... | collective-permute-start | bytes 147464 | tf_op jit(solution)/shard_map/ppermute | solution.py:554
  21.3 0.8 %collective-permute-start.9 = (f32[48,256]{1,0:T(8,128)S(1)}, f32[48,256]{1,0:T(8,128)S(1)}, u32[]{:S(2)}, u32[]{:S(2)}) collective-permute-start(f32[48,256]{1,0:T(8,128)S(1)} %root_part.1.first), channel_id=1, source_target_pairs={{0,6},{1,7},{2,4},{3,5},{4,2},{5,3},{6,0},{7,1},{8,14},{9,15},{10,... | collective-permute-start | bytes 147464 | tf_op jit(solution)/shard_map/ppermute | solution.py:554
  23.2 2.1 %collective-permute-done.10.more_2_ = f32[48,256]{1,0:T(8,128)S(1)} collective-permute-done((f32[48,256]{1,0:T(8,128)S(1)}, f32[48,256]{1,0:T(8,128)S(1)}, u32[]{:S(2)}, u32[]{:S(2)}) %collective-permute-start.10) | collective-permute-done | bytes 49184 | tf_op jit(solution)/shard_map/ppermute | solution.py:554
  25.3 1.0 %collective-permute-done.8.more_0_ = f32[48,256]{1,0:T(8,128)S(1)} collective-permute-done((f32[48,256]{1,0:T(8,128)S(1)}, f32[48,256]{1,0:T(8,128)S(1)}, u32[]{:S(2)}, u32[]{:S(2)}) %collective-permute-start.8) | collective-permute-done | bytes 49184 | tf_op jit(solution)/shard_map/ppermute | solution.py:554
  27.8 1.2 %update_product.1 = (f32[1024,256]{1,0:T(8,128)S(1)}, f32[1024,256]{1,0:T(8,128)S(1)}, f32[32,256]{1,0:T(8,128)S(1)}, f32[48,256]{1,0:T(8,128)S(1)}, f32[176,256...) custom-call(f32[1024,256]{1,0:T(8,128)S(1)} %base.2, ...), custom_call_target="tpu_custom_call" | custom-call | tf_op jit(solution)/shard_map/update_product/pallas_call | solution.py:106
  30.0 1.6 %collective-permute-start.15 = (f32[128,256]{1,0:T(8,128)S(1)}, f32[128,256]{1,0:T(8,128)S(1)}, u32[]{:S(2)}, u32[]{:S(2)}) collective-permute-start(f32[128,256]{1,0:T(8,128)S(1)} %get-tuple-element.67), channel_id=1, source_target_pairs={{0,1},{1,0},{2,3},{3,2},{4,5},{5,4},{6,7},{7,6},{8,9},{9,8},{10,11... | collective-permute-start | bytes 393224 | tf_op jit(solution)/shard_map/ppermute | solution.py:449
  31.6 1.0 %collective-permute-start.16 = (f32[128,256]{1,0:T(8,128)S(1)}, f32[128,256]{1,0:T(8,128)S(1)}, u32[]{:S(2)}, u32[]{:S(2)}) collective-permute-start(f32[128,256]{1,0:T(8,128)S(1)} %get-tuple-element.68), channel_id=1, source_target_pairs={{0,6},{1,7},{2,4},{3,5},{4,2},{5,3},{6,0},{7,1},{8,14},{9,15},{10,... | collective-permute-start | bytes 393224 | tf_op jit(solution)/shard_map/ppermute | solution.py:449
  32.6 2.0 %collective-permute-start.17 = (f32[48,256]{1,0:T(8,128)S(1)}, f32[48,256]{1,0:T(8,128)S(1)}, u32[]{:S(2)}, u32[]{:S(2)}) collective-permute-start(f32[48,256]{1,0:T(8,128)S(1)} %core_sum.3), channel_id=1, source_target_pairs={{0,16},{1,17},{2,26},{3,27},{4,20},{5,21},{6,30},{7,31},{8,24},{9,... | collective-permute-start | bytes 147464 | tf_op jit(solution)/shard_map/ppermute | solution.py:445
  34.5 1.3 %collective-permute-done.15.more_3_ = f32[128,256]{1,0:T(8,128)S(1)} collective-permute-done((f32[128,256]{1,0:T(8,128)S(1)}, f32[128,256]{1,0:T(8,128)S(1)}, u32[]{:S(2)}, u32[]{:S(2)}) %collective-permute-start.15) | collective-permute-done | bytes 131104 | tf_op jit(solution)/shard_map/ppermute | solution.py:449
  35.9 1.2 %collective-permute-done.16.more_4_ = f32[128,256]{1,0:T(8,128)S(1)} collective-permute-done((f32[128,256]{1,0:T(8,128)S(1)}, f32[128,256]{1,0:T(8,128)S(1)}, u32[]{:S(2)}, u32[]{:S(2)}) %collective-permute-start.16) | collective-permute-done | bytes 131104 | tf_op jit(solution)/shard_map/ppermute | solution.py:449
  38.2 1.3 %collective-permute-start.20 = (f32[48,256]{1,0:T(8,128)S(1)}, f32[48,256]{1,0:T(8,128)S(1)}, u32[]{:S(2)}, u32[]{:S(2)}) collective-permute-start(f32[48,256]{1,0:T(8,128)S(1)} %coarse_root.1.first), channel_id=1, source_target_pairs={{0,7},{1,6},{2,5},{3,4},{4,3},{5,2},{6,1},{7,0},{8,15},{9,14},{10,... | collective-permute-start | bytes 147464 | tf_op jit(solution)/shard_map/ppermute | solution.py:554
  39.5 0.9 %collective-permute-start.19 = (f32[48,256]{1,0:T(8,128)S(1)}, f32[48,256]{1,0:T(8,128)S(1)}, u32[]{:S(2)}, u32[]{:S(2)}) collective-permute-start(f32[48,256]{1,0:T(8,128)S(1)} %coarse_root.1.first), channel_id=1, source_target_pairs={{0,6},{1,7},{2,4},{3,5},{4,2},{5,3},{6,0},{7,1},{8,14},{9,15},{10,... | collective-permute-start | bytes 147464 | tf_op jit(solution)/shard_map/ppermute | solution.py:554
  40.4 1.0 %collective-permute-start.18 = (f32[48,256]{1,0:T(8,128)S(1)}, f32[48,256]{1,0:T(8,128)S(1)}, u32[]{:S(2)}, u32[]{:S(2)}) collective-permute-start(f32[48,256]{1,0:T(8,128)S(1)} %coarse_root.1.first), channel_id=1, source_target_pairs={{0,3},{1,2},{2,1},{3,0},{4,7},{5,6},{6,5},{7,4},{8,11},{9,10},{10,... | collective-permute-start | bytes 147464 | tf_op jit(solution)/shard_map/ppermute | solution.py:554
  41.4 1.2 %collective-permute-done.20.more_2_ = f32[48,256]{1,0:T(8,128)S(1)} collective-permute-done((f32[48,256]{1,0:T(8,128)S(1)}, f32[48,256]{1,0:T(8,128)S(1)}, u32[]{:S(2)}, u32[]{:S(2)}) %collective-permute-start.20) | collective-permute-done | bytes 49184 | tf_op jit(solution)/shard_map/ppermute | solution.py:554
  45.4 1.2 %update_last.1 = f32[1024,256]{1,0:T(8,128)} custom-call(f32[1024,256]{1,0:T(8,128)S(1)} %base.3, bf16[1024,96]{1,0:T(8,128)(2,1)S(1)} %get-tuple-element.49.modes_t, f32[32,256]{1,0:T(8,128)S(1)} %get-tuple-element.71.own, f32[32,256]{1,0:T(8,128)S(1)} %collective-permute-done.21.other), custom_call_target="tpu_custom_call" | custom-call | tf_op jit(solution)/shard_map/update_last/pallas_call | solution.py:106
  (45 shorter events, 8.2 us)
Async XLA Ops:
  2.7 9.1 %collective-permute-start = (f32[136,256]{1,0:T(8,128)S(1)}, f32[136,256]{1,0:T(8,128)S(1)}, u32[]{:S(2)}, u32[]{:S(2)}) collective-permute-start(f32[136,256]{1,0:T(8,128)S(1)} %get-tuple-element.44), channel_id=1, source_target_pairs={{0,8},{1,9},{2,10},{3,11},{4,12},{5,13},{6,14},{7,15},{8,0},{9,1},... | collective-permute-start | bytes 417800 | tf_op jit(solution)/shard_map/ppermute | solution.py:449
  5.8 6.0 %collective-permute-start.1 = (f32[136,256]{1,0:T(8,128)S(1)}, f32[136,256]{1,0:T(8,128)S(1)}, u32[]{:S(2)}, u32[]{:S(2)}) collective-permute-start(f32[136,256]{1,0:T(8,128)S(1)} %get-tuple-element.45), channel_id=1, source_target_pairs={{0,1},{1,0},{2,3},{3,2},{4,5},{5,4},{6,7},{7,6},{8,9},{9,8},{10,11... | collective-permute-start | bytes 417800 | tf_op jit(solution)/shard_map/ppermute | solution.py:449
  7.3 5.9 %collective-permute-start.2 = (f32[136,256]{1,0:T(8,128)S(1)}, f32[136,256]{1,0:T(8,128)S(1)}, u32[]{:S(2)}, u32[]{:S(2)}) collective-permute-start(f32[136,256]{1,0:T(8,128)S(1)} %get-tuple-element.46), channel_id=1, source_target_pairs={{0,6},{1,7},{2,4},{3,5},{4,2},{5,3},{6,0},{7,1},{8,14},{9,15},{10,... | collective-permute-start | bytes 417800 | tf_op jit(solution)/shard_map/ppermute | solution.py:449
  7.7 5.6 %collective-permute-start.3 = (f32[136,256]{1,0:T(8,128)S(1)}, f32[136,256]{1,0:T(8,128)S(1)}, u32[]{:S(2)}, u32[]{:S(2)}) collective-permute-start(f32[136,256]{1,0:T(8,128)S(1)} %get-tuple-element.47), channel_id=1, source_target_pairs={{0,2},{1,3},{2,0},{3,1},{4,6},{5,7},{6,4},{7,5},{8,16},{9,17},{10,... | collective-permute-start | bytes 417800 | tf_op jit(solution)/shard_map/ppermute | solution.py:449
  9.0 4.3 %collective-permute-start.4 = (f32[136,256]{1,0:T(8,128)S(1)}, f32[136,256]{1,0:T(8,128)S(1)}, u32[]{:S(2)}, u32[]{:S(2)}) collective-permute-start(f32[136,256]{1,0:T(8,128)S(1)} %get-tuple-element.48), channel_id=1, source_target_pairs={{0,2},{1,3},{2,0},{3,1},{4,6},{5,7},{6,4},{7,5},{8,10},{9,11},{10,... | collective-permute-start | bytes 417800 | tf_op jit(solution)/shard_map/ppermute | solution.py:449
  9.0 11.4 %copy-start.3 = (f32[16,64]{1,0:T(8,128)S(1)}, f32[16,64]{1,0:T(8,128)}, u32[]{:S(2)}) copy-start(f32[16,64]{1,0:T(8,128)} %root_inverse.3) | copy-start | bytes 12292
  9.0 17.7 %copy-start.1 = (bf16[1,1,1,1024,256]{4,3,2,1,0:T(8,128)(2,1)S(1)}, bf16[1,1,1,1024,256]{4,3,2,1,0:T(8,128)(2,1)}, u32[]{:S(2)}) copy-start(bf16[1,1,1,1024,256]{4,3,2,1,0:T(8,128)(2,1)} %param.10) | copy-start | bytes 1572868
  13.6 2.0 %collective-permute-start.5 = (f32[64,256]{1,0:T(8,128)S(1)}, f32[64,256]{1,0:T(8,128)S(1)}, u32[]{:S(2)}, u32[]{:S(2)}) collective-permute-start(f32[64,256]{1,0:T(8,128)S(1)} %get-tuple-element.52), channel_id=1, source_target_pairs={{0,2},{1,3},{2,0},{3,1},{4,6},{5,7},{6,4},{7,5},{8,10},{9,11},{10,... | collective-permute-start | bytes 196616 | tf_op jit(solution)/shard_map/ppermute | solution.py:503
  13.8 4.5 %collective-permute-start.7 = (f32[16,256]{1,0:T(8,128)S(1)}, f32[16,256]{1,0:T(8,128)S(1)}, u32[]{:S(2)}, u32[]{:S(2)}) collective-permute-start(f32[16,256]{1,0:T(8,128)S(1)} %get-tuple-element.54.own.root), channel_id=1, source_target_pairs={{0,8},{1,9},{2,10},{3,11},{4,12},{5,13},{6,14},{7,15},{8,0},{9,1},... | collective-permute-start | bytes 49160 | tf_op jit(solution)/shard_map/ppermute | solution.py:445
  15.6 4.7 %collective-permute-start.6 = (f32[16,256]{1,0:T(8,128)S(1)}, f32[16,256]{1,0:T(8,128)S(1)}, u32[]{:S(2)}, u32[]{:S(2)}) collective-permute-start(f32[16,256]{1,0:T(8,128)S(1)} %core_sum.2), channel_id=1, source_target_pairs={{0,16},{1,17},{2,26},{3,27},{4,20},{5,21},{6,30},{7,31},{8,24},{9,... | collective-permute-start | bytes 49160 | tf_op jit(solution)/shard_map/ppermute | solution.py:445
  20.5 4.8 %collective-permute-start.10 = (f32[48,256]{1,0:T(8,128)S(1)}, f32[48,256]{1,0:T(8,128)S(1)}, u32[]{:S(2)}, u32[]{:S(2)}) collective-permute-start(f32[48,256]{1,0:T(8,128)S(1)} %root_part.1.first), channel_id=1, source_target_pairs={{0,7},{1,6},{2,5},{3,4},{4,3},{5,2},{6,1},{7,0},{8,15},{9,14},{10,... | collective-permute-start | bytes 147464 | tf_op jit(solution)/shard_map/ppermute | solution.py:554
  21.3 4.0 %collective-permute-start.9 = (f32[48,256]{1,0:T(8,128)S(1)}, f32[48,256]{1,0:T(8,128)S(1)}, u32[]{:S(2)}, u32[]{:S(2)}) collective-permute-start(f32[48,256]{1,0:T(8,128)S(1)} %root_part.1.first), channel_id=1, source_target_pairs={{0,6},{1,7},{2,4},{3,5},{4,2},{5,3},{6,0},{7,1},{8,14},{9,15},{10,... | collective-permute-start | bytes 147464 | tf_op jit(solution)/shard_map/ppermute | solution.py:554
  22.2 4.2 %collective-permute-start.8 = (f32[48,256]{1,0:T(8,128)S(1)}, f32[48,256]{1,0:T(8,128)S(1)}, u32[]{:S(2)}, u32[]{:S(2)}) collective-permute-start(f32[48,256]{1,0:T(8,128)S(1)} %root_part.1.first), channel_id=1, source_target_pairs={{0,3},{1,2},{2,1},{3,0},{4,7},{5,6},{6,5},{7,4},{8,11},{9,10},{10,... | collective-permute-start | bytes 147464 | tf_op jit(solution)/shard_map/ppermute | solution.py:554
  26.5 1.3 %collective-permute-start.11 = (f32[32,256]{1,0:T(8,128)S(1)}, f32[32,256]{1,0:T(8,128)S(1)}, u32[]{:S(2)}, u32[]{:S(2)}) collective-permute-start(f32[32,256]{1,0:T(8,128)S(1)} %get-tuple-element.56), channel_id=1, source_target_pairs={{0,2},{1,3},{2,0},{3,1},{4,6},{5,7},{6,4},{7,5},{8,10},{9,11},{10,... | collective-permute-start | bytes 98312 | tf_op jit(solution)/shard_map/ppermute | solution.py:562
  29.0 3.5 %collective-permute-start.12 = (f32[176,256]{1,0:T(8,128)S(1)}, f32[176,256]{1,0:T(8,128)S(1)}, u32[]{:S(2)}, u32[]{:S(2)}) collective-permute-start(f32[176,256]{1,0:T(8,128)S(1)} %get-tuple-element.64), channel_id=1, source_target_pairs={{0,2},{1,3},{2,0},{3,1},{4,6},{5,7},{6,4},{7,5},{8,10},{9,11},{10,... | collective-permute-start | bytes 540680 | tf_op jit(solution)/shard_map/ppermute | solution.py:449
  29.4 7.6 %collective-permute-start.13 = (f32[176,256]{1,0:T(8,128)S(1)}, f32[176,256]{1,0:T(8,128)S(1)}, u32[]{:S(2)}, u32[]{:S(2)}) collective-permute-start(f32[176,256]{1,0:T(8,128)S(1)} %get-tuple-element.65), channel_id=1, source_target_pairs={{0,8},{1,9},{2,10},{3,11},{4,12},{5,13},{6,14},{7,15},{8,0},{9,1},... | collective-permute-start | bytes 540680 | tf_op jit(solution)/shard_map/ppermute | solution.py:449
  30.0 4.6 %collective-permute-start.14 = (f32[128,256]{1,0:T(8,128)S(1)}, f32[128,256]{1,0:T(8,128)S(1)}, u32[]{:S(2)}, u32[]{:S(2)}) collective-permute-start(f32[128,256]{1,0:T(8,128)S(1)} %get-tuple-element.66), channel_id=1, source_target_pairs={{0,2},{1,3},{2,0},{3,1},{4,6},{5,7},{6,4},{7,5},{8,16},{9,17},{10,... | collective-permute-start | bytes 393224 | tf_op jit(solution)/shard_map/ppermute | solution.py:449
  30.0 5.9 %collective-permute-start.15 = (f32[128,256]{1,0:T(8,128)S(1)}, f32[128,256]{1,0:T(8,128)S(1)}, u32[]{:S(2)}, u32[]{:S(2)}) collective-permute-start(f32[128,256]{1,0:T(8,128)S(1)} %get-tuple-element.67), channel_id=1, source_target_pairs={{0,1},{1,0},{2,3},{3,2},{4,5},{5,4},{6,7},{7,6},{8,9},{9,8},{10,11... | collective-permute-start | bytes 393224 | tf_op jit(solution)/shard_map/ppermute | solution.py:449
  31.6 5.5 %collective-permute-start.16 = (f32[128,256]{1,0:T(8,128)S(1)}, f32[128,256]{1,0:T(8,128)S(1)}, u32[]{:S(2)}, u32[]{:S(2)}) collective-permute-start(f32[128,256]{1,0:T(8,128)S(1)} %get-tuple-element.68), channel_id=1, source_target_pairs={{0,6},{1,7},{2,4},{3,5},{4,2},{5,3},{6,0},{7,1},{8,14},{9,15},{10,... | collective-permute-start | bytes 393224 | tf_op jit(solution)/shard_map/ppermute | solution.py:449
  32.6 5.3 %collective-permute-start.17 = (f32[48,256]{1,0:T(8,128)S(1)}, f32[48,256]{1,0:T(8,128)S(1)}, u32[]{:S(2)}, u32[]{:S(2)}) collective-permute-start(f32[48,256]{1,0:T(8,128)S(1)} %core_sum.3), channel_id=1, source_target_pairs={{0,16},{1,17},{2,26},{3,27},{4,20},{5,21},{6,30},{7,31},{8,24},{9,... | collective-permute-start | bytes 147464 | tf_op jit(solution)/shard_map/ppermute | solution.py:445
  38.2 4.5 %collective-permute-start.20 = (f32[48,256]{1,0:T(8,128)S(1)}, f32[48,256]{1,0:T(8,128)S(1)}, u32[]{:S(2)}, u32[]{:S(2)}) collective-permute-start(f32[48,256]{1,0:T(8,128)S(1)} %coarse_root.1.first), channel_id=1, source_target_pairs={{0,7},{1,6},{2,5},{3,4},{4,3},{5,2},{6,1},{7,0},{8,15},{9,14},{10,... | collective-permute-start | bytes 147464 | tf_op jit(solution)/shard_map/ppermute | solution.py:554
  39.5 4.0 %collective-permute-start.19 = (f32[48,256]{1,0:T(8,128)S(1)}, f32[48,256]{1,0:T(8,128)S(1)}, u32[]{:S(2)}, u32[]{:S(2)}) collective-permute-start(f32[48,256]{1,0:T(8,128)S(1)} %coarse_root.1.first), channel_id=1, source_target_pairs={{0,6},{1,7},{2,4},{3,5},{4,2},{5,3},{6,0},{7,1},{8,14},{9,15},{10,... | collective-permute-start | bytes 147464 | tf_op jit(solution)/shard_map/ppermute | solution.py:554
  40.4 3.5 %collective-permute-start.18 = (f32[48,256]{1,0:T(8,128)S(1)}, f32[48,256]{1,0:T(8,128)S(1)}, u32[]{:S(2)}, u32[]{:S(2)}) collective-permute-start(f32[48,256]{1,0:T(8,128)S(1)} %coarse_root.1.first), channel_id=1, source_target_pairs={{0,3},{1,2},{2,1},{3,0},{4,7},{5,6},{6,5},{7,4},{8,11},{9,10},{10,... | collective-permute-start | bytes 147464 | tf_op jit(solution)/shard_map/ppermute | solution.py:554
  44.1 1.3 %collective-permute-start.21 = (f32[32,256]{1,0:T(8,128)S(1)}, f32[32,256]{1,0:T(8,128)S(1)}, u32[]{:S(2)}, u32[]{:S(2)}) collective-permute-start(f32[32,256]{1,0:T(8,128)S(1)} %get-tuple-element.72), channel_id=1, source_target_pairs={{0,2},{1,3},{2,0},{3,1},{4,6},{5,7},{6,4},{7,5},{8,10},{9,11},{10,... | collective-permute-start | bytes 98312 | tf_op jit(solution)/shard_map/ppermute | solution.py:562
  (3 other events, 28.5 us)

commit v11 on v10

--- a/solution.py
+++ b/solution.py
@@ -296,8 +296,8 @@
     total[...] = own[...] + other[other.shape[0] - own.shape[0] :, :]
 
 
-def root_kernel(count, coarse, root_inverse, root, *more):
-    received, (message, stack) = more[:-2], more[-2:]
+def root_kernel(count, pieces, coarse, root_inverse, root, *more):
+    received, (message, stack) = more[:pieces], more[-2:]
     modes, height = coarse.shape[0], root.shape[0]
     me = lax.axis_index("gx")
     paired, single = far_offsets(count, 1 + nearest(count))
@@ -519,9 +519,9 @@
                 [pltpu.VMEM((3 * root_modes, iface), F32)],
             )
             (message,) = call(
-                functools.partial(root_kernel, sizes[0]),
+                functools.partial(root_kernel, sizes[0], len(received)),
                 [held(mode_count + root_modes)],
-                [coarse, root_inverse, root] + received,
+                [coarse, root_inverse, root] + received + [ahead_loads],
                 "root_part",
                 [pltpu.VMEM((root_inverse.shape[1], cases), F32)],
             )

time: 46.7 us -> 46.9 us (level)
    ppermute x3, waiting for transfers between devices: 2.9 us -> 2.09 us  [along(): return lax.ppermute(value, AXES, pairs)]
    ppermute x2, waiting for transfers between devices: 0.66 us -> 1.41 us  [per_device(): other = lax.ppermute(given, AXES, swap_pairs(sizes, 1, 0))]
  transfers between devices with their start and end apart: 22 -> 22, of which waited for: 12 -> 11; matrix products, arithmetic and copies ran while one was open for 0% -> 0% of each run, Pallas kernels for 9% -> 9%
where the time goes in v11:
time: 46.9 us; the launch traced here: 46.7 us
  starting transfers between devices  23.1 us (49%)
  waiting for transfers between devices  12.9 us (28%)
  Pallas kernels  10.5 us (22%)
    pallas_call x15, Pallas kernels, call(): pl.pallas_call(body, out_shape=[item(shape, dtype) for item, shape, dtype...  10.5 us
    ppermute x10, starting transfers between devices, exchange(): lax.ppermute(message, AXES, swap_pairs(sizes, dim, odd))  9.56 us
    ppermute x3, starting transfers between devices, along(): return lax.ppermute(value, AXES, pairs)  6.53 us
    ppermute x6, starting transfers between devices, per_device(): pieces.append(lax.ppermute(message, AXES, moves))  5.86 us
    ppermute x6, waiting for transfers between devices, per_device(): pieces.append(lax.ppermute(message, AXES, moves))  5.55 us
    ppermute x10, waiting for transfers between devices, exchange(): lax.ppermute(message, AXES, swap_pairs(sizes, dim, odd))  3.86 us
    ppermute x3, waiting for transfers between devices, along(): return lax.ppermute(value, AXES, pairs)  2.09 us
    ppermute x2, waiting for transfers between devices, per_device(): other = lax.ppermute(given, AXES, swap_pairs(sizes, 1, 0))  1.41 us
  transfers between devices with their start and end apart: 22, of which 11 were waited for; matrix products, arithmetic and copies ran while one was open for 0% of the time, Pallas kernels for 9%

profile of v11, /device:TPU:0, one launch (start us, length us, event | category | flops | bytes accessed | tf_op | source)
XLA Modules:
  0.0 46.7 jit_solution(16485205588849660371)
XLA Ops:
  0.0 2.7 %first_product.1 = (bf16[1024,1024]{1,0:T(8,128)(2,1)S(1)}, f32[32,1024]{1,0:T(8,128)S(1)}, f32[16,32]{1,0:T(8,128)S(1)}, f32[1024,256]{1,0:T(8,128)S(1)}, f32[1...) custom-call(s32[1,8]{1,0:T(1,128)} %bitcast.23, ...), custom_call_target="tpu_custom_call" | custom-call | tf_op jit(solution)/shard_map/first_product/pallas_call | solution.py:106
  2.7 3.1 %collective-permute-start = (f32[136,256]{1,0:T(8,128)S(1)}, f32[136,256]{1,0:T(8,128)S(1)}, u32[]{:S(2)}, u32[]{:S(2)}) collective-permute-start(f32[136,256]{1,0:T(8,128)S(1)} %get-tuple-element.44), channel_id=1, source_target_pairs={{0,8},{1,9},{2,10},{3,11},{4,12},{5,13},{6,14},{7,15},{8,0},{9,1},... | collective-permute-start | bytes 417800 | tf_op jit(solution)/shard_map/ppermute | solution.py:449
  5.8 1.5 %collective-permute-start.1 = (f32[136,256]{1,0:T(8,128)S(1)}, f32[136,256]{1,0:T(8,128)S(1)}, u32[]{:S(2)}, u32[]{:S(2)}) collective-permute-start(f32[136,256]{1,0:T(8,128)S(1)} %get-tuple-element.45), channel_id=1, source_target_pairs={{0,1},{1,0},{2,3},{3,2},{4,5},{5,4},{6,7},{7,6},{8,9},{9,8},{10,11... | collective-permute-start | bytes 417800 | tf_op jit(solution)/shard_map/ppermute | solution.py:449
  7.7 1.2 %collective-permute-start.3 = (f32[136,256]{1,0:T(8,128)S(1)}, f32[136,256]{1,0:T(8,128)S(1)}, u32[]{:S(2)}, u32[]{:S(2)}) collective-permute-start(f32[136,256]{1,0:T(8,128)S(1)} %get-tuple-element.47), channel_id=1, source_target_pairs={{0,2},{1,3},{2,0},{3,1},{4,6},{5,7},{6,4},{7,5},{8,16},{9,17},{10,... | collective-permute-start | bytes 417800 | tf_op jit(solution)/shard_map/ppermute | solution.py:449
  9.0 2.9 %constants.1 = (bf16[1024,96]{1,0:T(8,128)(2,1)S(1)}, f32[1024,128]{1,0:T(8,128)S(1)}, bf16[96,640]{1,0:T(8,128)(2,1)S(1)}, bf16[1024,1024]{1,0:T(8,128)(2,1)S(1...) custom-call(s32[1,8]{1,0:T(1,128)} %bitcast.24, ...), custom_call_target="tpu_custom_call" | custom-call | tf_op jit(solution)/shard_map/constants/pallas_call | solution.py:106
  11.9 1.4 %collective-permute-done.2.more_2_ = f32[136,256]{1,0:T(8,128)S(1)} collective-permute-done((f32[136,256]{1,0:T(8,128)S(1)}, f32[136,256]{1,0:T(8,128)S(1)}, u32[]{:S(2)}, u32[]{:S(2)}) %collective-permute-start.2) | collective-permute-done | bytes 139296 | tf_op jit(solution)/shard_map/ppermute | solution.py:449
  13.8 1.8 %collective-permute-start.7 = (f32[16,256]{1,0:T(8,128)S(1)}, f32[16,256]{1,0:T(8,128)S(1)}, u32[]{:S(2)}, u32[]{:S(2)}) collective-permute-start(f32[16,256]{1,0:T(8,128)S(1)} %get-tuple-element.54.own.root), channel_id=1, source_target_pairs={{0,8},{1,9},{2,10},{3,11},{4,12},{5,13},{6,14},{7,15},{8,0},{9,1},... | collective-permute-start | bytes 49160 | tf_op jit(solution)/shard_map/ppermute | solution.py:445
  15.6 2.6 %collective-permute-start.6 = (f32[16,256]{1,0:T(8,128)S(1)}, f32[16,256]{1,0:T(8,128)S(1)}, u32[]{:S(2)}, u32[]{:S(2)}) collective-permute-start(f32[16,256]{1,0:T(8,128)S(1)} %core_sum.2), channel_id=1, source_target_pairs={{0,16},{1,17},{2,26},{3,27},{4,20},{5,21},{6,30},{7,31},{8,24},{9,... | collective-permute-start | bytes 49160 | tf_op jit(solution)/shard_map/ppermute | solution.py:445
  19.0 1.4 %collective-permute-done.6.more_0_ = f32[16,256]{1,0:T(8,128)S(1)} collective-permute-done((f32[16,256]{1,0:T(8,128)S(1)}, f32[16,256]{1,0:T(8,128)S(1)}, u32[]{:S(2)}, u32[]{:S(2)}) %collective-permute-start.6) | collective-permute-done | bytes 16416 | tf_op jit(solution)/shard_map/ppermute | solution.py:445
  20.5 0.9 %collective-permute-start.10 = (f32[48,256]{1,0:T(8,128)S(1)}, f32[48,256]{1,0:T(8,128)S(1)}, u32[]{:S(2)}, u32[]{:S(2)}) collective-permute-start(f32[48,256]{1,0:T(8,128)S(1)} %root_part.1.first), channel_id=1, source_target_pairs={{0,7},{1,6},{2,5},{3,4},{4,3},{5,2},{6,1},{7,0},{8,15},{9,14},{10,... | collective-permute-start | bytes 147464 | tf_op jit(solution)/shard_map/ppermute | solution.py:554
  21.3 0.9 %collective-permute-start.9 = (f32[48,256]{1,0:T(8,128)S(1)}, f32[48,256]{1,0:T(8,128)S(1)}, u32[]{:S(2)}, u32[]{:S(2)}) collective-permute-start(f32[48,256]{1,0:T(8,128)S(1)} %root_part.1.first), channel_id=1, source_target_pairs={{0,6},{1,7},{2,4},{3,5},{4,2},{5,3},{6,0},{7,1},{8,14},{9,15},{10,... | collective-permute-start | bytes 147464 | tf_op jit(solution)/shard_map/ppermute | solution.py:554
  23.2 2.1 %collective-permute-done.10.more_2_ = f32[48,256]{1,0:T(8,128)S(1)} collective-permute-done((f32[48,256]{1,0:T(8,128)S(1)}, f32[48,256]{1,0:T(8,128)S(1)}, u32[]{:S(2)}, u32[]{:S(2)}) %collective-permute-start.10) | collective-permute-done | bytes 49184 | tf_op jit(solution)/shard_map/ppermute | solution.py:554
  25.3 1.0 %collective-permute-done.8.more_0_ = f32[48,256]{1,0:T(8,128)S(1)} collective-permute-done((f32[48,256]{1,0:T(8,128)S(1)}, f32[48,256]{1,0:T(8,128)S(1)}, u32[]{:S(2)}, u32[]{:S(2)}) %collective-permute-start.8) | collective-permute-done | bytes 49184 | tf_op jit(solution)/shard_map/ppermute | solution.py:554
  27.8 1.2 %update_product.1 = (f32[1024,256]{1,0:T(8,128)S(1)}, f32[1024,256]{1,0:T(8,128)S(1)}, f32[32,256]{1,0:T(8,128)S(1)}, f32[48,256]{1,0:T(8,128)S(1)}, f32[176,256...) custom-call(f32[1024,256]{1,0:T(8,128)S(1)} %base.2, ...), custom_call_target="tpu_custom_call" | custom-call | tf_op jit(solution)/shard_map/update_product/pallas_call | solution.py:106
  29.8 1.6 %collective-permute-start.15 = (f32[128,256]{1,0:T(8,128)S(1)}, f32[128,256]{1,0:T(8,128)S(1)}, u32[]{:S(2)}, u32[]{:S(2)}) collective-permute-start(f32[128,256]{1,0:T(8,128)S(1)} %get-tuple-element.67), channel_id=1, source_target_pairs={{0,1},{1,0},{2,3},{3,2},{4,5},{5,4},{6,7},{7,6},{8,9},{9,8},{10,11... | collective-permute-start | bytes 393224 | tf_op jit(solution)/shard_map/ppermute | solution.py:449
  31.5 0.9 %collective-permute-start.16 = (f32[128,256]{1,0:T(8,128)S(1)}, f32[128,256]{1,0:T(8,128)S(1)}, u32[]{:S(2)}, u32[]{:S(2)}) collective-permute-start(f32[128,256]{1,0:T(8,128)S(1)} %get-tuple-element.68), channel_id=1, source_target_pairs={{0,6},{1,7},{2,4},{3,5},{4,2},{5,3},{6,0},{7,1},{8,14},{9,15},{10,... | collective-permute-start | bytes 393224 | tf_op jit(solution)/shard_map/ppermute | solution.py:449
  32.4 2.1 %collective-permute-start.17 = (f32[48,256]{1,0:T(8,128)S(1)}, f32[48,256]{1,0:T(8,128)S(1)}, u32[]{:S(2)}, u32[]{:S(2)}) collective-permute-start(f32[48,256]{1,0:T(8,128)S(1)} %core_sum.3), channel_id=1, source_target_pairs={{0,16},{1,17},{2,26},{3,27},{4,20},{5,21},{6,30},{7,31},{8,24},{9,... | collective-permute-start | bytes 147464 | tf_op jit(solution)/shard_map/ppermute | solution.py:445
  34.5 1.2 %collective-permute-done.15.more_3_ = f32[128,256]{1,0:T(8,128)S(1)} collective-permute-done((f32[128,256]{1,0:T(8,128)S(1)}, f32[128,256]{1,0:T(8,128)S(1)}, u32[]{:S(2)}, u32[]{:S(2)}) %collective-permute-start.15) | collective-permute-done | bytes 131104 | tf_op jit(solution)/shard_map/ppermute | solution.py:449
  35.7 1.2 %collective-permute-done.16.more_4_ = f32[128,256]{1,0:T(8,128)S(1)} collective-permute-done((f32[128,256]{1,0:T(8,128)S(1)}, f32[128,256]{1,0:T(8,128)S(1)}, u32[]{:S(2)}, u32[]{:S(2)}) %collective-permute-start.16) | collective-permute-done | bytes 131104 | tf_op jit(solution)/shard_map/ppermute | solution.py:449
  37.9 1.8 %collective-permute-start.20 = (f32[48,256]{1,0:T(8,128)S(1)}, f32[48,256]{1,0:T(8,128)S(1)}, u32[]{:S(2)}, u32[]{:S(2)}) collective-permute-start(f32[48,256]{1,0:T(8,128)S(1)} %coarse_root.1.first), channel_id=1, source_target_pairs={{0,7},{1,6},{2,5},{3,4},{4,3},{5,2},{6,1},{7,0},{8,15},{9,14},{10,... | collective-permute-start | bytes 147464 | tf_op jit(solution)/shard_map/ppermute | solution.py:554
  40.1 1.2 %collective-permute-start.18 = (f32[48,256]{1,0:T(8,128)S(1)}, f32[48,256]{1,0:T(8,128)S(1)}, u32[]{:S(2)}, u32[]{:S(2)}) collective-permute-start(f32[48,256]{1,0:T(8,128)S(1)} %coarse_root.1.first), channel_id=1, source_target_pairs={{0,3},{1,2},{2,1},{3,0},{4,7},{5,6},{6,5},{7,4},{8,11},{9,10},{10,... | collective-permute-start | bytes 147464 | tf_op jit(solution)/shard_map/ppermute | solution.py:554
  41.3 1.1 %collective-permute-done.20.more_2_ = f32[48,256]{1,0:T(8,128)S(1)} collective-permute-done((f32[48,256]{1,0:T(8,128)S(1)}, f32[48,256]{1,0:T(8,128)S(1)}, u32[]{:S(2)}, u32[]{:S(2)}) %collective-permute-start.20) | collective-permute-done | bytes 49184 | tf_op jit(solution)/shard_map/ppermute | solution.py:554
  42.4 1.2 %collective-permute-done.19.more_1_ = f32[48,256]{1,0:T(8,128)S(1)} collective-permute-done((f32[48,256]{1,0:T(8,128)S(1)}, f32[48,256]{1,0:T(8,128)S(1)}, u32[]{:S(2)}, u32[]{:S(2)}) %collective-permute-start.19) | collective-permute-done | bytes 49184 | tf_op jit(solution)/shard_map/ppermute | solution.py:554
  45.5 1.2 %update_last.1 = f32[1024,256]{1,0:T(8,128)} custom-call(f32[1024,256]{1,0:T(8,128)S(1)} %base.3, bf16[1024,96]{1,0:T(8,128)(2,1)S(1)} %get-tuple-element.49.modes_t, f32[32,256]{1,0:T(8,128)S(1)} %get-tuple-element.71.own, f32[32,256]{1,0:T(8,128)S(1)} %collective-permute-done.21.other), custom_call_target="tpu_custom_call" | custom-call | tf_op jit(solution)/shard_map/update_last/pallas_call | solution.py:106
  (45 shorter events, 8.2 us)
Async XLA Ops:
  0.0 9.0 %copy-start = (bf16[1,1,1,1024,256]{4,3,2,1,0:T(8,128)(2,1)S(1)}, bf16[1,1,1,1024,256]{4,3,2,1,0:T(8,128)(2,1)}, u32[]{:S(2)}) copy-start(bf16[1,1,1,1024,256]{4,3,2,1,0:T(8,128)(2,1)} %param.9) | copy-start | bytes 1572868
  2.7 10.6 %copy-start.2 = (f32[1,32,256]{2,1,0:T(8,128)S(1)}, f32[1,32,256]{2,1,0:T(8,128)}, u32[]{:S(2)}) copy-start(f32[1,32,256]{2,1,0:T(8,128)} %param.16) | copy-start | bytes 98308
  2.7 9.1 %collective-permute-start = (f32[136,256]{1,0:T(8,128)S(1)}, f32[136,256]{1,0:T(8,128)S(1)}, u32[]{:S(2)}, u32[]{:S(2)}) collective-permute-start(f32[136,256]{1,0:T(8,128)S(1)} %get-tuple-element.44), channel_id=1, source_target_pairs={{0,8},{1,9},{2,10},{3,11},{4,12},{5,13},{6,14},{7,15},{8,0},{9,1},... | collective-permute-start | bytes 417800 | tf_op jit(solution)/shard_map/ppermute | solution.py:449
  5.8 6.0 %collective-permute-start.1 = (f32[136,256]{1,0:T(8,128)S(1)}, f32[136,256]{1,0:T(8,128)S(1)}, u32[]{:S(2)}, u32[]{:S(2)}) collective-permute-start(f32[136,256]{1,0:T(8,128)S(1)} %get-tuple-element.45), channel_id=1, source_target_pairs={{0,1},{1,0},{2,3},{3,2},{4,5},{5,4},{6,7},{7,6},{8,9},{9,8},{10,11... | collective-permute-start | bytes 417800 | tf_op jit(solution)/shard_map/ppermute | solution.py:449
  7.3 5.9 %collective-permute-start.2 = (f32[136,256]{1,0:T(8,128)S(1)}, f32[136,256]{1,0:T(8,128)S(1)}, u32[]{:S(2)}, u32[]{:S(2)}) collective-permute-start(f32[136,256]{1,0:T(8,128)S(1)} %get-tuple-element.46), channel_id=1, source_target_pairs={{0,6},{1,7},{2,4},{3,5},{4,2},{5,3},{6,0},{7,1},{8,14},{9,15},{10,... | collective-permute-start | bytes 417800 | tf_op jit(solution)/shard_map/ppermute | solution.py:449
  7.7 5.6 %collective-permute-start.3 = (f32[136,256]{1,0:T(8,128)S(1)}, f32[136,256]{1,0:T(8,128)S(1)}, u32[]{:S(2)}, u32[]{:S(2)}) collective-permute-start(f32[136,256]{1,0:T(8,128)S(1)} %get-tuple-element.47), channel_id=1, source_target_pairs={{0,2},{1,3},{2,0},{3,1},{4,6},{5,7},{6,4},{7,5},{8,16},{9,17},{10,... | collective-permute-start | bytes 417800 | tf_op jit(solution)/shard_map/ppermute | solution.py:449
  9.0 4.3 %collective-permute-start.4 = (f32[136,256]{1,0:T(8,128)S(1)}, f32[136,256]{1,0:T(8,128)S(1)}, u32[]{:S(2)}, u32[]{:S(2)}) collective-permute-start(f32[136,256]{1,0:T(8,128)S(1)} %get-tuple-element.48), channel_id=1, source_target_pairs={{0,2},{1,3},{2,0},{3,1},{4,6},{5,7},{6,4},{7,5},{8,10},{9,11},{10,... | collective-permute-start | bytes 417800 | tf_op jit(solution)/shard_map/ppermute | solution.py:449
  13.6 2.0 %collective-permute-start.5 = (f32[64,256]{1,0:T(8,128)S(1)}, f32[64,256]{1,0:T(8,128)S(1)}, u32[]{:S(2)}, u32[]{:S(2)}) collective-permute-start(f32[64,256]{1,0:T(8,128)S(1)} %get-tuple-element.52), channel_id=1, source_target_pairs={{0,2},{1,3},{2,0},{3,1},{4,6},{5,7},{6,4},{7,5},{8,10},{9,11},{10,... | collective-permute-start | bytes 196616 | tf_op jit(solution)/shard_map/ppermute | solution.py:503
  13.8 5.2 %collective-permute-start.7 = (f32[16,256]{1,0:T(8,128)S(1)}, f32[16,256]{1,0:T(8,128)S(1)}, u32[]{:S(2)}, u32[]{:S(2)}) collective-permute-start(f32[16,256]{1,0:T(8,128)S(1)} %get-tuple-element.54.own.root), channel_id=1, source_target_pairs={{0,8},{1,9},{2,10},{3,11},{4,12},{5,13},{6,14},{7,15},{8,0},{9,1},... | collective-permute-start | bytes 49160 | tf_op jit(solution)/shard_map/ppermute | solution.py:445
  15.6 4.7 %collective-permute-start.6 = (f32[16,256]{1,0:T(8,128)S(1)}, f32[16,256]{1,0:T(8,128)S(1)}, u32[]{:S(2)}, u32[]{:S(2)}) collective-permute-start(f32[16,256]{1,0:T(8,128)S(1)} %core_sum.2), channel_id=1, source_target_pairs={{0,16},{1,17},{2,26},{3,27},{4,20},{5,21},{6,30},{7,31},{8,24},{9,... | collective-permute-start | bytes 49160 | tf_op jit(solution)/shard_map/ppermute | solution.py:445
  20.5 4.8 %collective-permute-start.10 = (f32[48,256]{1,0:T(8,128)S(1)}, f32[48,256]{1,0:T(8,128)S(1)}, u32[]{:S(2)}, u32[]{:S(2)}) collective-permute-start(f32[48,256]{1,0:T(8,128)S(1)} %root_part.1.first), channel_id=1, source_target_pairs={{0,7},{1,6},{2,5},{3,4},{4,3},{5,2},{6,1},{7,0},{8,15},{9,14},{10,... | collective-permute-start | bytes 147464 | tf_op jit(solution)/shard_map/ppermute | solution.py:554
  21.3 4.0 %collective-permute-start.9 = (f32[48,256]{1,0:T(8,128)S(1)}, f32[48,256]{1,0:T(8,128)S(1)}, u32[]{:S(2)}, u32[]{:S(2)}) collective-permute-start(f32[48,256]{1,0:T(8,128)S(1)} %root_part.1.first), channel_id=1, source_target_pairs={{0,6},{1,7},{2,4},{3,5},{4,2},{5,3},{6,0},{7,1},{8,14},{9,15},{10,... | collective-permute-start | bytes 147464 | tf_op jit(solution)/shard_map/ppermute | solution.py:554
  22.2 4.1 %collective-permute-start.8 = (f32[48,256]{1,0:T(8,128)S(1)}, f32[48,256]{1,0:T(8,128)S(1)}, u32[]{:S(2)}, u32[]{:S(2)}) collective-permute-start(f32[48,256]{1,0:T(8,128)S(1)} %root_part.1.first), channel_id=1, source_target_pairs={{0,3},{1,2},{2,1},{3,0},{4,7},{5,6},{6,5},{7,4},{8,11},{9,10},{10,... | collective-permute-start | bytes 147464 | tf_op jit(solution)/shard_map/ppermute | solution.py:554
  26.5 1.3 %collective-permute-start.11 = (f32[32,256]{1,0:T(8,128)S(1)}, f32[32,256]{1,0:T(8,128)S(1)}, u32[]{:S(2)}, u32[]{:S(2)}) collective-permute-start(f32[32,256]{1,0:T(8,128)S(1)} %get-tuple-element.59), channel_id=1, source_target_pairs={{0,2},{1,3},{2,0},{3,1},{4,6},{5,7},{6,4},{7,5},{8,10},{9,11},{10,... | collective-permute-start | bytes 98312 | tf_op jit(solution)/shard_map/ppermute | solution.py:562
  29.0 3.4 %collective-permute-start.12 = (f32[176,256]{1,0:T(8,128)S(1)}, f32[176,256]{1,0:T(8,128)S(1)}, u32[]{:S(2)}, u32[]{:S(2)}) collective-permute-start(f32[176,256]{1,0:T(8,128)S(1)} %get-tuple-element.64), channel_id=1, source_target_pairs={{0,2},{1,3},{2,0},{3,1},{4,6},{5,7},{6,4},{7,5},{8,10},{9,11},{10,... | collective-permute-start | bytes 540680 | tf_op jit(solution)/shard_map/ppermute | solution.py:449
  29.2 7.7 %collective-permute-start.13 = (f32[176,256]{1,0:T(8,128)S(1)}, f32[176,256]{1,0:T(8,128)S(1)}, u32[]{:S(2)}, u32[]{:S(2)}) collective-permute-start(f32[176,256]{1,0:T(8,128)S(1)} %get-tuple-element.65), channel_id=1, source_target_pairs={{0,8},{1,9},{2,10},{3,11},{4,12},{5,13},{6,14},{7,15},{8,0},{9,1},... | collective-permute-start | bytes 540680 | tf_op jit(solution)/shard_map/ppermute | solution.py:449
  29.7 4.7 %collective-permute-start.14 = (f32[128,256]{1,0:T(8,128)S(1)}, f32[128,256]{1,0:T(8,128)S(1)}, u32[]{:S(2)}, u32[]{:S(2)}) collective-permute-start(f32[128,256]{1,0:T(8,128)S(1)} %get-tuple-element.66), channel_id=1, source_target_pairs={{0,2},{1,3},{2,0},{3,1},{4,6},{5,7},{6,4},{7,5},{8,16},{9,17},{10,... | collective-permute-start | bytes 393224 | tf_op jit(solution)/shard_map/ppermute | solution.py:449
  29.8 5.8 %collective-permute-start.15 = (f32[128,256]{1,0:T(8,128)S(1)}, f32[128,256]{1,0:T(8,128)S(1)}, u32[]{:S(2)}, u32[]{:S(2)}) collective-permute-start(f32[128,256]{1,0:T(8,128)S(1)} %get-tuple-element.67), channel_id=1, source_target_pairs={{0,1},{1,0},{2,3},{3,2},{4,5},{5,4},{6,7},{7,6},{8,9},{9,8},{10,11... | collective-permute-start | bytes 393224 | tf_op jit(solution)/shard_map/ppermute | solution.py:449
  31.5 5.5 %collective-permute-start.16 = (f32[128,256]{1,0:T(8,128)S(1)}, f32[128,256]{1,0:T(8,128)S(1)}, u32[]{:S(2)}, u32[]{:S(2)}) collective-permute-start(f32[128,256]{1,0:T(8,128)S(1)} %get-tuple-element.68), channel_id=1, source_target_pairs={{0,6},{1,7},{2,4},{3,5},{4,2},{5,3},{6,0},{7,1},{8,14},{9,15},{10,... | collective-permute-start | bytes 393224 | tf_op jit(solution)/shard_map/ppermute | solution.py:449
  32.4 5.2 %collective-permute-start.17 = (f32[48,256]{1,0:T(8,128)S(1)}, f32[48,256]{1,0:T(8,128)S(1)}, u32[]{:S(2)}, u32[]{:S(2)}) collective-permute-start(f32[48,256]{1,0:T(8,128)S(1)} %core_sum.3), channel_id=1, source_target_pairs={{0,16},{1,17},{2,26},{3,27},{4,20},{5,21},{6,30},{7,31},{8,24},{9,... | collective-permute-start | bytes 147464 | tf_op jit(solution)/shard_map/ppermute | solution.py:445
  37.9 4.5 %collective-permute-start.20 = (f32[48,256]{1,0:T(8,128)S(1)}, f32[48,256]{1,0:T(8,128)S(1)}, u32[]{:S(2)}, u32[]{:S(2)}) collective-permute-start(f32[48,256]{1,0:T(8,128)S(1)} %coarse_root.1.first), channel_id=1, source_target_pairs={{0,7},{1,6},{2,5},{3,4},{4,3},{5,2},{6,1},{7,0},{8,15},{9,14},{10,... | collective-permute-start | bytes 147464 | tf_op jit(solution)/shard_map/ppermute | solution.py:554
  39.7 4.0 %collective-permute-start.19 = (f32[48,256]{1,0:T(8,128)S(1)}, f32[48,256]{1,0:T(8,128)S(1)}, u32[]{:S(2)}, u32[]{:S(2)}) collective-permute-start(f32[48,256]{1,0:T(8,128)S(1)} %coarse_root.1.first), channel_id=1, source_target_pairs={{0,6},{1,7},{2,4},{3,5},{4,2},{5,3},{6,0},{7,1},{8,14},{9,15},{10,... | collective-permute-start | bytes 147464 | tf_op jit(solution)/shard_map/ppermute | solution.py:554
  40.1 3.5 %collective-permute-start.18 = (f32[48,256]{1,0:T(8,128)S(1)}, f32[48,256]{1,0:T(8,128)S(1)}, u32[]{:S(2)}, u32[]{:S(2)}) collective-permute-start(f32[48,256]{1,0:T(8,128)S(1)} %coarse_root.1.first), channel_id=1, source_target_pairs={{0,3},{1,2},{2,1},{3,0},{4,7},{5,6},{6,5},{7,4},{8,11},{9,10},{10,... | collective-permute-start | bytes 147464 | tf_op jit(solution)/shard_map/ppermute | solution.py:554
  43.8 1.7 %collective-permute-start.21 = (f32[32,256]{1,0:T(8,128)S(1)}, f32[32,256]{1,0:T(8,128)S(1)}, u32[]{:S(2)}, u32[]{:S(2)}) collective-permute-start(f32[32,256]{1,0:T(8,128)S(1)} %get-tuple-element.72), channel_id=1, source_target_pairs={{0,2},{1,3},{2,0},{3,1},{4,6},{5,7},{6,4},{7,5},{8,10},{9,11},{10,... | collective-permute-start | bytes 98312 | tf_op jit(solution)/shard_map/ppermute | solution.py:562
  (3 other events, 24.5 us)

commit v12 on v10

--- a/solution.py
+++ b/solution.py
@@ -133,8 +133,8 @@
     messages, (order, start, local_iter, mapped, sems) = more[: len(swaps)], more[len(swaps) :]
     pairs = [(order_hbm, order), (start_hbm, start)] + list(zip(hbm, held))
     copies = [pltpu.make_async_copy(*pair, sems.at[k]) for k, pair in enumerate(pairs)]
-    for copy in copies:
-        copy.start()
+    for k, copy in enumerate(copies):
+        copy.start(priority=int(k == 2))
     height, lanes = placed.shape[0] // FACES, placed.shape[1]
     copies[0].wait()
     copies[1].wait()

time: 46.7 us -> 46.9 us (level)
  no operation moved by 1% of the time
where the time goes in v12:
time: 46.9 us; the launch traced here: 46.7 us
  starting transfers between devices  22.6 us (48%)
  waiting for transfers between devices  13.5 us (29%)
  Pallas kernels  10.5 us (22%)
    pallas_call x15, Pallas kernels, call(): pl.pallas_call(body, out_shape=[item(shape, dtype) for item, shape, dtype...  10.5 us
    ppermute x10, starting transfers between devices, exchange(): lax.ppermute(message, AXES, swap_pairs(sizes, dim, odd))  9.77 us
    ppermute x3, starting transfers between devices, along(): return lax.ppermute(value, AXES, pairs)  6.4 us
    ppermute x6, starting transfers between devices, per_device(): pieces.append(lax.ppermute(message, AXES, moves))  5.83 us
    ppermute x6, waiting for transfers between devices, per_device(): pieces.append(lax.ppermute(message, AXES, moves))  5.81 us
    ppermute x10, waiting for transfers between devices, exchange(): lax.ppermute(message, AXES, swap_pairs(sizes, dim, odd))  3.93 us
    ppermute x3, waiting for transfers between devices, along(): return lax.ppermute(value, AXES, pairs)  2.93 us
  transfers between devices with their start and end apart: 22, of which 12 were waited for; matrix products, arithmetic and copies ran while one was open for 0% of the time, Pallas kernels for 9%

profile of v12, /device:TPU:0, one launch (start us, length us, event | category | flops | bytes accessed | tf_op | source)
XLA Modules:
  0.0 46.7 jit_solution(2382918425200393689)
XLA Ops:
  0.0 2.7 %first_product.1 = (bf16[1024,1024]{1,0:T(8,128)(2,1)S(1)}, f32[32,1024]{1,0:T(8,128)S(1)}, f32[16,32]{1,0:T(8,128)S(1)}, f32[1024,256]{1,0:T(8,128)S(1)}, f32[1...) custom-call(s32[1,8]{1,0:T(1,128)} %bitcast.23, ...), custom_call_target="tpu_custom_call" | custom-call | tf_op jit(solution)/shard_map/first_product/pallas_call | solution.py:106
  2.7 3.1 %collective-permute-start = (f32[136,256]{1,0:T(8,128)S(1)}, f32[136,256]{1,0:T(8,128)S(1)}, u32[]{:S(2)}, u32[]{:S(2)}) collective-permute-start(f32[136,256]{1,0:T(8,128)S(1)} %get-tuple-element.44), channel_id=1, source_target_pairs={{0,8},{1,9},{2,10},{3,11},{4,12},{5,13},{6,14},{7,15},{8,0},{9,1},... | collective-permute-start | bytes 417800 | tf_op jit(solution)/shard_map/ppermute | solution.py:449
  5.8 1.5 %collective-permute-start.1 = (f32[136,256]{1,0:T(8,128)S(1)}, f32[136,256]{1,0:T(8,128)S(1)}, u32[]{:S(2)}, u32[]{:S(2)}) collective-permute-start(f32[136,256]{1,0:T(8,128)S(1)} %get-tuple-element.45), channel_id=1, source_target_pairs={{0,1},{1,0},{2,3},{3,2},{4,5},{5,4},{6,7},{7,6},{8,9},{9,8},{10,11... | collective-permute-start | bytes 417800 | tf_op jit(solution)/shard_map/ppermute | solution.py:449
  7.7 1.2 %collective-permute-start.3 = (f32[136,256]{1,0:T(8,128)S(1)}, f32[136,256]{1,0:T(8,128)S(1)}, u32[]{:S(2)}, u32[]{:S(2)}) collective-permute-start(f32[136,256]{1,0:T(8,128)S(1)} %get-tuple-element.47), channel_id=1, source_target_pairs={{0,2},{1,3},{2,0},{3,1},{4,6},{5,7},{6,4},{7,5},{8,16},{9,17},{10,... | collective-permute-start | bytes 417800 | tf_op jit(solution)/shard_map/ppermute | solution.py:449
  8.9 2.9 %constants.1 = (bf16[1024,96]{1,0:T(8,128)(2,1)S(1)}, f32[1024,128]{1,0:T(8,128)S(1)}, bf16[96,640]{1,0:T(8,128)(2,1)S(1)}, bf16[1024,1024]{1,0:T(8,128)(2,1)S(1...) custom-call(s32[1,8]{1,0:T(1,128)} %bitcast.24, ...), custom_call_target="tpu_custom_call" | custom-call | tf_op jit(solution)/shard_map/constants/pallas_call | solution.py:106
  11.8 1.4 %collective-permute-done.2.more_2_ = f32[136,256]{1,0:T(8,128)S(1)} collective-permute-done((f32[136,256]{1,0:T(8,128)S(1)}, f32[136,256]{1,0:T(8,128)S(1)}, u32[]{:S(2)}, u32[]{:S(2)}) %collective-permute-start.2) | collective-permute-done | bytes 139296 | tf_op jit(solution)/shard_map/ppermute | solution.py:449
  13.7 1.8 %collective-permute-start.7 = (f32[16,256]{1,0:T(8,128)S(1)}, f32[16,256]{1,0:T(8,128)S(1)}, u32[]{:S(2)}, u32[]{:S(2)}) collective-permute-start(f32[16,256]{1,0:T(8,128)S(1)} %get-tuple-element.54.own.root), channel_id=1, source_target_pairs={{0,8},{1,9},{2,10},{3,11},{4,12},{5,13},{6,14},{7,15},{8,0},{9,1},... | collective-permute-start | bytes 49160 | tf_op jit(solution)/shard_map/ppermute | solution.py:445
  15.5 2.6 %collective-permute-start.6 = (f32[16,256]{1,0:T(8,128)S(1)}, f32[16,256]{1,0:T(8,128)S(1)}, u32[]{:S(2)}, u32[]{:S(2)}) collective-permute-start(f32[16,256]{1,0:T(8,128)S(1)} %core_sum.2), channel_id=1, source_target_pairs={{0,16},{1,17},{2,26},{3,27},{4,20},{5,21},{6,30},{7,31},{8,24},{9,... | collective-permute-start | bytes 49160 | tf_op jit(solution)/shard_map/ppermute | solution.py:445
  18.2 2.1 %collective-permute-done.6.more_0_ = f32[16,256]{1,0:T(8,128)S(1)} collective-permute-done((f32[16,256]{1,0:T(8,128)S(1)}, f32[16,256]{1,0:T(8,128)S(1)}, u32[]{:S(2)}, u32[]{:S(2)}) %collective-permute-start.6) | collective-permute-done | bytes 16416 | tf_op jit(solution)/shard_map/ppermute | solution.py:445
  20.4 0.9 %collective-permute-start.10 = (f32[48,256]{1,0:T(8,128)S(1)}, f32[48,256]{1,0:T(8,128)S(1)}, u32[]{:S(2)}, u32[]{:S(2)}) collective-permute-start(f32[48,256]{1,0:T(8,128)S(1)} %root_part.1.first), channel_id=1, source_target_pairs={{0,7},{1,6},{2,5},{3,4},{4,3},{5,2},{6,1},{7,0},{8,15},{9,14},{10,... | collective-permute-start | bytes 147464 | tf_op jit(solution)/shard_map/ppermute | solution.py:554
  21.3 0.8 %collective-permute-start.9 = (f32[48,256]{1,0:T(8,128)S(1)}, f32[48,256]{1,0:T(8,128)S(1)}, u32[]{:S(2)}, u32[]{:S(2)}) collective-permute-start(f32[48,256]{1,0:T(8,128)S(1)} %root_part.1.first), channel_id=1, source_target_pairs={{0,6},{1,7},{2,4},{3,5},{4,2},{5,3},{6,0},{7,1},{8,14},{9,15},{10,... | collective-permute-start | bytes 147464 | tf_op jit(solution)/shard_map/ppermute | solution.py:554
  23.1 2.1 %collective-permute-done.10.more_2_ = f32[48,256]{1,0:T(8,128)S(1)} collective-permute-done((f32[48,256]{1,0:T(8,128)S(1)}, f32[48,256]{1,0:T(8,128)S(1)}, u32[]{:S(2)}, u32[]{:S(2)}) %collective-permute-start.10) | collective-permute-done | bytes 49184 | tf_op jit(solution)/shard_map/ppermute | solution.py:554
  25.2 1.0 %collective-permute-done.8.more_0_ = f32[48,256]{1,0:T(8,128)S(1)} collective-permute-done((f32[48,256]{1,0:T(8,128)S(1)}, f32[48,256]{1,0:T(8,128)S(1)}, u32[]{:S(2)}, u32[]{:S(2)}) %collective-permute-start.8) | collective-permute-done | bytes 49184 | tf_op jit(solution)/shard_map/ppermute | solution.py:554
  27.7 1.2 %update_product.1 = (f32[1024,256]{1,0:T(8,128)S(1)}, f32[1024,256]{1,0:T(8,128)S(1)}, f32[32,256]{1,0:T(8,128)S(1)}, f32[48,256]{1,0:T(8,128)S(1)}, f32[176,256...) custom-call(f32[1024,256]{1,0:T(8,128)S(1)} %base.2, ...), custom_call_target="tpu_custom_call" | custom-call | tf_op jit(solution)/shard_map/update_product/pallas_call | solution.py:106
  29.9 1.6 %collective-permute-start.15 = (f32[128,256]{1,0:T(8,128)S(1)}, f32[128,256]{1,0:T(8,128)S(1)}, u32[]{:S(2)}, u32[]{:S(2)}) collective-permute-start(f32[128,256]{1,0:T(8,128)S(1)} %get-tuple-element.67), channel_id=1, source_target_pairs={{0,1},{1,0},{2,3},{3,2},{4,5},{5,4},{6,7},{7,6},{8,9},{9,8},{10,11... | collective-permute-start | bytes 393224 | tf_op jit(solution)/shard_map/ppermute | solution.py:449
  31.5 1.0 %collective-permute-start.16 = (f32[128,256]{1,0:T(8,128)S(1)}, f32[128,256]{1,0:T(8,128)S(1)}, u32[]{:S(2)}, u32[]{:S(2)}) collective-permute-start(f32[128,256]{1,0:T(8,128)S(1)} %get-tuple-element.68), channel_id=1, source_target_pairs={{0,6},{1,7},{2,4},{3,5},{4,2},{5,3},{6,0},{7,1},{8,14},{9,15},{10,... | collective-permute-start | bytes 393224 | tf_op jit(solution)/shard_map/ppermute | solution.py:449
  32.5 2.0 %collective-permute-start.17 = (f32[48,256]{1,0:T(8,128)S(1)}, f32[48,256]{1,0:T(8,128)S(1)}, u32[]{:S(2)}, u32[]{:S(2)}) collective-permute-start(f32[48,256]{1,0:T(8,128)S(1)} %core_sum.3), channel_id=1, source_target_pairs={{0,16},{1,17},{2,26},{3,27},{4,20},{5,21},{6,30},{7,31},{8,24},{9,... | collective-permute-start | bytes 147464 | tf_op jit(solution)/shard_map/ppermute | solution.py:445
  34.5 1.3 %collective-permute-done.15.more_3_ = f32[128,256]{1,0:T(8,128)S(1)} collective-permute-done((f32[128,256]{1,0:T(8,128)S(1)}, f32[128,256]{1,0:T(8,128)S(1)}, u32[]{:S(2)}, u32[]{:S(2)}) %collective-permute-start.15) | collective-permute-done | bytes 131104 | tf_op jit(solution)/shard_map/ppermute | solution.py:449
  35.8 1.2 %collective-permute-done.16.more_4_ = f32[128,256]{1,0:T(8,128)S(1)} collective-permute-done((f32[128,256]{1,0:T(8,128)S(1)}, f32[128,256]{1,0:T(8,128)S(1)}, u32[]{:S(2)}, u32[]{:S(2)}) %collective-permute-start.16) | collective-permute-done | bytes 131104 | tf_op jit(solution)/shard_map/ppermute | solution.py:449
  38.1 1.3 %collective-permute-start.20 = (f32[48,256]{1,0:T(8,128)S(1)}, f32[48,256]{1,0:T(8,128)S(1)}, u32[]{:S(2)}, u32[]{:S(2)}) collective-permute-start(f32[48,256]{1,0:T(8,128)S(1)} %coarse_root.1.first), channel_id=1, source_target_pairs={{0,7},{1,6},{2,5},{3,4},{4,3},{5,2},{6,1},{7,0},{8,15},{9,14},{10,... | collective-permute-start | bytes 147464 | tf_op jit(solution)/shard_map/ppermute | solution.py:554
  39.4 0.9 %collective-permute-start.19 = (f32[48,256]{1,0:T(8,128)S(1)}, f32[48,256]{1,0:T(8,128)S(1)}, u32[]{:S(2)}, u32[]{:S(2)}) collective-permute-start(f32[48,256]{1,0:T(8,128)S(1)} %coarse_root.1.first), channel_id=1, source_target_pairs={{0,6},{1,7},{2,4},{3,5},{4,2},{5,3},{6,0},{7,1},{8,14},{9,15},{10,... | collective-permute-start | bytes 147464 | tf_op jit(solution)/shard_map/ppermute | solution.py:554
  40.3 1.1 %collective-permute-start.18 = (f32[48,256]{1,0:T(8,128)S(1)}, f32[48,256]{1,0:T(8,128)S(1)}, u32[]{:S(2)}, u32[]{:S(2)}) collective-permute-start(f32[48,256]{1,0:T(8,128)S(1)} %coarse_root.1.first), channel_id=1, source_target_pairs={{0,3},{1,2},{2,1},{3,0},{4,7},{5,6},{6,5},{7,4},{8,11},{9,10},{10,... | collective-permute-start | bytes 147464 | tf_op jit(solution)/shard_map/ppermute | solution.py:554
  41.4 1.2 %collective-permute-done.20.more_2_ = f32[48,256]{1,0:T(8,128)S(1)} collective-permute-done((f32[48,256]{1,0:T(8,128)S(1)}, f32[48,256]{1,0:T(8,128)S(1)}, u32[]{:S(2)}, u32[]{:S(2)}) %collective-permute-start.20) | collective-permute-done | bytes 49184 | tf_op jit(solution)/shard_map/ppermute | solution.py:554
  45.5 1.2 %update_last.1 = f32[1024,256]{1,0:T(8,128)} custom-call(f32[1024,256]{1,0:T(8,128)S(1)} %base.3, bf16[1024,96]{1,0:T(8,128)(2,1)S(1)} %get-tuple-element.49.modes_t, f32[32,256]{1,0:T(8,128)S(1)} %get-tuple-element.71.own, f32[32,256]{1,0:T(8,128)S(1)} %collective-permute-done.21.other), custom_call_target="tpu_custom_call" | custom-call | tf_op jit(solution)/shard_map/update_last/pallas_call | solution.py:106
  (45 shorter events, 8.4 us)
Async XLA Ops:
  2.7 9.1 %collective-permute-start = (f32[136,256]{1,0:T(8,128)S(1)}, f32[136,256]{1,0:T(8,128)S(1)}, u32[]{:S(2)}, u32[]{:S(2)}) collective-permute-start(f32[136,256]{1,0:T(8,128)S(1)} %get-tuple-element.44), channel_id=1, source_target_pairs={{0,8},{1,9},{2,10},{3,11},{4,12},{5,13},{6,14},{7,15},{8,0},{9,1},... | collective-permute-start | bytes 417800 | tf_op jit(solution)/shard_map/ppermute | solution.py:449
  5.8 6.0 %collective-permute-start.1 = (f32[136,256]{1,0:T(8,128)S(1)}, f32[136,256]{1,0:T(8,128)S(1)}, u32[]{:S(2)}, u32[]{:S(2)}) collective-permute-start(f32[136,256]{1,0:T(8,128)S(1)} %get-tuple-element.45), channel_id=1, source_target_pairs={{0,1},{1,0},{2,3},{3,2},{4,5},{5,4},{6,7},{7,6},{8,9},{9,8},{10,11... | collective-permute-start | bytes 417800 | tf_op jit(solution)/shard_map/ppermute | solution.py:449
  7.3 5.9 %collective-permute-start.2 = (f32[136,256]{1,0:T(8,128)S(1)}, f32[136,256]{1,0:T(8,128)S(1)}, u32[]{:S(2)}, u32[]{:S(2)}) collective-permute-start(f32[136,256]{1,0:T(8,128)S(1)} %get-tuple-element.46), channel_id=1, source_target_pairs={{0,6},{1,7},{2,4},{3,5},{4,2},{5,3},{6,0},{7,1},{8,14},{9,15},{10,... | collective-permute-start | bytes 417800 | tf_op jit(solution)/shard_map/ppermute | solution.py:449
  7.7 5.6 %collective-permute-start.3 = (f32[136,256]{1,0:T(8,128)S(1)}, f32[136,256]{1,0:T(8,128)S(1)}, u32[]{:S(2)}, u32[]{:S(2)}) collective-permute-start(f32[136,256]{1,0:T(8,128)S(1)} %get-tuple-element.47), channel_id=1, source_target_pairs={{0,2},{1,3},{2,0},{3,1},{4,6},{5,7},{6,4},{7,5},{8,16},{9,17},{10,... | collective-permute-start | bytes 417800 | tf_op jit(solution)/shard_map/ppermute | solution.py:449
  8.9 4.3 %collective-permute-start.4 = (f32[136,256]{1,0:T(8,128)S(1)}, f32[136,256]{1,0:T(8,128)S(1)}, u32[]{:S(2)}, u32[]{:S(2)}) collective-permute-start(f32[136,256]{1,0:T(8,128)S(1)} %get-tuple-element.48), channel_id=1, source_target_pairs={{0,2},{1,3},{2,0},{3,1},{4,6},{5,7},{6,4},{7,5},{8,10},{9,11},{10,... | collective-permute-start | bytes 417800 | tf_op jit(solution)/shard_map/ppermute | solution.py:449
  8.9 11.4 %copy-start.3 = (f32[16,64]{1,0:T(8,128)S(1)}, f32[16,64]{1,0:T(8,128)}, u32[]{:S(2)}) copy-start(f32[16,64]{1,0:T(8,128)} %root_inverse.3) | copy-start | bytes 12292
  8.9 17.7 %copy-start.1 = (bf16[1,1,1,1024,256]{4,3,2,1,0:T(8,128)(2,1)S(1)}, bf16[1,1,1,1024,256]{4,3,2,1,0:T(8,128)(2,1)}, u32[]{:S(2)}) copy-start(bf16[1,1,1,1024,256]{4,3,2,1,0:T(8,128)(2,1)} %param.10) | copy-start | bytes 1572868
  13.5 2.0 %collective-permute-start.5 = (f32[64,256]{1,0:T(8,128)S(1)}, f32[64,256]{1,0:T(8,128)S(1)}, u32[]{:S(2)}, u32[]{:S(2)}) collective-permute-start(f32[64,256]{1,0:T(8,128)S(1)} %get-tuple-element.52), channel_id=1, source_target_pairs={{0,2},{1,3},{2,0},{3,1},{4,6},{5,7},{6,4},{7,5},{8,10},{9,11},{10,... | collective-permute-start | bytes 196616 | tf_op jit(solution)/shard_map/ppermute | solution.py:503
  13.7 4.5 %collective-permute-start.7 = (f32[16,256]{1,0:T(8,128)S(1)}, f32[16,256]{1,0:T(8,128)S(1)}, u32[]{:S(2)}, u32[]{:S(2)}) collective-permute-start(f32[16,256]{1,0:T(8,128)S(1)} %get-tuple-element.54.own.root), channel_id=1, source_target_pairs={{0,8},{1,9},{2,10},{3,11},{4,12},{5,13},{6,14},{7,15},{8,0},{9,1},... | collective-permute-start | bytes 49160 | tf_op jit(solution)/shard_map/ppermute | solution.py:445
  15.5 4.7 %collective-permute-start.6 = (f32[16,256]{1,0:T(8,128)S(1)}, f32[16,256]{1,0:T(8,128)S(1)}, u32[]{:S(2)}, u32[]{:S(2)}) collective-permute-start(f32[16,256]{1,0:T(8,128)S(1)} %core_sum.2), channel_id=1, source_target_pairs={{0,16},{1,17},{2,26},{3,27},{4,20},{5,21},{6,30},{7,31},{8,24},{9,... | collective-permute-start | bytes 49160 | tf_op jit(solution)/shard_map/ppermute | solution.py:445
  20.4 4.8 %collective-permute-start.10 = (f32[48,256]{1,0:T(8,128)S(1)}, f32[48,256]{1,0:T(8,128)S(1)}, u32[]{:S(2)}, u32[]{:S(2)}) collective-permute-start(f32[48,256]{1,0:T(8,128)S(1)} %root_part.1.first), channel_id=1, source_target_pairs={{0,7},{1,6},{2,5},{3,4},{4,3},{5,2},{6,1},{7,0},{8,15},{9,14},{10,... | collective-permute-start | bytes 147464 | tf_op jit(solution)/shard_map/ppermute | solution.py:554
  21.3 4.0 %collective-permute-start.9 = (f32[48,256]{1,0:T(8,128)S(1)}, f32[48,256]{1,0:T(8,128)S(1)}, u32[]{:S(2)}, u32[]{:S(2)}) collective-permute-start(f32[48,256]{1,0:T(8,128)S(1)} %root_part.1.first), channel_id=1, source_target_pairs={{0,6},{1,7},{2,4},{3,5},{4,2},{5,3},{6,0},{7,1},{8,14},{9,15},{10,... | collective-permute-start | bytes 147464 | tf_op jit(solution)/shard_map/ppermute | solution.py:554
  22.1 4.2 %collective-permute-start.8 = (f32[48,256]{1,0:T(8,128)S(1)}, f32[48,256]{1,0:T(8,128)S(1)}, u32[]{:S(2)}, u32[]{:S(2)}) collective-permute-start(f32[48,256]{1,0:T(8,128)S(1)} %root_part.1.first), channel_id=1, source_target_pairs={{0,3},{1,2},{2,1},{3,0},{4,7},{5,6},{6,5},{7,4},{8,11},{9,10},{10,... | collective-permute-start | bytes 147464 | tf_op jit(solution)/shard_map/ppermute | solution.py:554
  26.5 1.3 %collective-permute-start.11 = (f32[32,256]{1,0:T(8,128)S(1)}, f32[32,256]{1,0:T(8,128)S(1)}, u32[]{:S(2)}, u32[]{:S(2)}) collective-permute-start(f32[32,256]{1,0:T(8,128)S(1)} %get-tuple-element.56), channel_id=1, source_target_pairs={{0,2},{1,3},{2,0},{3,1},{4,6},{5,7},{6,4},{7,5},{8,10},{9,11},{10,... | collective-permute-start | bytes 98312 | tf_op jit(solution)/shard_map/ppermute | solution.py:562
  28.9 3.6 %collective-permute-start.12 = (f32[176,256]{1,0:T(8,128)S(1)}, f32[176,256]{1,0:T(8,128)S(1)}, u32[]{:S(2)}, u32[]{:S(2)}) collective-permute-start(f32[176,256]{1,0:T(8,128)S(1)} %get-tuple-element.64), channel_id=1, source_target_pairs={{0,2},{1,3},{2,0},{3,1},{4,6},{5,7},{6,4},{7,5},{8,10},{9,11},{10,... | collective-permute-start | bytes 540680 | tf_op jit(solution)/shard_map/ppermute | solution.py:449
  29.4 7.6 %collective-permute-start.13 = (f32[176,256]{1,0:T(8,128)S(1)}, f32[176,256]{1,0:T(8,128)S(1)}, u32[]{:S(2)}, u32[]{:S(2)}) collective-permute-start(f32[176,256]{1,0:T(8,128)S(1)} %get-tuple-element.65), channel_id=1, source_target_pairs={{0,8},{1,9},{2,10},{3,11},{4,12},{5,13},{6,14},{7,15},{8,0},{9,1},... | collective-permute-start | bytes 540680 | tf_op jit(solution)/shard_map/ppermute | solution.py:449
  29.9 4.6 %collective-permute-start.14 = (f32[128,256]{1,0:T(8,128)S(1)}, f32[128,256]{1,0:T(8,128)S(1)}, u32[]{:S(2)}, u32[]{:S(2)}) collective-permute-start(f32[128,256]{1,0:T(8,128)S(1)} %get-tuple-element.66), channel_id=1, source_target_pairs={{0,2},{1,3},{2,0},{3,1},{4,6},{5,7},{6,4},{7,5},{8,16},{9,17},{10,... | collective-permute-start | bytes 393224 | tf_op jit(solution)/shard_map/ppermute | solution.py:449
  29.9 5.9 %collective-permute-start.15 = (f32[128,256]{1,0:T(8,128)S(1)}, f32[128,256]{1,0:T(8,128)S(1)}, u32[]{:S(2)}, u32[]{:S(2)}) collective-permute-start(f32[128,256]{1,0:T(8,128)S(1)} %get-tuple-element.67), channel_id=1, source_target_pairs={{0,1},{1,0},{2,3},{3,2},{4,5},{5,4},{6,7},{7,6},{8,9},{9,8},{10,11... | collective-permute-start | bytes 393224 | tf_op jit(solution)/shard_map/ppermute | solution.py:449
  31.5 5.5 %collective-permute-start.16 = (f32[128,256]{1,0:T(8,128)S(1)}, f32[128,256]{1,0:T(8,128)S(1)}, u32[]{:S(2)}, u32[]{:S(2)}) collective-permute-start(f32[128,256]{1,0:T(8,128)S(1)} %get-tuple-element.68), channel_id=1, source_target_pairs={{0,6},{1,7},{2,4},{3,5},{4,2},{5,3},{6,0},{7,1},{8,14},{9,15},{10,... | collective-permute-start | bytes 393224 | tf_op jit(solution)/shard_map/ppermute | solution.py:449
  32.5 5.3 %collective-permute-start.17 = (f32[48,256]{1,0:T(8,128)S(1)}, f32[48,256]{1,0:T(8,128)S(1)}, u32[]{:S(2)}, u32[]{:S(2)}) collective-permute-start(f32[48,256]{1,0:T(8,128)S(1)} %core_sum.3), channel_id=1, source_target_pairs={{0,16},{1,17},{2,26},{3,27},{4,20},{5,21},{6,30},{7,31},{8,24},{9,... | collective-permute-start | bytes 147464 | tf_op jit(solution)/shard_map/ppermute | solution.py:445
  38.1 4.5 %collective-permute-start.20 = (f32[48,256]{1,0:T(8,128)S(1)}, f32[48,256]{1,0:T(8,128)S(1)}, u32[]{:S(2)}, u32[]{:S(2)}) collective-permute-start(f32[48,256]{1,0:T(8,128)S(1)} %coarse_root.1.first), channel_id=1, source_target_pairs={{0,7},{1,6},{2,5},{3,4},{4,3},{5,2},{6,1},{7,0},{8,15},{9,14},{10,... | collective-permute-start | bytes 147464 | tf_op jit(solution)/shard_map/ppermute | solution.py:554
  39.4 4.0 %collective-permute-start.19 = (f32[48,256]{1,0:T(8,128)S(1)}, f32[48,256]{1,0:T(8,128)S(1)}, u32[]{:S(2)}, u32[]{:S(2)}) collective-permute-start(f32[48,256]{1,0:T(8,128)S(1)} %coarse_root.1.first), channel_id=1, source_target_pairs={{0,6},{1,7},{2,4},{3,5},{4,2},{5,3},{6,0},{7,1},{8,14},{9,15},{10,... | collective-permute-start | bytes 147464 | tf_op jit(solution)/shard_map/ppermute | solution.py:554
  40.3 3.7 %collective-permute-start.18 = (f32[48,256]{1,0:T(8,128)S(1)}, f32[48,256]{1,0:T(8,128)S(1)}, u32[]{:S(2)}, u32[]{:S(2)}) collective-permute-start(f32[48,256]{1,0:T(8,128)S(1)} %coarse_root.1.first), channel_id=1, source_target_pairs={{0,3},{1,2},{2,1},{3,0},{4,7},{5,6},{6,5},{7,4},{8,11},{9,10},{10,... | collective-permute-start | bytes 147464 | tf_op jit(solution)/shard_map/ppermute | solution.py:554
  44.2 1.3 %collective-permute-start.21 = (f32[32,256]{1,0:T(8,128)S(1)}, f32[32,256]{1,0:T(8,128)S(1)}, u32[]{:S(2)}, u32[]{:S(2)}) collective-permute-start(f32[32,256]{1,0:T(8,128)S(1)} %get-tuple-element.72), channel_id=1, source_target_pairs={{0,2},{1,3},{2,0},{3,1},{4,6},{5,7},{6,4},{7,5},{8,10},{9,11},{10,... | collective-permute-start | bytes 98312 | tf_op jit(solution)/shard_map/ppermute | solution.py:562
  (3 other events, 28.4 us)
